TPU v7x, 32 devices: a whole 2x2x4 slice. The times are simulated.
32 devices in a mesh: ctx: 16 (over z, y, core), exp: 2 (over x).
Axes of the slice: x: 2, y: 2, z: 4, core: 2. Of those that a mesh axis runs over, the one named last changes fastest.
Arguments:
- hidden_in: bfloat16 [2, 3072, 1024], P('exp', 'ctx'), may hold values from -6 to 6
- queries: bfloat16 [2, 3072, 1024], P('exp', 'ctx'), may hold values from -128 to 128
- key_proj: bfloat16 [2, 3072, 256], P('exp', 'ctx'), may hold values from -16 to 16
- value_proj: bfloat16 [2, 3072, 256], P('exp', 'ctx'), may hold values from -6 to 6
- tile_mask: int32 [2, 96, 96], P('exp', 'ctx'), may hold values from 0 to 1, as said below
- out_weight: bfloat16 [1024, 1024], replicated, may hold values from -0.1875 to 0.1875
- moe_gain: float32 [1024], replicated, may hold values from 0.1 to 1.9
- gate_weight: bfloat16 [8, 1024, 1792], P('exp', 'ctx'), may hold values from -0.1875 to 0.1875
- up_weight: bfloat16 [8, 1024, 1792], P('exp', 'ctx'), may hold values from -0.1875 to 0.1875
- down_weight: bfloat16 [8, 1024, 1792], P('exp', 'ctx'), may hold values from -0.125 to 0.125
- expert_ids: int32 [2, 3072, 2], P('exp', 'ctx'), may hold values from 0 to 7, all different within a row; in each aligned block of 192 rows (0 to 191, 192 to 383, ..., all dimensions but the last counted through in order) at most 72 rows name the same one
- gate_probs: float32 [2, 3072, 2], P('exp', 'ctx'), may hold values from 0.05 to 0.95, as said below
Outputs:
- attention_out: bfloat16 [2, 3072, 1024], P('exp', 'ctx')
- layer_out: bfloat16 [2, 3072, 1024], P('exp', 'ctx')
Inputs may be any that keep to these rules, and one draw needn't show every extreme that they name: `expert_ids`: within one block of 192 tokens of a sequence (the tokens of one device), no expert is named by more than 72 pairs; the 2 ids of a token differ. tile_mask[s, i, i] = 1 for every tile i. `gate_probs`: the 2 weights of a token sum to 1.
All inputs are finite; a program needn't handle non-finite values.
Results may differ from a plain program's by a relative error of at most 0.0065.
Values may be sent and summed in bfloat16 or wider, within the bound.
No kernel may reach another device: no remote copies, remote signals or barrier semaphores. Data moves between devices by JAX's collectives and lax.ppermute only.
A program may use at most 128 MiB of HBM per device.

v0:
```python
import jax
import jax.numpy as jnp
from jax import lax
from jax.sharding import PartitionSpec as P

D = 1024
HEADS = 8
KV_HEADS = 2
EXPERTS = 8
TOP = 2
TILE = 32
CAP = 72


def rms_scale(row_block, gain):
    widened = row_block.astype(jnp.float32)
    inverse = lax.rsqrt(jnp.mean(widened * widened, axis=-1, keepdims=True) + 1e-05)
    return widened * inverse * gain


def shards(
    hidden_in,
    queries,
    key_proj,
    value_proj,
    tile_mask,
    out_weight,
    moe_gain,
    gate_weight,
    up_weight,
    down_weight,
    expert_ids,
    gate_probs,
):
    query_rows = queries[0]
    row_count = query_rows.shape[0]
    groups = HEADS // KV_HEADS
    head_size = D // HEADS
    query_heads = query_rows.reshape(row_count, KV_HEADS, groups, head_size)
    mask_block = tile_mask[0]
    key_piece = lax.all_gather(key_proj[0], "ctx", axis=0, tiled=True)
    value_piece = lax.all_gather(value_proj[0], "ctx", axis=0, tiled=True)
    piece_rows = key_piece.shape[0]
    running_max = jnp.full((KV_HEADS, groups, row_count, 1), -1e30, jnp.float32)
    allowed = jnp.repeat(jnp.repeat(mask_block, TILE, axis=0), TILE, axis=1) > 0
    key_heads = key_piece.reshape(piece_rows, KV_HEADS, head_size)
    value_heads = value_piece.reshape(piece_rows, KV_HEADS, head_size)
    scores = jnp.einsum(
        "qkgd,rkd->kgqr", query_heads, key_heads, preferred_element_type=jnp.float32
    ) * head_size ** (-0.5)
    scores = jnp.where(allowed, scores, -1e30)
    newest_max = jnp.maximum(running_max, jnp.max(scores, axis=-1, keepdims=True))
    weights = jnp.where(allowed, jnp.exp(scores - newest_max), 0.0)
    denominator = jnp.sum(weights, axis=-1, keepdims=True)
    accumulated = jnp.einsum(
        "kgqr,rkd->kgqd",
        weights.astype(jnp.bfloat16),
        value_heads,
        preferred_element_type=jnp.float32,
    )
    running_max, denominator, accumulated = (newest_max, denominator, accumulated)
    attended = (
        (accumulated / denominator).transpose(2, 0, 1, 3).reshape(row_count, D).astype(jnp.bfloat16)
    )
    projected = jnp.dot(attended, out_weight, preferred_element_type=jnp.float32)
    attention_out = projected.astype(jnp.bfloat16)
    residual = (hidden_in[0].astype(jnp.float32) + projected).astype(jnp.bfloat16)
    normed = rms_scale(residual, moe_gain).astype(jnp.bfloat16)
    id_row = expert_ids[0].reshape(-1)
    onehot = (id_row[:, None] == jnp.arange(EXPERTS, dtype=jnp.int32)[None, :]).astype(jnp.int32)
    before = jnp.cumsum(onehot, axis=0) - onehot
    slot_index = jnp.sum(before * onehot, axis=1)
    target = id_row * CAP + slot_index
    selector = (jnp.arange(EXPERTS * CAP, dtype=jnp.int32)[:, None] == target[None, :]).astype(
        jnp.bfloat16
    )
    repeated = jnp.repeat(normed, TOP, axis=0)
    outgoing = (
        jnp.dot(selector, repeated, preferred_element_type=jnp.float32)
        .astype(jnp.bfloat16)
        .reshape(EXPERTS, CAP, D)
    )
    arrived = lax.all_to_all(outgoing, "exp", split_axis=0, concat_axis=1, tiled=True)
    gate_piece = lax.all_gather(gate_weight, "ctx", axis=1, tiled=True)
    up_piece = lax.all_gather(up_weight, "ctx", axis=1, tiled=True)
    gate_sum = jnp.einsum("esd,edf->esf", arrived, gate_piece, preferred_element_type=jnp.float32)
    up_sum = jnp.einsum("esd,edf->esf", arrived, up_piece, preferred_element_type=jnp.float32)
    hidden = (jax.nn.silu(gate_sum) * up_sum).astype(jnp.bfloat16)
    expert_rows = jnp.einsum(
        "esf,edf->esd",
        hidden,
        lax.all_gather(down_weight, "ctx", axis=1, tiled=True),
        preferred_element_type=jnp.float32,
    ).astype(jnp.bfloat16)
    returned = lax.all_to_all(expert_rows, "exp", split_axis=1, concat_axis=0, tiled=True)
    picked = jnp.take(returned.reshape(EXPERTS * CAP, D), target, axis=0).reshape(row_count, TOP, D)
    mixture = jnp.sum(picked.astype(jnp.float32) * gate_probs[0][:, :, None], axis=1)
    layer_out = (residual.astype(jnp.float32) + mixture).astype(jnp.bfloat16)
    return (attention_out[None], layer_out[None])


def solution(mesh):
    return jax.shard_map(
        shards,
        mesh=mesh,
        in_specs=(
            P("exp", "ctx", None),
            P("exp", "ctx", None),
            P("exp", "ctx", None),
            P("exp", "ctx", None),
            P("exp", "ctx", None),
            P(),
            P(),
            P("exp", "ctx", None),
            P("exp", "ctx", None),
            P("exp", "ctx", None),
            P("exp", "ctx", None),
            P("exp", "ctx", None),
        ),
        out_specs=(P("exp", "ctx", None), P("exp", "ctx", None)),
        check_vma=False,
    )
```

profile of v0, /device:TPU:0, one launch (start us, length us, event | category | flops | bytes accessed | tf_op | source)
XLA Modules:
  0.0 489.6 jit_solution(9833595486412155853)
XLA Ops:
  7.2 0.7 all-gather.16.cloned.1.call-update
  8.0 0.7 all-gather.14.cloned.1.call-update
  8.7 0.7 all-gather.8.cloned.1.call-update
  10.6 0.8 copy.70
  11.7 0.7 broadcast_compare_fusion
  12.7 1.1 copy.63
  13.9 1.3 reshape_squeeze.6
  15.1 0.9 reduce-window.6
  16.4 36.3 %all-gather.16.cloned.1.call-done = bf16[1,3072,256]{2,1,0:T(8,128)(2,1)} async-done(((bf16[1,192,256]{2,1,0:T(8,128)(2,1)}), bf16[1,3072,256]{2,1,0:T(8,128)(2,1)}) %all-gather.16.cloned.1.call-update) | async-done | bytes 1572880 | tf_op jit(solution)/shard_map/all_gather | solution.py:42
  52.7 2.6 copy.67
  55.3 38.3 %all-gather.14.cloned.1.call-done = bf16[1,3072,256]{2,1,0:T(8,128)(2,1)} async-done(((bf16[1,192,256]{2,1,0:T(8,128)(2,1)}), bf16[1,3072,256]{2,1,0:T(8,128)(2,1)}) %all-gather.14.cloned.1.call-update) | async-done | bytes 1572880 | tf_op jit(solution)/shard_map/all_gather | solution.py:41
  93.6 2.6 copy.64
  96.2 10.4 %fusion = (f32[2,4,192]{2,1,0:T(4,128)S(1)}, f32[2,3072,192,4]{1,2,3,0:T(8,128)}) fusion(pred[192,3072]{1,0:T(8,128)(4,1)S(1)} %copy.63, bf16[3072,2,128,1]{0,2,3,1:T(8,128)(2,1)} %bitcast.81, bf16[192,2,4,128]{3,2,1,0:T(4,128)(2,1)S(1)} %reshape_squeeze.6), kind=kOutput, calls=%fused_computation.3 | convolution fusion | flops 1222113792 | bytes 21436416 | tf_op jit(solution)/shard_map/qkgd,rkd->kgqr/dot_general | solution.py:48
  106.6 11.9 %fusion.1 = f32[2,4,192]{2,1,0:T(4,128)S(1)} fusion(f32[2,3072,192,4]{1,2,3,0:T(8,128)} %get-tuple-element.6, f32[2,4,192]{2,1,0:T(4,128)S(1)} %broadcast_maximum_fusion, pred[192,3072]{1,0:T(8,128)(4,1)S(1)} %copy.63), kind=kLoop, calls=%fused_computation.4 | loop fusion | flops 23591424 | bytes 19476480 | tf_op jit(solution)/shard_map/reduce_sum | solution.py:54
  118.5 9.4 %fusion.15 = bf16[192,2,4,128]{3,0,2,1:T(8,128)(2,1)S(1)} fusion(bf16[3072,2,128,1]{0,2,3,1:T(8,128)(2,1)} %bitcast.87, f32[2,3072,192,4]{1,2,3,0:T(8,128)} %get-tuple-element.6, f32[2,4,192]{2,1,0:T(4,128)S(1)} %broadcast_maximum_fusion, pred[192,3072]{1,0:T(8,128)(4,1)S(1)} %copy.63, f32[192,2,4]{0,2,1:T(4,128)S(1)} %bitcast.89), kind=kOutput, calls=%fused_computation.20 | convolution fusion | flops 1231945728 | bytes 21442560 | tf_op jit(solution)/shard_map/kgqr,rkd->kgqd/dot_general | solution.py:55
  128.5 1.4 fusion.18
  129.9 0.7 copy-done.2
  131.5 1.8 convolution_convert_fusion
  133.3 3.6 all-to-all-start
  137.0 15.5 %all-to-all-done = bf16[8,72,1024]{2,1,0:T(8,128)(2,1)S(1)} async-done(((bf16[8,72,1024]{2,1,0:T(8,128)(2,1)}), bf16[8,72,1024]{2,1,0:T(8,128)(2,1)S(1)}, u32[]{:S(2)}, u32[]{:S(2)}) %all-to-all-start) | async-done | bytes 1179680 | tf_op jit(solution)/shard_map/all_to_all | solution.py:83
  152.7 56.0 %all-gather.8.cloned.1.call-done = bf16[4,1024,1792]{2,1,0:T(8,128)(2,1)} async-done(((bf16[4,64,1792]{2,1,0:T(8,128)(2,1)}), bf16[4,1024,1792]{2,1,0:T(8,128)(2,1)}) %all-gather.8.cloned.1.call-update) | async-done | bytes 14680080 | tf_op jit(solution)/shard_map/all_gather | solution.py:84
  208.7 9.4 %fusion.36 = f32[4,144,1792]{2,1,0:T(8,128)} fusion(bf16[4,144,1024]{2,1,0:T(8,128)(2,1)S(1)} %bitcast.82, bf16[4,1024,1792]{2,1,0:T(8,128)(2,1)} %all-gather.8.cloned.1.call-done), kind=kOutput, calls=%fused_computation.56 | convolution fusion | flops 2113929216 | bytes 19988480 | tf_op jit(solution)/shard_map/esd,edf->esf/dot_general | solution.py:86
  218.1 104.8 %all-gather.12.cloned.1.call-done = bf16[4,1024,1792]{2,1,0:T(8,128)(2,1)} async-done(((bf16[4,64,1792]{2,1,0:T(8,128)(2,1)}), bf16[4,1024,1792]{2,1,0:T(8,128)(2,1)}) %all-gather.12.cloned.1.call-update) | async-done | bytes 14680080 | tf_op jit(solution)/shard_map/all_gather | solution.py:92
  322.9 114.2 %all-gather.10.cloned.1.call-done = bf16[4,1024,1792]{2,1,0:T(8,128)(2,1)} async-done(((bf16[4,64,1792]{2,1,0:T(8,128)(2,1)}), bf16[4,1024,1792]{2,1,0:T(8,128)(2,1)}) %all-gather.10.cloned.1.call-update) | async-done | bytes 14680080 | tf_op jit(solution)/shard_map/all_gather | solution.py:85
  437.1 14.4 %fusion.8 = bf16[4,144,1024]{2,1,0:T(8,128)(2,1)S(1)} fusion(bf16[4,1024,1792]{2,1,0:T(8,128)(2,1)} %all-gather.12.cloned.1.call-done, f32[4,144,1792]{2,1,0:T(8,128)} %fusion.36, bf16[4,144,1024]{2,1,0:T(8,128)(2,1)S(1)} %bitcast.83, bf16[4,1024,1792]{2,1,0:T(8,128)(2,1)} %all-gather.10.cloned.1.call-done), kind=kOutput, calls=%fused_computation.14 | convolution fusion | flops 4234641408 | bytes 35848192 | tf_op jit(solution)/shard_map/esf,edf->esd/dot_general | solution.py:89
  451.5 1.9 copy.75
  453.4 3.6 all-to-all-start.1
  457.8 15.0 %all-to-all-done.1 = bf16[4,144,1024]{2,0,1:T(4,128)(2,1)S(1)} async-done(((bf16[4,144,1024]{2,0,1:T(4,128)(2,1)}), bf16[4,144,1024]{2,0,1:T(4,128)(2,1)S(1)}, u32[]{:S(2)}, u32[]{:S(2)}) %all-to-all-start.1) | async-done | bytes 1179680 | tf_op jit(solution)/shard_map/all_to_all | solution.py:95
  473.1 2.9 gather_fusion
  476.0 2.1 gather.7
  478.1 3.1 multiply_reduce_fusion
  481.3 1.8 fusion.24
  (50 shorter events, 5.0 us)
Async XLA Ops:
  7.2 121.3 %copy-start = (bf16[1024,1024]{1,0:T(8,128)(2,1)S(1)}, bf16[1024,1024]{1,0:T(8,128)(2,1)}, u32[]{:S(2)}) copy-start(bf16[1024,1024]{1,0:T(8,128)(2,1)} %param.17) | copy-start | bytes 6291460
  7.2 45.5 %all-gather.16.cloned.1.call-start = ((), (), s32[]{:S(2)}) async-start(), calls=%async_computation.6 | async-start | bytes 1671168 | tf_op jit(solution)/shard_map/all_gather | solution.py:42
  7.9 85.7 %all-gather.14.cloned.1.call-start = ((), (), s32[]{:S(2)}) async-start(), calls=%async_computation.5 | async-start | bytes 1671168 | tf_op jit(solution)/shard_map/all_gather | solution.py:41
  8.7 200.0 %all-gather.8.cloned.1.call-start = ((), (), s32[]{:S(2)}) async-start(), calls=%async_computation.2 | async-start | bytes 15597568 | tf_op jit(solution)/shard_map/all_gather | solution.py:84
  9.4 313.5 %all-gather.12.cloned.1.call-start = ((), (), s32[]{:S(2)}) async-start(), calls=%async_computation.4 | async-start | bytes 15597568 | tf_op jit(solution)/shard_map/all_gather | solution.py:92
  10.0 427.1 %all-gather.10.cloned.1.call-start = ((), (), s32[]{:S(2)}) async-start(), calls=%async_computation.3 | async-start | bytes 15597568 | tf_op jit(solution)/shard_map/all_gather | solution.py:85
  118.5 10.0 %copy-start.3 = (bf16[1,192,1024]{2,1,0:T(8,128)(2,1)S(1)}, bf16[1,192,1024]{2,1,0:T(8,128)(2,1)}, u32[]{:S(2)}) copy-start(bf16[1,192,1024]{2,1,0:T(8,128)(2,1)} %param.12) | copy-start | bytes 1179652
  127.9 2.7 copy-start.5
  129.8 0.7 copy-start.2
  133.3 19.3 %all-to-all-start = ((bf16[8,72,1024]{2,1,0:T(8,128)(2,1)}), bf16[8,72,1024]{2,1,0:T(8,128)(2,1)S(1)}, u32[]{:S(2)}, u32[]{:S(2)}) async-start(bf16[8,72,1024]{2,1,0:T(8,128)(2,1)} %bitcast.14), calls=%async_computation | async-start | bytes 2359296 | tf_op jit(solution)/shard_map/all_to_all | solution.py:83
  451.5 5.6 %copy-start.4 = (s32[1,192,2]{1,2,0:T(2,128)S(1)}, s32[1,192,2]{1,2,0:T(2,128)}, u32[]{:S(2)}) copy-start(s32[1,192,2]{1,2,0:T(2,128)} %param.22) | copy-start | bytes 4612
  451.5 6.1 %copy-start.6 = (f32[1,192,2]{1,2,0:T(2,128)S(1)}, f32[1,192,2]{1,2,0:T(2,128)}, u32[]{:S(2)}) copy-start(f32[1,192,2]{1,2,0:T(2,128)} %param.23) | copy-start | bytes 4612
  453.4 19.3 %all-to-all-start.1 = ((bf16[4,144,1024]{2,0,1:T(4,128)(2,1)}), bf16[4,144,1024]{2,0,1:T(4,128)(2,1)S(1)}, u32[]{:S(2)}, u32[]{:S(2)}) async-start(bf16[4,144,1024]{2,0,1:T(4,128)(2,1)} %copy.75), calls=%async_computation.1 | async-start | bytes 2359296 | tf_op jit(solution)/shard_map/all_to_all | solution.py:95
  473.1 10.0 %copy-start.1 = (bf16[1024,1024]{1,0:T(8,128)(2,1)S(1)}, bf16[1024,1024]{1,0:T(8,128)(2,1)}, u32[]{:S(2)}) copy-start(bf16[1024,1024]{1,0:T(8,128)(2,1)} %param.17) | copy-start | bytes 6291460
Sparse Core Ops, SparseCore 0:
  10.3 42.3 all-gather.15
  55.0 38.5 all-gather.13
  95.9 112.7 all-gather.7
  210.8 112.0 all-gather.11
  325.0 112.0 all-gather.9
where the time goes:
time: 490 us
  waiting for transfers between devices  383 us (78%)
  matrix products  46.7 us (10%)
  local copies, waits for them, and re-layouts  19.5 us (4%)
  other arithmetic  18.8 us (4%)
  between operations  14.1 us (3%)
  starting transfers between devices  7.39 us (2%)
    all_gather x1, waiting for transfers between devices, shards(): up_piece = lax.all_gather(up_weight, 'ctx', axis=1, tiled=True)  114 us
    all_gather x1, waiting for transfers between devices, shards(): lax.all_gather(down_weight, 'ctx', axis=1, tiled=True)  105 us
    all_gather x1, waiting for transfers between devices, shards(): gate_piece = lax.all_gather(gate_weight, 'ctx', axis=1, tiled=True)  56 us
    all_gather x1, waiting for transfers between devices, shards(): key_piece = lax.all_gather(key_proj[0], 'ctx', axis=0, tiled=True)  38.3 us
    all_gather x1, waiting for transfers between devices, shards(): value_piece = lax.all_gather(value_proj[0], 'ctx', axis=0, tiled=True)  36.3 us
    all_to_all x1, waiting for transfers between devices, shards(): lax.all_to_all(outgoing, 'exp', split_axis=0, concat_axis=1, tiled=True)  15.5 us
    all_to_all x1, waiting for transfers between devices, shards(): lax.all_to_all(expert_rows, 'exp', split_axis=1, concat_axis=0, tiled=True)  15 us
    dot_general x1, matrix products, shards(): jnp.einsum('esf,edf->esd', hidden, lax.all_gather(down_weight, 'ctx', axi...  14.4 us
  transfers between devices with their start and end apart: 7, of which 7 were waited for; matrix products, arithmetic and copies ran while one was open for 12% of the time, Pallas kernels for 0%

commit v1 on v0

v1 whole, which is shorter than its diff:
```python
import functools

import jax
import jax.numpy as jnp
from jax import lax
from jax.experimental import pallas as pl
from jax.experimental.pallas import tpu as pltpu
from jax.sharding import Mesh, PartitionSpec as P

D = 1024
HEADS = 8
KV_HEADS = 2
EXPERTS = 8
TOP = 2
TILE = 32
CAP = 72
HEAD = D // HEADS
GROUPS = HEADS // KV_HEADS
KVW = KV_HEADS * HEAD
SLOTS = EXPERTS * CAP
MB = 1 << 20

VMEM = pl.BlockSpec(memory_space=pltpu.VMEM)
SMEM = pl.BlockSpec(memory_space=pltpu.SMEM)
ANY = pl.BlockSpec(memory_space=pl.ANY)


def pack_kernel(planes, place_ref, gate_ref, up_ref, down_ref, *rest):
    outs, sems = rest[:planes], rest[planes]
    plane = place_ref[0]
    copies = []
    for k in range(planes):
        owner = plane ^ k
        for w, ref in enumerate((gate_ref, up_ref, down_ref)):
            copies.append(pltpu.make_async_copy(ref.at[owner], outs[k].at[w], sems.at[3 * k + w]))
    for copy in copies:
        copy.start()
    for copy in copies:
        copy.wait()


def pack(place, gate, up, down):
    planes, rows, ff = gate.shape
    return pl.pallas_call(
        functools.partial(pack_kernel, planes),
        out_shape=[jax.ShapeDtypeStruct((3, rows, ff), gate.dtype)] * planes,
        in_specs=[SMEM, ANY, ANY, ANY],
        out_specs=[ANY] * planes,
        scratch_shapes=[pltpu.SemaphoreType.DMA((3 * planes,))],
        name="pack_weights",
    )(place, gate, up, down)


def attend_kernel(blocks, chunk, live_ref, query_ref, bias_ref, target_ref, out_w_ref, hidden_ref, gain_ref, *rest):
    kv_refs = rest[:blocks]
    attention_ref, residual_ref, outgoing_ref, kv, scores, top, total, acc, attended = rest[blocks:]
    rows = query_ref.shape[0]
    chunks = scores.shape[0]
    for i in range(blocks):
        kv[pl.ds(i * rows, rows), :] = kv_refs[i][...]
    scale = HEAD ** (-0.5)
    for h in range(KV_HEADS):
        heads = [query_ref[:, (h * GROUPS + g) * HEAD : (h * GROUPS + g + 1) * HEAD] for g in range(GROUPS)]
        query = jnp.concatenate(heads, axis=0)
        top[...] = jnp.full(top.shape, -1e30, jnp.float32)
        total[...] = jnp.zeros(total.shape, jnp.float32)
        acc[...] = jnp.zeros(acc.shape, jnp.float32)

        @pl.loop(0, chunks)
        def _(j):
            @pl.when(live_ref[j] > 0)
            def _():
                keys = kv[pl.ds(pl.multiple_of(j * chunk, 128), chunk), h * HEAD : (h + 1) * HEAD]
                s = lax.dot_general(query, keys, (((1,), (1,)), ((), ())), preferred_element_type=jnp.float32)
                s = s.reshape(GROUPS, rows, chunk) + bias_ref[j][None]
                s = s.reshape(GROUPS * rows, chunk)
                scores[j] = s
                best = top[...]
                for c in range(0, chunk, 128):
                    best = jnp.maximum(best, s[:, c : c + 128])
                top[...] = best

        highest = jnp.max(top[...], axis=1, keepdims=True)
        top[...] = jnp.broadcast_to(highest, top.shape)

        @pl.loop(0, chunks)
        def _(j):
            @pl.when(live_ref[j] > 0)
            def _():
                values = kv[pl.ds(pl.multiple_of(j * chunk, 128), chunk), KVW + h * HEAD : KVW + (h + 1) * HEAD]
                high = top[...]
                s = scores[j]
                parts = []
                running = total[...]
                for c in range(0, chunk, 128):
                    w = jnp.exp((s[:, c : c + 128] - high) * scale)
                    running = running + w
                    parts.append(w.astype(jnp.bfloat16))
                total[...] = running
                weights = jnp.concatenate(parts, axis=1)
                acc[...] += jnp.dot(weights, values, preferred_element_type=jnp.float32)

        denominator = jnp.sum(total[...], axis=1, keepdims=True)
        result = (acc[...] / denominator).astype(jnp.bfloat16)
        for g in range(GROUPS):
            col = (h * GROUPS + g) * HEAD
            attended[:, col : col + HEAD] = result[g * rows : (g + 1) * rows]
    projected = jnp.dot(attended[...], out_w_ref[...], preferred_element_type=jnp.float32)
    attention_ref[...] = projected.astype(jnp.bfloat16)
    residual = (hidden_ref[...].astype(jnp.float32) + projected).astype(jnp.bfloat16)
    residual_ref[...] = residual
    wide = residual.astype(jnp.float32)
    inverse = lax.rsqrt(jnp.mean(wide * wide, axis=-1, keepdims=True) + 1e-05)
    normed = (wide * inverse * gain_ref[...]).astype(jnp.bfloat16)
    slot = lax.broadcasted_iota(jnp.int32, (SLOTS, rows), 0)
    chosen = (slot == target_ref[0:1, :]) | (slot == target_ref[1:2, :])
    selector = chosen.astype(jnp.float32).astype(jnp.bfloat16)
    outgoing_ref[...] = jnp.dot(selector, normed, preferred_element_type=jnp.float32).astype(jnp.bfloat16)


def attend(live, query, bias, target, out_w, hidden, gain, blocks):
    rows = query.shape[0]
    chunks, _, chunk = bias.shape
    n = len(blocks)
    return pl.pallas_call(
        functools.partial(attend_kernel, n, chunk),
        out_shape=[
            jax.ShapeDtypeStruct((rows, D), jnp.bfloat16),
            jax.ShapeDtypeStruct((rows, D), jnp.bfloat16),
            jax.ShapeDtypeStruct((SLOTS, D), jnp.bfloat16),
        ],
        in_specs=[SMEM] + [VMEM] * (6 + n),
        out_specs=[VMEM] * 3,
        scratch_shapes=[
            pltpu.VMEM((n * rows, 2 * KVW), jnp.bfloat16),
            pltpu.VMEM((chunks, GROUPS * rows, chunk), jnp.float32),
            pltpu.VMEM((GROUPS * rows, HEAD), jnp.float32),
            pltpu.VMEM((GROUPS * rows, HEAD), jnp.float32),
            pltpu.VMEM((GROUPS * rows, HEAD), jnp.float32),
            pltpu.VMEM((rows, D), jnp.bfloat16),
        ],
        compiler_params=pltpu.CompilerParams(vmem_limit_bytes=48 * MB),
        name="attend",
    )(live, query, bias, target, out_w, hidden, gain, *blocks)


def expert_kernel(planes, shared, place_ref, rows_ref, *rest):
    count = planes * shared
    pieces = rest[:count]
    out_ref, gate, up, down, total, sems = rest[count:]
    depth, ff = pieces[0].shape[1:]
    plane, seat = place_ref[0], place_ref[1]
    copies = [[], [], []]
    for w, full in enumerate((gate, up, down)):
        for m in range(shared):
            for k in range(planes):
                at = ((plane ^ k) * shared + (seat ^ m)) * depth
                target = full.at[pl.ds(pl.multiple_of(at, depth), depth), :]
                n = m * planes + k
                copies[w].append(pltpu.make_async_copy(pieces[n].at[w], target, sems.at[w * count + n]))
    for group in copies:
        for copy in group:
            copy.start()
    for group in copies[:2]:
        for copy in group:
            copy.wait()
    step = 256
    for n, c in enumerate(range(0, ff, step)):
        rows = rows_ref[...]
        gated = jnp.dot(rows, gate[:, c : c + step], preferred_element_type=jnp.float32)
        upper = jnp.dot(rows, up[:, c : c + step], preferred_element_type=jnp.float32)
        hidden = (gated / (1.0 + jnp.exp(-gated)) * upper).astype(jnp.bfloat16)
        if n == 0:
            for copy in copies[2]:
                copy.wait()
        part = lax.dot_general(
            hidden, down[:, c : c + step], (((1,), (1,)), ((), ())), preferred_element_type=jnp.float32
        )
        if n == 0:
            total[...] = part
        else:
            total[...] += part
    out_ref[...] = total[...].astype(jnp.bfloat16)


def run_expert(place, rows, pieces, planes, shared):
    depth, ff = pieces[0].shape[1:]
    count = planes * shared
    return pl.pallas_call(
        functools.partial(expert_kernel, planes, shared),
        out_shape=jax.ShapeDtypeStruct(rows.shape, jnp.bfloat16),
        in_specs=[SMEM, VMEM] + [ANY] * count,
        out_specs=VMEM,
        scratch_shapes=[
            pltpu.VMEM((D, ff), jnp.bfloat16),
            pltpu.VMEM((D, ff), jnp.bfloat16),
            pltpu.VMEM((D, ff), jnp.bfloat16),
            pltpu.VMEM(rows.shape, jnp.float32),
            pltpu.SemaphoreType.DMA((3 * count,)),
        ],
        compiler_params=pltpu.CompilerParams(vmem_limit_bytes=48 * MB),
        name="expert",
    )(place, rows, *pieces)


def combine_kernel(returned_ref, target_ref, probs_ref, residual_ref, out_ref):
    rows = residual_ref.shape[0]
    slot = lax.broadcasted_iota(jnp.int32, (rows, SLOTS), 1)
    returned = returned_ref[...]
    total = jnp.zeros((rows, D), jnp.float32)
    for k in range(TOP):
        selector = (slot == target_ref[:, k : k + 1]).astype(jnp.float32).astype(jnp.bfloat16)
        picked = jnp.dot(selector, returned, preferred_element_type=jnp.float32)
        total = total + picked * probs_ref[:, k : k + 1]
    out_ref[...] = (residual_ref[...].astype(jnp.float32) + total).astype(jnp.bfloat16)


def combine(returned, target, probs, residual):
    return pl.pallas_call(
        combine_kernel,
        out_shape=jax.ShapeDtypeStruct(residual.shape, jnp.bfloat16),
        in_specs=[VMEM] * 4,
        out_specs=VMEM,
        compiler_params=pltpu.CompilerParams(vmem_limit_bytes=32 * MB),
        name="combine",
    )(returned, target, probs, residual)


def slots_of(ids):
    rows = ids.shape[0]
    onehot = (ids[:, :, None] == jnp.arange(EXPERTS, dtype=jnp.int32)).astype(jnp.float32)
    named = jnp.sum(onehot, axis=1)
    earlier = (jnp.arange(rows)[:, None] > jnp.arange(rows)[None, :]).astype(jnp.bfloat16)
    before = jnp.dot(earlier, named.astype(jnp.bfloat16), preferred_element_type=jnp.float32)
    slot = jnp.sum(onehot * before[:, None, :], axis=2).astype(jnp.int32)
    return ids * CAP + slot


def shards(
    planes,
    shared,
    hidden_in,
    queries,
    key_proj,
    value_proj,
    tile_mask,
    out_weight,
    moe_gain,
    gate_weight,
    up_weight,
    down_weight,
    expert_ids,
    gate_probs,
):
    ctx = ("plane", "seat")
    world = planes * shared
    rows = queries.shape[1]
    tiles = rows // TILE
    plane = lax.axis_index("plane")
    seat = lax.axis_index("seat")
    me = plane * shared + seat
    place = jnp.stack([plane, seat]).astype(jnp.int32)

    def swap(x, bit):
        return lax.ppermute(x, ctx, [(i, i ^ bit) for i in range(world)])

    blocks = {0: jnp.concatenate([key_proj[0], value_proj[0]], axis=1)}
    bit = world // 2
    while bit:
        blocks.update({m | bit: swap(x, bit) for m, x in list(blocks.items())})
        bit //= 2
    packed = pack(place, gate_weight, up_weight, down_weight)
    pieces = {(0, 0): packed[0]}
    for k in range(1, planes):
        pieces[0, k] = swap(packed[k], k * shared)
    bit = shared // 2
    while bit:
        pieces.update({(m | bit, k): swap(x, bit) for (m, k), x in list(pieces.items())})
        bit //= 2

    target = slots_of(expert_ids[0])
    chunk = 2 * rows
    order = me ^ jnp.arange(world)
    mask = jnp.take(tile_mask[0].reshape(tiles, world, tiles), order, axis=1)
    mask = mask.reshape(tiles, world // 2, 2 * tiles).transpose(1, 0, 2)
    live = jnp.max(mask, axis=(1, 2)).astype(jnp.int32)
    bias = jnp.where(mask > 0, 0.0, -1e30).astype(jnp.float32)
    bias = jnp.repeat(jnp.repeat(bias, TILE, axis=1), TILE, axis=2)

    attention_out, residual, outgoing = attend(
        live,
        queries[0],
        bias,
        target.T,
        out_weight,
        hidden_in[0],
        moe_gain[None],
        [blocks[m] for m in range(world)],
    )
    arrived = lax.all_to_all(
        outgoing.reshape(EXPERTS, CAP, D), ("exp", "plane"), split_axis=0, concat_axis=0, tiled=True
    )
    expert_rows = run_expert(
        place,
        arrived.reshape(SLOTS, D),
        [pieces[m, k] for m in range(shared) for k in range(planes)],
        planes,
        shared,
    )
    returned = lax.all_to_all(
        expert_rows.reshape(EXPERTS, CAP, D), ("exp", "plane"), split_axis=0, concat_axis=0, tiled=True
    )
    layer_out = combine(returned.reshape(SLOTS, D), target, gate_probs[0], residual)
    return attention_out[None], layer_out[None]


def solution(mesh):
    n_ctx, n_exp = mesh.shape["ctx"], mesh.shape["exp"]
    planes = EXPERTS // n_exp
    shared = n_ctx // planes
    fine = Mesh(mesh.devices.reshape(planes, shared, n_exp), ("plane", "seat", "exp"))
    split = P("exp", ("plane", "seat"), None)
    return jax.shard_map(
        functools.partial(shards, planes, shared),
        mesh=fine,
        in_specs=(split, split, split, split, split, P(), P(), split, split, split, split, split),
        out_specs=(split, split),
        check_vma=False,
    )
```

time: 490 us -> 278 us (0.57)
  waiting for transfers between devices: 383 us -> 91.9 us
  Pallas kernels: 0 us -> 119 us
  matrix products: 46.7 us -> 0.15 us
  starting transfers between devices: 7.39 us -> 35.7 us
  other arithmetic: 18.8 us -> 3 us
  between operations: 14.1 us -> 0.99 us
  local copies, waits for them, and re-layouts: 19.5 us -> 26.8 us
    all_gather x5 -> x0, waiting for transfers between devices: 350 us -> none  [the longest x1 114 us: shards(): up_piece = lax.all_gather(up_weight, 'ctx', axis=1, tiled=True)]
    pallas_call x0 -> x4, Pallas kernels: none -> 119 us  [the longest x1 85.4 us: pack(): pl.pallas_call(functools.partial(pack_kernel, planes), out_shape=[jax.Sha...]
    ppermute x0 -> x30, waiting for transfers between devices: none -> 57.4 us  [swap(): return lax.ppermute(x, ctx, [(i, i ^ bit) for i in range(world)])]
    dot_general x6 -> x1, matrix products: 46.7 us -> 0.15 us  [slots_of(): jnp.dot(earlier, named.astype(jnp.bfloat16), preferred_element_type=jnp.f...]
    ppermute x0 -> x30, starting transfers between devices: none -> 19.6 us  [swap(): return lax.ppermute(x, ctx, [(i, i ^ bit) for i in range(world)])]
    unnamed x16 -> x80, local copies, waits for them, and re-layouts: 1.58 us -> 19.6 us
    reduce_sum x3 -> x2, other arithmetic: 15.1 us -> 0.05 us  [the longest x1 0.04 us: slots_of(): slot = jnp.sum(onehot * before[:, None, :], axis=2).astype(jnp.int32)]
    all_to_all x2, starting transfers between devices: 7.2 us -> 16 us  [the longest x1 11.5 us: shards(): lax.all_to_all(expert_rows.reshape(EXPERTS, CAP, D), ('exp', 'plane'), sp...]
  transfers between devices with their start and end apart: 7 -> 32, of which waited for: 7 -> 9; matrix products, arithmetic and copies ran while one was open for 12% -> 3% of each run, Pallas kernels for 0% -> 36%
where the time goes in v1:
time: 278 us; the launch traced here: 277 us
  Pallas kernels  119 us (43%)
  waiting for transfers between devices  91.9 us (33%)
  starting transfers between devices  35.7 us (13%)
  local copies, waits for them, and re-layouts  26.8 us (10%)
  other arithmetic  3 us (1%)
    pallas_call x1, Pallas kernels, pack(): pl.pallas_call(functools.partial(pack_kernel, planes), out_shape=[jax.Sha...  85.4 us
    ppermute x30, waiting for transfers between devices, swap(): return lax.ppermute(x, ctx, [(i, i ^ bit) for i in range(world)])  57.4 us
    all_to_all x1, waiting for transfers between devices, shards(): lax.all_to_all(expert_rows.reshape(EXPERTS, CAP, D), ('exp', 'plane'), sp...  29.8 us
    unnamed x80, local copies, waits for them, and re-layouts  19.6 us
    ppermute x30, starting transfers between devices, swap(): return lax.ppermute(x, ctx, [(i, i ^ bit) for i in range(world)])  19.6 us
    pallas_call x1, Pallas kernels, run_expert(): pl.pallas_call(functools.partial(expert_kernel, planes, shared), out_shap...  17.5 us
    pallas_call x1, Pallas kernels, attend(): pl.pallas_call(functools.partial(attend_kernel, n, chunk), out_shape=[jax...  14.2 us
    all_to_all x1, starting transfers between devices, shards(): lax.all_to_all(expert_rows.reshape(EXPERTS, CAP, D), ('exp', 'plane'), sp...  11.5 us
  transfers between devices with their start and end apart: 32, of which 9 were waited for; matrix products, arithmetic and copies ran while one was open for 3% of the time, Pallas kernels for 36%

profile of v1, /device:TPU:0, one launch (start us, length us, event | category | flops | bytes accessed | tf_op | source)
XLA Modules:
  0.0 277.2 jit_solution(8770928866697312428)
XLA Ops:
  0.6 1.0 pad_maximum_fusion.rest_0_
  1.6 4.1 %collective-permute-start.7 = (bf16[192,512]{1,0:T(8,128)(2,1)S(1)}, bf16[192,512]{1,0:T(8,128)(2,1)S(1)}, u32[]{:S(2)}, u32[]{:S(2)}) collective-permute-start(bf16[192,512]{1,0:T(8,128)(2,1)S(1)} %pad_maximum_fusion.rest_0_), channel_id=1, source_target_pairs={{0,16},{2,18},{4,20},{6,22},{8,24},{10,26},{12,28},{14,30},{16,0},... | collective-permute-start | bytes 589832 | tf_op jit(solution)/shard_map/ppermute | solution.py:265
  5.7 1.6 collective-permute-start.3
  7.3 1.5 collective-permute-start.1
  10.9 1.9 broadcast_in_dim.54
  12.8 3.4 %copy.63.bias_ref = f32[8,192,384]{2,1,0:T(8,128)} copy(f32[8,192,384]{1,2,0:T(8,128)} %bitcast.35) | data formatting | bytes 4718592 | tf_op jit(solution)/shard_map/reshape | solution.py:288
  18.1 1.6 collective-permute-start.5
  20.5 3.8 %collective-permute-done.11.rest_12_ = bf16[192,512]{1,0:T(8,128)(2,1)S(1)} collective-permute-done((bf16[192,512]{1,0:T(8,128)(2,1)S(1)}, bf16[192,512]{1,0:T(8,128)(2,1)S(1)}, u32[]{:S(2)}, u32[]{:S(2)}) %collective-permute-start.11) | collective-permute-done | bytes 196640 | tf_op jit(solution)/shard_map/ppermute | solution.py:265
  25.3 4.3 %collective-permute-done.5.rest_6_ = bf16[192,512]{1,0:T(8,128)(2,1)} collective-permute-done((bf16[192,512]{1,0:T(8,128)(2,1)S(1)}, bf16[192,512]{1,0:T(8,128)(2,1)}, u32[]{:S(2)}, u32[]{:S(2)}) %collective-permute-start.5) | collective-permute-done | bytes 196640 | tf_op jit(solution)/shard_map/ppermute | solution.py:265
  30.2 2.9 %collective-permute-done.13.rest_14_ = bf16[192,512]{1,0:T(8,128)(2,1)} collective-permute-done((bf16[192,512]{1,0:T(8,128)(2,1)S(1)}, bf16[192,512]{1,0:T(8,128)(2,1)}, u32[]{:S(2)}, u32[]{:S(2)}) %collective-permute-start.13) | collective-permute-done | bytes 196640 | tf_op jit(solution)/shard_map/ppermute | solution.py:265
  34.5 85.4 %pack_weights.1 = (bf16[3,64,1792]{2,1,0:T(8,128)(2,1)}, bf16[3,64,1792]{2,1,0:T(8,128)(2,1)}, bf16[3,64,1792]{2,1,0:T(8,128)(2,1)}, bf16[3,64,1792]{2,1,0:T(8,128)(2,1)}) custom-call(s32[2]{0:T(128)} %pad_add_fusion.place_ref, bf16[4,64,1792]{2,1,0:T(8,128)(2,1)} %gate_ref.1, bf16[4,64,1792]{2,1,0:T(8,128)(2,1)} %up_ref.1, bf16[4,64,1792]{2,1,0:T(8,128)(2,1)} %down_ref.1), custom_call_target="tpu_custom_call" | custom-call | tf_op jit(solution)/shard_map/pack_weights/pallas_call | solution.py:44
  122.7 1.6 collective-permute-start.15
  125.0 2.1 collective-permute-start.17
  128.1 0.9 copy-done.14
  129.9 0.9 copy-done.18
  130.9 0.9 copy-done.20
  131.8 0.9 copy-done.22
  132.7 0.9 copy-done.24
  135.5 14.2 %attend.1 = (bf16[192,1024]{1,0:T(8,128)(2,1)}, bf16[192,1024]{1,0:T(8,128)(2,1)S(1)}, bf16[576,1024]{1,0:T(8,128)(2,1)}) custom-call(s32[8]{0:T(128)S(1)} %reduce_max.18.live_ref, bf16[192,1024]{1,0:T(8,128)(2,1)S(1)} %bitcast.31, f32[8,192,384]{2,1,0:T(8,128)} %copy.63.bias_ref, s32[2,192]{1,0:T(2,128)S(1)} %copy.64.target_ref, ...), custom_call_target="tpu_custom_call" | custom-call | tf_op jit(solution)/shard_map/attend/pallas_call | solution.py:125
  150.5 4.6 %all-to-all-start = ((bf16[8,72,1024]{2,1,0:T(8,128)(2,1)}), bf16[8,72,1024]{2,1,0:T(8,128)(2,1)}, u32[]{:S(2)}, u32[]{:S(2)}) async-start(bf16[8,72,1024]{2,1,0:T(8,128)(2,1)} %bitcast.14), calls=%async_computation | async-start | bytes 2359296 | tf_op jit(solution)/shard_map/all_to_all | solution.py:300
  155.1 18.3 %collective-permute-done.16.rest_2_ = bf16[3,64,1792]{2,1,0:T(8,128)(2,1)} collective-permute-done((bf16[3,64,1792]{2,1,0:T(8,128)(2,1)}, bf16[3,64,1792]{2,1,0:T(8,128)(2,1)}, u32[]{:S(2)}, u32[]{:S(2)}) %collective-permute-start.16) | collective-permute-done | bytes 688160 | tf_op jit(solution)/shard_map/ppermute | solution.py:265
  173.4 1.5 collective-permute-start.24
  176.0 16.0 %collective-permute-done.24.rest_10_ = bf16[3,64,1792]{2,1,0:T(8,128)(2,1)S(1)} collective-permute-done((bf16[3,64,1792]{2,1,0:T(8,128)(2,1)}, bf16[3,64,1792]{2,1,0:T(8,128)(2,1)S(1)}, u32[]{:S(2)}, u32[]{:S(2)}) %collective-permute-start.24) | collective-permute-done | bytes 688160 | tf_op jit(solution)/shard_map/ppermute | solution.py:265
  192.0 11.7 %collective-permute-done.25.rest_11_ = bf16[3,64,1792]{2,1,0:T(8,128)(2,1)S(1)} collective-permute-done((bf16[3,64,1792]{2,1,0:T(8,128)(2,1)}, bf16[3,64,1792]{2,1,0:T(8,128)(2,1)S(1)}, u32[]{:S(2)}, u32[]{:S(2)}) %collective-permute-start.25) | collective-permute-done | bytes 688160 | tf_op jit(solution)/shard_map/ppermute | solution.py:265
  208.7 4.7 %all-to-all-done = bf16[8,72,1024]{2,1,0:T(8,128)(2,1)} async-done(((bf16[8,72,1024]{2,1,0:T(8,128)(2,1)}), bf16[8,72,1024]{2,1,0:T(8,128)(2,1)}, u32[]{:S(2)}, u32[]{:S(2)}) %all-to-all-start) | async-done | bytes 1179680 | tf_op jit(solution)/shard_map/all_to_all | solution.py:300
  213.4 1.1 copy-done.2
  214.5 1.1 copy-done.4
  215.6 1.1 copy-done.6
  216.7 17.5 %expert.1 = bf16[576,1024]{1,0:T(8,128)(2,1)} custom-call(s32[2]{0:T(128)S(1)} %copy-done.30, bf16[576,1024]{1,0:T(8,128)(2,1)} %bitcast.15.rows_ref, bf16[3,64,1792]{2,1,0:T(8,128)(2,1)S(1)} %copy-done, bf16[3,64,1792]{2,1,0:T(8,128)(2,1)S(1)} %collective-permute-done.15.rest_1_, bf16[3,64,1792]{2,1,0:T(8,128)(2,1)} %collective-permute-done.16.rest_2_, ...), custom_call_target="tpu_custom_call" | custom-call | tf_op jit(solution)/shard_map/expert/pallas_call | solution.py:189
  234.2 11.5 %all-to-all-start.1 = ((bf16[8,72,1024]{2,1,0:T(8,128)(2,1)}), bf16[8,72,1024]{2,1,0:T(8,128)(2,1)S(1)}, u32[]{:S(2)}, u32[]{:S(2)}) async-start(bf16[8,72,1024]{2,1,0:T(8,128)(2,1)} %bitcast.36), calls=%async_computation.1 | async-start | bytes 2359296 | tf_op jit(solution)/shard_map/all_to_all | solution.py:310
  245.8 29.8 %all-to-all-done.1 = bf16[8,72,1024]{2,1,0:T(8,128)(2,1)S(1)} async-done(((bf16[8,72,1024]{2,1,0:T(8,128)(2,1)}), bf16[8,72,1024]{2,1,0:T(8,128)(2,1)S(1)}, u32[]{:S(2)}, u32[]{:S(2)}) %all-to-all-start.1) | async-done | bytes 1179680 | tf_op jit(solution)/shard_map/all_to_all | solution.py:310
  275.6 1.6 combine.1
  (152 shorter events, 21.9 us)
Async XLA Ops:
  1.6 15.3 %collective-permute-start.7 = (bf16[192,512]{1,0:T(8,128)(2,1)S(1)}, bf16[192,512]{1,0:T(8,128)(2,1)S(1)}, u32[]{:S(2)}, u32[]{:S(2)}) collective-permute-start(bf16[192,512]{1,0:T(8,128)(2,1)S(1)} %pad_maximum_fusion.rest_0_), channel_id=1, source_target_pairs={{0,16},{2,18},{4,20},{6,22},{8,24},{10,26},{12,28},{14,30},{16,0},... | collective-permute-start | bytes 589832 | tf_op jit(solution)/shard_map/ppermute | solution.py:265
  5.7 12.4 %collective-permute-start.3 = (bf16[192,512]{1,0:T(8,128)(2,1)S(1)}, bf16[192,512]{1,0:T(8,128)(2,1)S(1)}, u32[]{:S(2)}, u32[]{:S(2)}) collective-permute-start(bf16[192,512]{1,0:T(8,128)(2,1)S(1)} %pad_maximum_fusion.rest_0_), channel_id=1, source_target_pairs={{0,8},{2,10},{4,12},{6,14},{8,0},{10,2},{12,4},{14,6},{16,24},{18,... | collective-permute-start | bytes 589832 | tf_op jit(solution)/shard_map/ppermute | solution.py:265
  7.3 10.8 %collective-permute-start.1 = (bf16[192,512]{1,0:T(8,128)(2,1)S(1)}, bf16[192,512]{1,0:T(8,128)(2,1)S(1)}, u32[]{:S(2)}, u32[]{:S(2)}) collective-permute-start(bf16[192,512]{1,0:T(8,128)(2,1)S(1)} %pad_maximum_fusion.rest_0_), channel_id=1, source_target_pairs={{0,4},{2,6},{4,0},{6,2},{8,12},{10,14},{12,8},{14,10},{16,20},{18,... | collective-permute-start | bytes 589832 | tf_op jit(solution)/shard_map/ppermute | solution.py:265
  8.8 10.9 %collective-permute-start = (bf16[192,512]{1,0:T(8,128)(2,1)S(1)}, bf16[192,512]{1,0:T(8,128)(2,1)S(1)}, u32[]{:S(2)}, u32[]{:S(2)}) collective-permute-start(bf16[192,512]{1,0:T(8,128)(2,1)S(1)} %pad_maximum_fusion.rest_0_), channel_id=1, source_target_pairs={{0,2},{2,0},{4,6},{6,4},{8,10},{10,8},{12,14},{14,12},{16,18},{18,... | collective-permute-start | bytes 589832 | tf_op jit(solution)/shard_map/ppermute | solution.py:265
  16.9 7.4 %collective-permute-start.11 = (bf16[192,512]{1,0:T(8,128)(2,1)S(1)}, bf16[192,512]{1,0:T(8,128)(2,1)S(1)}, u32[]{:S(2)}, u32[]{:S(2)}) collective-permute-start(bf16[192,512]{1,0:T(8,128)(2,1)S(1)} %collective-permute-done.7.rest_8_), channel_id=1, source_target_pairs={{0,8},{2,10},{4,12},{6,14},{8,0},{10,2},{12,4},{14,6},{16,24},{18,... | collective-permute-start | bytes 589832 | tf_op jit(solution)/shard_map/ppermute | solution.py:265
  17.5 7.8 %collective-permute-start.9 = (bf16[192,512]{1,0:T(8,128)(2,1)S(1)}, bf16[192,512]{1,0:T(8,128)(2,1)S(1)}, u32[]{:S(2)}, u32[]{:S(2)}) collective-permute-start(bf16[192,512]{1,0:T(8,128)(2,1)S(1)} %collective-permute-done.7.rest_8_), channel_id=1, source_target_pairs={{0,4},{2,6},{4,0},{6,2},{8,12},{10,14},{12,8},{14,10},{16,20},{18,... | collective-permute-start | bytes 589832 | tf_op jit(solution)/shard_map/ppermute | solution.py:265
  18.0 11.6 %collective-permute-start.8 = (bf16[192,512]{1,0:T(8,128)(2,1)S(1)}, bf16[192,512]{1,0:T(8,128)(2,1)S(1)}, u32[]{:S(2)}, u32[]{:S(2)}) collective-permute-start(bf16[192,512]{1,0:T(8,128)(2,1)S(1)} %collective-permute-done.7.rest_8_), channel_id=1, source_target_pairs={{0,2},{2,0},{4,6},{6,4},{8,10},{10,8},{12,14},{14,12},{16,18},{18,... | collective-permute-start | bytes 589832 | tf_op jit(solution)/shard_map/ppermute | solution.py:265
  18.1 11.5 %collective-permute-start.5 = (bf16[192,512]{1,0:T(8,128)(2,1)S(1)}, bf16[192,512]{1,0:T(8,128)(2,1)}, u32[]{:S(2)}, u32[]{:S(2)}) collective-permute-start(bf16[192,512]{1,0:T(8,128)(2,1)S(1)} %collective-permute-done.3.rest_4_), channel_id=1, source_target_pairs={{0,4},{2,6},{4,0},{6,2},{8,12},{10,14},{12,8},{14,10},{16,20},{18,... | collective-permute-start | bytes 589832 | tf_op jit(solution)/shard_map/ppermute | solution.py:265
  20.3 9.8 %collective-permute-start.4 = (bf16[192,512]{1,0:T(8,128)(2,1)S(1)}, bf16[192,512]{1,0:T(8,128)(2,1)S(1)}, u32[]{:S(2)}, u32[]{:S(2)}) collective-permute-start(bf16[192,512]{1,0:T(8,128)(2,1)S(1)} %collective-permute-done.3.rest_4_), channel_id=1, source_target_pairs={{0,2},{2,0},{4,6},{6,4},{8,10},{10,8},{12,14},{14,12},{16,18},{18,... | collective-permute-start | bytes 589832 | tf_op jit(solution)/shard_map/ppermute | solution.py:265
  24.3 8.8 %collective-permute-start.13 = (bf16[192,512]{1,0:T(8,128)(2,1)S(1)}, bf16[192,512]{1,0:T(8,128)(2,1)}, u32[]{:S(2)}, u32[]{:S(2)}) collective-permute-start(bf16[192,512]{1,0:T(8,128)(2,1)S(1)} %collective-permute-done.11.rest_12_), channel_id=1, source_target_pairs={{0,4},{2,6},{4,0},{6,2},{8,12},{10,14},{12,8},{14,10},{16,20},{18,... | collective-permute-start | bytes 589832 | tf_op jit(solution)/shard_map/ppermute | solution.py:265
  25.3 94.7 %collective-permute-start.2 = (bf16[192,512]{1,0:T(8,128)(2,1)S(1)}, bf16[192,512]{1,0:T(8,128)(2,1)S(1)}, u32[]{:S(2)}, u32[]{:S(2)}) collective-permute-start(bf16[192,512]{1,0:T(8,128)(2,1)S(1)} %collective-permute-done.1.rest_2_), channel_id=1, source_target_pairs={{0,2},{2,0},{4,6},{6,4},{8,10},{10,8},{12,14},{14,12},{16,18},{18,... | collective-permute-start | bytes 589832 | tf_op jit(solution)/shard_map/ppermute | solution.py:265
  29.6 91.5 %collective-permute-start.12 = (bf16[192,512]{1,0:T(8,128)(2,1)S(1)}, bf16[192,512]{1,0:T(8,128)(2,1)S(1)}, u32[]{:S(2)}, u32[]{:S(2)}) collective-permute-start(bf16[192,512]{1,0:T(8,128)(2,1)S(1)} %collective-permute-done.11.rest_12_), channel_id=1, source_target_pairs={{0,2},{2,0},{4,6},{6,4},{8,10},{10,8},{12,14},{14,12},{16,18},{18,... | collective-permute-start | bytes 589832 | tf_op jit(solution)/shard_map/ppermute | solution.py:265
  29.6 92.5 %collective-permute-start.10 = (bf16[192,512]{1,0:T(8,128)(2,1)S(1)}, bf16[192,512]{1,0:T(8,128)(2,1)S(1)}, u32[]{:S(2)}, u32[]{:S(2)}) collective-permute-start(bf16[192,512]{1,0:T(8,128)(2,1)S(1)} %collective-permute-done.9.rest_10_), channel_id=1, source_target_pairs={{0,2},{2,0},{4,6},{6,4},{8,10},{10,8},{12,14},{14,12},{16,18},{18,... | collective-permute-start | bytes 589832 | tf_op jit(solution)/shard_map/ppermute | solution.py:265
  30.1 94.2 %collective-permute-start.6 = (bf16[192,512]{1,0:T(8,128)(2,1)}, bf16[192,512]{1,0:T(8,128)(2,1)}, u32[]{:S(2)}, u32[]{:S(2)}) collective-permute-start(bf16[192,512]{1,0:T(8,128)(2,1)} %collective-permute-done.5.rest_6_), channel_id=1, source_target_pairs={{0,2},{2,0},{4,6},{6,4},{8,10},{10,8},{12,14},{14,12},{16,18},{18,... | collective-permute-start | bytes 589832 | tf_op jit(solution)/shard_map/ppermute | solution.py:265
  33.1 91.9 %collective-permute-start.14 = (bf16[192,512]{1,0:T(8,128)(2,1)}, bf16[192,512]{1,0:T(8,128)(2,1)}, u32[]{:S(2)}, u32[]{:S(2)}) collective-permute-start(bf16[192,512]{1,0:T(8,128)(2,1)} %collective-permute-done.13.rest_14_), channel_id=1, source_target_pairs={{0,2},{2,0},{4,6},{6,4},{8,10},{10,8},{12,14},{14,12},{16,18},{18,... | collective-permute-start | bytes 589832 | tf_op jit(solution)/shard_map/ppermute | solution.py:265
  120.6 54.8 %collective-permute-start.22 = (bf16[3,64,1792]{2,1,0:T(8,128)(2,1)}, bf16[3,64,1792]{2,1,0:T(8,128)(2,1)S(1)}, u32[]{:S(2)}, u32[]{:S(2)}) collective-permute-start(bf16[3,64,1792]{2,1,0:T(8,128)(2,1)} %get-tuple-element.11.rest_0_), channel_id=1, source_target_pairs={{0,4},{2,6},{4,0},{6,2},{8,12},{10,14},{12,8},{14,10},{16,20},{18,... | collective-permute-start | bytes 2064392 | tf_op jit(solution)/shard_map/ppermute | solution.py:265
  121.8 53.6 %collective-permute-start.18 = (bf16[3,64,1792]{2,1,0:T(8,128)(2,1)}, bf16[3,64,1792]{2,1,0:T(8,128)(2,1)S(1)}, u32[]{:S(2)}, u32[]{:S(2)}) collective-permute-start(bf16[3,64,1792]{2,1,0:T(8,128)(2,1)} %get-tuple-element.11.rest_0_), channel_id=1, source_target_pairs={{0,2},{2,0},{4,6},{6,4},{8,10},{10,8},{12,14},{14,12},{16,18},{18,... | collective-permute-start | bytes 2064392 | tf_op jit(solution)/shard_map/ppermute | solution.py:265
  122.7 32.3 %collective-permute-start.15 = (bf16[3,64,1792]{2,1,0:T(8,128)(2,1)}, bf16[3,64,1792]{2,1,0:T(8,128)(2,1)S(1)}, u32[]{:S(2)}, u32[]{:S(2)}) collective-permute-start(bf16[3,64,1792]{2,1,0:T(8,128)(2,1)} %get-tuple-element.12), channel_id=1, source_target_pairs={{0,8},{2,10},{4,12},{6,14},{8,0},{10,2},{12,4},{14,6},{16,24},{18,... | collective-permute-start | bytes 2064392 | tf_op jit(solution)/shard_map/ppermute | solution.py:265
  124.3 49.1 %collective-permute-start.16 = (bf16[3,64,1792]{2,1,0:T(8,128)(2,1)}, bf16[3,64,1792]{2,1,0:T(8,128)(2,1)}, u32[]{:S(2)}, u32[]{:S(2)}) collective-permute-start(bf16[3,64,1792]{2,1,0:T(8,128)(2,1)} %get-tuple-element.13), channel_id=1, source_target_pairs={{0,16},{2,18},{4,20},{6,22},{8,24},{10,26},{12,28},{14,30},{16,0},... | collective-permute-start | bytes 2064392 | tf_op jit(solution)/shard_map/ppermute | solution.py:265
  125.0 49.9 %collective-permute-start.17 = (bf16[3,64,1792]{2,1,0:T(8,128)(2,1)}, bf16[3,64,1792]{2,1,0:T(8,128)(2,1)}, u32[]{:S(2)}, u32[]{:S(2)}) collective-permute-start(bf16[3,64,1792]{2,1,0:T(8,128)(2,1)} %get-tuple-element.14), channel_id=1, source_target_pairs={{0,24},{2,26},{4,28},{6,30},{8,16},{10,18},{12,20},{14,22},{16,8},... | collective-permute-start | bytes 2064392 | tf_op jit(solution)/shard_map/ppermute | solution.py:265
  150.5 62.9 %all-to-all-start = ((bf16[8,72,1024]{2,1,0:T(8,128)(2,1)}), bf16[8,72,1024]{2,1,0:T(8,128)(2,1)}, u32[]{:S(2)}, u32[]{:S(2)}) async-start(bf16[8,72,1024]{2,1,0:T(8,128)(2,1)} %bitcast.14), calls=%async_computation | async-start | bytes 2359296 | tf_op jit(solution)/shard_map/all_to_all | solution.py:300
  155.1 20.9 %collective-permute-start.23 = (bf16[3,64,1792]{2,1,0:T(8,128)(2,1)S(1)}, bf16[3,64,1792]{2,1,0:T(8,128)(2,1)S(1)}, u32[]{:S(2)}, u32[]{:S(2)}) collective-permute-start(bf16[3,64,1792]{2,1,0:T(8,128)(2,1)S(1)} %collective-permute-done.15.rest_1_), channel_id=1, source_target_pairs={{0,4},{2,6},{4,0},{6,2},{8,12},{10,14},{12,8},{14,10},{16,20},{18,... | collective-permute-start | bytes 2064392 | tf_op jit(solution)/shard_map/ppermute | solution.py:265
  173.4 18.6 %collective-permute-start.24 = (bf16[3,64,1792]{2,1,0:T(8,128)(2,1)}, bf16[3,64,1792]{2,1,0:T(8,128)(2,1)S(1)}, u32[]{:S(2)}, u32[]{:S(2)}) collective-permute-start(bf16[3,64,1792]{2,1,0:T(8,128)(2,1)} %collective-permute-done.16.rest_2_), channel_id=1, source_target_pairs={{0,4},{2,6},{4,0},{6,2},{8,12},{10,14},{12,8},{14,10},{16,20},{18,... | collective-permute-start | bytes 2064392 | tf_op jit(solution)/shard_map/ppermute | solution.py:265
  174.9 28.8 %collective-permute-start.25 = (bf16[3,64,1792]{2,1,0:T(8,128)(2,1)}, bf16[3,64,1792]{2,1,0:T(8,128)(2,1)S(1)}, u32[]{:S(2)}, u32[]{:S(2)}) collective-permute-start(bf16[3,64,1792]{2,1,0:T(8,128)(2,1)} %collective-permute-done.17.rest_3_), channel_id=1, source_target_pairs={{0,4},{2,6},{4,0},{6,2},{8,12},{10,14},{12,8},{14,10},{16,20},{18,... | collective-permute-start | bytes 2064392 | tf_op jit(solution)/shard_map/ppermute | solution.py:265
  175.4 28.2 %collective-permute-start.26 = (bf16[3,64,1792]{2,1,0:T(8,128)(2,1)S(1)}, bf16[3,64,1792]{2,1,0:T(8,128)(2,1)S(1)}, u32[]{:S(2)}, u32[]{:S(2)}) collective-permute-start(bf16[3,64,1792]{2,1,0:T(8,128)(2,1)S(1)} %collective-permute-done.22.rest_8_), channel_id=1, source_target_pairs={{0,2},{2,0},{4,6},{6,4},{8,10},{10,8},{12,14},{14,12},{16,18},{18,... | collective-permute-start | bytes 2064392 | tf_op jit(solution)/shard_map/ppermute | solution.py:265
  175.5 28.8 %collective-permute-start.19 = (bf16[3,64,1792]{2,1,0:T(8,128)(2,1)S(1)}, bf16[3,64,1792]{2,1,0:T(8,128)(2,1)S(1)}, u32[]{:S(2)}, u32[]{:S(2)}) collective-permute-start(bf16[3,64,1792]{2,1,0:T(8,128)(2,1)S(1)} %collective-permute-done.15.rest_1_), channel_id=1, source_target_pairs={{0,2},{2,0},{4,6},{6,4},{8,10},{10,8},{12,14},{14,12},{16,18},{18,... | collective-permute-start | bytes 2064392 | tf_op jit(solution)/shard_map/ppermute | solution.py:265
  176.0 29.3 %collective-permute-start.20 = (bf16[3,64,1792]{2,1,0:T(8,128)(2,1)}, bf16[3,64,1792]{2,1,0:T(8,128)(2,1)S(1)}, u32[]{:S(2)}, u32[]{:S(2)}) collective-permute-start(bf16[3,64,1792]{2,1,0:T(8,128)(2,1)} %collective-permute-done.16.rest_2_), channel_id=1, source_target_pairs={{0,2},{2,0},{4,6},{6,4},{8,10},{10,8},{12,14},{14,12},{16,18},{18,... | collective-permute-start | bytes 2064392 | tf_op jit(solution)/shard_map/ppermute | solution.py:265
  192.0 14.1 %collective-permute-start.21 = (bf16[3,64,1792]{2,1,0:T(8,128)(2,1)}, bf16[3,64,1792]{2,1,0:T(8,128)(2,1)S(1)}, u32[]{:S(2)}, u32[]{:S(2)}) collective-permute-start(bf16[3,64,1792]{2,1,0:T(8,128)(2,1)} %collective-permute-done.17.rest_3_), channel_id=1, source_target_pairs={{0,2},{2,0},{4,6},{6,4},{8,10},{10,8},{12,14},{14,12},{16,18},{18,... | collective-permute-start | bytes 2064392 | tf_op jit(solution)/shard_map/ppermute | solution.py:265
  203.7 3.3 %collective-permute-start.27 = (bf16[3,64,1792]{2,1,0:T(8,128)(2,1)S(1)}, bf16[3,64,1792]{2,1,0:T(8,128)(2,1)S(1)}, u32[]{:S(2)}, u32[]{:S(2)}) collective-permute-start(bf16[3,64,1792]{2,1,0:T(8,128)(2,1)S(1)} %collective-permute-done.23.rest_9_), channel_id=1, source_target_pairs={{0,2},{2,0},{4,6},{6,4},{8,10},{10,8},{12,14},{14,12},{16,18},{18,... | collective-permute-start | bytes 2064392 | tf_op jit(solution)/shard_map/ppermute | solution.py:265
  203.7 3.3 %collective-permute-start.28 = (bf16[3,64,1792]{2,1,0:T(8,128)(2,1)S(1)}, bf16[3,64,1792]{2,1,0:T(8,128)(2,1)S(1)}, u32[]{:S(2)}, u32[]{:S(2)}) collective-permute-start(bf16[3,64,1792]{2,1,0:T(8,128)(2,1)S(1)} %collective-permute-done.24.rest_10_), channel_id=1, source_target_pairs={{0,2},{2,0},{4,6},{6,4},{8,10},{10,8},{12,14},{14,12},{16,18},{18,... | collective-permute-start | bytes 2064392 | tf_op jit(solution)/shard_map/ppermute | solution.py:265
  205.1 3.6 %collective-permute-start.29 = (bf16[3,64,1792]{2,1,0:T(8,128)(2,1)S(1)}, bf16[3,64,1792]{2,1,0:T(8,128)(2,1)}, u32[]{:S(2)}, u32[]{:S(2)}) collective-permute-start(bf16[3,64,1792]{2,1,0:T(8,128)(2,1)S(1)} %collective-permute-done.25.rest_11_), channel_id=1, source_target_pairs={{0,2},{2,0},{4,6},{6,4},{8,10},{10,8},{12,14},{14,12},{16,18},{18,... | collective-permute-start | bytes 2064392 | tf_op jit(solution)/shard_map/ppermute | solution.py:265
  234.2 41.4 %all-to-all-start.1 = ((bf16[8,72,1024]{2,1,0:T(8,128)(2,1)}), bf16[8,72,1024]{2,1,0:T(8,128)(2,1)S(1)}, u32[]{:S(2)}, u32[]{:S(2)}) async-start(bf16[8,72,1024]{2,1,0:T(8,128)(2,1)} %bitcast.36), calls=%async_computation.1 | async-start | bytes 2359296 | tf_op jit(solution)/shard_map/all_to_all | solution.py:310
  (39 other events, 1003.5 us)

commit v2 on v1

--- a/solution.py
+++ b/solution.py
@@ -45,7 +45,7 @@
         functools.partial(pack_kernel, planes),
         out_shape=[jax.ShapeDtypeStruct((3, rows, ff), gate.dtype)] * planes,
         in_specs=[SMEM, ANY, ANY, ANY],
-        out_specs=[ANY] * planes,
+        out_specs=[VMEM] * planes,
         scratch_shapes=[pltpu.SemaphoreType.DMA((3 * planes,))],
         name="pack_weights",
     )(place, gate, up, down)
@@ -265,11 +265,13 @@
         return lax.ppermute(x, ctx, [(i, i ^ bit) for i in range(world)])
 
     blocks = {0: jnp.concatenate([key_proj[0], value_proj[0]], axis=1)}
+    packed = pack(place, gate_weight, up_weight, down_weight)
     bit = world // 2
     while bit:
         blocks.update({m | bit: swap(x, bit) for m, x in list(blocks.items())})
+        if bit == world // 2:
+            blocks, packed = lax.optimization_barrier((blocks, packed))
         bit //= 2
-    packed = pack(place, gate_weight, up_weight, down_weight)
     pieces = {(0, 0): packed[0]}
     for k in range(1, planes):
         pieces[0, k] = swap(packed[k], k * shared)

time: 278 us -> 198 us (0.71)
  Pallas kernels: 119 us -> 36.4 us
  starting transfers between devices: 35.7 us -> 38.5 us
    pallas_call x1, Pallas kernels: 85.4 us -> 4.3 us  [pack(): pl.pallas_call(functools.partial(pack_kernel, planes), out_shape=[jax.Sha...]
    unnamed x80 -> x84, local copies, waits for them, and re-layouts: 19.6 us -> 21.5 us
  transfers between devices with their start and end apart: 32 -> 32, of which waited for: 9 -> 10; matrix products, arithmetic and copies ran while one was open for 3% -> 3% of each run, Pallas kernels for 36% -> 9%
where the time goes in v2:
time: 198 us; the launch traced here: 197 us
  waiting for transfers between devices  92.2 us (47%)
  starting transfers between devices  38.5 us (19%)
  Pallas kernels  36.4 us (18%)
  local copies, waits for them, and re-layouts  25.8 us (13%)
  other arithmetic  3 us (2%)
    ppermute x30, waiting for transfers between devices, swap(): return lax.ppermute(x, ctx, [(i, i ^ bit) for i in range(world)])  55.5 us
    all_to_all x1, waiting for transfers between devices, shards(): lax.all_to_all(expert_rows.reshape(EXPERTS, CAP, D), ('exp', 'plane'), sp...  29.8 us
    ppermute x30, starting transfers between devices, swap(): return lax.ppermute(x, ctx, [(i, i ^ bit) for i in range(world)])  22.1 us
    unnamed x84, local copies, waits for them, and re-layouts  21.5 us
    pallas_call x1, Pallas kernels, run_expert(): pl.pallas_call(functools.partial(expert_kernel, planes, shared), out_shap...  17.5 us
    pallas_call x1, Pallas kernels, attend(): pl.pallas_call(functools.partial(attend_kernel, n, chunk), out_shape=[jax...  12.9 us
    all_to_all x1, starting transfers between devices, shards(): lax.all_to_all(expert_rows.reshape(EXPERTS, CAP, D), ('exp', 'plane'), sp...  11.8 us
    all_to_all x1, waiting for transfers between devices, shards(): lax.all_to_all(outgoing.reshape(EXPERTS, CAP, D), ('exp', 'plane'), split...  6.84 us
  transfers between devices with their start and end apart: 32, of which 10 were waited for; matrix products, arithmetic and copies ran while one was open for 3% of the time, Pallas kernels for 9%

profile of v2, /device:TPU:0, one launch (start us, length us, event | category | flops | bytes accessed | tf_op | source)
XLA Modules:
  0.0 197.0 jit_solution(16402287363715909355)
XLA Ops:
  0.6 1.0 pad_maximum_fusion.rest_0_
  1.6 4.1 %collective-permute-start = (bf16[192,512]{1,0:T(8,128)(2,1)S(1)}, bf16[192,512]{1,0:T(8,128)(2,1)S(1)}, u32[]{:S(2)}, u32[]{:S(2)}) collective-permute-start(bf16[192,512]{1,0:T(8,128)(2,1)S(1)} %pad_maximum_fusion.rest_0_), channel_id=1, source_target_pairs={{0,16},{2,18},{4,20},{6,22},{8,24},{10,26},{12,28},{14,30},{16,0},... | collective-permute-start | bytes 589832 | tf_op jit(solution)/shard_map/ppermute | solution.py:265
  8.5 2.2 %copy.63.bias_ref = f32[8,192,384]{2,1,0:T(8,128)} copy(f32[8,192,384]{1,2,0:T(8,128)S(1)} %bitcast.35) | data formatting | bytes 4718592 | tf_op jit(solution)/shard_map/reshape | solution.py:290
  11.8 4.3 %pack_weights.1 = (bf16[3,64,1792]{2,1,0:T(8,128)(2,1)}, bf16[3,64,1792]{2,1,0:T(8,128)(2,1)}, bf16[3,64,1792]{2,1,0:T(8,128)(2,1)}, bf16[3,64,1792]{2,1,0:T(8,128)(2,1)}) custom-call(s32[2]{0:T(128)} %pad_add_fusion.place_ref, bf16[4,64,1792]{2,1,0:T(8,128)(2,1)} %gate_ref.1, bf16[4,64,1792]{2,1,0:T(8,128)(2,1)} %up_ref.1, bf16[4,64,1792]{2,1,0:T(8,128)(2,1)} %down_ref.1), custom_call_target="tpu_custom_call" | custom-call | tf_op jit(solution)/shard_map/pack_weights/pallas_call | solution.py:44
  16.2 1.6 collective-permute-start.11
  17.8 1.5 collective-permute-start.9
  20.3 3.8 %collective-permute-done.11.rest_12_ = bf16[192,512]{1,0:T(8,128)(2,1)S(1)} collective-permute-done((bf16[192,512]{1,0:T(8,128)(2,1)S(1)}, bf16[192,512]{1,0:T(8,128)(2,1)S(1)}, u32[]{:S(2)}, u32[]{:S(2)}) %collective-permute-start.11) | collective-permute-done | bytes 196640 | tf_op jit(solution)/shard_map/ppermute | solution.py:265
  24.1 2.7 %collective-permute-done.4.rest_4_ = bf16[192,512]{1,0:T(8,128)(2,1)S(1)} collective-permute-done((bf16[192,512]{1,0:T(8,128)(2,1)S(1)}, bf16[192,512]{1,0:T(8,128)(2,1)S(1)}, u32[]{:S(2)}, u32[]{:S(2)}) %collective-permute-start.4) | collective-permute-done | bytes 196640 | tf_op jit(solution)/shard_map/ppermute | solution.py:265
  26.8 1.5 collective-permute-start.13
  28.4 1.3 collective-permute-start.6
  32.2 1.4 collective-permute-done.13.rest_14_
  33.6 3.2 %collective-permute-done.6.rest_6_ = bf16[192,512]{1,0:T(8,128)(2,1)} collective-permute-done((bf16[192,512]{1,0:T(8,128)(2,1)S(1)}, bf16[192,512]{1,0:T(8,128)(2,1)}, u32[]{:S(2)}, u32[]{:S(2)}) %collective-permute-start.6) | collective-permute-done | bytes 196640 | tf_op jit(solution)/shard_map/ppermute | solution.py:265
  38.9 1.5 collective-permute-start.22
  41.8 1.6 collective-permute-start.15
  43.4 1.9 collective-permute-start.16
  45.3 1.0 collective-permute-start.17
  47.2 0.9 copy-done.14
  54.6 12.9 %attend.1 = (bf16[192,1024]{1,0:T(8,128)(2,1)}, bf16[192,1024]{1,0:T(8,128)(2,1)S(1)}, bf16[576,1024]{1,0:T(8,128)(2,1)}) custom-call(s32[8]{0:T(128)S(1)} %reduce_max.18.live_ref, bf16[192,1024]{1,0:T(8,128)(2,1)S(1)} %bitcast.31, f32[8,192,384]{2,1,0:T(8,128)} %copy.63.bias_ref, s32[2,192]{1,0:T(2,128)S(1)} %copy.64.target_ref, ...), custom_call_target="tpu_custom_call" | custom-call | tf_op jit(solution)/shard_map/attend/pallas_call | solution.py:125
  68.3 4.6 %all-to-all-start = ((bf16[8,72,1024]{2,1,0:T(8,128)(2,1)}), bf16[8,72,1024]{2,1,0:T(8,128)(2,1)}, u32[]{:S(2)}, u32[]{:S(2)}) async-start(bf16[8,72,1024]{2,1,0:T(8,128)(2,1)} %bitcast.14), calls=%async_computation | async-start | bytes 2359296 | tf_op jit(solution)/shard_map/all_to_all | solution.py:302
  72.9 1.1 collective-permute-done.15.rest_1_
  74.8 17.6 %collective-permute-done.16.rest_2_ = bf16[3,64,1792]{2,1,0:T(8,128)(2,1)} collective-permute-done((bf16[3,64,1792]{2,1,0:T(8,128)(2,1)}, bf16[3,64,1792]{2,1,0:T(8,128)(2,1)}, u32[]{:S(2)}, u32[]{:S(2)}) %collective-permute-start.16) | collective-permute-done | bytes 688160 | tf_op jit(solution)/shard_map/ppermute | solution.py:265
  93.0 1.5 collective-permute-start.25
  95.1 15.9 %collective-permute-done.24.rest_10_ = bf16[3,64,1792]{2,1,0:T(8,128)(2,1)S(1)} collective-permute-done((bf16[3,64,1792]{2,1,0:T(8,128)(2,1)}, bf16[3,64,1792]{2,1,0:T(8,128)(2,1)S(1)}, u32[]{:S(2)}, u32[]{:S(2)}) %collective-permute-start.24) | collective-permute-done | bytes 688160 | tf_op jit(solution)/shard_map/ppermute | solution.py:265
  111.1 9.7 %collective-permute-done.25.rest_11_ = bf16[3,64,1792]{2,1,0:T(8,128)(2,1)S(1)} collective-permute-done((bf16[3,64,1792]{2,1,0:T(8,128)(2,1)}, bf16[3,64,1792]{2,1,0:T(8,128)(2,1)S(1)}, u32[]{:S(2)}, u32[]{:S(2)}) %collective-permute-start.25) | collective-permute-done | bytes 688160 | tf_op jit(solution)/shard_map/ppermute | solution.py:265
  125.9 6.8 %all-to-all-done = bf16[8,72,1024]{2,1,0:T(8,128)(2,1)} async-done(((bf16[8,72,1024]{2,1,0:T(8,128)(2,1)}), bf16[8,72,1024]{2,1,0:T(8,128)(2,1)}, u32[]{:S(2)}, u32[]{:S(2)}) %all-to-all-start) | async-done | bytes 1179680 | tf_op jit(solution)/shard_map/all_to_all | solution.py:302
  132.7 1.1 copy-done.2
  133.8 1.1 copy-done.4
  134.9 1.1 copy-done.6
  136.0 17.5 %expert.1 = bf16[576,1024]{1,0:T(8,128)(2,1)} custom-call(s32[2]{0:T(128)S(1)} %copy-done.30, bf16[576,1024]{1,0:T(8,128)(2,1)} %bitcast.15.rows_ref, bf16[3,64,1792]{2,1,0:T(8,128)(2,1)S(1)} %copy-done, bf16[3,64,1792]{2,1,0:T(8,128)(2,1)S(1)} %collective-permute-done.15.rest_1_, bf16[3,64,1792]{2,1,0:T(8,128)(2,1)} %collective-permute-done.16.rest_2_, ...), custom_call_target="tpu_custom_call" | custom-call | tf_op jit(solution)/shard_map/expert/pallas_call | solution.py:189
  153.6 11.8 %all-to-all-start.1 = ((bf16[8,72,1024]{2,1,0:T(8,128)(2,1)}), bf16[8,72,1024]{2,1,0:T(8,128)(2,1)S(1)}, u32[]{:S(2)}, u32[]{:S(2)}) async-start(bf16[8,72,1024]{2,1,0:T(8,128)(2,1)} %bitcast.36), calls=%async_computation.1 | async-start | bytes 2359296 | tf_op jit(solution)/shard_map/all_to_all | solution.py:312
  165.6 29.8 %all-to-all-done.1 = bf16[8,72,1024]{2,1,0:T(8,128)(2,1)S(1)} async-done(((bf16[8,72,1024]{2,1,0:T(8,128)(2,1)}), bf16[8,72,1024]{2,1,0:T(8,128)(2,1)S(1)}, u32[]{:S(2)}, u32[]{:S(2)}) %all-to-all-start.1) | async-done | bytes 1179680 | tf_op jit(solution)/shard_map/all_to_all | solution.py:312
  195.4 1.6 combine.1
  (156 shorter events, 26.3 us)
Async XLA Ops:
  1.6 14.6 %collective-permute-start = (bf16[192,512]{1,0:T(8,128)(2,1)S(1)}, bf16[192,512]{1,0:T(8,128)(2,1)S(1)}, u32[]{:S(2)}, u32[]{:S(2)}) collective-permute-start(bf16[192,512]{1,0:T(8,128)(2,1)S(1)} %pad_maximum_fusion.rest_0_), channel_id=1, source_target_pairs={{0,16},{2,18},{4,20},{6,22},{8,24},{10,26},{12,28},{14,30},{16,0},... | collective-permute-start | bytes 589832 | tf_op jit(solution)/shard_map/ppermute | solution.py:265
  16.2 7.9 %collective-permute-start.11 = (bf16[192,512]{1,0:T(8,128)(2,1)S(1)}, bf16[192,512]{1,0:T(8,128)(2,1)S(1)}, u32[]{:S(2)}, u32[]{:S(2)}) collective-permute-start(bf16[192,512]{1,0:T(8,128)(2,1)S(1)} %collective-permute-done.rest_8_), channel_id=1, source_target_pairs={{0,8},{2,10},{4,12},{6,14},{8,0},{10,2},{12,4},{14,6},{16,24},{18,... | collective-permute-start | bytes 589832 | tf_op jit(solution)/shard_map/ppermute | solution.py:265
  17.8 10.5 %collective-permute-start.9 = (bf16[192,512]{1,0:T(8,128)(2,1)S(1)}, bf16[192,512]{1,0:T(8,128)(2,1)S(1)}, u32[]{:S(2)}, u32[]{:S(2)}) collective-permute-start(bf16[192,512]{1,0:T(8,128)(2,1)S(1)} %collective-permute-done.rest_8_), channel_id=1, source_target_pairs={{0,4},{2,6},{4,0},{6,2},{8,12},{10,14},{12,8},{14,10},{16,20},{18,... | collective-permute-start | bytes 589832 | tf_op jit(solution)/shard_map/ppermute | solution.py:265
  19.3 7.5 %collective-permute-start.4 = (bf16[192,512]{1,0:T(8,128)(2,1)S(1)}, bf16[192,512]{1,0:T(8,128)(2,1)S(1)}, u32[]{:S(2)}, u32[]{:S(2)}) collective-permute-start(bf16[192,512]{1,0:T(8,128)(2,1)S(1)} %pad_maximum_fusion.rest_0_), channel_id=1, source_target_pairs={{0,8},{2,10},{4,12},{6,14},{8,0},{10,2},{12,4},{14,6},{16,24},{18,... | collective-permute-start | bytes 589832 | tf_op jit(solution)/shard_map/ppermute | solution.py:265
  19.8 8.6 %collective-permute-start.2 = (bf16[192,512]{1,0:T(8,128)(2,1)S(1)}, bf16[192,512]{1,0:T(8,128)(2,1)S(1)}, u32[]{:S(2)}, u32[]{:S(2)}) collective-permute-start(bf16[192,512]{1,0:T(8,128)(2,1)S(1)} %pad_maximum_fusion.rest_0_), channel_id=1, source_target_pairs={{0,4},{2,6},{4,0},{6,2},{8,12},{10,14},{12,8},{14,10},{16,20},{18,... | collective-permute-start | bytes 589832 | tf_op jit(solution)/shard_map/ppermute | solution.py:265
  20.3 10.0 %collective-permute-start.1 = (bf16[192,512]{1,0:T(8,128)(2,1)S(1)}, bf16[192,512]{1,0:T(8,128)(2,1)S(1)}, u32[]{:S(2)}, u32[]{:S(2)}) collective-permute-start(bf16[192,512]{1,0:T(8,128)(2,1)S(1)} %pad_maximum_fusion.rest_0_), channel_id=1, source_target_pairs={{0,2},{2,0},{4,6},{6,4},{8,10},{10,8},{12,14},{14,12},{16,18},{18,... | collective-permute-start | bytes 589832 | tf_op jit(solution)/shard_map/ppermute | solution.py:265
  24.1 7.0 %collective-permute-start.8 = (bf16[192,512]{1,0:T(8,128)(2,1)S(1)}, bf16[192,512]{1,0:T(8,128)(2,1)S(1)}, u32[]{:S(2)}, u32[]{:S(2)}) collective-permute-start(bf16[192,512]{1,0:T(8,128)(2,1)S(1)} %collective-permute-done.rest_8_), channel_id=1, source_target_pairs={{0,2},{2,0},{4,6},{6,4},{8,10},{10,8},{12,14},{14,12},{16,18},{18,... | collective-permute-start | bytes 589832 | tf_op jit(solution)/shard_map/ppermute | solution.py:265
  26.8 6.8 %collective-permute-start.13 = (bf16[192,512]{1,0:T(8,128)(2,1)S(1)}, bf16[192,512]{1,0:T(8,128)(2,1)}, u32[]{:S(2)}, u32[]{:S(2)}) collective-permute-start(bf16[192,512]{1,0:T(8,128)(2,1)S(1)} %collective-permute-done.11.rest_12_), channel_id=1, source_target_pairs={{0,4},{2,6},{4,0},{6,2},{8,12},{10,14},{12,8},{14,10},{16,20},{18,... | collective-permute-start | bytes 589832 | tf_op jit(solution)/shard_map/ppermute | solution.py:265
  28.3 8.5 %collective-permute-start.12 = (bf16[192,512]{1,0:T(8,128)(2,1)S(1)}, bf16[192,512]{1,0:T(8,128)(2,1)S(1)}, u32[]{:S(2)}, u32[]{:S(2)}) collective-permute-start(bf16[192,512]{1,0:T(8,128)(2,1)S(1)} %collective-permute-done.11.rest_12_), channel_id=1, source_target_pairs={{0,2},{2,0},{4,6},{6,4},{8,10},{10,8},{12,14},{14,12},{16,18},{18,... | collective-permute-start | bytes 589832 | tf_op jit(solution)/shard_map/ppermute | solution.py:265
  28.4 8.4 %collective-permute-start.6 = (bf16[192,512]{1,0:T(8,128)(2,1)S(1)}, bf16[192,512]{1,0:T(8,128)(2,1)}, u32[]{:S(2)}, u32[]{:S(2)}) collective-permute-start(bf16[192,512]{1,0:T(8,128)(2,1)S(1)} %collective-permute-done.4.rest_4_), channel_id=1, source_target_pairs={{0,4},{2,6},{4,0},{6,2},{8,12},{10,14},{12,8},{14,10},{16,20},{18,... | collective-permute-start | bytes 589832 | tf_op jit(solution)/shard_map/ppermute | solution.py:265
  31.0 7.2 %collective-permute-start.5 = (bf16[192,512]{1,0:T(8,128)(2,1)S(1)}, bf16[192,512]{1,0:T(8,128)(2,1)S(1)}, u32[]{:S(2)}, u32[]{:S(2)}) collective-permute-start(bf16[192,512]{1,0:T(8,128)(2,1)S(1)} %collective-permute-done.4.rest_4_), channel_id=1, source_target_pairs={{0,2},{2,0},{4,6},{6,4},{8,10},{10,8},{12,14},{14,12},{16,18},{18,... | collective-permute-start | bytes 589832 | tf_op jit(solution)/shard_map/ppermute | solution.py:265
  31.7 8.8 %collective-permute-start.10 = (bf16[192,512]{1,0:T(8,128)(2,1)S(1)}, bf16[192,512]{1,0:T(8,128)(2,1)S(1)}, u32[]{:S(2)}, u32[]{:S(2)}) collective-permute-start(bf16[192,512]{1,0:T(8,128)(2,1)S(1)} %collective-permute-done.9.rest_10_), channel_id=1, source_target_pairs={{0,2},{2,0},{4,6},{6,4},{8,10},{10,8},{12,14},{14,12},{16,18},{18,... | collective-permute-start | bytes 589832 | tf_op jit(solution)/shard_map/ppermute | solution.py:265
  33.6 7.5 %collective-permute-start.3 = (bf16[192,512]{1,0:T(8,128)(2,1)S(1)}, bf16[192,512]{1,0:T(8,128)(2,1)S(1)}, u32[]{:S(2)}, u32[]{:S(2)}) collective-permute-start(bf16[192,512]{1,0:T(8,128)(2,1)S(1)} %collective-permute-done.2.rest_2_), channel_id=1, source_target_pairs={{0,2},{2,0},{4,6},{6,4},{8,10},{10,8},{12,14},{14,12},{16,18},{18,... | collective-permute-start | bytes 589832 | tf_op jit(solution)/shard_map/ppermute | solution.py:265
  36.8 6.6 %collective-permute-start.14 = (bf16[192,512]{1,0:T(8,128)(2,1)}, bf16[192,512]{1,0:T(8,128)(2,1)}, u32[]{:S(2)}, u32[]{:S(2)}) collective-permute-start(bf16[192,512]{1,0:T(8,128)(2,1)} %collective-permute-done.13.rest_14_), channel_id=1, source_target_pairs={{0,2},{2,0},{4,6},{6,4},{8,10},{10,8},{12,14},{14,12},{16,18},{18,... | collective-permute-start | bytes 589832 | tf_op jit(solution)/shard_map/ppermute | solution.py:265
  37.5 7.8 %collective-permute-start.7 = (bf16[192,512]{1,0:T(8,128)(2,1)}, bf16[192,512]{1,0:T(8,128)(2,1)}, u32[]{:S(2)}, u32[]{:S(2)}) collective-permute-start(bf16[192,512]{1,0:T(8,128)(2,1)} %collective-permute-done.6.rest_6_), channel_id=1, source_target_pairs={{0,2},{2,0},{4,6},{6,4},{8,10},{10,8},{12,14},{14,12},{16,18},{18,... | collective-permute-start | bytes 589832 | tf_op jit(solution)/shard_map/ppermute | solution.py:265
  38.9 55.6 %collective-permute-start.22 = (bf16[3,64,1792]{2,1,0:T(8,128)(2,1)}, bf16[3,64,1792]{2,1,0:T(8,128)(2,1)S(1)}, u32[]{:S(2)}, u32[]{:S(2)}) collective-permute-start(bf16[3,64,1792]{2,1,0:T(8,128)(2,1)} %get-tuple-element.23.rest_0_), channel_id=1, source_target_pairs={{0,4},{2,6},{4,0},{6,2},{8,12},{10,14},{12,8},{14,10},{16,20},{18,... | collective-permute-start | bytes 2064392 | tf_op jit(solution)/shard_map/ppermute | solution.py:265
  41.1 53.4 %collective-permute-start.18 = (bf16[3,64,1792]{2,1,0:T(8,128)(2,1)}, bf16[3,64,1792]{2,1,0:T(8,128)(2,1)S(1)}, u32[]{:S(2)}, u32[]{:S(2)}) collective-permute-start(bf16[3,64,1792]{2,1,0:T(8,128)(2,1)} %get-tuple-element.23.rest_0_), channel_id=1, source_target_pairs={{0,2},{2,0},{4,6},{6,4},{8,10},{10,8},{12,14},{14,12},{16,18},{18,... | collective-permute-start | bytes 2064392 | tf_op jit(solution)/shard_map/ppermute | solution.py:265
  41.8 32.1 %collective-permute-start.15 = (bf16[3,64,1792]{2,1,0:T(8,128)(2,1)}, bf16[3,64,1792]{2,1,0:T(8,128)(2,1)S(1)}, u32[]{:S(2)}, u32[]{:S(2)}) collective-permute-start(bf16[3,64,1792]{2,1,0:T(8,128)(2,1)} %get-tuple-element.24), channel_id=1, source_target_pairs={{0,8},{2,10},{4,12},{6,14},{8,0},{10,2},{12,4},{14,6},{16,24},{18,... | collective-permute-start | bytes 2064392 | tf_op jit(solution)/shard_map/ppermute | solution.py:265
  43.4 49.1 %collective-permute-start.16 = (bf16[3,64,1792]{2,1,0:T(8,128)(2,1)}, bf16[3,64,1792]{2,1,0:T(8,128)(2,1)}, u32[]{:S(2)}, u32[]{:S(2)}) collective-permute-start(bf16[3,64,1792]{2,1,0:T(8,128)(2,1)} %get-tuple-element.25), channel_id=1, source_target_pairs={{0,16},{2,18},{4,20},{6,22},{8,24},{10,26},{12,28},{14,30},{16,0},... | collective-permute-start | bytes 2064392 | tf_op jit(solution)/shard_map/ppermute | solution.py:265
  45.3 47.7 %collective-permute-start.17 = (bf16[3,64,1792]{2,1,0:T(8,128)(2,1)}, bf16[3,64,1792]{2,1,0:T(8,128)(2,1)}, u32[]{:S(2)}, u32[]{:S(2)}) collective-permute-start(bf16[3,64,1792]{2,1,0:T(8,128)(2,1)} %get-tuple-element.26), channel_id=1, source_target_pairs={{0,24},{2,26},{4,28},{6,30},{8,16},{10,18},{12,20},{14,22},{16,8},... | collective-permute-start | bytes 2064392 | tf_op jit(solution)/shard_map/ppermute | solution.py:265
  68.3 64.4 %all-to-all-start = ((bf16[8,72,1024]{2,1,0:T(8,128)(2,1)}), bf16[8,72,1024]{2,1,0:T(8,128)(2,1)}, u32[]{:S(2)}, u32[]{:S(2)}) async-start(bf16[8,72,1024]{2,1,0:T(8,128)(2,1)} %bitcast.14), calls=%async_computation | async-start | bytes 2359296 | tf_op jit(solution)/shard_map/all_to_all | solution.py:302
  73.9 21.1 %collective-permute-start.23 = (bf16[3,64,1792]{2,1,0:T(8,128)(2,1)S(1)}, bf16[3,64,1792]{2,1,0:T(8,128)(2,1)S(1)}, u32[]{:S(2)}, u32[]{:S(2)}) collective-permute-start(bf16[3,64,1792]{2,1,0:T(8,128)(2,1)S(1)} %collective-permute-done.15.rest_1_), channel_id=1, source_target_pairs={{0,4},{2,6},{4,0},{6,2},{8,12},{10,14},{12,8},{14,10},{16,20},{18,... | collective-permute-start | bytes 2064392 | tf_op jit(solution)/shard_map/ppermute | solution.py:265
  92.5 18.6 %collective-permute-start.24 = (bf16[3,64,1792]{2,1,0:T(8,128)(2,1)}, bf16[3,64,1792]{2,1,0:T(8,128)(2,1)S(1)}, u32[]{:S(2)}, u32[]{:S(2)}) collective-permute-start(bf16[3,64,1792]{2,1,0:T(8,128)(2,1)} %collective-permute-done.16.rest_2_), channel_id=1, source_target_pairs={{0,4},{2,6},{4,0},{6,2},{8,12},{10,14},{12,8},{14,10},{16,20},{18,... | collective-permute-start | bytes 2064392 | tf_op jit(solution)/shard_map/ppermute | solution.py:265
  93.0 27.8 %collective-permute-start.25 = (bf16[3,64,1792]{2,1,0:T(8,128)(2,1)}, bf16[3,64,1792]{2,1,0:T(8,128)(2,1)S(1)}, u32[]{:S(2)}, u32[]{:S(2)}) collective-permute-start(bf16[3,64,1792]{2,1,0:T(8,128)(2,1)} %collective-permute-done.17.rest_3_), channel_id=1, source_target_pairs={{0,4},{2,6},{4,0},{6,2},{8,12},{10,14},{12,8},{14,10},{16,20},{18,... | collective-permute-start | bytes 2064392 | tf_op jit(solution)/shard_map/ppermute | solution.py:265
  94.5 26.3 %collective-permute-start.26 = (bf16[3,64,1792]{2,1,0:T(8,128)(2,1)S(1)}, bf16[3,64,1792]{2,1,0:T(8,128)(2,1)S(1)}, u32[]{:S(2)}, u32[]{:S(2)}) collective-permute-start(bf16[3,64,1792]{2,1,0:T(8,128)(2,1)S(1)} %collective-permute-done.22.rest_8_), channel_id=1, source_target_pairs={{0,2},{2,0},{4,6},{6,4},{8,10},{10,8},{12,14},{14,12},{16,18},{18,... | collective-permute-start | bytes 2064392 | tf_op jit(solution)/shard_map/ppermute | solution.py:265
  94.5 26.8 %collective-permute-start.19 = (bf16[3,64,1792]{2,1,0:T(8,128)(2,1)S(1)}, bf16[3,64,1792]{2,1,0:T(8,128)(2,1)S(1)}, u32[]{:S(2)}, u32[]{:S(2)}) collective-permute-start(bf16[3,64,1792]{2,1,0:T(8,128)(2,1)S(1)} %collective-permute-done.15.rest_1_), channel_id=1, source_target_pairs={{0,2},{2,0},{4,6},{6,4},{8,10},{10,8},{12,14},{14,12},{16,18},{18,... | collective-permute-start | bytes 2064392 | tf_op jit(solution)/shard_map/ppermute | solution.py:265
  95.0 27.3 %collective-permute-start.20 = (bf16[3,64,1792]{2,1,0:T(8,128)(2,1)}, bf16[3,64,1792]{2,1,0:T(8,128)(2,1)S(1)}, u32[]{:S(2)}, u32[]{:S(2)}) collective-permute-start(bf16[3,64,1792]{2,1,0:T(8,128)(2,1)} %collective-permute-done.16.rest_2_), channel_id=1, source_target_pairs={{0,2},{2,0},{4,6},{6,4},{8,10},{10,8},{12,14},{14,12},{16,18},{18,... | collective-permute-start | bytes 2064392 | tf_op jit(solution)/shard_map/ppermute | solution.py:265
  111.1 12.2 %collective-permute-start.21 = (bf16[3,64,1792]{2,1,0:T(8,128)(2,1)}, bf16[3,64,1792]{2,1,0:T(8,128)(2,1)S(1)}, u32[]{:S(2)}, u32[]{:S(2)}) collective-permute-start(bf16[3,64,1792]{2,1,0:T(8,128)(2,1)} %collective-permute-done.17.rest_3_), channel_id=1, source_target_pairs={{0,2},{2,0},{4,6},{6,4},{8,10},{10,8},{12,14},{14,12},{16,18},{18,... | collective-permute-start | bytes 2064392 | tf_op jit(solution)/shard_map/ppermute | solution.py:265
  120.8 3.3 %collective-permute-start.27 = (bf16[3,64,1792]{2,1,0:T(8,128)(2,1)S(1)}, bf16[3,64,1792]{2,1,0:T(8,128)(2,1)S(1)}, u32[]{:S(2)}, u32[]{:S(2)}) collective-permute-start(bf16[3,64,1792]{2,1,0:T(8,128)(2,1)S(1)} %collective-permute-done.23.rest_9_), channel_id=1, source_target_pairs={{0,2},{2,0},{4,6},{6,4},{8,10},{10,8},{12,14},{14,12},{16,18},{18,... | collective-permute-start | bytes 2064392 | tf_op jit(solution)/shard_map/ppermute | solution.py:265
  120.8 3.3 %collective-permute-start.28 = (bf16[3,64,1792]{2,1,0:T(8,128)(2,1)S(1)}, bf16[3,64,1792]{2,1,0:T(8,128)(2,1)S(1)}, u32[]{:S(2)}, u32[]{:S(2)}) collective-permute-start(bf16[3,64,1792]{2,1,0:T(8,128)(2,1)S(1)} %collective-permute-done.24.rest_10_), channel_id=1, source_target_pairs={{0,2},{2,0},{4,6},{6,4},{8,10},{10,8},{12,14},{14,12},{16,18},{18,... | collective-permute-start | bytes 2064392 | tf_op jit(solution)/shard_map/ppermute | solution.py:265
  122.2 3.7 %collective-permute-start.29 = (bf16[3,64,1792]{2,1,0:T(8,128)(2,1)S(1)}, bf16[3,64,1792]{2,1,0:T(8,128)(2,1)}, u32[]{:S(2)}, u32[]{:S(2)}) collective-permute-start(bf16[3,64,1792]{2,1,0:T(8,128)(2,1)S(1)} %collective-permute-done.25.rest_11_), channel_id=1, source_target_pairs={{0,2},{2,0},{4,6},{6,4},{8,10},{10,8},{12,14},{14,12},{16,18},{18,... | collective-permute-start | bytes 2064392 | tf_op jit(solution)/shard_map/ppermute | solution.py:265
  153.6 41.8 %all-to-all-start.1 = ((bf16[8,72,1024]{2,1,0:T(8,128)(2,1)}), bf16[8,72,1024]{2,1,0:T(8,128)(2,1)S(1)}, u32[]{:S(2)}, u32[]{:S(2)}) async-start(bf16[8,72,1024]{2,1,0:T(8,128)(2,1)} %bitcast.36), calls=%async_computation.1 | async-start | bytes 2359296 | tf_op jit(solution)/shard_map/all_to_all | solution.py:312
  (41 other events, 412.0 us)

commit v3 on v2

--- a/solution.py
+++ b/solution.py
@@ -51,13 +51,42 @@
     )(place, gate, up, down)
 
 
-def attend_kernel(blocks, chunk, live_ref, query_ref, bias_ref, target_ref, out_w_ref, hidden_ref, gain_ref, *rest):
-    kv_refs = rest[:blocks]
-    attention_ref, residual_ref, outgoing_ref, kv, scores, top, total, acc, attended = rest[blocks:]
+def attend_kernel(blocks, live_ref, spot_ref, allowed_ref, query_in, target_ref, out_w_in, hidden_in, gain_ref, *rest):
+    kv_in = rest[:blocks]
+    attention_ref, residual_ref, outgoing_ref = rest[blocks : blocks + 3]
+    query_ref, out_w_ref, hidden_ref, kv, packed, scores, top, total, acc, attended, sems = rest[blocks + 3 :]
     rows = query_ref.shape[0]
-    chunks = scores.shape[0]
+    chunk = scores.shape[2]
+    tiles = live_ref.shape[0]
+    per_chunk = chunk // TILE
+    first = [pltpu.make_async_copy(query_in, query_ref, sems.at[0])]
     for i in range(blocks):
-        kv[pl.ds(i * rows, rows), :] = kv_refs[i][...]
+        first.append(pltpu.make_async_copy(kv_in[i], kv.at[pl.ds(i * rows, rows)], sems.at[3 + i]))
+    late = [
+        pltpu.make_async_copy(hidden_in, hidden_ref, sems.at[1]),
+        pltpu.make_async_copy(out_w_in, out_w_ref, sems.at[2]),
+    ]
+    for copy in first + late:
+        copy.start()
+    for copy in first:
+        copy.wait()
+
+    @pl.loop(0, tiles)
+    def _(i):
+        @pl.when(live_ref[i] > 0)
+        def _():
+            source = pl.ds(pl.multiple_of(i * TILE, TILE), TILE)
+            packed[pl.ds(pl.multiple_of(spot_ref[i] * TILE, TILE), TILE), :] = kv[source, :]
+
+    used = spot_ref[tiles - 1] + live_ref[tiles - 1]
+    chunks = (used + per_chunk - 1) // per_chunk
+
+    @pl.loop(used, chunks * per_chunk)
+    def _(i):
+        packed[pl.ds(pl.multiple_of(i * TILE, TILE), TILE), :] = jnp.zeros((TILE, 2 * KVW), jnp.bfloat16)
+
+    lane_tile = lax.broadcasted_iota(jnp.int32, (128, chunk), 1) // TILE
+    widen = (lane_tile == lax.broadcasted_iota(jnp.int32, (128, chunk), 0)).astype(jnp.float32).astype(jnp.bfloat16)
     scale = HEAD ** (-0.5)
     for h in range(KV_HEADS):
         heads = [query_ref[:, (h * GROUPS + g) * HEAD : (h * GROUPS + g + 1) * HEAD] for g in range(GROUPS)]
@@ -68,43 +97,45 @@
 
         @pl.loop(0, chunks)
         def _(j):
-            @pl.when(live_ref[j] > 0)
-            def _():
-                keys = kv[pl.ds(pl.multiple_of(j * chunk, 128), chunk), h * HEAD : (h + 1) * HEAD]
-                s = lax.dot_general(query, keys, (((1,), (1,)), ((), ())), preferred_element_type=jnp.float32)
-                s = s.reshape(GROUPS, rows, chunk) + bias_ref[j][None]
-                s = s.reshape(GROUPS * rows, chunk)
-                scores[j] = s
-                best = top[...]
-                for c in range(0, chunk, 128):
-                    best = jnp.maximum(best, s[:, c : c + 128])
-                top[...] = best
+            keys = packed[pl.ds(pl.multiple_of(j * chunk, 128), chunk), h * HEAD : (h + 1) * HEAD]
+            s = lax.dot_general(query, keys, (((1,), (1,)), ((), ())), preferred_element_type=jnp.float32)
+            allowed = jnp.dot(allowed_ref[j], widen, preferred_element_type=jnp.float32)
+            bias = (allowed - 1.0) * 1e30
+            bias = [jnp.broadcast_to(bias[t : t + 1], (TILE, chunk)) for t in range(rows // TILE)]
+            bias = jnp.concatenate(bias, axis=0)
+            s = s.reshape(GROUPS, rows, chunk) + bias[None]
+            s = s.reshape(GROUPS * rows, chunk)
+            scores[j] = s
+            best = top[...]
+            for c in range(0, chunk, 128):
+                best = jnp.maximum(best, s[:, c : c + 128])
+            top[...] = best
 
         highest = jnp.max(top[...], axis=1, keepdims=True)
         top[...] = jnp.broadcast_to(highest, top.shape)
 
         @pl.loop(0, chunks)
         def _(j):
-            @pl.when(live_ref[j] > 0)
-            def _():
-                values = kv[pl.ds(pl.multiple_of(j * chunk, 128), chunk), KVW + h * HEAD : KVW + (h + 1) * HEAD]
-                high = top[...]
-                s = scores[j]
-                parts = []
-                running = total[...]
-                for c in range(0, chunk, 128):
-                    w = jnp.exp((s[:, c : c + 128] - high) * scale)
-                    running = running + w
-                    parts.append(w.astype(jnp.bfloat16))
-                total[...] = running
-                weights = jnp.concatenate(parts, axis=1)
-                acc[...] += jnp.dot(weights, values, preferred_element_type=jnp.float32)
+            values = packed[pl.ds(pl.multiple_of(j * chunk, 128), chunk), KVW + h * HEAD : KVW + (h + 1) * HEAD]
+            high = top[...]
+            s = scores[j]
+            parts = []
+            running = total[...]
+            for c in range(0, chunk, 128):
+                w = jnp.exp((s[:, c : c + 128] - high) * scale)
+                running = running + w
+                parts.append(w.astype(jnp.bfloat16))
+            total[...] = running
+            weights = jnp.concatenate(parts, axis=1)
+            acc[...] += jnp.dot(weights, values, preferred_element_type=jnp.float32)
 
         denominator = jnp.sum(total[...], axis=1, keepdims=True)
         result = (acc[...] / denominator).astype(jnp.bfloat16)
         for g in range(GROUPS):
             col = (h * GROUPS + g) * HEAD
             attended[:, col : col + HEAD] = result[g * rows : (g + 1) * rows]
+    for copy in late:
+        copy.wait()
     projected = jnp.dot(attended[...], out_w_ref[...], preferred_element_type=jnp.float32)
     attention_ref[...] = projected.astype(jnp.bfloat16)
     residual = (hidden_ref[...].astype(jnp.float32) + projected).astype(jnp.bfloat16)
@@ -118,30 +149,52 @@
     outgoing_ref[...] = jnp.dot(selector, normed, preferred_element_type=jnp.float32).astype(jnp.bfloat16)
 
 
-def attend(live, query, bias, target, out_w, hidden, gain, blocks):
+def attend(live, spot, allowed, query, target, out_w, hidden, gain, blocks):
     rows = query.shape[0]
-    chunks, _, chunk = bias.shape
+    chunks = allowed.shape[0]
     n = len(blocks)
+    chunk = n * rows // chunks
     return pl.pallas_call(
-        functools.partial(attend_kernel, n, chunk),
+        functools.partial(attend_kernel, n),
         out_shape=[
             jax.ShapeDtypeStruct((rows, D), jnp.bfloat16),
             jax.ShapeDtypeStruct((rows, D), jnp.bfloat16),
             jax.ShapeDtypeStruct((SLOTS, D), jnp.bfloat16),
         ],
-        in_specs=[SMEM] + [VMEM] * (6 + n),
+        in_specs=[SMEM, SMEM, VMEM, ANY, VMEM, ANY, ANY, VMEM] + [ANY] * n,
         out_specs=[VMEM] * 3,
         scratch_shapes=[
+            pltpu.VMEM((rows, D), jnp.bfloat16),
+            pltpu.VMEM((D, D), jnp.bfloat16),
+            pltpu.VMEM((rows, D), jnp.bfloat16),
+            pltpu.VMEM((n * rows, 2 * KVW), jnp.bfloat16),
             pltpu.VMEM((n * rows, 2 * KVW), jnp.bfloat16),
             pltpu.VMEM((chunks, GROUPS * rows, chunk), jnp.float32),
             pltpu.VMEM((GROUPS * rows, HEAD), jnp.float32),
             pltpu.VMEM((GROUPS * rows, HEAD), jnp.float32),
             pltpu.VMEM((GROUPS * rows, HEAD), jnp.float32),
             pltpu.VMEM((rows, D), jnp.bfloat16),
+            pltpu.SemaphoreType.DMA((3 + n,)),
         ],
-        compiler_params=pltpu.CompilerParams(vmem_limit_bytes=48 * MB),
+        compiler_params=pltpu.CompilerParams(vmem_limit_bytes=56 * MB),
         name="attend",
-    )(live, query, bias, target, out_w, hidden, gain, *blocks)
+    )(live, spot, allowed, query, target, out_w, hidden, gain, *blocks)
+
+
+def key_order(tile_mask, me, world):
+    tiles, count = tile_mask.shape
+    order = me ^ jnp.arange(world)
+    mask = jnp.take(tile_mask.reshape(tiles, world, tiles), order, axis=1, mode="clip").reshape(tiles, count)
+    mask = (mask > 0).astype(jnp.bfloat16)
+    live = jnp.max(mask, axis=0)
+    index = jnp.arange(count)
+    spot = jnp.dot(live, (index[:, None] < index[None, :]).astype(jnp.bfloat16), preferred_element_type=jnp.float32)
+    move = (spot[:, None] == index[None, :].astype(jnp.float32)) & (live[:, None] > 0)
+    placed = jnp.dot(mask, move.astype(jnp.bfloat16), preferred_element_type=jnp.float32)
+    per_chunk = 2 * tiles
+    placed = placed.reshape(tiles, count // per_chunk, per_chunk).transpose(1, 0, 2)
+    placed = jnp.pad(placed, ((0, 0), (0, -tiles % 16), (0, 128 - per_chunk))).astype(jnp.bfloat16)
+    return live.astype(jnp.int32), spot.astype(jnp.int32), placed
 
 
 def expert_kernel(planes, shared, place_ref, rows_ref, *rest):
@@ -198,7 +251,7 @@
             pltpu.VMEM(rows.shape, jnp.float32),
             pltpu.SemaphoreType.DMA((3 * count,)),
         ],
-        compiler_params=pltpu.CompilerParams(vmem_limit_bytes=48 * MB),
+        compiler_params=pltpu.CompilerParams(vmem_limit_bytes=60 * MB),
         name="expert",
     )(place, rows, *pieces)
 
@@ -221,7 +274,7 @@
         out_shape=jax.ShapeDtypeStruct(residual.shape, jnp.bfloat16),
         in_specs=[VMEM] * 4,
         out_specs=VMEM,
-        compiler_params=pltpu.CompilerParams(vmem_limit_bytes=32 * MB),
+        compiler_params=pltpu.CompilerParams(vmem_limit_bytes=16 * MB),
         name="combine",
     )(returned, target, probs, residual)
 
@@ -254,8 +307,6 @@
 ):
     ctx = ("plane", "seat")
     world = planes * shared
-    rows = queries.shape[1]
-    tiles = rows // TILE
     plane = lax.axis_index("plane")
     seat = lax.axis_index("seat")
     me = plane * shared + seat
@@ -266,33 +317,35 @@
 
     blocks = {0: jnp.concatenate([key_proj[0], value_proj[0]], axis=1)}
     packed = pack(place, gate_weight, up_weight, down_weight)
+    pieces = {(0, 0): packed[0]}
     bit = world // 2
+    blocks[bit] = swap(blocks[0], bit)
+    far = [k for k in range(planes) if k >= planes // 2 and k]
+    near = [k for k in range(planes) if k < planes // 2 and k]
+    if far:
+        pieces[0, far[0]] = swap(packed[far[0]], far[0] * shared)
+    for k in near:
+        pieces[0, k] = swap(packed[k], k * shared)
+    bit //= 2
     while bit:
         blocks.update({m | bit: swap(x, bit) for m, x in list(blocks.items())})
-        if bit == world // 2:
-            blocks, packed = lax.optimization_barrier((blocks, packed))
         bit //= 2
-    pieces = {(0, 0): packed[0]}
-    for k in range(1, planes):
-        pieces[0, k] = swap(packed[k], k * shared)
+    if far:
+        blocks, pieces[0, far[0]] = lax.optimization_barrier((blocks, pieces[0, far[0]]))
+        last, pieces[0, far[0]] = lax.optimization_barrier((packed[far[1]], pieces[0, far[0]]))
+        pieces[0, far[1]] = swap(last, far[1] * shared)
     bit = shared // 2
     while bit:
         pieces.update({(m | bit, k): swap(x, bit) for (m, k), x in list(pieces.items())})
         bit //= 2
 
     target = slots_of(expert_ids[0])
-    chunk = 2 * rows
-    order = me ^ jnp.arange(world)
-    mask = jnp.take(tile_mask[0].reshape(tiles, world, tiles), order, axis=1)
-    mask = mask.reshape(tiles, world // 2, 2 * tiles).transpose(1, 0, 2)
-    live = jnp.max(mask, axis=(1, 2)).astype(jnp.int32)
-    bias = jnp.where(mask > 0, 0.0, -1e30).astype(jnp.float32)
-    bias = jnp.repeat(jnp.repeat(bias, TILE, axis=1), TILE, axis=2)
-
+    live, spot, allowed = key_order(tile_mask[0], me, world)
     attention_out, residual, outgoing = attend(
         live,
+        spot,
+        allowed,
         queries[0],
-        bias,
         target.T,
         out_weight,
         hidden_in[0],

time: 198 us -> 166 us (0.84)
  local copies, waits for them, and re-layouts: 25.8 us -> 5.45 us
  Pallas kernels: 36.4 us -> 28.2 us
  starting transfers between devices: 38.5 us -> 32.9 us
  waiting for transfers between devices: 92.2 us -> 94.3 us
    unnamed x84 -> x64, local copies, waits for them, and re-layouts: 21.5 us -> 2.98 us
    ppermute x30, waiting for transfers between devices: 55.5 us -> 64.3 us  [swap(): return lax.ppermute(x, ctx, [(i, i ^ bit) for i in range(world)])]
    all_to_all x1, waiting for transfers between devices: 6.84 us -> 0.01 us  [shards(): lax.all_to_all(outgoing.reshape(EXPERTS, CAP, D), ('exp', 'plane'), split...]
    all_to_all x1, starting transfers between devices: 11.8 us -> 5.79 us  [shards(): lax.all_to_all(expert_rows.reshape(EXPERTS, CAP, D), ('exp', 'plane'), sp...]
    pallas_call x1, Pallas kernels: 17.5 us -> 13 us  [run_expert(): pl.pallas_call(functools.partial(expert_kernel, planes, shared), out_shap...]
    pallas_call x1, Pallas kernels: 12.9 us -> 9.31 us  [attend(): pl.pallas_call(functools.partial(attend_kernel, n), out_shape=[jax.ShapeD...]
    reshape x3 -> x0, local copies, waits for them, and re-layouts: 2.36 us -> none  [shards(): bias = jnp.repeat(jnp.repeat(bias, TILE, axis=1), TILE, axis=2)]
  transfers between devices with their start and end apart: 32 -> 32, of which waited for: 10 -> 9; matrix products, arithmetic and copies ran while one was open for 3% -> 3% of each run, Pallas kernels for 9% -> 8%
where the time goes in v3:
time: 166 us; the launch traced here: 165 us
  waiting for transfers between devices  94.3 us (57%)
  starting transfers between devices  32.9 us (20%)
  Pallas kernels  28.2 us (17%)
  local copies, waits for them, and re-layouts  5.45 us (3%)
  other arithmetic  2.29 us (1%)
    ppermute x30, waiting for transfers between devices, swap(): return lax.ppermute(x, ctx, [(i, i ^ bit) for i in range(world)])  64.3 us
    all_to_all x1, waiting for transfers between devices, shards(): lax.all_to_all(expert_rows.reshape(EXPERTS, CAP, D), ('exp', 'plane'), sp...  30 us
    ppermute x30, starting transfers between devices, swap(): return lax.ppermute(x, ctx, [(i, i ^ bit) for i in range(world)])  20.8 us
    pallas_call x1, Pallas kernels, run_expert(): pl.pallas_call(functools.partial(expert_kernel, planes, shared), out_shap...  13 us
    pallas_call x1, Pallas kernels, attend(): pl.pallas_call(functools.partial(attend_kernel, n), out_shape=[jax.ShapeD...  9.31 us
    all_to_all x1, starting transfers between devices, shards(): lax.all_to_all(outgoing.reshape(EXPERTS, CAP, D), ('exp', 'plane'), split...  6.37 us
    all_to_all x1, starting transfers between devices, shards(): lax.all_to_all(expert_rows.reshape(EXPERTS, CAP, D), ('exp', 'plane'), sp...  5.79 us
    pallas_call x1, Pallas kernels, pack(): pl.pallas_call(functools.partial(pack_kernel, planes), out_shape=[jax.Sha...  4.3 us
  transfers between devices with their start and end apart: 32, of which 9 were waited for; matrix products, arithmetic and copies ran while one was open for 3% of the time, Pallas kernels for 8%

profile of v3, /device:TPU:0, one launch (start us, length us, event | category | flops | bytes accessed | tf_op | source)
XLA Modules:
  0.0 165.3 jit_solution(12889801172640159413)
XLA Ops:
  0.6 1.0 pad_maximum_fusion.rest_0_
  1.6 4.1 %collective-permute-start.7 = (bf16[192,512]{1,0:T(8,128)(2,1)S(1)}, bf16[192,512]{1,0:T(8,128)(2,1)S(1)}, u32[]{:S(2)}, u32[]{:S(2)}) collective-permute-start(bf16[192,512]{1,0:T(8,128)(2,1)S(1)} %pad_maximum_fusion.rest_0_), channel_id=1, source_target_pairs={{0,16},{2,18},{4,20},{6,22},{8,24},{10,26},{12,28},{14,30},{16,0},... | collective-permute-start | bytes 589832 | tf_op jit(solution)/shard_map/ppermute | solution.py:316
  5.7 1.6 collective-permute-start.3
  7.3 1.5 collective-permute-start.1
  8.8 0.7 pad_add_fusion.place_ref
  9.5 4.3 %pack_weights.1 = (bf16[3,64,1792]{2,1,0:T(8,128)(2,1)}, bf16[3,64,1792]{2,1,0:T(8,128)(2,1)}, bf16[3,64,1792]{2,1,0:T(8,128)(2,1)}, bf16[3,64,1792]{2,1,0:T(8,128)(2,1)}) custom-call(s32[2]{0:T(128)} %pad_add_fusion.place_ref, bf16[4,64,1792]{2,1,0:T(8,128)(2,1)} %gate_ref.1, bf16[4,64,1792]{2,1,0:T(8,128)(2,1)} %up_ref.1, bf16[4,64,1792]{2,1,0:T(8,128)(2,1)} %down_ref.1), custom_call_target="tpu_custom_call" | custom-call | tf_op jit(solution)/shard_map/pack_weights/pallas_call | solution.py:44
  16.4 0.7 copy.29.target_ref
  17.8 1.8 %collective-permute-start.5 = (bf16[192,512]{1,0:T(8,128)(2,1)S(1)}, bf16[192,512]{1,0:T(8,128)(2,1)S(1)}, u32[]{:S(2)}, u32[]{:S(2)}) collective-permute-start(bf16[192,512]{1,0:T(8,128)(2,1)S(1)} %collective-permute-done.3.rest_4_), channel_id=1, source_target_pairs={{0,4},{2,6},{4,0},{6,2},{8,12},{10,14},{12,8},{14,10},{16,20},{18,... | collective-permute-start | bytes 589832 | tf_op jit(solution)/shard_map/ppermute | solution.py:316
  19.7 14.4 %collective-permute-done.11.rest_12_ = bf16[192,512]{1,0:T(8,128)(2,1)S(1)} collective-permute-done((bf16[192,512]{1,0:T(8,128)(2,1)S(1)}, bf16[192,512]{1,0:T(8,128)(2,1)S(1)}, u32[]{:S(2)}, u32[]{:S(2)}) %collective-permute-start.11) | collective-permute-done | bytes 196640 | tf_op jit(solution)/shard_map/ppermute | solution.py:316
  35.2 0.6 fusion.8
  36.4 5.0 %collective-permute-done.13.rest_14_ = bf16[192,512]{1,0:T(8,128)(2,1)S(1)} collective-permute-done((bf16[192,512]{1,0:T(8,128)(2,1)S(1)}, bf16[192,512]{1,0:T(8,128)(2,1)S(1)}, u32[]{:S(2)}, u32[]{:S(2)}) %collective-permute-start.13) | collective-permute-done | bytes 196640 | tf_op jit(solution)/shard_map/ppermute | solution.py:316
  41.7 0.6 pad.5.allowed_ref
  42.3 0.7 collective-permute-start.22
  43.2 2.5 %collective-permute-start.16 = (bf16[3,64,1792]{2,1,0:T(8,128)(2,1)}, bf16[3,64,1792]{2,1,0:T(8,128)(2,1)}, u32[]{:S(2)}, u32[]{:S(2)}) collective-permute-start(bf16[3,64,1792]{2,1,0:T(8,128)(2,1)} %get-tuple-element.48), channel_id=1, source_target_pairs={{0,8},{2,10},{4,12},{6,14},{8,0},{10,2},{12,4},{14,6},{16,24},{18,... | collective-permute-start | bytes 2064392 | tf_op jit(solution)/shard_map/ppermute | solution.py:316
  45.7 1.7 %collective-permute-done.15.rest_2_ = bf16[3,64,1792]{2,1,0:T(8,128)(2,1)S(1)} collective-permute-done((bf16[3,64,1792]{2,1,0:T(8,128)(2,1)}, bf16[3,64,1792]{2,1,0:T(8,128)(2,1)S(1)}, u32[]{:S(2)}, u32[]{:S(2)}) %collective-permute-start.15) | collective-permute-done | bytes 688160 | tf_op jit(solution)/shard_map/ppermute | solution.py:316
  47.5 0.7 collective-permute-start.17
  48.3 9.3 %attend.1 = (bf16[192,1024]{1,0:T(8,128)(2,1)}, bf16[192,1024]{1,0:T(8,128)(2,1)}, bf16[576,1024]{1,0:T(8,128)(2,1)}) custom-call(s32[96]{0:T(128)} %convert_element_type.35.live_ref, s32[96]{0:T(128)} %get-tuple-element.56.spot_ref, bf16[8,16,128]{2,1,0:T(8,128)(2,1)} %pad.5.allowed_ref, bf16[192,1024]{1,0:T(8,128)(2,1)} %bitcast.37, ...), custom_call_target="tpu_custom_call" | custom-call | tf_op jit(solution)/shard_map/attend/pallas_call | solution.py:157
  57.6 6.4 %all-to-all-start = ((bf16[8,72,1024]{2,1,0:T(8,128)(2,1)}), bf16[8,72,1024]{2,1,0:T(8,128)(2,1)S(1)}, u32[]{:S(2)}, u32[]{:S(2)}) async-start(bf16[8,72,1024]{2,1,0:T(8,128)(2,1)} %bitcast.34), calls=%async_computation | async-start | bytes 2359296 | tf_op jit(solution)/shard_map/all_to_all | solution.py:355
  64.0 0.9 collective-permute-start.23
  64.9 1.4 collective-permute-start.24
  66.3 13.1 %collective-permute-done.17.rest_3_ = bf16[3,64,1792]{2,1,0:T(8,128)(2,1)} collective-permute-done((bf16[3,64,1792]{2,1,0:T(8,128)(2,1)}, bf16[3,64,1792]{2,1,0:T(8,128)(2,1)}, u32[]{:S(2)}, u32[]{:S(2)}) %collective-permute-start.17) | collective-permute-done | bytes 688160 | tf_op jit(solution)/shard_map/ppermute | solution.py:316
  79.4 1.5 collective-permute-start.25
  81.0 1.6 collective-permute-done.23.rest_9_
  83.0 14.2 %collective-permute-done.24.rest_10_ = bf16[3,64,1792]{2,1,0:T(8,128)(2,1)S(1)} collective-permute-done((bf16[3,64,1792]{2,1,0:T(8,128)(2,1)S(1)}, bf16[3,64,1792]{2,1,0:T(8,128)(2,1)S(1)}, u32[]{:S(2)}, u32[]{:S(2)}) %collective-permute-start.24) | collective-permute-done | bytes 688160 | tf_op jit(solution)/shard_map/ppermute | solution.py:316
  97.8 13.9 %collective-permute-done.25.rest_11_ = bf16[3,64,1792]{2,1,0:T(8,128)(2,1)} collective-permute-done((bf16[3,64,1792]{2,1,0:T(8,128)(2,1)}, bf16[3,64,1792]{2,1,0:T(8,128)(2,1)}, u32[]{:S(2)}, u32[]{:S(2)}) %collective-permute-start.25) | collective-permute-done | bytes 688160 | tf_op jit(solution)/shard_map/ppermute | solution.py:316
  111.7 0.9 copy-done.10
  112.8 0.9 copy-done.12
  114.1 0.6 copy-done.1
  114.8 13.0 %expert.1 = bf16[576,1024]{1,0:T(8,128)(2,1)} custom-call(s32[2]{0:T(128)} %pad_add_fusion.place_ref, bf16[576,1024]{1,0:T(8,128)(2,1)} %bitcast.32, bf16[3,64,1792]{2,1,0:T(8,128)(2,1)} %get-tuple-element.47.rest_0_, bf16[3,64,1792]{2,1,0:T(8,128)(2,1)} %collective-permute-done.16.rest_1_, bf16[3,64,1792]{2,1,0:T(8,128)(2,1)} %copy-done.4, ...), custom_call_target="tpu_custom_call" | custom-call | tf_op jit(solution)/shard_map/expert/pallas_call | solution.py:242
  127.8 5.8 %all-to-all-start.1 = ((bf16[8,72,1024]{2,1,0:T(8,128)(2,1)}), bf16[8,72,1024]{2,1,0:T(8,128)(2,1)S(1)}, u32[]{:S(2)}, u32[]{:S(2)}) async-start(bf16[8,72,1024]{2,1,0:T(8,128)(2,1)} %bitcast.33), calls=%async_computation.1 | async-start | bytes 2359296 | tf_op jit(solution)/shard_map/all_to_all | solution.py:365
  133.7 30.0 %all-to-all-done.1 = bf16[8,72,1024]{2,1,0:T(8,128)(2,1)S(1)} async-done(((bf16[8,72,1024]{2,1,0:T(8,128)(2,1)}), bf16[8,72,1024]{2,1,0:T(8,128)(2,1)S(1)}, u32[]{:S(2)}, u32[]{:S(2)}) %all-to-all-start.1) | async-done | bytes 1179680 | tf_op jit(solution)/shard_map/all_to_all | solution.py:365
  163.7 1.6 combine.1
  (127 shorter events, 7.4 us)
Async XLA Ops:
  1.6 15.5 %collective-permute-start.7 = (bf16[192,512]{1,0:T(8,128)(2,1)S(1)}, bf16[192,512]{1,0:T(8,128)(2,1)S(1)}, u32[]{:S(2)}, u32[]{:S(2)}) collective-permute-start(bf16[192,512]{1,0:T(8,128)(2,1)S(1)} %pad_maximum_fusion.rest_0_), channel_id=1, source_target_pairs={{0,16},{2,18},{4,20},{6,22},{8,24},{10,26},{12,28},{14,30},{16,0},... | collective-permute-start | bytes 589832 | tf_op jit(solution)/shard_map/ppermute | solution.py:316
  5.7 11.8 %collective-permute-start.3 = (bf16[192,512]{1,0:T(8,128)(2,1)S(1)}, bf16[192,512]{1,0:T(8,128)(2,1)S(1)}, u32[]{:S(2)}, u32[]{:S(2)}) collective-permute-start(bf16[192,512]{1,0:T(8,128)(2,1)S(1)} %pad_maximum_fusion.rest_0_), channel_id=1, source_target_pairs={{0,8},{2,10},{4,12},{6,14},{8,0},{10,2},{12,4},{14,6},{16,24},{18,... | collective-permute-start | bytes 589832 | tf_op jit(solution)/shard_map/ppermute | solution.py:316
  7.3 10.5 %collective-permute-start.1 = (bf16[192,512]{1,0:T(8,128)(2,1)S(1)}, bf16[192,512]{1,0:T(8,128)(2,1)S(1)}, u32[]{:S(2)}, u32[]{:S(2)}) collective-permute-start(bf16[192,512]{1,0:T(8,128)(2,1)S(1)} %pad_maximum_fusion.rest_0_), channel_id=1, source_target_pairs={{0,4},{2,6},{4,0},{6,2},{8,12},{10,14},{12,8},{14,10},{16,20},{18,... | collective-permute-start | bytes 589832 | tf_op jit(solution)/shard_map/ppermute | solution.py:316
  8.8 10.8 %collective-permute-start = (bf16[192,512]{1,0:T(8,128)(2,1)S(1)}, bf16[192,512]{1,0:T(8,128)(2,1)S(1)}, u32[]{:S(2)}, u32[]{:S(2)}) collective-permute-start(bf16[192,512]{1,0:T(8,128)(2,1)S(1)} %pad_maximum_fusion.rest_0_), channel_id=1, source_target_pairs={{0,2},{2,0},{4,6},{6,4},{8,10},{10,8},{12,14},{14,12},{16,18},{18,... | collective-permute-start | bytes 589832 | tf_op jit(solution)/shard_map/ppermute | solution.py:316
  13.8 33.7 %collective-permute-start.15 = (bf16[3,64,1792]{2,1,0:T(8,128)(2,1)}, bf16[3,64,1792]{2,1,0:T(8,128)(2,1)S(1)}, u32[]{:S(2)}, u32[]{:S(2)}) collective-permute-start(bf16[3,64,1792]{2,1,0:T(8,128)(2,1)} %get-tuple-element.28), channel_id=1, source_target_pairs={{0,16},{2,18},{4,20},{6,22},{8,24},{10,26},{12,28},{14,30},{16,0},... | collective-permute-start | bytes 2064392 | tf_op jit(solution)/shard_map/ppermute | solution.py:316
  17.1 16.9 %collective-permute-start.11 = (bf16[192,512]{1,0:T(8,128)(2,1)S(1)}, bf16[192,512]{1,0:T(8,128)(2,1)S(1)}, u32[]{:S(2)}, u32[]{:S(2)}) collective-permute-start(bf16[192,512]{1,0:T(8,128)(2,1)S(1)} %collective-permute-done.7.rest_8_), channel_id=1, source_target_pairs={{0,8},{2,10},{4,12},{6,14},{8,0},{10,2},{12,4},{14,6},{16,24},{18,... | collective-permute-start | bytes 589832 | tf_op jit(solution)/shard_map/ppermute | solution.py:316
  17.5 16.5 %collective-permute-start.9 = (bf16[192,512]{1,0:T(8,128)(2,1)S(1)}, bf16[192,512]{1,0:T(8,128)(2,1)S(1)}, u32[]{:S(2)}, u32[]{:S(2)}) collective-permute-start(bf16[192,512]{1,0:T(8,128)(2,1)S(1)} %collective-permute-done.7.rest_8_), channel_id=1, source_target_pairs={{0,4},{2,6},{4,0},{6,2},{8,12},{10,14},{12,8},{14,10},{16,20},{18,... | collective-permute-start | bytes 589832 | tf_op jit(solution)/shard_map/ppermute | solution.py:316
  17.8 16.8 %collective-permute-start.5 = (bf16[192,512]{1,0:T(8,128)(2,1)S(1)}, bf16[192,512]{1,0:T(8,128)(2,1)S(1)}, u32[]{:S(2)}, u32[]{:S(2)}) collective-permute-start(bf16[192,512]{1,0:T(8,128)(2,1)S(1)} %collective-permute-done.3.rest_4_), channel_id=1, source_target_pairs={{0,4},{2,6},{4,0},{6,2},{8,12},{10,14},{12,8},{14,10},{16,20},{18,... | collective-permute-start | bytes 589832 | tf_op jit(solution)/shard_map/ppermute | solution.py:316
  19.6 16.2 %collective-permute-start.8 = (bf16[192,512]{1,0:T(8,128)(2,1)S(1)}, bf16[192,512]{1,0:T(8,128)(2,1)S(1)}, u32[]{:S(2)}, u32[]{:S(2)}) collective-permute-start(bf16[192,512]{1,0:T(8,128)(2,1)S(1)} %collective-permute-done.7.rest_8_), channel_id=1, source_target_pairs={{0,2},{2,0},{4,6},{6,4},{8,10},{10,8},{12,14},{14,12},{16,18},{18,... | collective-permute-start | bytes 589832 | tf_op jit(solution)/shard_map/ppermute | solution.py:316
  34.0 1.8 %collective-permute-start.4 = (bf16[192,512]{1,0:T(8,128)(2,1)S(1)}, bf16[192,512]{1,0:T(8,128)(2,1)S(1)}, u32[]{:S(2)}, u32[]{:S(2)}) collective-permute-start(bf16[192,512]{1,0:T(8,128)(2,1)S(1)} %collective-permute-done.3.rest_4_), channel_id=1, source_target_pairs={{0,2},{2,0},{4,6},{6,4},{8,10},{10,8},{12,14},{14,12},{16,18},{18,... | collective-permute-start | bytes 589832 | tf_op jit(solution)/shard_map/ppermute | solution.py:316
  34.0 2.3 %collective-permute-start.2 = (bf16[192,512]{1,0:T(8,128)(2,1)S(1)}, bf16[192,512]{1,0:T(8,128)(2,1)S(1)}, u32[]{:S(2)}, u32[]{:S(2)}) collective-permute-start(bf16[192,512]{1,0:T(8,128)(2,1)S(1)} %collective-permute-done.1.rest_2_), channel_id=1, source_target_pairs={{0,2},{2,0},{4,6},{6,4},{8,10},{10,8},{12,14},{14,12},{16,18},{18,... | collective-permute-start | bytes 589832 | tf_op jit(solution)/shard_map/ppermute | solution.py:316
  34.5 6.9 %collective-permute-start.13 = (bf16[192,512]{1,0:T(8,128)(2,1)S(1)}, bf16[192,512]{1,0:T(8,128)(2,1)S(1)}, u32[]{:S(2)}, u32[]{:S(2)}) collective-permute-start(bf16[192,512]{1,0:T(8,128)(2,1)S(1)} %collective-permute-done.11.rest_12_), channel_id=1, source_target_pairs={{0,4},{2,6},{4,0},{6,2},{8,12},{10,14},{12,8},{14,10},{16,20},{18,... | collective-permute-start | bytes 589832 | tf_op jit(solution)/shard_map/ppermute | solution.py:316
  35.8 6.5 %collective-permute-start.12 = (bf16[192,512]{1,0:T(8,128)(2,1)S(1)}, bf16[192,512]{1,0:T(8,128)(2,1)S(1)}, u32[]{:S(2)}, u32[]{:S(2)}) collective-permute-start(bf16[192,512]{1,0:T(8,128)(2,1)S(1)} %collective-permute-done.11.rest_12_), channel_id=1, source_target_pairs={{0,2},{2,0},{4,6},{6,4},{8,10},{10,8},{12,14},{14,12},{16,18},{18,... | collective-permute-start | bytes 589832 | tf_op jit(solution)/shard_map/ppermute | solution.py:316
  35.8 7.2 %collective-permute-start.10 = (bf16[192,512]{1,0:T(8,128)(2,1)S(1)}, bf16[192,512]{1,0:T(8,128)(2,1)S(1)}, u32[]{:S(2)}, u32[]{:S(2)}) collective-permute-start(bf16[192,512]{1,0:T(8,128)(2,1)S(1)} %collective-permute-done.9.rest_10_), channel_id=1, source_target_pairs={{0,2},{2,0},{4,6},{6,4},{8,10},{10,8},{12,14},{14,12},{16,18},{18,... | collective-permute-start | bytes 589832 | tf_op jit(solution)/shard_map/ppermute | solution.py:316
  36.3 6.9 %collective-permute-start.6 = (bf16[192,512]{1,0:T(8,128)(2,1)S(1)}, bf16[192,512]{1,0:T(8,128)(2,1)S(1)}, u32[]{:S(2)}, u32[]{:S(2)}) collective-permute-start(bf16[192,512]{1,0:T(8,128)(2,1)S(1)} %collective-permute-done.5.rest_6_), channel_id=1, source_target_pairs={{0,2},{2,0},{4,6},{6,4},{8,10},{10,8},{12,14},{14,12},{16,18},{18,... | collective-permute-start | bytes 589832 | tf_op jit(solution)/shard_map/ppermute | solution.py:316
  41.4 6.0 %collective-permute-start.14 = (bf16[192,512]{1,0:T(8,128)(2,1)S(1)}, bf16[192,512]{1,0:T(8,128)(2,1)S(1)}, u32[]{:S(2)}, u32[]{:S(2)}) collective-permute-start(bf16[192,512]{1,0:T(8,128)(2,1)S(1)} %collective-permute-done.13.rest_14_), channel_id=1, source_target_pairs={{0,2},{2,0},{4,6},{6,4},{8,10},{10,8},{12,14},{14,12},{16,18},{18,... | collective-permute-start | bytes 589832 | tf_op jit(solution)/shard_map/ppermute | solution.py:316
  42.3 22.5 %collective-permute-start.22 = (bf16[3,64,1792]{2,1,0:T(8,128)(2,1)S(1)}, bf16[3,64,1792]{2,1,0:T(8,128)(2,1)S(1)}, u32[]{:S(2)}, u32[]{:S(2)}) collective-permute-start(bf16[3,64,1792]{2,1,0:T(8,128)(2,1)S(1)} %copy-done.3), channel_id=1, source_target_pairs={{0,4},{2,6},{4,0},{6,2},{8,12},{10,14},{12,8},{14,10},{16,20},{18,... | collective-permute-start | bytes 2064392 | tf_op jit(solution)/shard_map/ppermute | solution.py:316
  43.0 23.2 %collective-permute-start.18 = (bf16[3,64,1792]{2,1,0:T(8,128)(2,1)S(1)}, bf16[3,64,1792]{2,1,0:T(8,128)(2,1)}, u32[]{:S(2)}, u32[]{:S(2)}) collective-permute-start(bf16[3,64,1792]{2,1,0:T(8,128)(2,1)S(1)} %copy-done.3), channel_id=1, source_target_pairs={{0,2},{2,0},{4,6},{6,4},{8,10},{10,8},{12,14},{14,12},{16,18},{18,... | collective-permute-start | bytes 2064392 | tf_op jit(solution)/shard_map/ppermute | solution.py:316
  43.2 20.7 %collective-permute-start.16 = (bf16[3,64,1792]{2,1,0:T(8,128)(2,1)}, bf16[3,64,1792]{2,1,0:T(8,128)(2,1)}, u32[]{:S(2)}, u32[]{:S(2)}) collective-permute-start(bf16[3,64,1792]{2,1,0:T(8,128)(2,1)} %get-tuple-element.48), channel_id=1, source_target_pairs={{0,8},{2,10},{4,12},{6,14},{8,0},{10,2},{12,4},{14,6},{16,24},{18,... | collective-permute-start | bytes 2064392 | tf_op jit(solution)/shard_map/ppermute | solution.py:316
  47.5 32.0 %collective-permute-start.17 = (bf16[3,64,1792]{2,1,0:T(8,128)(2,1)}, bf16[3,64,1792]{2,1,0:T(8,128)(2,1)}, u32[]{:S(2)}, u32[]{:S(2)}) collective-permute-start(bf16[3,64,1792]{2,1,0:T(8,128)(2,1)} %get-tuple-element.52), channel_id=1, source_target_pairs={{0,24},{2,26},{4,28},{6,30},{8,16},{10,18},{12,20},{14,22},{16,8},... | collective-permute-start | bytes 2064392 | tf_op jit(solution)/shard_map/ppermute | solution.py:316
  57.6 56.1 %all-to-all-start = ((bf16[8,72,1024]{2,1,0:T(8,128)(2,1)}), bf16[8,72,1024]{2,1,0:T(8,128)(2,1)S(1)}, u32[]{:S(2)}, u32[]{:S(2)}) async-start(bf16[8,72,1024]{2,1,0:T(8,128)(2,1)} %bitcast.34), calls=%async_computation | async-start | bytes 2359296 | tf_op jit(solution)/shard_map/all_to_all | solution.py:355
  64.0 18.5 %collective-permute-start.23 = (bf16[3,64,1792]{2,1,0:T(8,128)(2,1)}, bf16[3,64,1792]{2,1,0:T(8,128)(2,1)S(1)}, u32[]{:S(2)}, u32[]{:S(2)}) collective-permute-start(bf16[3,64,1792]{2,1,0:T(8,128)(2,1)} %collective-permute-done.16.rest_1_), channel_id=1, source_target_pairs={{0,4},{2,6},{4,0},{6,2},{8,12},{10,14},{12,8},{14,10},{16,20},{18,... | collective-permute-start | bytes 2064392 | tf_op jit(solution)/shard_map/ppermute | solution.py:316
  64.9 17.7 %collective-permute-start.26 = (bf16[3,64,1792]{2,1,0:T(8,128)(2,1)S(1)}, bf16[3,64,1792]{2,1,0:T(8,128)(2,1)S(1)}, u32[]{:S(2)}, u32[]{:S(2)}) collective-permute-start(bf16[3,64,1792]{2,1,0:T(8,128)(2,1)S(1)} %collective-permute-done.22.rest_8_), channel_id=1, source_target_pairs={{0,2},{2,0},{4,6},{6,4},{8,10},{10,8},{12,14},{14,12},{16,18},{18,... | collective-permute-start | bytes 2064392 | tf_op jit(solution)/shard_map/ppermute | solution.py:316
  64.9 32.4 %collective-permute-start.24 = (bf16[3,64,1792]{2,1,0:T(8,128)(2,1)S(1)}, bf16[3,64,1792]{2,1,0:T(8,128)(2,1)S(1)}, u32[]{:S(2)}, u32[]{:S(2)}) collective-permute-start(bf16[3,64,1792]{2,1,0:T(8,128)(2,1)S(1)} %collective-permute-done.15.rest_2_), channel_id=1, source_target_pairs={{0,4},{2,6},{4,0},{6,2},{8,12},{10,14},{12,8},{14,10},{16,20},{18,... | collective-permute-start | bytes 2064392 | tf_op jit(solution)/shard_map/ppermute | solution.py:316
  66.3 31.0 %collective-permute-start.19 = (bf16[3,64,1792]{2,1,0:T(8,128)(2,1)}, bf16[3,64,1792]{2,1,0:T(8,128)(2,1)S(1)}, u32[]{:S(2)}, u32[]{:S(2)}) collective-permute-start(bf16[3,64,1792]{2,1,0:T(8,128)(2,1)} %collective-permute-done.16.rest_1_), channel_id=1, source_target_pairs={{0,2},{2,0},{4,6},{6,4},{8,10},{10,8},{12,14},{14,12},{16,18},{18,... | collective-permute-start | bytes 2064392 | tf_op jit(solution)/shard_map/ppermute | solution.py:316
  79.4 32.2 %collective-permute-start.25 = (bf16[3,64,1792]{2,1,0:T(8,128)(2,1)}, bf16[3,64,1792]{2,1,0:T(8,128)(2,1)}, u32[]{:S(2)}, u32[]{:S(2)}) collective-permute-start(bf16[3,64,1792]{2,1,0:T(8,128)(2,1)} %collective-permute-done.17.rest_3_), channel_id=1, source_target_pairs={{0,4},{2,6},{4,0},{6,2},{8,12},{10,14},{12,8},{14,10},{16,20},{18,... | collective-permute-start | bytes 2064392 | tf_op jit(solution)/shard_map/ppermute | solution.py:316
  82.5 29.1 %collective-permute-start.20 = (bf16[3,64,1792]{2,1,0:T(8,128)(2,1)S(1)}, bf16[3,64,1792]{2,1,0:T(8,128)(2,1)S(1)}, u32[]{:S(2)}, u32[]{:S(2)}) collective-permute-start(bf16[3,64,1792]{2,1,0:T(8,128)(2,1)S(1)} %collective-permute-done.15.rest_2_), channel_id=1, source_target_pairs={{0,2},{2,0},{4,6},{6,4},{8,10},{10,8},{12,14},{14,12},{16,18},{18,... | collective-permute-start | bytes 2064392 | tf_op jit(solution)/shard_map/ppermute | solution.py:316
  82.5 29.1 %collective-permute-start.27 = (bf16[3,64,1792]{2,1,0:T(8,128)(2,1)S(1)}, bf16[3,64,1792]{2,1,0:T(8,128)(2,1)S(1)}, u32[]{:S(2)}, u32[]{:S(2)}) collective-permute-start(bf16[3,64,1792]{2,1,0:T(8,128)(2,1)S(1)} %collective-permute-done.23.rest_9_), channel_id=1, source_target_pairs={{0,2},{2,0},{4,6},{6,4},{8,10},{10,8},{12,14},{14,12},{16,18},{18,... | collective-permute-start | bytes 2064392 | tf_op jit(solution)/shard_map/ppermute | solution.py:316
  97.3 14.4 %collective-permute-start.28 = (bf16[3,64,1792]{2,1,0:T(8,128)(2,1)S(1)}, bf16[3,64,1792]{2,1,0:T(8,128)(2,1)S(1)}, u32[]{:S(2)}, u32[]{:S(2)}) collective-permute-start(bf16[3,64,1792]{2,1,0:T(8,128)(2,1)S(1)} %collective-permute-done.24.rest_10_), channel_id=1, source_target_pairs={{0,2},{2,0},{4,6},{6,4},{8,10},{10,8},{12,14},{14,12},{16,18},{18,... | collective-permute-start | bytes 2064392 | tf_op jit(solution)/shard_map/ppermute | solution.py:316
  97.3 16.4 %collective-permute-start.21 = (bf16[3,64,1792]{2,1,0:T(8,128)(2,1)}, bf16[3,64,1792]{2,1,0:T(8,128)(2,1)}, u32[]{:S(2)}, u32[]{:S(2)}) collective-permute-start(bf16[3,64,1792]{2,1,0:T(8,128)(2,1)} %collective-permute-done.17.rest_3_), channel_id=1, source_target_pairs={{0,2},{2,0},{4,6},{6,4},{8,10},{10,8},{12,14},{14,12},{16,18},{18,... | collective-permute-start | bytes 2064392 | tf_op jit(solution)/shard_map/ppermute | solution.py:316
  111.6 2.5 %collective-permute-start.29 = (bf16[3,64,1792]{2,1,0:T(8,128)(2,1)}, bf16[3,64,1792]{2,1,0:T(8,128)(2,1)}, u32[]{:S(2)}, u32[]{:S(2)}) collective-permute-start(bf16[3,64,1792]{2,1,0:T(8,128)(2,1)} %collective-permute-done.25.rest_11_), channel_id=1, source_target_pairs={{0,2},{2,0},{4,6},{6,4},{8,10},{10,8},{12,14},{14,12},{16,18},{18,... | collective-permute-start | bytes 2064392 | tf_op jit(solution)/shard_map/ppermute | solution.py:316
  127.8 35.9 %all-to-all-start.1 = ((bf16[8,72,1024]{2,1,0:T(8,128)(2,1)}), bf16[8,72,1024]{2,1,0:T(8,128)(2,1)S(1)}, u32[]{:S(2)}, u32[]{:S(2)}) async-start(bf16[8,72,1024]{2,1,0:T(8,128)(2,1)} %bitcast.33), calls=%async_computation.1 | async-start | bytes 2359296 | tf_op jit(solution)/shard_map/all_to_all | solution.py:365
  (31 other events, 493.4 us)

commit v4 on v3

--- a/solution.py
+++ b/solution.py
@@ -315,32 +315,45 @@
     def swap(x, bit):
         return lax.ppermute(x, ctx, [(i, i ^ bit) for i in range(world)])
 
-    blocks = {0: jnp.concatenate([key_proj[0], value_proj[0]], axis=1)}
+    def tie(value, places):
+        places = [at for at in places if at in pieces]
+        value, found = lax.optimization_barrier((value, [pieces[at] for at in places]))
+        pieces.update(zip(places, found))
+        return value
+
+    target = slots_of(expert_ids[0])
+    order = key_order(tile_mask[0], me, world)
+    own = jnp.concatenate([key_proj[0], value_proj[0]], axis=1)
+    bit = world // 2
+    half = shared // 2
+    blocks = {0: own, bit: swap(own, bit)}
     packed = pack(place, gate_weight, up_weight, down_weight)
-    pieces = {(0, 0): packed[0]}
-    bit = world // 2
-    blocks[bit] = swap(blocks[0], bit)
     far = [k for k in range(planes) if k >= planes // 2 and k]
     near = [k for k in range(planes) if k < planes // 2 and k]
-    if far:
-        pieces[0, far[0]] = swap(packed[far[0]], far[0] * shared)
-    for k in near:
+    pieces = {(0, 0): packed[0]}
+    for k in far[:1] + near:
         pieces[0, k] = swap(packed[k], k * shared)
+    pieces[half, 0] = swap(packed[0], half)
     bit //= 2
     while bit:
+        if bit == 1:
+            last = world - 2
+            blocks[last] = tie(blocks[last], [(2, 0)])
+            blocks[last], order, target = lax.optimization_barrier((blocks[last], order, target))
         blocks.update({m | bit: swap(x, bit) for m, x in list(blocks.items())})
         bit //= 2
+    blocks = tie(blocks, [(0, 2)])
     if far:
-        blocks, pieces[0, far[0]] = lax.optimization_barrier((blocks, pieces[0, far[0]]))
-        last, pieces[0, far[0]] = lax.optimization_barrier((packed[far[1]], pieces[0, far[0]]))
+        last = tie(packed[far[1]], [(0, far[0])])
         pieces[0, far[1]] = swap(last, far[1] * shared)
-    bit = shared // 2
+    bit = half
     while bit:
-        pieces.update({(m | bit, k): swap(x, bit) for (m, k), x in list(pieces.items())})
+        for (m, k), x in list(pieces.items()):
+            if (m | bit, k) not in pieces:
+                pieces[m | bit, k] = swap(x, bit)
         bit //= 2
 
-    target = slots_of(expert_ids[0])
-    live, spot, allowed = key_order(tile_mask[0], me, world)
+    live, spot, allowed = order
     attention_out, residual, outgoing = attend(
         live,
         spot,
@@ -352,6 +365,7 @@
         moe_gain[None],
         [blocks[m] for m in range(world)],
     )
+    outgoing = tie(outgoing, [(2, 2)])
     arrived = lax.all_to_all(
         outgoing.reshape(EXPERTS, CAP, D), ("exp", "plane"), split_axis=0, concat_axis=0, tiled=True
     )

time: 166 us -> 158 us (0.952)
  waiting for transfers between devices: 94.3 us -> 87.2 us
  starting transfers between devices: 32.9 us -> 30.8 us
    ppermute x30, waiting for transfers between devices: 64.3 us -> 53.7 us  [swap(): return lax.ppermute(x, ctx, [(i, i ^ bit) for i in range(world)])]
    all_to_all x1, waiting for transfers between devices: 0.01 us -> 3.75 us  [shards(): lax.all_to_all(outgoing.reshape(EXPERTS, CAP, D), ('exp', 'plane'), split...]
    all_to_all x1, starting transfers between devices: 5.79 us -> 3.71 us  [shards(): lax.all_to_all(expert_rows.reshape(EXPERTS, CAP, D), ('exp', 'plane'), sp...]
    all_to_all x1, starting transfers between devices: 6.37 us -> 4.65 us  [shards(): lax.all_to_all(outgoing.reshape(EXPERTS, CAP, D), ('exp', 'plane'), split...]
    ppermute x30, starting transfers between devices: 20.8 us -> 22.5 us  [swap(): return lax.ppermute(x, ctx, [(i, i ^ bit) for i in range(world)])]
    unnamed x64 -> x70, local copies, waits for them, and re-layouts: 2.98 us -> 4.17 us
  transfers between devices with their start and end apart: 32 -> 32, of which waited for: 9 -> 14; matrix products, arithmetic and copies ran while one was open for 3% -> 3% of each run, Pallas kernels for 8% -> 9%
where the time goes in v4:
time: 158 us; the launch traced here: 157 us
  waiting for transfers between devices  87.2 us (55%)
  starting transfers between devices  30.8 us (19%)
  Pallas kernels  28.1 us (18%)
  local copies, waits for them, and re-layouts  6.6 us (4%)
  other arithmetic  2.26 us (1%)
    ppermute x30, waiting for transfers between devices, swap(): return lax.ppermute(x, ctx, [(i, i ^ bit) for i in range(world)])  53.7 us
    all_to_all x1, waiting for transfers between devices, shards(): lax.all_to_all(expert_rows.reshape(EXPERTS, CAP, D), ('exp', 'plane'), sp...  29.8 us
    ppermute x30, starting transfers between devices, swap(): return lax.ppermute(x, ctx, [(i, i ^ bit) for i in range(world)])  22.5 us
    pallas_call x1, Pallas kernels, run_expert(): pl.pallas_call(functools.partial(expert_kernel, planes, shared), out_shap...  13 us
    pallas_call x1, Pallas kernels, attend(): pl.pallas_call(functools.partial(attend_kernel, n), out_shape=[jax.ShapeD...  9.3 us
    all_to_all x1, starting transfers between devices, shards(): lax.all_to_all(outgoing.reshape(EXPERTS, CAP, D), ('exp', 'plane'), split...  4.65 us
    pallas_call x1, Pallas kernels, pack(): pl.pallas_call(functools.partial(pack_kernel, planes), out_shape=[jax.Sha...  4.25 us
    unnamed x70, local copies, waits for them, and re-layouts  4.17 us
  transfers between devices with their start and end apart: 32, of which 14 were waited for; matrix products, arithmetic and copies ran while one was open for 3% of the time, Pallas kernels for 9%

profile of v4, /device:TPU:0, one launch (start us, length us, event | category | flops | bytes accessed | tf_op | source)
XLA Modules:
  0.0 157.2 jit_solution(3992575610364490900)
XLA Ops:
  0.6 1.0 pad_maximum_fusion.rest_0_
  1.6 4.1 %collective-permute-start = (bf16[192,512]{1,0:T(8,128)(2,1)S(1)}, bf16[192,512]{1,0:T(8,128)(2,1)S(1)}, u32[]{:S(2)}, u32[]{:S(2)}) collective-permute-start(bf16[192,512]{1,0:T(8,128)(2,1)S(1)} %pad_maximum_fusion.rest_0_), channel_id=1, source_target_pairs={{0,16},{2,18},{4,20},{6,22},{8,24},{10,26},{12,28},{14,30},{16,0},... | collective-permute-start | bytes 589832 | tf_op jit(solution)/shard_map/ppermute | solution.py:316
  5.7 1.6 %collective-permute-start.7 = (bf16[192,512]{1,0:T(8,128)(2,1)S(1)}, bf16[192,512]{1,0:T(8,128)(2,1)S(1)}, u32[]{:S(2)}, u32[]{:S(2)}) collective-permute-start(bf16[192,512]{1,0:T(8,128)(2,1)S(1)} %pad_maximum_fusion.rest_0_), channel_id=1, source_target_pairs={{0,8},{2,10},{4,12},{6,14},{8,0},{10,2},{12,4},{14,6},{16,24},{18,... | collective-permute-start | bytes 589832 | tf_op jit(solution)/shard_map/ppermute | solution.py:316
  7.3 1.5 collective-permute-start.5
  9.4 4.2 %pack_weights.1 = (bf16[3,64,1792]{2,1,0:T(8,128)(2,1)}, bf16[3,64,1792]{2,1,0:T(8,128)(2,1)}, bf16[3,64,1792]{2,1,0:T(8,128)(2,1)}, bf16[3,64,1792]{2,1,0:T(8,128)(2,1)}) custom-call(s32[2]{0:T(128)} %pad_add_fusion.place_ref, bf16[4,64,1792]{2,1,0:T(8,128)(2,1)} %gate_ref.1, bf16[4,64,1792]{2,1,0:T(8,128)(2,1)} %up_ref.1, bf16[4,64,1792]{2,1,0:T(8,128)(2,1)} %down_ref.1), custom_call_target="tpu_custom_call" | custom-call | tf_op jit(solution)/shard_map/pack_weights/pallas_call | solution.py:44
  15.8 0.7 fusion.8
  17.9 1.8 %collective-permute-start.12 = (bf16[192,512]{1,0:T(8,128)(2,1)S(1)}, bf16[192,512]{1,0:T(8,128)(2,1)S(1)}, u32[]{:S(2)}, u32[]{:S(2)}) collective-permute-start(bf16[192,512]{1,0:T(8,128)(2,1)S(1)} %collective-permute-done.rest_8_), channel_id=1, source_target_pairs={{0,4},{2,6},{4,0},{6,2},{8,12},{10,14},{12,8},{14,10},{16,20},{18,... | collective-permute-start | bytes 589832 | tf_op jit(solution)/shard_map/ppermute | solution.py:316
  19.7 13.4 %collective-permute-done.1.rest_12_ = bf16[192,512]{1,0:T(8,128)(2,1)S(1)} collective-permute-done((bf16[192,512]{1,0:T(8,128)(2,1)S(1)}, bf16[192,512]{1,0:T(8,128)(2,1)S(1)}, u32[]{:S(2)}, u32[]{:S(2)}) %collective-permute-start.1) | collective-permute-done | bytes 196640 | tf_op jit(solution)/shard_map/ppermute | solution.py:316
  33.1 1.5 collective-permute-start.2
  34.9 0.6 pad.5.allowed_ref
  36.1 2.9 %collective-permute-done.2.rest_14_ = bf16[192,512]{1,0:T(8,128)(2,1)S(1)} collective-permute-done((bf16[192,512]{1,0:T(8,128)(2,1)S(1)}, bf16[192,512]{1,0:T(8,128)(2,1)S(1)}, u32[]{:S(2)}, u32[]{:S(2)}) %collective-permute-start.2) | collective-permute-done | bytes 196640 | tf_op jit(solution)/shard_map/ppermute | solution.py:316
  39.5 3.5 %collective-permute-done.9.rest_6_ = bf16[192,512]{1,0:T(8,128)(2,1)S(1)} collective-permute-done((bf16[192,512]{1,0:T(8,128)(2,1)S(1)}, bf16[192,512]{1,0:T(8,128)(2,1)S(1)}, u32[]{:S(2)}, u32[]{:S(2)}) %collective-permute-start.9) | collective-permute-done | bytes 196640 | tf_op jit(solution)/shard_map/ppermute | solution.py:316
  45.0 1.0 collective-permute-done.16.rest_2_
  46.1 1.6 %collective-permute-start.17 = (bf16[3,64,1792]{2,1,0:T(8,128)(2,1)S(1)}, bf16[3,64,1792]{2,1,0:T(8,128)(2,1)S(1)}, u32[]{:S(2)}, u32[]{:S(2)}) collective-permute-start(bf16[3,64,1792]{2,1,0:T(8,128)(2,1)S(1)} %collective-permute-done.16.rest_2_), channel_id=1, source_target_pairs={{0,4},{2,6},{4,0},{6,2},{8,12},{10,14},{12,8},{14,10},{16,20},{18,... | collective-permute-start | bytes 2064392 | tf_op jit(solution)/shard_map/ppermute | solution.py:316
  47.7 1.7 %collective-permute-start.18 = (bf16[3,64,1792]{2,1,0:T(8,128)(2,1)}, bf16[3,64,1792]{2,1,0:T(8,128)(2,1)}, u32[]{:S(2)}, u32[]{:S(2)}) collective-permute-start(bf16[3,64,1792]{2,1,0:T(8,128)(2,1)} %get-tuple-element.67), channel_id=1, source_target_pairs={{0,8},{2,10},{4,12},{6,14},{8,0},{10,2},{12,4},{14,6},{16,24},{18,... | collective-permute-start | bytes 2064392 | tf_op jit(solution)/shard_map/ppermute | solution.py:316
  50.0 2.0 %collective-permute-start.19 = (bf16[3,64,1792]{2,1,0:T(8,128)(2,1)}, bf16[3,64,1792]{2,1,0:T(8,128)(2,1)}, u32[]{:S(2)}, u32[]{:S(2)}) collective-permute-start(bf16[3,64,1792]{2,1,0:T(8,128)(2,1)} %get-tuple-element.68), channel_id=1, source_target_pairs={{0,24},{2,26},{4,28},{6,30},{8,16},{10,18},{12,20},{14,22},{16,8},... | collective-permute-start | bytes 2064392 | tf_op jit(solution)/shard_map/ppermute | solution.py:316
  52.0 9.3 %attend.1 = (bf16[192,1024]{1,0:T(8,128)(2,1)}, bf16[192,1024]{1,0:T(8,128)(2,1)}, bf16[576,1024]{1,0:T(8,128)(2,1)}) custom-call(s32[96]{0:T(128)} %convert_element_type.35.live_ref, s32[96]{0:T(128)} %get-tuple-element.40.spot_ref, bf16[8,16,128]{2,1,0:T(8,128)(2,1)} %pad.5.allowed_ref, bf16[192,1024]{1,0:T(8,128)(2,1)} %bitcast.37, ...), custom_call_target="tpu_custom_call" | custom-call | tf_op jit(solution)/shard_map/attend/pallas_call | solution.py:157
  61.3 2.2 %collective-permute-done.17.rest_10_ = bf16[3,64,1792]{2,1,0:T(8,128)(2,1)S(1)} collective-permute-done((bf16[3,64,1792]{2,1,0:T(8,128)(2,1)S(1)}, bf16[3,64,1792]{2,1,0:T(8,128)(2,1)S(1)}, u32[]{:S(2)}, u32[]{:S(2)}) %collective-permute-start.17) | collective-permute-done | bytes 688160 | tf_op jit(solution)/shard_map/ppermute | solution.py:316
  63.5 0.9 copy-done.6
  64.4 4.7 %all-to-all-start = ((bf16[8,72,1024]{2,1,0:T(8,128)(2,1)}), bf16[8,72,1024]{2,1,0:T(8,128)(2,1)S(1)}, u32[]{:S(2)}, u32[]{:S(2)}) async-start(bf16[8,72,1024]{2,1,0:T(8,128)(2,1)} %bitcast.34), calls=%async_computation | async-start | bytes 2359296 | tf_op jit(solution)/shard_map/all_to_all | solution.py:369
  69.1 1.6 %collective-permute-start.24 = (bf16[3,64,1792]{2,1,0:T(8,128)(2,1)}, bf16[3,64,1792]{2,1,0:T(8,128)(2,1)S(1)}, u32[]{:S(2)}, u32[]{:S(2)}) collective-permute-start(bf16[3,64,1792]{2,1,0:T(8,128)(2,1)} %collective-permute-done.18.rest_1_), channel_id=1, source_target_pairs={{0,4},{2,6},{4,0},{6,2},{8,12},{10,14},{12,8},{14,10},{16,20},{18,... | collective-permute-start | bytes 2064392 | tf_op jit(solution)/shard_map/ppermute | solution.py:316
  71.2 11.6 %collective-permute-done.19.rest_3_ = bf16[3,64,1792]{2,1,0:T(8,128)(2,1)} collective-permute-done((bf16[3,64,1792]{2,1,0:T(8,128)(2,1)}, bf16[3,64,1792]{2,1,0:T(8,128)(2,1)}, u32[]{:S(2)}, u32[]{:S(2)}) %collective-permute-start.19) | collective-permute-done | bytes 688160 | tf_op jit(solution)/shard_map/ppermute | solution.py:316
  83.4 4.2 %collective-permute-done.24.rest_9_ = bf16[3,64,1792]{2,1,0:T(8,128)(2,1)S(1)} collective-permute-done((bf16[3,64,1792]{2,1,0:T(8,128)(2,1)}, bf16[3,64,1792]{2,1,0:T(8,128)(2,1)S(1)}, u32[]{:S(2)}, u32[]{:S(2)}) %collective-permute-start.24) | collective-permute-done | bytes 688160 | tf_op jit(solution)/shard_map/ppermute | solution.py:316
  88.2 13.7 %collective-permute-done.25.rest_11_ = bf16[3,64,1792]{2,1,0:T(8,128)(2,1)S(1)} collective-permute-done((bf16[3,64,1792]{2,1,0:T(8,128)(2,1)}, bf16[3,64,1792]{2,1,0:T(8,128)(2,1)S(1)}, u32[]{:S(2)}, u32[]{:S(2)}) %collective-permute-start.25) | collective-permute-done | bytes 688160 | tf_op jit(solution)/shard_map/ppermute | solution.py:316
  102.0 1.0 copy-done.11
  103.0 0.9 copy-done.15
  104.2 3.8 %all-to-all-done = bf16[8,72,1024]{2,1,0:T(8,128)(2,1)S(1)} async-done(((bf16[8,72,1024]{2,1,0:T(8,128)(2,1)}), bf16[8,72,1024]{2,1,0:T(8,128)(2,1)S(1)}, u32[]{:S(2)}, u32[]{:S(2)}) %all-to-all-start) | async-done | bytes 1179680 | tf_op jit(solution)/shard_map/all_to_all | solution.py:369
  107.9 1.0 copy-done.1
  109.0 13.0 %expert.1 = bf16[576,1024]{1,0:T(8,128)(2,1)} custom-call(s32[2]{0:T(128)} %pad_add_fusion.place_ref, bf16[576,1024]{1,0:T(8,128)(2,1)} %bitcast.32, bf16[3,64,1792]{2,1,0:T(8,128)(2,1)} %get-tuple-element.37.rest_0_, bf16[3,64,1792]{2,1,0:T(8,128)(2,1)} %collective-permute-done.18.rest_1_, bf16[3,64,1792]{2,1,0:T(8,128)(2,1)} %copy-done.5, ...), custom_call_target="tpu_custom_call" | custom-call | tf_op jit(solution)/shard_map/expert/pallas_call | solution.py:242
  122.0 3.7 %all-to-all-start.1 = ((bf16[8,72,1024]{2,1,0:T(8,128)(2,1)}), bf16[8,72,1024]{2,1,0:T(8,128)(2,1)S(1)}, u32[]{:S(2)}, u32[]{:S(2)}) async-start(bf16[8,72,1024]{2,1,0:T(8,128)(2,1)} %bitcast.33), calls=%async_computation.1 | async-start | bytes 2359296 | tf_op jit(solution)/shard_map/all_to_all | solution.py:379
  125.9 29.8 %all-to-all-done.1 = bf16[8,72,1024]{2,1,0:T(8,128)(2,1)S(1)} async-done(((bf16[8,72,1024]{2,1,0:T(8,128)(2,1)}), bf16[8,72,1024]{2,1,0:T(8,128)(2,1)S(1)}, u32[]{:S(2)}, u32[]{:S(2)}) %all-to-all-start.1) | async-done | bytes 1179680 | tf_op jit(solution)/shard_map/all_to_all | solution.py:379
  155.6 1.6 %combine.1 = bf16[192,1024]{1,0:T(8,128)(2,1)} custom-call(bf16[576,1024]{1,0:T(8,128)(2,1)S(1)} %bitcast.29, s32[192,2]{1,0:T(8,128)S(1)} %multiply_add_fusion.target_ref, f32[192,2]{1,0:T(8,128)S(1)} %bitcast.31, bf16[192,1024]{1,0:T(8,128)(2,1)S(1)} %copy-done), custom_call_target="tpu_custom_call" | custom-call | tf_op jit(solution)/shard_map/combine/pallas_call | solution.py:272
  (133 shorter events, 10.2 us)
Async XLA Ops:
  1.6 15.0 %collective-permute-start = (bf16[192,512]{1,0:T(8,128)(2,1)S(1)}, bf16[192,512]{1,0:T(8,128)(2,1)S(1)}, u32[]{:S(2)}, u32[]{:S(2)}) collective-permute-start(bf16[192,512]{1,0:T(8,128)(2,1)S(1)} %pad_maximum_fusion.rest_0_), channel_id=1, source_target_pairs={{0,16},{2,18},{4,20},{6,22},{8,24},{10,26},{12,28},{14,30},{16,0},... | collective-permute-start | bytes 589832 | tf_op jit(solution)/shard_map/ppermute | solution.py:316
  5.7 12.0 %collective-permute-start.7 = (bf16[192,512]{1,0:T(8,128)(2,1)S(1)}, bf16[192,512]{1,0:T(8,128)(2,1)S(1)}, u32[]{:S(2)}, u32[]{:S(2)}) collective-permute-start(bf16[192,512]{1,0:T(8,128)(2,1)S(1)} %pad_maximum_fusion.rest_0_), channel_id=1, source_target_pairs={{0,8},{2,10},{4,12},{6,14},{8,0},{10,2},{12,4},{14,6},{16,24},{18,... | collective-permute-start | bytes 589832 | tf_op jit(solution)/shard_map/ppermute | solution.py:316
  7.3 10.6 %collective-permute-start.5 = (bf16[192,512]{1,0:T(8,128)(2,1)S(1)}, bf16[192,512]{1,0:T(8,128)(2,1)S(1)}, u32[]{:S(2)}, u32[]{:S(2)}) collective-permute-start(bf16[192,512]{1,0:T(8,128)(2,1)S(1)} %pad_maximum_fusion.rest_0_), channel_id=1, source_target_pairs={{0,4},{2,6},{4,0},{6,2},{8,12},{10,14},{12,8},{14,10},{16,20},{18,... | collective-permute-start | bytes 589832 | tf_op jit(solution)/shard_map/ppermute | solution.py:316
  13.7 25.3 %collective-permute-start.3 = (bf16[3,64,1792]{2,1,0:T(8,128)(2,1)}, bf16[3,64,1792]{2,1,0:T(8,128)(2,1)S(1)}, u32[]{:S(2)}, u32[]{:S(2)}) collective-permute-start(bf16[3,64,1792]{2,1,0:T(8,128)(2,1)} %get-tuple-element.37.rest_0_), channel_id=1, source_target_pairs={{0,4},{2,6},{4,0},{6,2},{8,12},{10,14},{12,8},{14,10},{16,20},{18,... | collective-permute-start | bytes 2064392 | tf_op jit(solution)/shard_map/ppermute | solution.py:316
  14.2 31.8 %collective-permute-start.16 = (bf16[3,64,1792]{2,1,0:T(8,128)(2,1)}, bf16[3,64,1792]{2,1,0:T(8,128)(2,1)S(1)}, u32[]{:S(2)}, u32[]{:S(2)}) collective-permute-start(bf16[3,64,1792]{2,1,0:T(8,128)(2,1)} %get-tuple-element.44), channel_id=1, source_target_pairs={{0,16},{2,18},{4,20},{6,22},{8,24},{10,26},{12,28},{14,30},{16,0},... | collective-permute-start | bytes 2064392 | tf_op jit(solution)/shard_map/ppermute | solution.py:316
  16.6 16.5 %collective-permute-start.1 = (bf16[192,512]{1,0:T(8,128)(2,1)S(1)}, bf16[192,512]{1,0:T(8,128)(2,1)S(1)}, u32[]{:S(2)}, u32[]{:S(2)}) collective-permute-start(bf16[192,512]{1,0:T(8,128)(2,1)S(1)} %collective-permute-done.rest_8_), channel_id=1, source_target_pairs={{0,8},{2,10},{4,12},{6,14},{8,0},{10,2},{12,4},{14,6},{16,24},{18,... | collective-permute-start | bytes 589832 | tf_op jit(solution)/shard_map/ppermute | solution.py:316
  17.8 17.8 %collective-permute-start.4 = (bf16[192,512]{1,0:T(8,128)(2,1)S(1)}, bf16[192,512]{1,0:T(8,128)(2,1)S(1)}, u32[]{:S(2)}, u32[]{:S(2)}) collective-permute-start(bf16[192,512]{1,0:T(8,128)(2,1)S(1)} %pad_maximum_fusion.rest_0_), channel_id=1, source_target_pairs={{0,2},{2,0},{4,6},{6,4},{8,10},{10,8},{12,14},{14,12},{16,18},{18,... | collective-permute-start | bytes 589832 | tf_op jit(solution)/shard_map/ppermute | solution.py:316
  17.9 17.7 %collective-permute-start.12 = (bf16[192,512]{1,0:T(8,128)(2,1)S(1)}, bf16[192,512]{1,0:T(8,128)(2,1)S(1)}, u32[]{:S(2)}, u32[]{:S(2)}) collective-permute-start(bf16[192,512]{1,0:T(8,128)(2,1)S(1)} %collective-permute-done.rest_8_), channel_id=1, source_target_pairs={{0,4},{2,6},{4,0},{6,2},{8,12},{10,14},{12,8},{14,10},{16,20},{18,... | collective-permute-start | bytes 589832 | tf_op jit(solution)/shard_map/ppermute | solution.py:316
  33.1 5.9 %collective-permute-start.2 = (bf16[192,512]{1,0:T(8,128)(2,1)S(1)}, bf16[192,512]{1,0:T(8,128)(2,1)S(1)}, u32[]{:S(2)}, u32[]{:S(2)}) collective-permute-start(bf16[192,512]{1,0:T(8,128)(2,1)S(1)} %collective-permute-done.1.rest_12_), channel_id=1, source_target_pairs={{0,4},{2,6},{4,0},{6,2},{8,12},{10,14},{12,8},{14,10},{16,20},{18,... | collective-permute-start | bytes 589832 | tf_op jit(solution)/shard_map/ppermute | solution.py:316
  35.5 7.5 %collective-permute-start.11 = (bf16[192,512]{1,0:T(8,128)(2,1)S(1)}, bf16[192,512]{1,0:T(8,128)(2,1)S(1)}, u32[]{:S(2)}, u32[]{:S(2)}) collective-permute-start(bf16[192,512]{1,0:T(8,128)(2,1)S(1)} %collective-permute-done.rest_8_), channel_id=1, source_target_pairs={{0,2},{2,0},{4,6},{6,4},{8,10},{10,8},{12,14},{14,12},{16,18},{18,... | collective-permute-start | bytes 589832 | tf_op jit(solution)/shard_map/ppermute | solution.py:316
  35.6 7.5 %collective-permute-start.9 = (bf16[192,512]{1,0:T(8,128)(2,1)S(1)}, bf16[192,512]{1,0:T(8,128)(2,1)S(1)}, u32[]{:S(2)}, u32[]{:S(2)}) collective-permute-start(bf16[192,512]{1,0:T(8,128)(2,1)S(1)} %collective-permute-done.7.rest_4_), channel_id=1, source_target_pairs={{0,4},{2,6},{4,0},{6,2},{8,12},{10,14},{12,8},{14,10},{16,20},{18,... | collective-permute-start | bytes 589832 | tf_op jit(solution)/shard_map/ppermute | solution.py:316
  39.0 4.5 %collective-permute-start.8 = (bf16[192,512]{1,0:T(8,128)(2,1)S(1)}, bf16[192,512]{1,0:T(8,128)(2,1)S(1)}, u32[]{:S(2)}, u32[]{:S(2)}) collective-permute-start(bf16[192,512]{1,0:T(8,128)(2,1)S(1)} %collective-permute-done.7.rest_4_), channel_id=1, source_target_pairs={{0,2},{2,0},{4,6},{6,4},{8,10},{10,8},{12,14},{14,12},{16,18},{18,... | collective-permute-start | bytes 589832 | tf_op jit(solution)/shard_map/ppermute | solution.py:316
  39.0 4.6 %collective-permute-start.6 = (bf16[192,512]{1,0:T(8,128)(2,1)S(1)}, bf16[192,512]{1,0:T(8,128)(2,1)S(1)}, u32[]{:S(2)}, u32[]{:S(2)}) collective-permute-start(bf16[192,512]{1,0:T(8,128)(2,1)S(1)} %collective-permute-done.5.rest_2_), channel_id=1, source_target_pairs={{0,2},{2,0},{4,6},{6,4},{8,10},{10,8},{12,14},{14,12},{16,18},{18,... | collective-permute-start | bytes 589832 | tf_op jit(solution)/shard_map/ppermute | solution.py:316
  43.0 1.4 collective-permute-start.14
  43.0 1.7 %collective-permute-start.13 = (bf16[192,512]{1,0:T(8,128)(2,1)S(1)}, bf16[192,512]{1,0:T(8,128)(2,1)S(1)}, u32[]{:S(2)}, u32[]{:S(2)}) collective-permute-start(bf16[192,512]{1,0:T(8,128)(2,1)S(1)} %collective-permute-done.12.rest_10_), channel_id=1, source_target_pairs={{0,2},{2,0},{4,6},{6,4},{8,10},{10,8},{12,14},{14,12},{16,18},{18,... | collective-permute-start | bytes 589832 | tf_op jit(solution)/shard_map/ppermute | solution.py:316
  43.5 1.5 collective-permute-start.10
  43.6 2.4 %collective-permute-start.15 = (bf16[192,512]{1,0:T(8,128)(2,1)S(1)}, bf16[192,512]{1,0:T(8,128)(2,1)S(1)}, u32[]{:S(2)}, u32[]{:S(2)}) collective-permute-start(bf16[192,512]{1,0:T(8,128)(2,1)S(1)} %collective-permute-done.2.rest_14_), channel_id=1, source_target_pairs={{0,2},{2,0},{4,6},{6,4},{8,10},{10,8},{12,14},{14,12},{16,18},{18,... | collective-permute-start | bytes 589832 | tf_op jit(solution)/shard_map/ppermute | solution.py:316
  46.1 17.4 %collective-permute-start.17 = (bf16[3,64,1792]{2,1,0:T(8,128)(2,1)S(1)}, bf16[3,64,1792]{2,1,0:T(8,128)(2,1)S(1)}, u32[]{:S(2)}, u32[]{:S(2)}) collective-permute-start(bf16[3,64,1792]{2,1,0:T(8,128)(2,1)S(1)} %collective-permute-done.16.rest_2_), channel_id=1, source_target_pairs={{0,4},{2,6},{4,0},{6,2},{8,12},{10,14},{12,8},{14,10},{16,20},{18,... | collective-permute-start | bytes 2064392 | tf_op jit(solution)/shard_map/ppermute | solution.py:316
  47.7 21.4 %collective-permute-start.18 = (bf16[3,64,1792]{2,1,0:T(8,128)(2,1)}, bf16[3,64,1792]{2,1,0:T(8,128)(2,1)}, u32[]{:S(2)}, u32[]{:S(2)}) collective-permute-start(bf16[3,64,1792]{2,1,0:T(8,128)(2,1)} %get-tuple-element.67), channel_id=1, source_target_pairs={{0,8},{2,10},{4,12},{6,14},{8,0},{10,2},{12,4},{14,6},{16,24},{18,... | collective-permute-start | bytes 2064392 | tf_op jit(solution)/shard_map/ppermute | solution.py:316
  50.0 32.8 %collective-permute-start.19 = (bf16[3,64,1792]{2,1,0:T(8,128)(2,1)}, bf16[3,64,1792]{2,1,0:T(8,128)(2,1)}, u32[]{:S(2)}, u32[]{:S(2)}) collective-permute-start(bf16[3,64,1792]{2,1,0:T(8,128)(2,1)} %get-tuple-element.68), channel_id=1, source_target_pairs={{0,24},{2,26},{4,28},{6,30},{8,16},{10,18},{12,20},{14,22},{16,8},... | collective-permute-start | bytes 2064392 | tf_op jit(solution)/shard_map/ppermute | solution.py:316
  64.4 43.6 %all-to-all-start = ((bf16[8,72,1024]{2,1,0:T(8,128)(2,1)}), bf16[8,72,1024]{2,1,0:T(8,128)(2,1)S(1)}, u32[]{:S(2)}, u32[]{:S(2)}) async-start(bf16[8,72,1024]{2,1,0:T(8,128)(2,1)} %bitcast.34), calls=%async_computation | async-start | bytes 2359296 | tf_op jit(solution)/shard_map/all_to_all | solution.py:369
  69.0 14.3 %collective-permute-start.20 = (bf16[3,64,1792]{2,1,0:T(8,128)(2,1)S(1)}, bf16[3,64,1792]{2,1,0:T(8,128)(2,1)S(1)}, u32[]{:S(2)}, u32[]{:S(2)}) collective-permute-start(bf16[3,64,1792]{2,1,0:T(8,128)(2,1)S(1)} %copy-done.3), channel_id=1, source_target_pairs={{0,2},{2,0},{4,6},{6,4},{8,10},{10,8},{12,14},{14,12},{16,18},{18,... | collective-permute-start | bytes 2064392 | tf_op jit(solution)/shard_map/ppermute | solution.py:316
  69.1 18.5 %collective-permute-start.24 = (bf16[3,64,1792]{2,1,0:T(8,128)(2,1)}, bf16[3,64,1792]{2,1,0:T(8,128)(2,1)S(1)}, u32[]{:S(2)}, u32[]{:S(2)}) collective-permute-start(bf16[3,64,1792]{2,1,0:T(8,128)(2,1)} %collective-permute-done.18.rest_1_), channel_id=1, source_target_pairs={{0,4},{2,6},{4,0},{6,2},{8,12},{10,14},{12,8},{14,10},{16,20},{18,... | collective-permute-start | bytes 2064392 | tf_op jit(solution)/shard_map/ppermute | solution.py:316
  70.7 16.9 %collective-permute-start.26 = (bf16[3,64,1792]{2,1,0:T(8,128)(2,1)S(1)}, bf16[3,64,1792]{2,1,0:T(8,128)(2,1)S(1)}, u32[]{:S(2)}, u32[]{:S(2)}) collective-permute-start(bf16[3,64,1792]{2,1,0:T(8,128)(2,1)S(1)} %collective-permute-done.3.rest_8_), channel_id=1, source_target_pairs={{0,2},{2,0},{4,6},{6,4},{8,10},{10,8},{12,14},{14,12},{16,18},{18,... | collective-permute-start | bytes 2064392 | tf_op jit(solution)/shard_map/ppermute | solution.py:316
  70.9 17.3 %collective-permute-start.21 = (bf16[3,64,1792]{2,1,0:T(8,128)(2,1)}, bf16[3,64,1792]{2,1,0:T(8,128)(2,1)S(1)}, u32[]{:S(2)}, u32[]{:S(2)}) collective-permute-start(bf16[3,64,1792]{2,1,0:T(8,128)(2,1)} %collective-permute-done.18.rest_1_), channel_id=1, source_target_pairs={{0,2},{2,0},{4,6},{6,4},{8,10},{10,8},{12,14},{14,12},{16,18},{18,... | collective-permute-start | bytes 2064392 | tf_op jit(solution)/shard_map/ppermute | solution.py:316
  82.8 19.1 %collective-permute-start.25 = (bf16[3,64,1792]{2,1,0:T(8,128)(2,1)}, bf16[3,64,1792]{2,1,0:T(8,128)(2,1)S(1)}, u32[]{:S(2)}, u32[]{:S(2)}) collective-permute-start(bf16[3,64,1792]{2,1,0:T(8,128)(2,1)} %collective-permute-done.19.rest_3_), channel_id=1, source_target_pairs={{0,4},{2,6},{4,0},{6,2},{8,12},{10,14},{12,8},{14,10},{16,20},{18,... | collective-permute-start | bytes 2064392 | tf_op jit(solution)/shard_map/ppermute | solution.py:316
  83.3 18.6 %collective-permute-start.22 = (bf16[3,64,1792]{2,1,0:T(8,128)(2,1)S(1)}, bf16[3,64,1792]{2,1,0:T(8,128)(2,1)S(1)}, u32[]{:S(2)}, u32[]{:S(2)}) collective-permute-start(bf16[3,64,1792]{2,1,0:T(8,128)(2,1)S(1)} %collective-permute-done.16.rest_2_), channel_id=1, source_target_pairs={{0,2},{2,0},{4,6},{6,4},{8,10},{10,8},{12,14},{14,12},{16,18},{18,... | collective-permute-start | bytes 2064392 | tf_op jit(solution)/shard_map/ppermute | solution.py:316
  87.6 14.3 %collective-permute-start.27 = (bf16[3,64,1792]{2,1,0:T(8,128)(2,1)S(1)}, bf16[3,64,1792]{2,1,0:T(8,128)(2,1)S(1)}, u32[]{:S(2)}, u32[]{:S(2)}) collective-permute-start(bf16[3,64,1792]{2,1,0:T(8,128)(2,1)S(1)} %collective-permute-done.24.rest_9_), channel_id=1, source_target_pairs={{0,2},{2,0},{4,6},{6,4},{8,10},{10,8},{12,14},{14,12},{16,18},{18,... | collective-permute-start | bytes 2064392 | tf_op jit(solution)/shard_map/ppermute | solution.py:316
  87.6 14.3 %collective-permute-start.23 = (bf16[3,64,1792]{2,1,0:T(8,128)(2,1)}, bf16[3,64,1792]{2,1,0:T(8,128)(2,1)S(1)}, u32[]{:S(2)}, u32[]{:S(2)}) collective-permute-start(bf16[3,64,1792]{2,1,0:T(8,128)(2,1)} %collective-permute-done.19.rest_3_), channel_id=1, source_target_pairs={{0,2},{2,0},{4,6},{6,4},{8,10},{10,8},{12,14},{14,12},{16,18},{18,... | collective-permute-start | bytes 2064392 | tf_op jit(solution)/shard_map/ppermute | solution.py:316
  88.1 13.8 %collective-permute-start.28 = (bf16[3,64,1792]{2,1,0:T(8,128)(2,1)}, bf16[3,64,1792]{2,1,0:T(8,128)(2,1)S(1)}, u32[]{:S(2)}, u32[]{:S(2)}) collective-permute-start(bf16[3,64,1792]{2,1,0:T(8,128)(2,1)} %copy-done.6), channel_id=1, source_target_pairs={{0,2},{2,0},{4,6},{6,4},{8,10},{10,8},{12,14},{14,12},{16,18},{18,... | collective-permute-start | bytes 2064392 | tf_op jit(solution)/shard_map/ppermute | solution.py:316
  101.9 2.3 %collective-permute-start.29 = (bf16[3,64,1792]{2,1,0:T(8,128)(2,1)S(1)}, bf16[3,64,1792]{2,1,0:T(8,128)(2,1)}, u32[]{:S(2)}, u32[]{:S(2)}) collective-permute-start(bf16[3,64,1792]{2,1,0:T(8,128)(2,1)S(1)} %collective-permute-done.25.rest_11_), channel_id=1, source_target_pairs={{0,2},{2,0},{4,6},{6,4},{8,10},{10,8},{12,14},{14,12},{16,18},{18,... | collective-permute-start | bytes 2064392 | tf_op jit(solution)/shard_map/ppermute | solution.py:316
  122.0 33.6 %all-to-all-start.1 = ((bf16[8,72,1024]{2,1,0:T(8,128)(2,1)}), bf16[8,72,1024]{2,1,0:T(8,128)(2,1)S(1)}, u32[]{:S(2)}, u32[]{:S(2)}) async-start(bf16[8,72,1024]{2,1,0:T(8,128)(2,1)} %bitcast.33), calls=%async_computation.1 | async-start | bytes 2359296 | tf_op jit(solution)/shard_map/all_to_all | solution.py:379
  (34 other events, 411.1 us)

commit v5 on v4

--- a/solution.py
+++ b/solution.py
@@ -197,59 +197,58 @@
     return live.astype(jnp.int32), spot.astype(jnp.int32), placed
 
 
-def expert_kernel(planes, shared, place_ref, rows_ref, *rest):
+def expert_kernel(planes, shared, cuts, step, place_ref, rows_in, *rest):
     count = planes * shared
     pieces = rest[:count]
-    out_ref, gate, up, down, total, sems = rest[count:]
-    depth, ff = pieces[0].shape[1:]
+    out_ref, rows_ref, full, total, sems = rest[count:]
+    depth = pieces[0].shape[1]
     plane, seat = place_ref[0], place_ref[1]
-    copies = [[], [], []]
-    for w, full in enumerate((gate, up, down)):
-        for m in range(shared):
-            for k in range(planes):
-                at = ((plane ^ k) * shared + (seat ^ m)) * depth
-                target = full.at[pl.ds(pl.multiple_of(at, depth), depth), :]
-                n = m * planes + k
-                copies[w].append(pltpu.make_async_copy(pieces[n].at[w], target, sems.at[w * count + n]))
-    for group in copies:
-        for copy in group:
-            copy.start()
-    for group in copies[:2]:
-        for copy in group:
+    rows_copy = pltpu.make_async_copy(rows_in, rows_ref, sems.at[count * len(cuts)])
+    copies = []
+    for c, (low, high) in enumerate(cuts):
+        for n in range(count):
+            m, k = divmod(n, planes)
+            at = ((plane ^ k) * shared + (seat ^ m)) * depth
+            target = full.at[:, pl.ds(pl.multiple_of(at, depth), depth), pl.ds(low, high - low)]
+            copies.append(pltpu.make_async_copy(pieces[n].at[:, :, pl.ds(low, high - low)], target, sems.at[c * count + n]))
+            copies[-1].start()
+        if c == 0:
+            rows_copy.start()
+    rows_copy.wait()
+    for c, (low, high) in enumerate(cuts):
+        for copy in copies[c * count : (c + 1) * count]:
             copy.wait()
-    step = 256
-    for n, c in enumerate(range(0, ff, step)):
-        rows = rows_ref[...]
-        gated = jnp.dot(rows, gate[:, c : c + step], preferred_element_type=jnp.float32)
-        upper = jnp.dot(rows, up[:, c : c + step], preferred_element_type=jnp.float32)
-        hidden = (gated / (1.0 + jnp.exp(-gated)) * upper).astype(jnp.bfloat16)
-        if n == 0:
-            for copy in copies[2]:
-                copy.wait()
-        part = lax.dot_general(
-            hidden, down[:, c : c + step], (((1,), (1,)), ((), ())), preferred_element_type=jnp.float32
-        )
-        if n == 0:
-            total[...] = part
-        else:
-            total[...] += part
+        for at in range(low, high, step):
+            rows = rows_ref[...]
+            gated = jnp.dot(rows, full[0, :, at : at + step], preferred_element_type=jnp.float32)
+            upper = jnp.dot(rows, full[1, :, at : at + step], preferred_element_type=jnp.float32)
+            hidden = (gated / (1.0 + jnp.exp(-gated)) * upper).astype(jnp.bfloat16)
+            part = lax.dot_general(
+                hidden, full[2, :, at : at + step], (((1,), (1,)), ((), ())), preferred_element_type=jnp.float32
+            )
+            if at == 0:
+                total[...] = part
+            else:
+                total[...] += part
     out_ref[...] = total[...].astype(jnp.bfloat16)
 
 
 def run_expert(place, rows, pieces, planes, shared):
     depth, ff = pieces[0].shape[1:]
     count = planes * shared
+    step = 256
+    edges = [0, step, 3 * step, ff]
+    cuts = list(zip(edges[:-1], edges[1:]))
     return pl.pallas_call(
-        functools.partial(expert_kernel, planes, shared),
+        functools.partial(expert_kernel, planes, shared, cuts, step),
         out_shape=jax.ShapeDtypeStruct(rows.shape, jnp.bfloat16),
-        in_specs=[SMEM, VMEM] + [ANY] * count,
+        in_specs=[SMEM, ANY] + [ANY] * count,
         out_specs=VMEM,
         scratch_shapes=[
-            pltpu.VMEM((D, ff), jnp.bfloat16),
-            pltpu.VMEM((D, ff), jnp.bfloat16),
-            pltpu.VMEM((D, ff), jnp.bfloat16),
+            pltpu.VMEM(rows.shape, jnp.bfloat16),
+            pltpu.VMEM((3, D, ff), jnp.bfloat16),
             pltpu.VMEM(rows.shape, jnp.float32),
-            pltpu.SemaphoreType.DMA((3 * count,)),
+            pltpu.SemaphoreType.DMA((count * len(cuts) + 1,)),
         ],
         compiler_params=pltpu.CompilerParams(vmem_limit_bytes=60 * MB),
         name="expert",
@@ -340,12 +339,13 @@
             last = world - 2
             blocks[last] = tie(blocks[last], [(2, 0)])
             blocks[last], order, target = lax.optimization_barrier((blocks[last], order, target))
+            if far:
+                early = half + shared
+                blocks[early], second = lax.optimization_barrier((blocks[early], packed[far[1]]))
+                pieces[0, far[1]] = swap(second, far[1] * shared)
         blocks.update({m | bit: swap(x, bit) for m, x in list(blocks.items())})
         bit //= 2
     blocks = tie(blocks, [(0, 2)])
-    if far:
-        last = tie(packed[far[1]], [(0, far[0])])
-        pieces[0, far[1]] = swap(last, far[1] * shared)
     bit = half
     while bit:
         for (m, k), x in list(pieces.items()):

time: 158 us -> 155 us (0.981)
  starting transfers between devices: 30.8 us -> 29.2 us
    pallas_call x1, Pallas kernels: 13 us -> 11 us  [run_expert(): pl.pallas_call(functools.partial(expert_kernel, planes, shared, cuts, ste...]
    pallas_call x1, Pallas kernels: 9.3 us -> 11.2 us  [attend(): pl.pallas_call(functools.partial(attend_kernel, n), out_shape=[jax.ShapeD...]
  transfers between devices with their start and end apart: 32 -> 32, of which waited for: 14 -> 14; matrix products, arithmetic and copies ran while one was open for 3% -> 3% of each run, Pallas kernels for 9% -> 10%
where the time goes in v5:
time: 155 us; the launch traced here: 154 us
  waiting for transfers between devices  85.8 us (55%)
  starting transfers between devices  29.2 us (19%)
  Pallas kernels  28.1 us (18%)
  local copies, waits for them, and re-layouts  6.59 us (4%)
  other arithmetic  2.26 us (1%)
    ppermute x30, waiting for transfers between devices, swap(): return lax.ppermute(x, ctx, [(i, i ^ bit) for i in range(world)])  52.7 us
    all_to_all x1, waiting for transfers between devices, shards(): lax.all_to_all(expert_rows.reshape(EXPERTS, CAP, D), ('exp', 'plane'), sp...  29.5 us
    ppermute x30, starting transfers between devices, swap(): return lax.ppermute(x, ctx, [(i, i ^ bit) for i in range(world)])  21.6 us
    pallas_call x1, Pallas kernels, attend(): pl.pallas_call(functools.partial(attend_kernel, n), out_shape=[jax.ShapeD...  11.2 us
    pallas_call x1, Pallas kernels, run_expert(): pl.pallas_call(functools.partial(expert_kernel, planes, shared, cuts, ste...  11 us
    pallas_call x1, Pallas kernels, pack(): pl.pallas_call(functools.partial(pack_kernel, planes), out_shape=[jax.Sha...  4.25 us
    unnamed x70, local copies, waits for them, and re-layouts  4.16 us
    all_to_all x1, starting transfers between devices, shards(): lax.all_to_all(outgoing.reshape(EXPERTS, CAP, D), ('exp', 'plane'), split...  3.91 us
  transfers between devices with their start and end apart: 32, of which 14 were waited for; matrix products, arithmetic and copies ran while one was open for 3% of the time, Pallas kernels for 10%

profile of v5, /device:TPU:0, one launch (start us, length us, event | category | flops | bytes accessed | tf_op | source)
XLA Modules:
  0.0 154.2 jit_solution(12871623004758900904)
XLA Ops:
  0.6 1.0 pad_maximum_fusion.rest_0_
  1.6 4.1 %collective-permute-start = (bf16[192,512]{1,0:T(8,128)(2,1)S(1)}, bf16[192,512]{1,0:T(8,128)(2,1)S(1)}, u32[]{:S(2)}, u32[]{:S(2)}) collective-permute-start(bf16[192,512]{1,0:T(8,128)(2,1)S(1)} %pad_maximum_fusion.rest_0_), channel_id=1, source_target_pairs={{0,16},{2,18},{4,20},{6,22},{8,24},{10,26},{12,28},{14,30},{16,0},... | collective-permute-start | bytes 589832 | tf_op jit(solution)/shard_map/ppermute | solution.py:315
  5.7 1.6 %collective-permute-start.7 = (bf16[192,512]{1,0:T(8,128)(2,1)S(1)}, bf16[192,512]{1,0:T(8,128)(2,1)S(1)}, u32[]{:S(2)}, u32[]{:S(2)}) collective-permute-start(bf16[192,512]{1,0:T(8,128)(2,1)S(1)} %pad_maximum_fusion.rest_0_), channel_id=1, source_target_pairs={{0,8},{2,10},{4,12},{6,14},{8,0},{10,2},{12,4},{14,6},{16,24},{18,... | collective-permute-start | bytes 589832 | tf_op jit(solution)/shard_map/ppermute | solution.py:315
  7.3 1.5 collective-permute-start.5
  9.4 4.2 %pack_weights.1 = (bf16[3,64,1792]{2,1,0:T(8,128)(2,1)}, bf16[3,64,1792]{2,1,0:T(8,128)(2,1)}, bf16[3,64,1792]{2,1,0:T(8,128)(2,1)}, bf16[3,64,1792]{2,1,0:T(8,128)(2,1)}) custom-call(s32[2]{0:T(128)} %pad_add_fusion.place_ref, bf16[4,64,1792]{2,1,0:T(8,128)(2,1)} %gate_ref.1, bf16[4,64,1792]{2,1,0:T(8,128)(2,1)} %up_ref.1, bf16[4,64,1792]{2,1,0:T(8,128)(2,1)} %down_ref.1), custom_call_target="tpu_custom_call" | custom-call | tf_op jit(solution)/shard_map/pack_weights/pallas_call | solution.py:44
  15.8 0.7 fusion.8
  17.9 1.8 %collective-permute-start.9 = (bf16[192,512]{1,0:T(8,128)(2,1)S(1)}, bf16[192,512]{1,0:T(8,128)(2,1)S(1)}, u32[]{:S(2)}, u32[]{:S(2)}) collective-permute-start(bf16[192,512]{1,0:T(8,128)(2,1)S(1)} %collective-permute-done.7.rest_4_), channel_id=1, source_target_pairs={{0,4},{2,6},{4,0},{6,2},{8,12},{10,14},{12,8},{14,10},{16,20},{18,... | collective-permute-start | bytes 589832 | tf_op jit(solution)/shard_map/ppermute | solution.py:315
  19.7 13.4 %collective-permute-done.1.rest_12_ = bf16[192,512]{1,0:T(8,128)(2,1)S(1)} collective-permute-done((bf16[192,512]{1,0:T(8,128)(2,1)S(1)}, bf16[192,512]{1,0:T(8,128)(2,1)S(1)}, u32[]{:S(2)}, u32[]{:S(2)}) %collective-permute-start.1) | collective-permute-done | bytes 196640 | tf_op jit(solution)/shard_map/ppermute | solution.py:315
  33.1 1.5 collective-permute-start.2
  34.9 0.6 pad.5.allowed_ref
  36.0 4.8 %collective-permute-done.2.rest_14_ = bf16[192,512]{1,0:T(8,128)(2,1)S(1)} collective-permute-done((bf16[192,512]{1,0:T(8,128)(2,1)S(1)}, bf16[192,512]{1,0:T(8,128)(2,1)S(1)}, u32[]{:S(2)}, u32[]{:S(2)}) %collective-permute-start.2) | collective-permute-done | bytes 196640 | tf_op jit(solution)/shard_map/ppermute | solution.py:315
  41.3 1.6 %collective-permute-done.12.rest_10_ = bf16[192,512]{1,0:T(8,128)(2,1)S(1)} collective-permute-done((bf16[192,512]{1,0:T(8,128)(2,1)S(1)}, bf16[192,512]{1,0:T(8,128)(2,1)S(1)}, u32[]{:S(2)}, u32[]{:S(2)}) %collective-permute-start.12) | collective-permute-done | bytes 196640 | tf_op jit(solution)/shard_map/ppermute | solution.py:315
  44.9 1.1 collective-permute-done.16.rest_2_
  46.1 1.6 %collective-permute-start.17 = (bf16[3,64,1792]{2,1,0:T(8,128)(2,1)S(1)}, bf16[3,64,1792]{2,1,0:T(8,128)(2,1)S(1)}, u32[]{:S(2)}, u32[]{:S(2)}) collective-permute-start(bf16[3,64,1792]{2,1,0:T(8,128)(2,1)S(1)} %collective-permute-done.16.rest_2_), channel_id=1, source_target_pairs={{0,4},{2,6},{4,0},{6,2},{8,12},{10,14},{12,8},{14,10},{16,20},{18,... | collective-permute-start | bytes 2064392 | tf_op jit(solution)/shard_map/ppermute | solution.py:315
  47.7 1.1 collective-permute-start.18
  48.8 1.5 collective-permute-start.19
  50.9 11.2 %attend.1 = (bf16[192,1024]{1,0:T(8,128)(2,1)}, bf16[192,1024]{1,0:T(8,128)(2,1)}, bf16[576,1024]{1,0:T(8,128)(2,1)}) custom-call(s32[96]{0:T(128)} %convert_element_type.35.live_ref, s32[96]{0:T(128)} %get-tuple-element.40.spot_ref, bf16[8,16,128]{2,1,0:T(8,128)(2,1)} %pad.5.allowed_ref, bf16[192,1024]{1,0:T(8,128)(2,1)} %bitcast.37, ...), custom_call_target="tpu_custom_call" | custom-call | tf_op jit(solution)/shard_map/attend/pallas_call | solution.py:157
  62.1 1.4 collective-permute-done.17.rest_10_
  63.5 0.9 copy-done.6
  64.4 3.9 %all-to-all-start = ((bf16[8,72,1024]{2,1,0:T(8,128)(2,1)}), bf16[8,72,1024]{2,1,0:T(8,128)(2,1)S(1)}, u32[]{:S(2)}, u32[]{:S(2)}) async-start(bf16[8,72,1024]{2,1,0:T(8,128)(2,1)} %bitcast.34), calls=%async_computation | async-start | bytes 2359296 | tf_op jit(solution)/shard_map/all_to_all | solution.py:369
  68.9 1.5 collective-permute-start.24
  70.4 11.3 %collective-permute-done.19.rest_3_ = bf16[3,64,1792]{2,1,0:T(8,128)(2,1)} collective-permute-done((bf16[3,64,1792]{2,1,0:T(8,128)(2,1)}, bf16[3,64,1792]{2,1,0:T(8,128)(2,1)}, u32[]{:S(2)}, u32[]{:S(2)}) %collective-permute-start.19) | collective-permute-done | bytes 688160 | tf_op jit(solution)/shard_map/ppermute | solution.py:315
  82.8 4.6 %collective-permute-done.24.rest_9_ = bf16[3,64,1792]{2,1,0:T(8,128)(2,1)S(1)} collective-permute-done((bf16[3,64,1792]{2,1,0:T(8,128)(2,1)}, bf16[3,64,1792]{2,1,0:T(8,128)(2,1)S(1)}, u32[]{:S(2)}, u32[]{:S(2)}) %collective-permute-start.24) | collective-permute-done | bytes 688160 | tf_op jit(solution)/shard_map/ppermute | solution.py:315
  87.9 13.4 %collective-permute-done.25.rest_11_ = bf16[3,64,1792]{2,1,0:T(8,128)(2,1)S(1)} collective-permute-done((bf16[3,64,1792]{2,1,0:T(8,128)(2,1)}, bf16[3,64,1792]{2,1,0:T(8,128)(2,1)S(1)}, u32[]{:S(2)}, u32[]{:S(2)}) %collective-permute-start.25) | collective-permute-done | bytes 688160 | tf_op jit(solution)/shard_map/ppermute | solution.py:315
  101.4 1.0 copy-done.11
  102.4 0.9 copy-done.15
  103.5 3.6 %all-to-all-done = bf16[8,72,1024]{2,1,0:T(8,128)(2,1)S(1)} async-done(((bf16[8,72,1024]{2,1,0:T(8,128)(2,1)}), bf16[8,72,1024]{2,1,0:T(8,128)(2,1)S(1)}, u32[]{:S(2)}, u32[]{:S(2)}) %all-to-all-start) | async-done | bytes 1179680 | tf_op jit(solution)/shard_map/all_to_all | solution.py:369
  107.1 1.0 copy-done.1
  108.2 11.0 %expert.1 = bf16[576,1024]{1,0:T(8,128)(2,1)} custom-call(s32[2]{0:T(128)} %pad_add_fusion.place_ref, bf16[576,1024]{1,0:T(8,128)(2,1)} %bitcast.32, bf16[3,64,1792]{2,1,0:T(8,128)(2,1)} %get-tuple-element.37.rest_0_, bf16[3,64,1792]{2,1,0:T(8,128)(2,1)} %collective-permute-done.18.rest_1_, bf16[3,64,1792]{2,1,0:T(8,128)(2,1)} %copy-done.5, ...), custom_call_target="tpu_custom_call" | custom-call | tf_op jit(solution)/shard_map/expert/pallas_call | solution.py:242
  119.2 3.7 %all-to-all-start.1 = ((bf16[8,72,1024]{2,1,0:T(8,128)(2,1)}), bf16[8,72,1024]{2,1,0:T(8,128)(2,1)S(1)}, u32[]{:S(2)}, u32[]{:S(2)}) async-start(bf16[8,72,1024]{2,1,0:T(8,128)(2,1)} %bitcast.33), calls=%async_computation.1 | async-start | bytes 2359296 | tf_op jit(solution)/shard_map/all_to_all | solution.py:379
  123.1 29.5 %all-to-all-done.1 = bf16[8,72,1024]{2,1,0:T(8,128)(2,1)S(1)} async-done(((bf16[8,72,1024]{2,1,0:T(8,128)(2,1)}), bf16[8,72,1024]{2,1,0:T(8,128)(2,1)S(1)}, u32[]{:S(2)}, u32[]{:S(2)}) %all-to-all-start.1) | async-done | bytes 1179680 | tf_op jit(solution)/shard_map/all_to_all | solution.py:379
  152.6 1.6 %combine.1 = bf16[192,1024]{1,0:T(8,128)(2,1)} custom-call(bf16[576,1024]{1,0:T(8,128)(2,1)S(1)} %bitcast.29, s32[192,2]{1,0:T(8,128)S(1)} %multiply_add_fusion.target_ref, f32[192,2]{1,0:T(8,128)S(1)} %bitcast.31, bf16[192,1024]{1,0:T(8,128)(2,1)S(1)} %copy-done), custom_call_target="tpu_custom_call" | custom-call | tf_op jit(solution)/shard_map/combine/pallas_call | solution.py:271
  (133 shorter events, 10.5 us)
Async XLA Ops:
  1.6 15.0 %collective-permute-start = (bf16[192,512]{1,0:T(8,128)(2,1)S(1)}, bf16[192,512]{1,0:T(8,128)(2,1)S(1)}, u32[]{:S(2)}, u32[]{:S(2)}) collective-permute-start(bf16[192,512]{1,0:T(8,128)(2,1)S(1)} %pad_maximum_fusion.rest_0_), channel_id=1, source_target_pairs={{0,16},{2,18},{4,20},{6,22},{8,24},{10,26},{12,28},{14,30},{16,0},... | collective-permute-start | bytes 589832 | tf_op jit(solution)/shard_map/ppermute | solution.py:315
  5.7 12.0 %collective-permute-start.7 = (bf16[192,512]{1,0:T(8,128)(2,1)S(1)}, bf16[192,512]{1,0:T(8,128)(2,1)S(1)}, u32[]{:S(2)}, u32[]{:S(2)}) collective-permute-start(bf16[192,512]{1,0:T(8,128)(2,1)S(1)} %pad_maximum_fusion.rest_0_), channel_id=1, source_target_pairs={{0,8},{2,10},{4,12},{6,14},{8,0},{10,2},{12,4},{14,6},{16,24},{18,... | collective-permute-start | bytes 589832 | tf_op jit(solution)/shard_map/ppermute | solution.py:315
  7.3 10.6 %collective-permute-start.5 = (bf16[192,512]{1,0:T(8,128)(2,1)S(1)}, bf16[192,512]{1,0:T(8,128)(2,1)S(1)}, u32[]{:S(2)}, u32[]{:S(2)}) collective-permute-start(bf16[192,512]{1,0:T(8,128)(2,1)S(1)} %pad_maximum_fusion.rest_0_), channel_id=1, source_target_pairs={{0,4},{2,6},{4,0},{6,2},{8,12},{10,14},{12,8},{14,10},{16,20},{18,... | collective-permute-start | bytes 589832 | tf_op jit(solution)/shard_map/ppermute | solution.py:315
  13.7 27.2 %collective-permute-start.3 = (bf16[3,64,1792]{2,1,0:T(8,128)(2,1)}, bf16[3,64,1792]{2,1,0:T(8,128)(2,1)S(1)}, u32[]{:S(2)}, u32[]{:S(2)}) collective-permute-start(bf16[3,64,1792]{2,1,0:T(8,128)(2,1)} %get-tuple-element.37.rest_0_), channel_id=1, source_target_pairs={{0,4},{2,6},{4,0},{6,2},{8,12},{10,14},{12,8},{14,10},{16,20},{18,... | collective-permute-start | bytes 2064392 | tf_op jit(solution)/shard_map/ppermute | solution.py:315
  14.2 31.8 %collective-permute-start.16 = (bf16[3,64,1792]{2,1,0:T(8,128)(2,1)}, bf16[3,64,1792]{2,1,0:T(8,128)(2,1)S(1)}, u32[]{:S(2)}, u32[]{:S(2)}) collective-permute-start(bf16[3,64,1792]{2,1,0:T(8,128)(2,1)} %get-tuple-element.46), channel_id=1, source_target_pairs={{0,16},{2,18},{4,20},{6,22},{8,24},{10,26},{12,28},{14,30},{16,0},... | collective-permute-start | bytes 2064392 | tf_op jit(solution)/shard_map/ppermute | solution.py:315
  16.6 16.5 %collective-permute-start.1 = (bf16[192,512]{1,0:T(8,128)(2,1)S(1)}, bf16[192,512]{1,0:T(8,128)(2,1)S(1)}, u32[]{:S(2)}, u32[]{:S(2)}) collective-permute-start(bf16[192,512]{1,0:T(8,128)(2,1)S(1)} %collective-permute-done.rest_8_), channel_id=1, source_target_pairs={{0,8},{2,10},{4,12},{6,14},{8,0},{10,2},{12,4},{14,6},{16,24},{18,... | collective-permute-start | bytes 589832 | tf_op jit(solution)/shard_map/ppermute | solution.py:315
  17.8 17.8 %collective-permute-start.4 = (bf16[192,512]{1,0:T(8,128)(2,1)S(1)}, bf16[192,512]{1,0:T(8,128)(2,1)S(1)}, u32[]{:S(2)}, u32[]{:S(2)}) collective-permute-start(bf16[192,512]{1,0:T(8,128)(2,1)S(1)} %pad_maximum_fusion.rest_0_), channel_id=1, source_target_pairs={{0,2},{2,0},{4,6},{6,4},{8,10},{10,8},{12,14},{14,12},{16,18},{18,... | collective-permute-start | bytes 589832 | tf_op jit(solution)/shard_map/ppermute | solution.py:315
  17.9 18.2 %collective-permute-start.9 = (bf16[192,512]{1,0:T(8,128)(2,1)S(1)}, bf16[192,512]{1,0:T(8,128)(2,1)S(1)}, u32[]{:S(2)}, u32[]{:S(2)}) collective-permute-start(bf16[192,512]{1,0:T(8,128)(2,1)S(1)} %collective-permute-done.7.rest_4_), channel_id=1, source_target_pairs={{0,4},{2,6},{4,0},{6,2},{8,12},{10,14},{12,8},{14,10},{16,20},{18,... | collective-permute-start | bytes 589832 | tf_op jit(solution)/shard_map/ppermute | solution.py:315
  33.1 7.7 %collective-permute-start.2 = (bf16[192,512]{1,0:T(8,128)(2,1)S(1)}, bf16[192,512]{1,0:T(8,128)(2,1)S(1)}, u32[]{:S(2)}, u32[]{:S(2)}) collective-permute-start(bf16[192,512]{1,0:T(8,128)(2,1)S(1)} %collective-permute-done.1.rest_12_), channel_id=1, source_target_pairs={{0,4},{2,6},{4,0},{6,2},{8,12},{10,14},{12,8},{14,10},{16,20},{18,... | collective-permute-start | bytes 589832 | tf_op jit(solution)/shard_map/ppermute | solution.py:315
  35.5 7.4 %collective-permute-start.12 = (bf16[192,512]{1,0:T(8,128)(2,1)S(1)}, bf16[192,512]{1,0:T(8,128)(2,1)S(1)}, u32[]{:S(2)}, u32[]{:S(2)}) collective-permute-start(bf16[192,512]{1,0:T(8,128)(2,1)S(1)} %collective-permute-done.rest_8_), channel_id=1, source_target_pairs={{0,4},{2,6},{4,0},{6,2},{8,12},{10,14},{12,8},{14,10},{16,20},{18,... | collective-permute-start | bytes 589832 | tf_op jit(solution)/shard_map/ppermute | solution.py:315
  36.0 6.9 %collective-permute-start.11 = (bf16[192,512]{1,0:T(8,128)(2,1)S(1)}, bf16[192,512]{1,0:T(8,128)(2,1)S(1)}, u32[]{:S(2)}, u32[]{:S(2)}) collective-permute-start(bf16[192,512]{1,0:T(8,128)(2,1)S(1)} %collective-permute-done.rest_8_), channel_id=1, source_target_pairs={{0,2},{2,0},{4,6},{6,4},{8,10},{10,8},{12,14},{14,12},{16,18},{18,... | collective-permute-start | bytes 589832 | tf_op jit(solution)/shard_map/ppermute | solution.py:315
  40.8 2.6 %collective-permute-start.8 = (bf16[192,512]{1,0:T(8,128)(2,1)S(1)}, bf16[192,512]{1,0:T(8,128)(2,1)S(1)}, u32[]{:S(2)}, u32[]{:S(2)}) collective-permute-start(bf16[192,512]{1,0:T(8,128)(2,1)S(1)} %collective-permute-done.7.rest_4_), channel_id=1, source_target_pairs={{0,2},{2,0},{4,6},{6,4},{8,10},{10,8},{12,14},{14,12},{16,18},{18,... | collective-permute-start | bytes 589832 | tf_op jit(solution)/shard_map/ppermute | solution.py:315
  40.8 2.7 %collective-permute-start.6 = (bf16[192,512]{1,0:T(8,128)(2,1)S(1)}, bf16[192,512]{1,0:T(8,128)(2,1)S(1)}, u32[]{:S(2)}, u32[]{:S(2)}) collective-permute-start(bf16[192,512]{1,0:T(8,128)(2,1)S(1)} %collective-permute-done.5.rest_2_), channel_id=1, source_target_pairs={{0,2},{2,0},{4,6},{6,4},{8,10},{10,8},{12,14},{14,12},{16,18},{18,... | collective-permute-start | bytes 589832 | tf_op jit(solution)/shard_map/ppermute | solution.py:315
  42.9 1.4 collective-permute-start.10
  42.9 1.7 %collective-permute-start.14 = (bf16[192,512]{1,0:T(8,128)(2,1)S(1)}, bf16[192,512]{1,0:T(8,128)(2,1)S(1)}, u32[]{:S(2)}, u32[]{:S(2)}) collective-permute-start(bf16[192,512]{1,0:T(8,128)(2,1)S(1)} %collective-permute-done.1.rest_12_), channel_id=1, source_target_pairs={{0,2},{2,0},{4,6},{6,4},{8,10},{10,8},{12,14},{14,12},{16,18},{18,... | collective-permute-start | bytes 589832 | tf_op jit(solution)/shard_map/ppermute | solution.py:315
  43.4 1.5 collective-permute-start.13
  43.5 2.5 %collective-permute-start.15 = (bf16[192,512]{1,0:T(8,128)(2,1)S(1)}, bf16[192,512]{1,0:T(8,128)(2,1)S(1)}, u32[]{:S(2)}, u32[]{:S(2)}) collective-permute-start(bf16[192,512]{1,0:T(8,128)(2,1)S(1)} %collective-permute-done.2.rest_14_), channel_id=1, source_target_pairs={{0,2},{2,0},{4,6},{6,4},{8,10},{10,8},{12,14},{14,12},{16,18},{18,... | collective-permute-start | bytes 589832 | tf_op jit(solution)/shard_map/ppermute | solution.py:315
  46.1 17.4 %collective-permute-start.17 = (bf16[3,64,1792]{2,1,0:T(8,128)(2,1)S(1)}, bf16[3,64,1792]{2,1,0:T(8,128)(2,1)S(1)}, u32[]{:S(2)}, u32[]{:S(2)}) collective-permute-start(bf16[3,64,1792]{2,1,0:T(8,128)(2,1)S(1)} %collective-permute-done.16.rest_2_), channel_id=1, source_target_pairs={{0,4},{2,6},{4,0},{6,2},{8,12},{10,14},{12,8},{14,10},{16,20},{18,... | collective-permute-start | bytes 2064392 | tf_op jit(solution)/shard_map/ppermute | solution.py:315
  47.7 21.2 %collective-permute-start.18 = (bf16[3,64,1792]{2,1,0:T(8,128)(2,1)}, bf16[3,64,1792]{2,1,0:T(8,128)(2,1)}, u32[]{:S(2)}, u32[]{:S(2)}) collective-permute-start(bf16[3,64,1792]{2,1,0:T(8,128)(2,1)} %get-tuple-element.67), channel_id=1, source_target_pairs={{0,8},{2,10},{4,12},{6,14},{8,0},{10,2},{12,4},{14,6},{16,24},{18,... | collective-permute-start | bytes 2064392 | tf_op jit(solution)/shard_map/ppermute | solution.py:315
  48.8 32.9 %collective-permute-start.19 = (bf16[3,64,1792]{2,1,0:T(8,128)(2,1)}, bf16[3,64,1792]{2,1,0:T(8,128)(2,1)}, u32[]{:S(2)}, u32[]{:S(2)}) collective-permute-start(bf16[3,64,1792]{2,1,0:T(8,128)(2,1)} %get-tuple-element.68), channel_id=1, source_target_pairs={{0,24},{2,26},{4,28},{6,30},{8,16},{10,18},{12,20},{14,22},{16,8},... | collective-permute-start | bytes 2064392 | tf_op jit(solution)/shard_map/ppermute | solution.py:315
  64.4 42.7 %all-to-all-start = ((bf16[8,72,1024]{2,1,0:T(8,128)(2,1)}), bf16[8,72,1024]{2,1,0:T(8,128)(2,1)S(1)}, u32[]{:S(2)}, u32[]{:S(2)}) async-start(bf16[8,72,1024]{2,1,0:T(8,128)(2,1)} %bitcast.34), calls=%async_computation | async-start | bytes 2359296 | tf_op jit(solution)/shard_map/all_to_all | solution.py:369
  68.3 13.9 %collective-permute-start.20 = (bf16[3,64,1792]{2,1,0:T(8,128)(2,1)S(1)}, bf16[3,64,1792]{2,1,0:T(8,128)(2,1)S(1)}, u32[]{:S(2)}, u32[]{:S(2)}) collective-permute-start(bf16[3,64,1792]{2,1,0:T(8,128)(2,1)S(1)} %copy-done.3), channel_id=1, source_target_pairs={{0,2},{2,0},{4,6},{6,4},{8,10},{10,8},{12,14},{14,12},{16,18},{18,... | collective-permute-start | bytes 2064392 | tf_op jit(solution)/shard_map/ppermute | solution.py:315
  68.4 13.9 %collective-permute-start.26 = (bf16[3,64,1792]{2,1,0:T(8,128)(2,1)S(1)}, bf16[3,64,1792]{2,1,0:T(8,128)(2,1)S(1)}, u32[]{:S(2)}, u32[]{:S(2)}) collective-permute-start(bf16[3,64,1792]{2,1,0:T(8,128)(2,1)S(1)} %collective-permute-done.3.rest_8_), channel_id=1, source_target_pairs={{0,2},{2,0},{4,6},{6,4},{8,10},{10,8},{12,14},{14,12},{16,18},{18,... | collective-permute-start | bytes 2064392 | tf_op jit(solution)/shard_map/ppermute | solution.py:315
  68.9 18.5 %collective-permute-start.24 = (bf16[3,64,1792]{2,1,0:T(8,128)(2,1)}, bf16[3,64,1792]{2,1,0:T(8,128)(2,1)S(1)}, u32[]{:S(2)}, u32[]{:S(2)}) collective-permute-start(bf16[3,64,1792]{2,1,0:T(8,128)(2,1)} %collective-permute-done.18.rest_1_), channel_id=1, source_target_pairs={{0,4},{2,6},{4,0},{6,2},{8,12},{10,14},{12,8},{14,10},{16,20},{18,... | collective-permute-start | bytes 2064392 | tf_op jit(solution)/shard_map/ppermute | solution.py:315
  70.4 17.0 %collective-permute-start.21 = (bf16[3,64,1792]{2,1,0:T(8,128)(2,1)}, bf16[3,64,1792]{2,1,0:T(8,128)(2,1)S(1)}, u32[]{:S(2)}, u32[]{:S(2)}) collective-permute-start(bf16[3,64,1792]{2,1,0:T(8,128)(2,1)} %collective-permute-done.18.rest_1_), channel_id=1, source_target_pairs={{0,2},{2,0},{4,6},{6,4},{8,10},{10,8},{12,14},{14,12},{16,18},{18,... | collective-permute-start | bytes 2064392 | tf_op jit(solution)/shard_map/ppermute | solution.py:315
  81.7 19.6 %collective-permute-start.25 = (bf16[3,64,1792]{2,1,0:T(8,128)(2,1)}, bf16[3,64,1792]{2,1,0:T(8,128)(2,1)S(1)}, u32[]{:S(2)}, u32[]{:S(2)}) collective-permute-start(bf16[3,64,1792]{2,1,0:T(8,128)(2,1)} %collective-permute-done.19.rest_3_), channel_id=1, source_target_pairs={{0,4},{2,6},{4,0},{6,2},{8,12},{10,14},{12,8},{14,10},{16,20},{18,... | collective-permute-start | bytes 2064392 | tf_op jit(solution)/shard_map/ppermute | solution.py:315
  82.2 19.0 %collective-permute-start.22 = (bf16[3,64,1792]{2,1,0:T(8,128)(2,1)S(1)}, bf16[3,64,1792]{2,1,0:T(8,128)(2,1)S(1)}, u32[]{:S(2)}, u32[]{:S(2)}) collective-permute-start(bf16[3,64,1792]{2,1,0:T(8,128)(2,1)S(1)} %collective-permute-done.16.rest_2_), channel_id=1, source_target_pairs={{0,2},{2,0},{4,6},{6,4},{8,10},{10,8},{12,14},{14,12},{16,18},{18,... | collective-permute-start | bytes 2064392 | tf_op jit(solution)/shard_map/ppermute | solution.py:315
  82.3 19.0 %collective-permute-start.23 = (bf16[3,64,1792]{2,1,0:T(8,128)(2,1)}, bf16[3,64,1792]{2,1,0:T(8,128)(2,1)S(1)}, u32[]{:S(2)}, u32[]{:S(2)}) collective-permute-start(bf16[3,64,1792]{2,1,0:T(8,128)(2,1)} %collective-permute-done.19.rest_3_), channel_id=1, source_target_pairs={{0,2},{2,0},{4,6},{6,4},{8,10},{10,8},{12,14},{14,12},{16,18},{18,... | collective-permute-start | bytes 2064392 | tf_op jit(solution)/shard_map/ppermute | solution.py:315
  87.4 13.9 %collective-permute-start.27 = (bf16[3,64,1792]{2,1,0:T(8,128)(2,1)S(1)}, bf16[3,64,1792]{2,1,0:T(8,128)(2,1)S(1)}, u32[]{:S(2)}, u32[]{:S(2)}) collective-permute-start(bf16[3,64,1792]{2,1,0:T(8,128)(2,1)S(1)} %collective-permute-done.24.rest_9_), channel_id=1, source_target_pairs={{0,2},{2,0},{4,6},{6,4},{8,10},{10,8},{12,14},{14,12},{16,18},{18,... | collective-permute-start | bytes 2064392 | tf_op jit(solution)/shard_map/ppermute | solution.py:315
  87.4 13.9 %collective-permute-start.28 = (bf16[3,64,1792]{2,1,0:T(8,128)(2,1)}, bf16[3,64,1792]{2,1,0:T(8,128)(2,1)S(1)}, u32[]{:S(2)}, u32[]{:S(2)}) collective-permute-start(bf16[3,64,1792]{2,1,0:T(8,128)(2,1)} %copy-done.6), channel_id=1, source_target_pairs={{0,2},{2,0},{4,6},{6,4},{8,10},{10,8},{12,14},{14,12},{16,18},{18,... | collective-permute-start | bytes 2064392 | tf_op jit(solution)/shard_map/ppermute | solution.py:315
  101.2 2.3 %collective-permute-start.29 = (bf16[3,64,1792]{2,1,0:T(8,128)(2,1)S(1)}, bf16[3,64,1792]{2,1,0:T(8,128)(2,1)}, u32[]{:S(2)}, u32[]{:S(2)}) collective-permute-start(bf16[3,64,1792]{2,1,0:T(8,128)(2,1)S(1)} %collective-permute-done.25.rest_11_), channel_id=1, source_target_pairs={{0,2},{2,0},{4,6},{6,4},{8,10},{10,8},{12,14},{14,12},{16,18},{18,... | collective-permute-start | bytes 2064392 | tf_op jit(solution)/shard_map/ppermute | solution.py:315
  119.2 33.4 %all-to-all-start.1 = ((bf16[8,72,1024]{2,1,0:T(8,128)(2,1)}), bf16[8,72,1024]{2,1,0:T(8,128)(2,1)S(1)}, u32[]{:S(2)}, u32[]{:S(2)}) async-start(bf16[8,72,1024]{2,1,0:T(8,128)(2,1)} %bitcast.33), calls=%async_computation.1 | async-start | bytes 2359296 | tf_op jit(solution)/shard_map/all_to_all | solution.py:379
  (34 other events, 400.0 us)

commit v6 on v5

--- a/solution.py
+++ b/solution.py
@@ -197,13 +197,16 @@
     return live.astype(jnp.int32), spot.astype(jnp.int32), placed
 
 
-def expert_kernel(planes, shared, cuts, step, place_ref, rows_in, *rest):
-    count = planes * shared
-    pieces = rest[:count]
-    out_ref, rows_ref, full, total, sems = rest[count:]
+def expert_kernel(planes, shared, cuts, step, group, place_ref, rows_in, *rest):
+    count, groups = planes * shared, len(group)
+    pieces, out_refs = rest[:count], rest[count : count + groups]
+    loaded, rows_ref, full, total, sems = rest[count + groups :]
     depth = pieces[0].shape[1]
     plane, seat = place_ref[0], place_ref[1]
-    rows_copy = pltpu.make_async_copy(rows_in, rows_ref, sems.at[count * len(cuts)])
+    loads = [
+        pltpu.make_async_copy(rows_in.at[place_ref[2] ^ j], loaded.at[g], sems.at[count * len(cuts) + g])
+        for g, j in enumerate(group)
+    ]
     copies = []
     for c, (low, high) in enumerate(cuts):
         for n in range(count):
@@ -213,8 +216,11 @@
             copies.append(pltpu.make_async_copy(pieces[n].at[:, :, pl.ds(low, high - low)], target, sems.at[c * count + n]))
             copies[-1].start()
         if c == 0:
-            rows_copy.start()
-    rows_copy.wait()
+            for load in loads:
+                load.start()
+    for load in loads:
+        load.wait()
+    rows_ref[...] = loaded[...].astype(jnp.float32).reshape(rows_ref.shape).astype(jnp.bfloat16)
     for c, (low, high) in enumerate(cuts):
         for copy in copies[c * count : (c + 1) * count]:
             copy.wait()
@@ -230,40 +236,48 @@
                 total[...] = part
             else:
                 total[...] += part
-    out_ref[...] = total[...].astype(jnp.bfloat16)
-
-
-def run_expert(place, rows, pieces, planes, shared):
+    for g in range(groups):
+        out_refs[g][...] = total[g * CAP : (g + 1) * CAP, :].astype(jnp.bfloat16)
+
+
+def run_expert(place, rows, group, pieces, planes, shared):
     depth, ff = pieces[0].shape[1:]
-    count = planes * shared
+    count, groups = planes * shared, len(group)
     step = 256
-    edges = [0, step, 3 * step, ff]
+    edges = [0, step, 3 * step, 5 * step, ff]
     cuts = list(zip(edges[:-1], edges[1:]))
     return pl.pallas_call(
-        functools.partial(expert_kernel, planes, shared, cuts, step),
-        out_shape=jax.ShapeDtypeStruct(rows.shape, jnp.bfloat16),
+        functools.partial(expert_kernel, planes, shared, cuts, step, group),
+        out_shape=[jax.ShapeDtypeStruct((CAP, D), jnp.bfloat16)] * groups,
         in_specs=[SMEM, ANY] + [ANY] * count,
-        out_specs=VMEM,
+        out_specs=[VMEM] * groups,
         scratch_shapes=[
-            pltpu.VMEM(rows.shape, jnp.bfloat16),
+            pltpu.VMEM((groups, CAP, D), jnp.bfloat16),
+            pltpu.VMEM((groups * CAP, D), jnp.bfloat16),
             pltpu.VMEM((3, D, ff), jnp.bfloat16),
-            pltpu.VMEM(rows.shape, jnp.float32),
-            pltpu.SemaphoreType.DMA((count * len(cuts) + 1,)),
+            pltpu.VMEM((groups * CAP, D), jnp.float32),
+            pltpu.SemaphoreType.DMA((count * len(cuts) + groups,)),
         ],
         compiler_params=pltpu.CompilerParams(vmem_limit_bytes=60 * MB),
+        cost_estimate=pl.CostEstimate(
+            flops=6 * groups * CAP * D * ff, bytes_accessed=3 * D * ff * 2, transcendentals=groups * CAP * ff
+        ),
         name="expert",
     )(place, rows, *pieces)
 
 
-def combine_kernel(returned_ref, target_ref, probs_ref, residual_ref, out_ref):
+def combine_kernel(target_ref, probs_ref, residual_ref, *rest):
+    returned_refs, out_ref = rest[:-1], rest[-1]
     rows = residual_ref.shape[0]
-    slot = lax.broadcasted_iota(jnp.int32, (rows, SLOTS), 1)
-    returned = returned_ref[...]
+    slot = lax.broadcasted_iota(jnp.int32, (rows, CAP), 1)
+    picked = jnp.zeros((TOP * rows, D), jnp.float32)
+    for j, returned_ref in enumerate(returned_refs):
+        selector = [(slot + j * CAP == target_ref[:, k : k + 1]).astype(jnp.float32) for k in range(TOP)]
+        selector = jnp.concatenate(selector, axis=0).astype(jnp.bfloat16)
+        picked = picked + jnp.dot(selector, returned_ref[...], preferred_element_type=jnp.float32)
     total = jnp.zeros((rows, D), jnp.float32)
     for k in range(TOP):
-        selector = (slot == target_ref[:, k : k + 1]).astype(jnp.float32).astype(jnp.bfloat16)
-        picked = jnp.dot(selector, returned, preferred_element_type=jnp.float32)
-        total = total + picked * probs_ref[:, k : k + 1]
+        total = total + picked[k * rows : (k + 1) * rows] * probs_ref[:, k : k + 1]
     out_ref[...] = (residual_ref[...].astype(jnp.float32) + total).astype(jnp.bfloat16)
 
 
@@ -271,21 +285,21 @@
     return pl.pallas_call(
         combine_kernel,
         out_shape=jax.ShapeDtypeStruct(residual.shape, jnp.bfloat16),
-        in_specs=[VMEM] * 4,
+        in_specs=[VMEM] * (3 + len(returned)),
         out_specs=VMEM,
-        compiler_params=pltpu.CompilerParams(vmem_limit_bytes=16 * MB),
+        compiler_params=pltpu.CompilerParams(vmem_limit_bytes=24 * MB),
         name="combine",
-    )(returned, target, probs, residual)
-
-
-def slots_of(ids):
+    )(target, probs, residual, *returned)
+
+
+def places_of(ids):
     rows = ids.shape[0]
     onehot = (ids[:, :, None] == jnp.arange(EXPERTS, dtype=jnp.int32)).astype(jnp.float32)
     named = jnp.sum(onehot, axis=1)
     earlier = (jnp.arange(rows)[:, None] > jnp.arange(rows)[None, :]).astype(jnp.bfloat16)
     before = jnp.dot(earlier, named.astype(jnp.bfloat16), preferred_element_type=jnp.float32)
     slot = jnp.sum(onehot * before[:, None, :], axis=2).astype(jnp.int32)
-    return ids * CAP + slot
+    return slot
 
 
 def shards(
@@ -309,7 +323,8 @@
     plane = lax.axis_index("plane")
     seat = lax.axis_index("seat")
     me = plane * shared + seat
-    place = jnp.stack([plane, seat]).astype(jnp.int32)
+    mine = lax.axis_index("exp") * planes + plane
+    place = jnp.stack([plane, seat, mine]).astype(jnp.int32)
 
     def swap(x, bit):
         return lax.ppermute(x, ctx, [(i, i ^ bit) for i in range(world)])
@@ -320,7 +335,10 @@
         pieces.update(zip(places, found))
         return value
 
-    target = slots_of(expert_ids[0])
+    ids = expert_ids[0]
+    spot = places_of(ids)
+    target = ids * CAP + spot
+    back = (ids ^ mine) * CAP + spot
     order = key_order(tile_mask[0], me, world)
     own = jnp.concatenate([key_proj[0], value_proj[0]], axis=1)
     bit = world // 2
@@ -338,7 +356,7 @@
         if bit == 1:
             last = world - 2
             blocks[last] = tie(blocks[last], [(2, 0)])
-            blocks[last], order, target = lax.optimization_barrier((blocks[last], order, target))
+            blocks[last], order, target, back = lax.optimization_barrier((blocks[last], order, target, back))
             if far:
                 early = half + shared
                 blocks[early], second = lax.optimization_barrier((blocks[early], packed[far[1]]))
@@ -353,10 +371,10 @@
                 pieces[m | bit, k] = swap(x, bit)
         bit //= 2
 
-    live, spot, allowed = order
+    live, where, allowed = order
     attention_out, residual, outgoing = attend(
         live,
-        spot,
+        where,
         allowed,
         queries[0],
         target.T,
@@ -369,17 +387,17 @@
     arrived = lax.all_to_all(
         outgoing.reshape(EXPERTS, CAP, D), ("exp", "plane"), split_axis=0, concat_axis=0, tiled=True
     )
-    expert_rows = run_expert(
-        place,
-        arrived.reshape(SLOTS, D),
-        [pieces[m, k] for m in range(shared) for k in range(planes)],
-        planes,
-        shared,
-    )
-    returned = lax.all_to_all(
-        expert_rows.reshape(EXPERTS, CAP, D), ("exp", "plane"), split_axis=0, concat_axis=0, tiled=True
-    )
-    layer_out = combine(returned.reshape(SLOTS, D), target, gate_probs[0], residual)
+    weights = [pieces[m, k] for m in range(shared) for k in range(planes)]
+    first = [j for j in range(EXPERTS) if planes > 1 and j % planes >= planes // 2]
+    first += [j for j in range(planes, EXPERTS) if j not in first]
+    second = [j for j in range(EXPERTS) if j not in first]
+    returned = {}
+    for group in (first, second):
+        for j, x in zip(group, run_expert(place, arrived, group, weights, planes, shared)):
+            step = j % planes * (EXPERTS // planes) + j // planes
+            pairs = [(i, i ^ step) for i in range(EXPERTS)]
+            returned[j] = lax.ppermute(x, ("plane", "exp"), pairs) if j else x
+    layer_out = combine([returned[j] for j in range(EXPERTS)], back, gate_probs[0], residual)
     return attention_out[None], layer_out[None]
 
 

time: 155 us -> 149 us (0.961)
  waiting for transfers between devices: 85.8 us -> 62.4 us
  starting transfers between devices: 29.2 us -> 38.8 us
  Pallas kernels: 28.1 us -> 35.4 us
    all_to_all x1 -> x0, waiting for transfers between devices: 29.5 us -> none  [shards(): lax.all_to_all(expert_rows.reshape(EXPERTS, CAP, D), ('exp', 'plane'), sp...]
    ppermute x0 -> x7, starting transfers between devices: none -> 13.3 us  [shards(): returned[j] = lax.ppermute(x, ('plane', 'exp'), pairs) if j else x]
    pallas_call x1 -> x2, Pallas kernels: 11 us -> 17.3 us  [run_expert(): pl.pallas_call(functools.partial(expert_kernel, planes, shared, cuts, ste...]
    ppermute x0 -> x7, waiting for transfers between devices: none -> 6.02 us  [shards(): returned[j] = lax.ppermute(x, ('plane', 'exp'), pairs) if j else x]
    all_to_all x1 -> x0, starting transfers between devices: 3.71 us -> none  [shards(): lax.all_to_all(expert_rows.reshape(EXPERTS, CAP, D), ('exp', 'plane'), sp...]
    unnamed x70 -> x74, local copies, waits for them, and re-layouts: 4.16 us -> 4.96 us
  transfers between devices with their start and end apart: 32 -> 38, of which waited for: 14 -> 15; matrix products, arithmetic and copies ran while one was open for 3% -> 3% of each run, Pallas kernels for 10% -> 15%
where the time goes in v6:
time: 149 us
  waiting for transfers between devices  62.4 us (42%)
  starting transfers between devices  38.8 us (26%)
  Pallas kernels  35.4 us (24%)
  local copies, waits for them, and re-layouts  7.45 us (5%)
  other arithmetic  2.35 us (2%)
    ppermute x30, waiting for transfers between devices, swap(): return lax.ppermute(x, ctx, [(i, i ^ bit) for i in range(world)])  52.7 us
    ppermute x30, starting transfers between devices, swap(): return lax.ppermute(x, ctx, [(i, i ^ bit) for i in range(world)])  21.7 us
    pallas_call x2, Pallas kernels, run_expert(): pl.pallas_call(functools.partial(expert_kernel, planes, shared, cuts, ste...  17.3 us
    ppermute x7, starting transfers between devices, shards(): returned[j] = lax.ppermute(x, ('plane', 'exp'), pairs) if j else x  13.3 us
    pallas_call x1, Pallas kernels, attend(): pl.pallas_call(functools.partial(attend_kernel, n), out_shape=[jax.ShapeD...  11.2 us
    ppermute x7, waiting for transfers between devices, shards(): returned[j] = lax.ppermute(x, ('plane', 'exp'), pairs) if j else x  6.02 us
    unnamed x74, local copies, waits for them, and re-layouts  4.96 us
    pallas_call x1, Pallas kernels, pack(): pl.pallas_call(functools.partial(pack_kernel, planes), out_shape=[jax.Sha...  4.31 us
  transfers between devices with their start and end apart: 38, of which 15 were waited for; matrix products, arithmetic and copies ran while one was open for 3% of the time, Pallas kernels for 15%

profile of v6, /device:TPU:0, one launch (start us, length us, event | category | flops | bytes accessed | tf_op | source)
XLA Modules:
  0.0 148.6 jit_solution(5948316711828955223)
XLA Ops:
  0.6 1.0 pad_maximum_fusion.rest_0_
  1.6 4.1 %collective-permute-start = (bf16[192,512]{1,0:T(8,128)(2,1)S(1)}, bf16[192,512]{1,0:T(8,128)(2,1)S(1)}, u32[]{:S(2)}, u32[]{:S(2)}) collective-permute-start(bf16[192,512]{1,0:T(8,128)(2,1)S(1)} %pad_maximum_fusion.rest_0_), channel_id=1, source_target_pairs={{0,16},{2,18},{4,20},{6,22},{8,24},{10,26},{12,28},{14,30},{16,0},... | collective-permute-start | bytes 589832 | tf_op jit(solution)/shard_map/ppermute | solution.py:330
  5.7 1.6 %collective-permute-start.7 = (bf16[192,512]{1,0:T(8,128)(2,1)S(1)}, bf16[192,512]{1,0:T(8,128)(2,1)S(1)}, u32[]{:S(2)}, u32[]{:S(2)}) collective-permute-start(bf16[192,512]{1,0:T(8,128)(2,1)S(1)} %pad_maximum_fusion.rest_0_), channel_id=1, source_target_pairs={{0,8},{2,10},{4,12},{6,14},{8,0},{10,2},{12,4},{14,6},{16,24},{18,... | collective-permute-start | bytes 589832 | tf_op jit(solution)/shard_map/ppermute | solution.py:330
  7.3 1.5 %collective-permute-start.5 = (bf16[192,512]{1,0:T(8,128)(2,1)S(1)}, bf16[192,512]{1,0:T(8,128)(2,1)S(1)}, u32[]{:S(2)}, u32[]{:S(2)}) collective-permute-start(bf16[192,512]{1,0:T(8,128)(2,1)S(1)} %pad_maximum_fusion.rest_0_), channel_id=1, source_target_pairs={{0,4},{2,6},{4,0},{6,2},{8,12},{10,14},{12,8},{14,10},{16,20},{18,... | collective-permute-start | bytes 589832 | tf_op jit(solution)/shard_map/ppermute | solution.py:330
  9.5 4.3 %pack_weights.1 = (bf16[3,64,1792]{2,1,0:T(8,128)(2,1)}, bf16[3,64,1792]{2,1,0:T(8,128)(2,1)}, bf16[3,64,1792]{2,1,0:T(8,128)(2,1)}, bf16[3,64,1792]{2,1,0:T(8,128)(2,1)}) custom-call(s32[3]{0:T(128)} %pad_add_fusion.place_ref, bf16[4,64,1792]{2,1,0:T(8,128)(2,1)} %gate_ref.1, bf16[4,64,1792]{2,1,0:T(8,128)(2,1)} %up_ref.1, bf16[4,64,1792]{2,1,0:T(8,128)(2,1)} %down_ref.1), custom_call_target="tpu_custom_call" | custom-call | tf_op jit(solution)/shard_map/pack_weights/pallas_call | solution.py:44
  18.0 1.8 %collective-permute-start.9 = (bf16[192,512]{1,0:T(8,128)(2,1)S(1)}, bf16[192,512]{1,0:T(8,128)(2,1)S(1)}, u32[]{:S(2)}, u32[]{:S(2)}) collective-permute-start(bf16[192,512]{1,0:T(8,128)(2,1)S(1)} %collective-permute-done.7.rest_4_), channel_id=1, source_target_pairs={{0,4},{2,6},{4,0},{6,2},{8,12},{10,14},{12,8},{14,10},{16,20},{18,... | collective-permute-start | bytes 589832 | tf_op jit(solution)/shard_map/ppermute | solution.py:330
  19.8 13.3 %collective-permute-done.1.rest_12_ = bf16[192,512]{1,0:T(8,128)(2,1)S(1)} collective-permute-done((bf16[192,512]{1,0:T(8,128)(2,1)S(1)}, bf16[192,512]{1,0:T(8,128)(2,1)S(1)}, u32[]{:S(2)}, u32[]{:S(2)}) %collective-permute-start.1) | collective-permute-done | bytes 196640 | tf_op jit(solution)/shard_map/ppermute | solution.py:330
  33.1 1.5 %collective-permute-start.2 = (bf16[192,512]{1,0:T(8,128)(2,1)S(1)}, bf16[192,512]{1,0:T(8,128)(2,1)S(1)}, u32[]{:S(2)}, u32[]{:S(2)}) collective-permute-start(bf16[192,512]{1,0:T(8,128)(2,1)S(1)} %collective-permute-done.1.rest_12_), channel_id=1, source_target_pairs={{0,4},{2,6},{4,0},{6,2},{8,12},{10,14},{12,8},{14,10},{16,20},{18,... | collective-permute-start | bytes 589832 | tf_op jit(solution)/shard_map/ppermute | solution.py:330
  36.1 4.8 %collective-permute-done.2.rest_14_ = bf16[192,512]{1,0:T(8,128)(2,1)S(1)} collective-permute-done((bf16[192,512]{1,0:T(8,128)(2,1)S(1)}, bf16[192,512]{1,0:T(8,128)(2,1)S(1)}, u32[]{:S(2)}, u32[]{:S(2)}) %collective-permute-start.2) | collective-permute-done | bytes 196640 | tf_op jit(solution)/shard_map/ppermute | solution.py:330
  41.5 1.6 %collective-permute-done.12.rest_10_ = bf16[192,512]{1,0:T(8,128)(2,1)S(1)} collective-permute-done((bf16[192,512]{1,0:T(8,128)(2,1)S(1)}, bf16[192,512]{1,0:T(8,128)(2,1)S(1)}, u32[]{:S(2)}, u32[]{:S(2)}) %collective-permute-start.12) | collective-permute-done | bytes 196640 | tf_op jit(solution)/shard_map/ppermute | solution.py:330
  45.0 1.1 collective-permute-done.16.rest_2_
  46.2 1.6 %collective-permute-start.17 = (bf16[3,64,1792]{2,1,0:T(8,128)(2,1)S(1)}, bf16[3,64,1792]{2,1,0:T(8,128)(2,1)S(1)}, u32[]{:S(2)}, u32[]{:S(2)}) collective-permute-start(bf16[3,64,1792]{2,1,0:T(8,128)(2,1)S(1)} %collective-permute-done.16.rest_2_), channel_id=1, source_target_pairs={{0,4},{2,6},{4,0},{6,2},{8,12},{10,14},{12,8},{14,10},{16,20},{18,... | collective-permute-start | bytes 2064392 | tf_op jit(solution)/shard_map/ppermute | solution.py:330
  48.7 1.7 %collective-permute-start.19 = (bf16[3,64,1792]{2,1,0:T(8,128)(2,1)}, bf16[3,64,1792]{2,1,0:T(8,128)(2,1)}, u32[]{:S(2)}, u32[]{:S(2)}) collective-permute-start(bf16[3,64,1792]{2,1,0:T(8,128)(2,1)} %get-tuple-element.79), channel_id=1, source_target_pairs={{0,24},{2,26},{4,28},{6,30},{8,16},{10,18},{12,20},{14,22},{16,8},... | collective-permute-start | bytes 2064392 | tf_op jit(solution)/shard_map/ppermute | solution.py:330
  51.1 11.2 %attend.1 = (bf16[192,1024]{1,0:T(8,128)(2,1)}, bf16[192,1024]{1,0:T(8,128)(2,1)}, bf16[576,1024]{1,0:T(8,128)(2,1)}) custom-call(s32[96]{0:T(128)} %convert_element_type.35.live_ref, s32[96]{0:T(128)} %get-tuple-element.49.spot_ref, bf16[8,16,128]{2,1,0:T(8,128)(2,1)} %pad.5.allowed_ref, bf16[192,1024]{1,0:T(8,128)(2,1)} %bitcast.33, ...), custom_call_target="tpu_custom_call" | custom-call | tf_op jit(solution)/shard_map/attend/pallas_call | solution.py:157
  62.3 1.3 collective-permute-done.17.rest_10_
  64.5 3.8 %all-to-all-start = ((bf16[8,72,1024]{2,1,0:T(8,128)(2,1)}), bf16[8,72,1024]{2,1,0:T(8,128)(2,1)S(1)}, u32[]{:S(2)}, u32[]{:S(2)}) async-start(bf16[8,72,1024]{2,1,0:T(8,128)(2,1)} %bitcast.29), calls=%async_computation | async-start | bytes 2359296 | tf_op jit(solution)/shard_map/all_to_all | solution.py:387
  68.8 1.5 %collective-permute-start.24 = (bf16[3,64,1792]{2,1,0:T(8,128)(2,1)}, bf16[3,64,1792]{2,1,0:T(8,128)(2,1)S(1)}, u32[]{:S(2)}, u32[]{:S(2)}) collective-permute-start(bf16[3,64,1792]{2,1,0:T(8,128)(2,1)} %collective-permute-done.18.rest_1_), channel_id=1, source_target_pairs={{0,4},{2,6},{4,0},{6,2},{8,12},{10,14},{12,8},{14,10},{16,20},{18,... | collective-permute-start | bytes 2064392 | tf_op jit(solution)/shard_map/ppermute | solution.py:330
  70.4 11.4 %collective-permute-done.19.rest_3_ = bf16[3,64,1792]{2,1,0:T(8,128)(2,1)} collective-permute-done((bf16[3,64,1792]{2,1,0:T(8,128)(2,1)}, bf16[3,64,1792]{2,1,0:T(8,128)(2,1)}, u32[]{:S(2)}, u32[]{:S(2)}) %collective-permute-start.19) | collective-permute-done | bytes 688160 | tf_op jit(solution)/shard_map/ppermute | solution.py:330
  82.9 4.4 %collective-permute-done.24.rest_9_ = bf16[3,64,1792]{2,1,0:T(8,128)(2,1)S(1)} collective-permute-done((bf16[3,64,1792]{2,1,0:T(8,128)(2,1)}, bf16[3,64,1792]{2,1,0:T(8,128)(2,1)S(1)}, u32[]{:S(2)}, u32[]{:S(2)}) %collective-permute-start.24) | collective-permute-done | bytes 688160 | tf_op jit(solution)/shard_map/ppermute | solution.py:330
  87.9 13.4 %collective-permute-done.25.rest_11_ = bf16[3,64,1792]{2,1,0:T(8,128)(2,1)S(1)} collective-permute-done((bf16[3,64,1792]{2,1,0:T(8,128)(2,1)}, bf16[3,64,1792]{2,1,0:T(8,128)(2,1)S(1)}, u32[]{:S(2)}, u32[]{:S(2)}) %collective-permute-start.25) | collective-permute-done | bytes 688160 | tf_op jit(solution)/shard_map/ppermute | solution.py:330
  103.5 3.7 %all-to-all-done.rows_in = bf16[8,72,1024]{2,1,0:T(8,128)(2,1)S(1)} async-done(((bf16[8,72,1024]{2,1,0:T(8,128)(2,1)}), bf16[8,72,1024]{2,1,0:T(8,128)(2,1)S(1)}, u32[]{:S(2)}, u32[]{:S(2)}) %all-to-all-start) | async-done | bytes 1179680 | tf_op jit(solution)/shard_map/all_to_all | solution.py:387
  107.2 1.1 copy-done.2
  108.3 9.9 %expert.3 = (bf16[72,1024]{1,0:T(8,128)(2,1)}, bf16[72,1024]{1,0:T(8,128)(2,1)}, bf16[72,1024]{1,0:T(8,128)(2,1)}, bf16[72,1024]{1,0:T(8,128)(2,1)}, bf16[72,1024]{1,0:T(8,128)(2,1)}, /*index=5*/bf16[72,1024]{1,0:T(8,128)(2,1)}) custom-call(s32[3]{0:T(128)} %pad_add_fusion.place_ref, bf16[8,72,1024]{2,1,0:T(8,128)(2,1)} %copy-done.2, ...), custom_call_target="tpu_custom_call" | custom-call | flops 4756340736 | bytes 11010048 | tf_op jit(solution)/shard_map/expert/pallas_call | solution.py:249
  118.9 1.5 collective-permute-start.33
  120.3 2.9 %collective-permute-start.34 = (bf16[72,1024]{1,0:T(8,128)(2,1)}, bf16[72,1024]{1,0:T(8,128)(2,1)S(1)}, u32[]{:S(2)}, u32[]{:S(2)}) collective-permute-start(bf16[72,1024]{1,0:T(8,128)(2,1)} %get-tuple-element.87), channel_id=1, source_target_pairs={{0,9},{1,8},{8,1},{9,0},{16,25},{17,24},{24,17},{25,16},{2,11},{3,... | collective-permute-start | bytes 442376 | tf_op jit(solution)/shard_map/ppermute | solution.py:399
  123.2 1.8 %collective-permute-start.35 = (bf16[72,1024]{1,0:T(8,128)(2,1)}, bf16[72,1024]{1,0:T(8,128)(2,1)S(1)}, u32[]{:S(2)}, u32[]{:S(2)}) collective-permute-start(bf16[72,1024]{1,0:T(8,128)(2,1)} %get-tuple-element.88), channel_id=1, source_target_pairs={{0,17},{1,16},{8,25},{9,24},{16,1},{17,0},{24,9},{25,8},{2,19},{3,... | collective-permute-start | bytes 442376 | tf_op jit(solution)/shard_map/ppermute | solution.py:399
  125.0 7.4 %expert.2 = (bf16[72,1024]{1,0:T(8,128)(2,1)}, bf16[72,1024]{1,0:T(8,128)(2,1)}) custom-call(s32[3]{0:T(128)} %pad_add_fusion.place_ref, bf16[8,72,1024]{2,1,0:T(8,128)(2,1)} %copy-done.2, bf16[3,64,1792]{2,1,0:T(8,128)(2,1)} %get-tuple-element.46.rest_0_, bf16[3,64,1792]{2,1,0:T(8,128)(2,1)} %collective-permute-done.18.rest_1_, ...), custom_call_target="tpu_custom_call" | custom-call | flops 1585446912 | bytes 11010048 | tf_op jit(solution)/shard_map/expert/pallas_call | solution.py:249
  132.4 1.9 %collective-permute-start.36 = (bf16[72,1024]{1,0:T(8,128)(2,1)S(1)}, bf16[72,1024]{1,0:T(8,128)(2,1)S(1)}, u32[]{:S(2)}, u32[]{:S(2)}) collective-permute-start(bf16[72,1024]{1,0:T(8,128)(2,1)S(1)} %copy-done.35), channel_id=1, source_target_pairs={{0,25},{1,24},{8,17},{9,16},{16,9},{17,8},{24,1},{25,0},{2,27},{3,... | collective-permute-start | bytes 442376 | tf_op jit(solution)/shard_map/ppermute | solution.py:399
  134.3 4.6 %collective-permute-start.30 = (bf16[72,1024]{1,0:T(8,128)(2,1)}, bf16[72,1024]{1,0:T(8,128)(2,1)S(1)}, u32[]{:S(2)}, u32[]{:S(2)}) collective-permute-start(bf16[72,1024]{1,0:T(8,128)(2,1)} %get-tuple-element.83), channel_id=1, source_target_pairs={{0,8},{1,9},{8,0},{9,1},{16,24},{17,25},{24,16},{25,17},{2,10},{3,... | collective-permute-start | bytes 442376 | tf_op jit(solution)/shard_map/ppermute | solution.py:399
  139.1 3.9 %collective-permute-done.35.rest_6_ = bf16[72,1024]{1,0:T(8,128)(2,1)S(1)} collective-permute-done((bf16[72,1024]{1,0:T(8,128)(2,1)}, bf16[72,1024]{1,0:T(8,128)(2,1)S(1)}, u32[]{:S(2)}, u32[]{:S(2)}) %collective-permute-start.35) | collective-permute-done | bytes 147488 | tf_op jit(solution)/shard_map/ppermute | solution.py:399
  143.0 2.1 %collective-permute-done.30.rest_1_ = bf16[72,1024]{1,0:T(8,128)(2,1)S(1)} collective-permute-done((bf16[72,1024]{1,0:T(8,128)(2,1)}, bf16[72,1024]{1,0:T(8,128)(2,1)S(1)}, u32[]{:S(2)}, u32[]{:S(2)}) %collective-permute-start.30) | collective-permute-done | bytes 147488 | tf_op jit(solution)/shard_map/ppermute | solution.py:399
  146.0 2.6 %combine.1 = bf16[192,1024]{1,0:T(8,128)(2,1)} custom-call(s32[192,2]{1,0:T(8,128)S(1)} %get-tuple-element.73.target_ref, f32[192,2]{1,0:T(8,128)S(1)} %bitcast.28, bf16[192,1024]{1,0:T(8,128)(2,1)S(1)} %copy-done, bf16[72,1024]{1,0:T(8,128)(2,1)S(1)} %copy-done.1, bf16[72,1024]{1,0:T(8,128)(2,1)S(1)} %collective-permute-done.30.rest_1_, ...), custom_call_target="tpu_custom_call" | custom-call | tf_op jit(solution)/shard_map/combine/pallas_call | solution.py:285
  (149 shorter events, 17.2 us)
Async XLA Ops:
  1.6 15.1 %collective-permute-start = (bf16[192,512]{1,0:T(8,128)(2,1)S(1)}, bf16[192,512]{1,0:T(8,128)(2,1)S(1)}, u32[]{:S(2)}, u32[]{:S(2)}) collective-permute-start(bf16[192,512]{1,0:T(8,128)(2,1)S(1)} %pad_maximum_fusion.rest_0_), channel_id=1, source_target_pairs={{0,16},{2,18},{4,20},{6,22},{8,24},{10,26},{12,28},{14,30},{16,0},... | collective-permute-start | bytes 589832 | tf_op jit(solution)/shard_map/ppermute | solution.py:330
  5.7 12.2 %collective-permute-start.7 = (bf16[192,512]{1,0:T(8,128)(2,1)S(1)}, bf16[192,512]{1,0:T(8,128)(2,1)S(1)}, u32[]{:S(2)}, u32[]{:S(2)}) collective-permute-start(bf16[192,512]{1,0:T(8,128)(2,1)S(1)} %pad_maximum_fusion.rest_0_), channel_id=1, source_target_pairs={{0,8},{2,10},{4,12},{6,14},{8,0},{10,2},{12,4},{14,6},{16,24},{18,... | collective-permute-start | bytes 589832 | tf_op jit(solution)/shard_map/ppermute | solution.py:330
  7.3 10.7 %collective-permute-start.5 = (bf16[192,512]{1,0:T(8,128)(2,1)S(1)}, bf16[192,512]{1,0:T(8,128)(2,1)S(1)}, u32[]{:S(2)}, u32[]{:S(2)}) collective-permute-start(bf16[192,512]{1,0:T(8,128)(2,1)S(1)} %pad_maximum_fusion.rest_0_), channel_id=1, source_target_pairs={{0,4},{2,6},{4,0},{6,2},{8,12},{10,14},{12,8},{14,10},{16,20},{18,... | collective-permute-start | bytes 589832 | tf_op jit(solution)/shard_map/ppermute | solution.py:330
  13.8 27.2 %collective-permute-start.3 = (bf16[3,64,1792]{2,1,0:T(8,128)(2,1)}, bf16[3,64,1792]{2,1,0:T(8,128)(2,1)S(1)}, u32[]{:S(2)}, u32[]{:S(2)}) collective-permute-start(bf16[3,64,1792]{2,1,0:T(8,128)(2,1)} %get-tuple-element.46.rest_0_), channel_id=1, source_target_pairs={{0,4},{2,6},{4,0},{6,2},{8,12},{10,14},{12,8},{14,10},{16,20},{18,... | collective-permute-start | bytes 2064392 | tf_op jit(solution)/shard_map/ppermute | solution.py:330
  14.3 31.8 %collective-permute-start.16 = (bf16[3,64,1792]{2,1,0:T(8,128)(2,1)}, bf16[3,64,1792]{2,1,0:T(8,128)(2,1)S(1)}, u32[]{:S(2)}, u32[]{:S(2)}) collective-permute-start(bf16[3,64,1792]{2,1,0:T(8,128)(2,1)} %get-tuple-element.55), channel_id=1, source_target_pairs={{0,16},{2,18},{4,20},{6,22},{8,24},{10,26},{12,28},{14,30},{16,0},... | collective-permute-start | bytes 2064392 | tf_op jit(solution)/shard_map/ppermute | solution.py:330
  16.7 16.4 %collective-permute-start.1 = (bf16[192,512]{1,0:T(8,128)(2,1)S(1)}, bf16[192,512]{1,0:T(8,128)(2,1)S(1)}, u32[]{:S(2)}, u32[]{:S(2)}) collective-permute-start(bf16[192,512]{1,0:T(8,128)(2,1)S(1)} %collective-permute-done.rest_8_), channel_id=1, source_target_pairs={{0,8},{2,10},{4,12},{6,14},{8,0},{10,2},{12,4},{14,6},{16,24},{18,... | collective-permute-start | bytes 589832 | tf_op jit(solution)/shard_map/ppermute | solution.py:330
  17.9 17.6 %collective-permute-start.4 = (bf16[192,512]{1,0:T(8,128)(2,1)S(1)}, bf16[192,512]{1,0:T(8,128)(2,1)S(1)}, u32[]{:S(2)}, u32[]{:S(2)}) collective-permute-start(bf16[192,512]{1,0:T(8,128)(2,1)S(1)} %pad_maximum_fusion.rest_0_), channel_id=1, source_target_pairs={{0,2},{2,0},{4,6},{6,4},{8,10},{10,8},{12,14},{14,12},{16,18},{18,... | collective-permute-start | bytes 589832 | tf_op jit(solution)/shard_map/ppermute | solution.py:330
  18.0 18.1 %collective-permute-start.9 = (bf16[192,512]{1,0:T(8,128)(2,1)S(1)}, bf16[192,512]{1,0:T(8,128)(2,1)S(1)}, u32[]{:S(2)}, u32[]{:S(2)}) collective-permute-start(bf16[192,512]{1,0:T(8,128)(2,1)S(1)} %collective-permute-done.7.rest_4_), channel_id=1, source_target_pairs={{0,4},{2,6},{4,0},{6,2},{8,12},{10,14},{12,8},{14,10},{16,20},{18,... | collective-permute-start | bytes 589832 | tf_op jit(solution)/shard_map/ppermute | solution.py:330
  33.1 7.8 %collective-permute-start.2 = (bf16[192,512]{1,0:T(8,128)(2,1)S(1)}, bf16[192,512]{1,0:T(8,128)(2,1)S(1)}, u32[]{:S(2)}, u32[]{:S(2)}) collective-permute-start(bf16[192,512]{1,0:T(8,128)(2,1)S(1)} %collective-permute-done.1.rest_12_), channel_id=1, source_target_pairs={{0,4},{2,6},{4,0},{6,2},{8,12},{10,14},{12,8},{14,10},{16,20},{18,... | collective-permute-start | bytes 589832 | tf_op jit(solution)/shard_map/ppermute | solution.py:330
  35.5 7.5 %collective-permute-start.12 = (bf16[192,512]{1,0:T(8,128)(2,1)S(1)}, bf16[192,512]{1,0:T(8,128)(2,1)S(1)}, u32[]{:S(2)}, u32[]{:S(2)}) collective-permute-start(bf16[192,512]{1,0:T(8,128)(2,1)S(1)} %collective-permute-done.rest_8_), channel_id=1, source_target_pairs={{0,4},{2,6},{4,0},{6,2},{8,12},{10,14},{12,8},{14,10},{16,20},{18,... | collective-permute-start | bytes 589832 | tf_op jit(solution)/shard_map/ppermute | solution.py:330
  36.1 7.0 %collective-permute-start.11 = (bf16[192,512]{1,0:T(8,128)(2,1)S(1)}, bf16[192,512]{1,0:T(8,128)(2,1)S(1)}, u32[]{:S(2)}, u32[]{:S(2)}) collective-permute-start(bf16[192,512]{1,0:T(8,128)(2,1)S(1)} %collective-permute-done.rest_8_), channel_id=1, source_target_pairs={{0,2},{2,0},{4,6},{6,4},{8,10},{10,8},{12,14},{14,12},{16,18},{18,... | collective-permute-start | bytes 589832 | tf_op jit(solution)/shard_map/ppermute | solution.py:330
  40.9 2.7 %collective-permute-start.6 = (bf16[192,512]{1,0:T(8,128)(2,1)S(1)}, bf16[192,512]{1,0:T(8,128)(2,1)S(1)}, u32[]{:S(2)}, u32[]{:S(2)}) collective-permute-start(bf16[192,512]{1,0:T(8,128)(2,1)S(1)} %collective-permute-done.5.rest_2_), channel_id=1, source_target_pairs={{0,2},{2,0},{4,6},{6,4},{8,10},{10,8},{12,14},{14,12},{16,18},{18,... | collective-permute-start | bytes 589832 | tf_op jit(solution)/shard_map/ppermute | solution.py:330
  46.2 17.4 %collective-permute-start.17 = (bf16[3,64,1792]{2,1,0:T(8,128)(2,1)S(1)}, bf16[3,64,1792]{2,1,0:T(8,128)(2,1)S(1)}, u32[]{:S(2)}, u32[]{:S(2)}) collective-permute-start(bf16[3,64,1792]{2,1,0:T(8,128)(2,1)S(1)} %collective-permute-done.16.rest_2_), channel_id=1, source_target_pairs={{0,4},{2,6},{4,0},{6,2},{8,12},{10,14},{12,8},{14,10},{16,20},{18,... | collective-permute-start | bytes 2064392 | tf_op jit(solution)/shard_map/ppermute | solution.py:330
  47.8 21.1 %collective-permute-start.18 = (bf16[3,64,1792]{2,1,0:T(8,128)(2,1)}, bf16[3,64,1792]{2,1,0:T(8,128)(2,1)}, u32[]{:S(2)}, u32[]{:S(2)}) collective-permute-start(bf16[3,64,1792]{2,1,0:T(8,128)(2,1)} %get-tuple-element.78), channel_id=1, source_target_pairs={{0,8},{2,10},{4,12},{6,14},{8,0},{10,2},{12,4},{14,6},{16,24},{18,... | collective-permute-start | bytes 2064392 | tf_op jit(solution)/shard_map/ppermute | solution.py:330
  48.7 33.1 %collective-permute-start.19 = (bf16[3,64,1792]{2,1,0:T(8,128)(2,1)}, bf16[3,64,1792]{2,1,0:T(8,128)(2,1)}, u32[]{:S(2)}, u32[]{:S(2)}) collective-permute-start(bf16[3,64,1792]{2,1,0:T(8,128)(2,1)} %get-tuple-element.79), channel_id=1, source_target_pairs={{0,24},{2,26},{4,28},{6,30},{8,16},{10,18},{12,20},{14,22},{16,8},... | collective-permute-start | bytes 2064392 | tf_op jit(solution)/shard_map/ppermute | solution.py:330
  64.5 42.8 %all-to-all-start = ((bf16[8,72,1024]{2,1,0:T(8,128)(2,1)}), bf16[8,72,1024]{2,1,0:T(8,128)(2,1)S(1)}, u32[]{:S(2)}, u32[]{:S(2)}) async-start(bf16[8,72,1024]{2,1,0:T(8,128)(2,1)} %bitcast.29), calls=%async_computation | async-start | bytes 2359296 | tf_op jit(solution)/shard_map/all_to_all | solution.py:387
  68.3 14.1 %collective-permute-start.20 = (bf16[3,64,1792]{2,1,0:T(8,128)(2,1)S(1)}, bf16[3,64,1792]{2,1,0:T(8,128)(2,1)S(1)}, u32[]{:S(2)}, u32[]{:S(2)}) collective-permute-start(bf16[3,64,1792]{2,1,0:T(8,128)(2,1)S(1)} %copy-done.4), channel_id=1, source_target_pairs={{0,2},{2,0},{4,6},{6,4},{8,10},{10,8},{12,14},{14,12},{16,18},{18,... | collective-permute-start | bytes 2064392 | tf_op jit(solution)/shard_map/ppermute | solution.py:330
  68.3 14.1 %collective-permute-start.26 = (bf16[3,64,1792]{2,1,0:T(8,128)(2,1)S(1)}, bf16[3,64,1792]{2,1,0:T(8,128)(2,1)S(1)}, u32[]{:S(2)}, u32[]{:S(2)}) collective-permute-start(bf16[3,64,1792]{2,1,0:T(8,128)(2,1)S(1)} %collective-permute-done.3.rest_8_), channel_id=1, source_target_pairs={{0,2},{2,0},{4,6},{6,4},{8,10},{10,8},{12,14},{14,12},{16,18},{18,... | collective-permute-start | bytes 2064392 | tf_op jit(solution)/shard_map/ppermute | solution.py:330
  68.8 18.5 %collective-permute-start.24 = (bf16[3,64,1792]{2,1,0:T(8,128)(2,1)}, bf16[3,64,1792]{2,1,0:T(8,128)(2,1)S(1)}, u32[]{:S(2)}, u32[]{:S(2)}) collective-permute-start(bf16[3,64,1792]{2,1,0:T(8,128)(2,1)} %collective-permute-done.18.rest_1_), channel_id=1, source_target_pairs={{0,4},{2,6},{4,0},{6,2},{8,12},{10,14},{12,8},{14,10},{16,20},{18,... | collective-permute-start | bytes 2064392 | tf_op jit(solution)/shard_map/ppermute | solution.py:330
  70.4 17.0 %collective-permute-start.21 = (bf16[3,64,1792]{2,1,0:T(8,128)(2,1)}, bf16[3,64,1792]{2,1,0:T(8,128)(2,1)S(1)}, u32[]{:S(2)}, u32[]{:S(2)}) collective-permute-start(bf16[3,64,1792]{2,1,0:T(8,128)(2,1)} %collective-permute-done.18.rest_1_), channel_id=1, source_target_pairs={{0,2},{2,0},{4,6},{6,4},{8,10},{10,8},{12,14},{14,12},{16,18},{18,... | collective-permute-start | bytes 2064392 | tf_op jit(solution)/shard_map/ppermute | solution.py:330
  81.8 19.4 %collective-permute-start.25 = (bf16[3,64,1792]{2,1,0:T(8,128)(2,1)}, bf16[3,64,1792]{2,1,0:T(8,128)(2,1)S(1)}, u32[]{:S(2)}, u32[]{:S(2)}) collective-permute-start(bf16[3,64,1792]{2,1,0:T(8,128)(2,1)} %collective-permute-done.19.rest_3_), channel_id=1, source_target_pairs={{0,4},{2,6},{4,0},{6,2},{8,12},{10,14},{12,8},{14,10},{16,20},{18,... | collective-permute-start | bytes 2064392 | tf_op jit(solution)/shard_map/ppermute | solution.py:330
  82.3 18.9 %collective-permute-start.22 = (bf16[3,64,1792]{2,1,0:T(8,128)(2,1)S(1)}, bf16[3,64,1792]{2,1,0:T(8,128)(2,1)S(1)}, u32[]{:S(2)}, u32[]{:S(2)}) collective-permute-start(bf16[3,64,1792]{2,1,0:T(8,128)(2,1)S(1)} %collective-permute-done.16.rest_2_), channel_id=1, source_target_pairs={{0,2},{2,0},{4,6},{6,4},{8,10},{10,8},{12,14},{14,12},{16,18},{18,... | collective-permute-start | bytes 2064392 | tf_op jit(solution)/shard_map/ppermute | solution.py:330
  82.4 18.8 %collective-permute-start.23 = (bf16[3,64,1792]{2,1,0:T(8,128)(2,1)}, bf16[3,64,1792]{2,1,0:T(8,128)(2,1)S(1)}, u32[]{:S(2)}, u32[]{:S(2)}) collective-permute-start(bf16[3,64,1792]{2,1,0:T(8,128)(2,1)} %collective-permute-done.19.rest_3_), channel_id=1, source_target_pairs={{0,2},{2,0},{4,6},{6,4},{8,10},{10,8},{12,14},{14,12},{16,18},{18,... | collective-permute-start | bytes 2064392 | tf_op jit(solution)/shard_map/ppermute | solution.py:330
  87.3 13.9 %collective-permute-start.27 = (bf16[3,64,1792]{2,1,0:T(8,128)(2,1)S(1)}, bf16[3,64,1792]{2,1,0:T(8,128)(2,1)S(1)}, u32[]{:S(2)}, u32[]{:S(2)}) collective-permute-start(bf16[3,64,1792]{2,1,0:T(8,128)(2,1)S(1)} %collective-permute-done.24.rest_9_), channel_id=1, source_target_pairs={{0,2},{2,0},{4,6},{6,4},{8,10},{10,8},{12,14},{14,12},{16,18},{18,... | collective-permute-start | bytes 2064392 | tf_op jit(solution)/shard_map/ppermute | solution.py:330
  87.4 13.9 %collective-permute-start.28 = (bf16[3,64,1792]{2,1,0:T(8,128)(2,1)}, bf16[3,64,1792]{2,1,0:T(8,128)(2,1)S(1)}, u32[]{:S(2)}, u32[]{:S(2)}) collective-permute-start(bf16[3,64,1792]{2,1,0:T(8,128)(2,1)} %copy-done.7), channel_id=1, source_target_pairs={{0,2},{2,0},{4,6},{6,4},{8,10},{10,8},{12,14},{14,12},{16,18},{18,... | collective-permute-start | bytes 2064392 | tf_op jit(solution)/shard_map/ppermute | solution.py:330
  118.2 14.2 %collective-permute-start.31 = (bf16[72,1024]{1,0:T(8,128)(2,1)}, bf16[72,1024]{1,0:T(8,128)(2,1)S(1)}, u32[]{:S(2)}, u32[]{:S(2)}) collective-permute-start(bf16[72,1024]{1,0:T(8,128)(2,1)} %get-tuple-element.84), channel_id=1, source_target_pairs={{0,16},{1,17},{8,24},{9,25},{16,0},{17,1},{24,8},{25,9},{2,18},{3,... | collective-permute-start | bytes 442376 | tf_op jit(solution)/shard_map/ppermute | solution.py:399
  118.3 16.0 %collective-permute-start.32 = (bf16[72,1024]{1,0:T(8,128)(2,1)}, bf16[72,1024]{1,0:T(8,128)(2,1)S(1)}, u32[]{:S(2)}, u32[]{:S(2)}) collective-permute-start(bf16[72,1024]{1,0:T(8,128)(2,1)} %get-tuple-element.85), channel_id=1, source_target_pairs={{0,24},{1,25},{8,16},{9,17},{16,8},{17,9},{24,0},{25,1},{2,26},{3,... | collective-permute-start | bytes 442376 | tf_op jit(solution)/shard_map/ppermute | solution.py:399
  118.9 20.2 %collective-permute-start.33 = (bf16[72,1024]{1,0:T(8,128)(2,1)}, bf16[72,1024]{1,0:T(8,128)(2,1)S(1)}, u32[]{:S(2)}, u32[]{:S(2)}) collective-permute-start(bf16[72,1024]{1,0:T(8,128)(2,1)} %get-tuple-element.86), channel_id=1, source_target_pairs={{0,1},{1,0},{8,9},{9,8},{16,17},{17,16},{24,25},{25,24},{2,3},{3,2... | collective-permute-start | bytes 442376 | tf_op jit(solution)/shard_map/ppermute | solution.py:399
  120.3 18.7 %collective-permute-start.34 = (bf16[72,1024]{1,0:T(8,128)(2,1)}, bf16[72,1024]{1,0:T(8,128)(2,1)S(1)}, u32[]{:S(2)}, u32[]{:S(2)}) collective-permute-start(bf16[72,1024]{1,0:T(8,128)(2,1)} %get-tuple-element.87), channel_id=1, source_target_pairs={{0,9},{1,8},{8,1},{9,0},{16,25},{17,24},{24,17},{25,16},{2,11},{3,... | collective-permute-start | bytes 442376 | tf_op jit(solution)/shard_map/ppermute | solution.py:399
  123.2 19.8 %collective-permute-start.35 = (bf16[72,1024]{1,0:T(8,128)(2,1)}, bf16[72,1024]{1,0:T(8,128)(2,1)S(1)}, u32[]{:S(2)}, u32[]{:S(2)}) collective-permute-start(bf16[72,1024]{1,0:T(8,128)(2,1)} %get-tuple-element.88), channel_id=1, source_target_pairs={{0,17},{1,16},{8,25},{9,24},{16,1},{17,0},{24,9},{25,8},{2,19},{3,... | collective-permute-start | bytes 442376 | tf_op jit(solution)/shard_map/ppermute | solution.py:399
  132.4 10.6 %collective-permute-start.36 = (bf16[72,1024]{1,0:T(8,128)(2,1)S(1)}, bf16[72,1024]{1,0:T(8,128)(2,1)S(1)}, u32[]{:S(2)}, u32[]{:S(2)}) collective-permute-start(bf16[72,1024]{1,0:T(8,128)(2,1)S(1)} %copy-done.35), channel_id=1, source_target_pairs={{0,25},{1,24},{8,17},{9,16},{16,9},{17,8},{24,1},{25,0},{2,27},{3,... | collective-permute-start | bytes 442376 | tf_op jit(solution)/shard_map/ppermute | solution.py:399
  134.3 10.8 %collective-permute-start.30 = (bf16[72,1024]{1,0:T(8,128)(2,1)}, bf16[72,1024]{1,0:T(8,128)(2,1)S(1)}, u32[]{:S(2)}, u32[]{:S(2)}) collective-permute-start(bf16[72,1024]{1,0:T(8,128)(2,1)} %get-tuple-element.83), channel_id=1, source_target_pairs={{0,8},{1,9},{8,0},{9,1},{16,24},{17,25},{24,16},{25,17},{2,10},{3,... | collective-permute-start | bytes 442376 | tf_op jit(solution)/shard_map/ppermute | solution.py:399
  (42 other events, 422.1 us)

commit v7 on v6

--- a/solution.py
+++ b/solution.py
@@ -266,15 +266,18 @@
     )(place, rows, *pieces)
 
 
-def combine_kernel(target_ref, probs_ref, residual_ref, *rest):
-    returned_refs, out_ref = rest[:-1], rest[-1]
+def combine_kernel(target_ref, probs_ref, residual_ref, own_in, *rest):
+    returned_refs, out_ref, own_ref, sem = rest[:-3], rest[-3], rest[-2], rest[-1]
+    load = pltpu.make_async_copy(own_in, own_ref, sem.at[0])
+    load.start()
     rows = residual_ref.shape[0]
-    slot = lax.broadcasted_iota(jnp.int32, (rows, CAP), 1)
-    picked = jnp.zeros((TOP * rows, D), jnp.float32)
-    for j, returned_ref in enumerate(returned_refs):
-        selector = [(slot + j * CAP == target_ref[:, k : k + 1]).astype(jnp.float32) for k in range(TOP)]
-        selector = jnp.concatenate(selector, axis=0).astype(jnp.bfloat16)
-        picked = picked + jnp.dot(selector, returned_ref[...], preferred_element_type=jnp.float32)
+    load.wait()
+    slot = lax.broadcasted_iota(jnp.int32, (rows, EXPERTS * CAP), 1)
+    parts = [own_ref[...], *[ref[...] for ref in returned_refs]]
+    parts = jnp.concatenate([part.astype(jnp.float32) for part in parts], axis=0).astype(jnp.bfloat16)
+    selector = [(slot == target_ref[:, k : k + 1]).astype(jnp.float32) for k in range(TOP)]
+    selector = jnp.concatenate(selector, axis=0).astype(jnp.bfloat16)
+    picked = jnp.dot(selector, parts, preferred_element_type=jnp.float32)
     total = jnp.zeros((rows, D), jnp.float32)
     for k in range(TOP):
         total = total + picked[k * rows : (k + 1) * rows] * probs_ref[:, k : k + 1]
@@ -285,8 +288,9 @@
     return pl.pallas_call(
         combine_kernel,
         out_shape=jax.ShapeDtypeStruct(residual.shape, jnp.bfloat16),
-        in_specs=[VMEM] * (3 + len(returned)),
+        in_specs=[VMEM] * 3 + [ANY] + [VMEM] * (len(returned) - 1),
         out_specs=VMEM,
+        scratch_shapes=[pltpu.VMEM((CAP, D), jnp.bfloat16), pltpu.SemaphoreType.DMA((1,))],
         compiler_params=pltpu.CompilerParams(vmem_limit_bytes=24 * MB),
         name="combine",
     )(target, probs, residual, *returned)

time: 149 us -> 148 us (level)
  Pallas kernels: 35.4 us -> 32.7 us
  waiting for transfers between devices: 62.4 us -> 64.3 us
    pallas_call x1, Pallas kernels: 11.2 us -> 9.3 us  [attend(): pl.pallas_call(functools.partial(attend_kernel, n), out_shape=[jax.ShapeD...]
    ppermute x30, waiting for transfers between devices: 52.7 us -> 54.6 us  [swap(): return lax.ppermute(x, ctx, [(i, i ^ bit) for i in range(world)])]
  transfers between devices with their start and end apart: 38 -> 38, of which waited for: 15 -> 15; matrix products, arithmetic and copies ran while one was open for 3% -> 3% of each run, Pallas kernels for 15% -> 14%
where the time goes in v7:
time: 148 us
  waiting for transfers between devices  64.3 us (43%)
  starting transfers between devices  38.8 us (26%)
  Pallas kernels  32.7 us (22%)
  local copies, waits for them, and re-layouts  7.45 us (5%)
  other arithmetic  2.35 us (2%)
    ppermute x30, waiting for transfers between devices, swap(): return lax.ppermute(x, ctx, [(i, i ^ bit) for i in range(world)])  54.6 us
    ppermute x30, starting transfers between devices, swap(): return lax.ppermute(x, ctx, [(i, i ^ bit) for i in range(world)])  21.7 us
    pallas_call x2, Pallas kernels, run_expert(): pl.pallas_call(functools.partial(expert_kernel, planes, shared, cuts, ste...  17.3 us
    ppermute x7, starting transfers between devices, shards(): returned[j] = lax.ppermute(x, ('plane', 'exp'), pairs) if j else x  13.3 us
    pallas_call x1, Pallas kernels, attend(): pl.pallas_call(functools.partial(attend_kernel, n), out_shape=[jax.ShapeD...  9.3 us
    ppermute x7, waiting for transfers between devices, shards(): returned[j] = lax.ppermute(x, ('plane', 'exp'), pairs) if j else x  6.02 us
    unnamed x74, local copies, waits for them, and re-layouts  4.96 us
    pallas_call x1, Pallas kernels, pack(): pl.pallas_call(functools.partial(pack_kernel, planes), out_shape=[jax.Sha...  4.31 us
  transfers between devices with their start and end apart: 38, of which 15 were waited for; matrix products, arithmetic and copies ran while one was open for 3% of the time, Pallas kernels for 14%

profile of v7, /device:TPU:0, one launch (start us, length us, event | category | flops | bytes accessed | tf_op | source)
XLA Modules:
  0.0 148.0 jit_solution(12501871317929238688)
XLA Ops:
  0.6 1.0 pad_maximum_fusion.rest_0_
  1.6 4.1 %collective-permute-start = (bf16[192,512]{1,0:T(8,128)(2,1)S(1)}, bf16[192,512]{1,0:T(8,128)(2,1)S(1)}, u32[]{:S(2)}, u32[]{:S(2)}) collective-permute-start(bf16[192,512]{1,0:T(8,128)(2,1)S(1)} %pad_maximum_fusion.rest_0_), channel_id=1, source_target_pairs={{0,16},{2,18},{4,20},{6,22},{8,24},{10,26},{12,28},{14,30},{16,0},... | collective-permute-start | bytes 589832 | tf_op jit(solution)/shard_map/ppermute | solution.py:334
  5.7 1.6 %collective-permute-start.7 = (bf16[192,512]{1,0:T(8,128)(2,1)S(1)}, bf16[192,512]{1,0:T(8,128)(2,1)S(1)}, u32[]{:S(2)}, u32[]{:S(2)}) collective-permute-start(bf16[192,512]{1,0:T(8,128)(2,1)S(1)} %pad_maximum_fusion.rest_0_), channel_id=1, source_target_pairs={{0,8},{2,10},{4,12},{6,14},{8,0},{10,2},{12,4},{14,6},{16,24},{18,... | collective-permute-start | bytes 589832 | tf_op jit(solution)/shard_map/ppermute | solution.py:334
  7.3 1.5 %collective-permute-start.5 = (bf16[192,512]{1,0:T(8,128)(2,1)S(1)}, bf16[192,512]{1,0:T(8,128)(2,1)S(1)}, u32[]{:S(2)}, u32[]{:S(2)}) collective-permute-start(bf16[192,512]{1,0:T(8,128)(2,1)S(1)} %pad_maximum_fusion.rest_0_), channel_id=1, source_target_pairs={{0,4},{2,6},{4,0},{6,2},{8,12},{10,14},{12,8},{14,10},{16,20},{18,... | collective-permute-start | bytes 589832 | tf_op jit(solution)/shard_map/ppermute | solution.py:334
  9.5 4.3 %pack_weights.1 = (bf16[3,64,1792]{2,1,0:T(8,128)(2,1)}, bf16[3,64,1792]{2,1,0:T(8,128)(2,1)}, bf16[3,64,1792]{2,1,0:T(8,128)(2,1)}, bf16[3,64,1792]{2,1,0:T(8,128)(2,1)}) custom-call(s32[3]{0:T(128)} %pad_add_fusion.place_ref, bf16[4,64,1792]{2,1,0:T(8,128)(2,1)} %gate_ref.1, bf16[4,64,1792]{2,1,0:T(8,128)(2,1)} %up_ref.1, bf16[4,64,1792]{2,1,0:T(8,128)(2,1)} %down_ref.1), custom_call_target="tpu_custom_call" | custom-call | tf_op jit(solution)/shard_map/pack_weights/pallas_call | solution.py:44
  18.0 1.8 %collective-permute-start.9 = (bf16[192,512]{1,0:T(8,128)(2,1)S(1)}, bf16[192,512]{1,0:T(8,128)(2,1)S(1)}, u32[]{:S(2)}, u32[]{:S(2)}) collective-permute-start(bf16[192,512]{1,0:T(8,128)(2,1)S(1)} %collective-permute-done.7.rest_4_), channel_id=1, source_target_pairs={{0,4},{2,6},{4,0},{6,2},{8,12},{10,14},{12,8},{14,10},{16,20},{18,... | collective-permute-start | bytes 589832 | tf_op jit(solution)/shard_map/ppermute | solution.py:334
  19.8 13.3 %collective-permute-done.1.rest_12_ = bf16[192,512]{1,0:T(8,128)(2,1)S(1)} collective-permute-done((bf16[192,512]{1,0:T(8,128)(2,1)S(1)}, bf16[192,512]{1,0:T(8,128)(2,1)S(1)}, u32[]{:S(2)}, u32[]{:S(2)}) %collective-permute-start.1) | collective-permute-done | bytes 196640 | tf_op jit(solution)/shard_map/ppermute | solution.py:334
  33.1 1.5 %collective-permute-start.2 = (bf16[192,512]{1,0:T(8,128)(2,1)S(1)}, bf16[192,512]{1,0:T(8,128)(2,1)S(1)}, u32[]{:S(2)}, u32[]{:S(2)}) collective-permute-start(bf16[192,512]{1,0:T(8,128)(2,1)S(1)} %collective-permute-done.1.rest_12_), channel_id=1, source_target_pairs={{0,4},{2,6},{4,0},{6,2},{8,12},{10,14},{12,8},{14,10},{16,20},{18,... | collective-permute-start | bytes 589832 | tf_op jit(solution)/shard_map/ppermute | solution.py:334
  36.1 4.8 %collective-permute-done.2.rest_14_ = bf16[192,512]{1,0:T(8,128)(2,1)S(1)} collective-permute-done((bf16[192,512]{1,0:T(8,128)(2,1)S(1)}, bf16[192,512]{1,0:T(8,128)(2,1)S(1)}, u32[]{:S(2)}, u32[]{:S(2)}) %collective-permute-start.2) | collective-permute-done | bytes 196640 | tf_op jit(solution)/shard_map/ppermute | solution.py:334
  41.5 1.6 %collective-permute-done.12.rest_10_ = bf16[192,512]{1,0:T(8,128)(2,1)S(1)} collective-permute-done((bf16[192,512]{1,0:T(8,128)(2,1)S(1)}, bf16[192,512]{1,0:T(8,128)(2,1)S(1)}, u32[]{:S(2)}, u32[]{:S(2)}) %collective-permute-start.12) | collective-permute-done | bytes 196640 | tf_op jit(solution)/shard_map/ppermute | solution.py:334
  45.0 1.1 collective-permute-done.16.rest_2_
  46.2 1.6 %collective-permute-start.17 = (bf16[3,64,1792]{2,1,0:T(8,128)(2,1)S(1)}, bf16[3,64,1792]{2,1,0:T(8,128)(2,1)S(1)}, u32[]{:S(2)}, u32[]{:S(2)}) collective-permute-start(bf16[3,64,1792]{2,1,0:T(8,128)(2,1)S(1)} %collective-permute-done.16.rest_2_), channel_id=1, source_target_pairs={{0,4},{2,6},{4,0},{6,2},{8,12},{10,14},{12,8},{14,10},{16,20},{18,... | collective-permute-start | bytes 2064392 | tf_op jit(solution)/shard_map/ppermute | solution.py:334
  48.7 1.7 %collective-permute-start.19 = (bf16[3,64,1792]{2,1,0:T(8,128)(2,1)}, bf16[3,64,1792]{2,1,0:T(8,128)(2,1)}, u32[]{:S(2)}, u32[]{:S(2)}) collective-permute-start(bf16[3,64,1792]{2,1,0:T(8,128)(2,1)} %get-tuple-element.79), channel_id=1, source_target_pairs={{0,24},{2,26},{4,28},{6,30},{8,16},{10,18},{12,20},{14,22},{16,8},... | collective-permute-start | bytes 2064392 | tf_op jit(solution)/shard_map/ppermute | solution.py:334
  51.1 9.3 %attend.1 = (bf16[192,1024]{1,0:T(8,128)(2,1)}, bf16[192,1024]{1,0:T(8,128)(2,1)}, bf16[576,1024]{1,0:T(8,128)(2,1)}) custom-call(s32[96]{0:T(128)} %convert_element_type.35.live_ref, s32[96]{0:T(128)} %get-tuple-element.49.spot_ref, bf16[8,16,128]{2,1,0:T(8,128)(2,1)} %pad.5.allowed_ref, bf16[192,1024]{1,0:T(8,128)(2,1)} %bitcast.33, ...), custom_call_target="tpu_custom_call" | custom-call | tf_op jit(solution)/shard_map/attend/pallas_call | solution.py:157
  60.4 3.2 %collective-permute-done.17.rest_10_ = bf16[3,64,1792]{2,1,0:T(8,128)(2,1)S(1)} collective-permute-done((bf16[3,64,1792]{2,1,0:T(8,128)(2,1)S(1)}, bf16[3,64,1792]{2,1,0:T(8,128)(2,1)S(1)}, u32[]{:S(2)}, u32[]{:S(2)}) %collective-permute-start.17) | collective-permute-done | bytes 688160 | tf_op jit(solution)/shard_map/ppermute | solution.py:334
  64.5 3.8 %all-to-all-start = ((bf16[8,72,1024]{2,1,0:T(8,128)(2,1)}), bf16[8,72,1024]{2,1,0:T(8,128)(2,1)S(1)}, u32[]{:S(2)}, u32[]{:S(2)}) async-start(bf16[8,72,1024]{2,1,0:T(8,128)(2,1)} %bitcast.29), calls=%async_computation | async-start | bytes 2359296 | tf_op jit(solution)/shard_map/all_to_all | solution.py:391
  68.8 1.5 %collective-permute-start.24 = (bf16[3,64,1792]{2,1,0:T(8,128)(2,1)}, bf16[3,64,1792]{2,1,0:T(8,128)(2,1)S(1)}, u32[]{:S(2)}, u32[]{:S(2)}) collective-permute-start(bf16[3,64,1792]{2,1,0:T(8,128)(2,1)} %collective-permute-done.18.rest_1_), channel_id=1, source_target_pairs={{0,4},{2,6},{4,0},{6,2},{8,12},{10,14},{12,8},{14,10},{16,20},{18,... | collective-permute-start | bytes 2064392 | tf_op jit(solution)/shard_map/ppermute | solution.py:334
  70.4 11.4 %collective-permute-done.19.rest_3_ = bf16[3,64,1792]{2,1,0:T(8,128)(2,1)} collective-permute-done((bf16[3,64,1792]{2,1,0:T(8,128)(2,1)}, bf16[3,64,1792]{2,1,0:T(8,128)(2,1)}, u32[]{:S(2)}, u32[]{:S(2)}) %collective-permute-start.19) | collective-permute-done | bytes 688160 | tf_op jit(solution)/shard_map/ppermute | solution.py:334
  82.9 4.4 %collective-permute-done.24.rest_9_ = bf16[3,64,1792]{2,1,0:T(8,128)(2,1)S(1)} collective-permute-done((bf16[3,64,1792]{2,1,0:T(8,128)(2,1)}, bf16[3,64,1792]{2,1,0:T(8,128)(2,1)S(1)}, u32[]{:S(2)}, u32[]{:S(2)}) %collective-permute-start.24) | collective-permute-done | bytes 688160 | tf_op jit(solution)/shard_map/ppermute | solution.py:334
  87.9 13.4 %collective-permute-done.25.rest_11_ = bf16[3,64,1792]{2,1,0:T(8,128)(2,1)S(1)} collective-permute-done((bf16[3,64,1792]{2,1,0:T(8,128)(2,1)}, bf16[3,64,1792]{2,1,0:T(8,128)(2,1)S(1)}, u32[]{:S(2)}, u32[]{:S(2)}) %collective-permute-start.25) | collective-permute-done | bytes 688160 | tf_op jit(solution)/shard_map/ppermute | solution.py:334
  103.5 3.7 %all-to-all-done.rows_in = bf16[8,72,1024]{2,1,0:T(8,128)(2,1)S(1)} async-done(((bf16[8,72,1024]{2,1,0:T(8,128)(2,1)}), bf16[8,72,1024]{2,1,0:T(8,128)(2,1)S(1)}, u32[]{:S(2)}, u32[]{:S(2)}) %all-to-all-start) | async-done | bytes 1179680 | tf_op jit(solution)/shard_map/all_to_all | solution.py:391
  107.2 1.1 copy-done.2
  108.3 9.9 %expert.3 = (bf16[72,1024]{1,0:T(8,128)(2,1)}, bf16[72,1024]{1,0:T(8,128)(2,1)}, bf16[72,1024]{1,0:T(8,128)(2,1)}, bf16[72,1024]{1,0:T(8,128)(2,1)}, bf16[72,1024]{1,0:T(8,128)(2,1)}, /*index=5*/bf16[72,1024]{1,0:T(8,128)(2,1)}) custom-call(s32[3]{0:T(128)} %pad_add_fusion.place_ref, bf16[8,72,1024]{2,1,0:T(8,128)(2,1)} %copy-done.2, ...), custom_call_target="tpu_custom_call" | custom-call | flops 4756340736 | bytes 11010048 | tf_op jit(solution)/shard_map/expert/pallas_call | solution.py:249
  118.9 1.5 collective-permute-start.33
  120.3 2.9 %collective-permute-start.34 = (bf16[72,1024]{1,0:T(8,128)(2,1)}, bf16[72,1024]{1,0:T(8,128)(2,1)S(1)}, u32[]{:S(2)}, u32[]{:S(2)}) collective-permute-start(bf16[72,1024]{1,0:T(8,128)(2,1)} %get-tuple-element.87), channel_id=1, source_target_pairs={{0,9},{1,8},{8,1},{9,0},{16,25},{17,24},{24,17},{25,16},{2,11},{3,... | collective-permute-start | bytes 442376 | tf_op jit(solution)/shard_map/ppermute | solution.py:403
  123.2 1.8 %collective-permute-start.35 = (bf16[72,1024]{1,0:T(8,128)(2,1)}, bf16[72,1024]{1,0:T(8,128)(2,1)S(1)}, u32[]{:S(2)}, u32[]{:S(2)}) collective-permute-start(bf16[72,1024]{1,0:T(8,128)(2,1)} %get-tuple-element.88), channel_id=1, source_target_pairs={{0,17},{1,16},{8,25},{9,24},{16,1},{17,0},{24,9},{25,8},{2,19},{3,... | collective-permute-start | bytes 442376 | tf_op jit(solution)/shard_map/ppermute | solution.py:403
  125.0 7.4 %expert.2 = (bf16[72,1024]{1,0:T(8,128)(2,1)}, bf16[72,1024]{1,0:T(8,128)(2,1)}) custom-call(s32[3]{0:T(128)} %pad_add_fusion.place_ref, bf16[8,72,1024]{2,1,0:T(8,128)(2,1)} %copy-done.2, bf16[3,64,1792]{2,1,0:T(8,128)(2,1)} %get-tuple-element.46.rest_0_, bf16[3,64,1792]{2,1,0:T(8,128)(2,1)} %collective-permute-done.18.rest_1_, ...), custom_call_target="tpu_custom_call" | custom-call | flops 1585446912 | bytes 11010048 | tf_op jit(solution)/shard_map/expert/pallas_call | solution.py:249
  132.4 1.9 %collective-permute-start.36 = (bf16[72,1024]{1,0:T(8,128)(2,1)S(1)}, bf16[72,1024]{1,0:T(8,128)(2,1)S(1)}, u32[]{:S(2)}, u32[]{:S(2)}) collective-permute-start(bf16[72,1024]{1,0:T(8,128)(2,1)S(1)} %copy-done.35), channel_id=1, source_target_pairs={{0,25},{1,24},{8,17},{9,16},{16,9},{17,8},{24,1},{25,0},{2,27},{3,... | collective-permute-start | bytes 442376 | tf_op jit(solution)/shard_map/ppermute | solution.py:403
  134.3 4.6 %collective-permute-start.30 = (bf16[72,1024]{1,0:T(8,128)(2,1)}, bf16[72,1024]{1,0:T(8,128)(2,1)S(1)}, u32[]{:S(2)}, u32[]{:S(2)}) collective-permute-start(bf16[72,1024]{1,0:T(8,128)(2,1)} %get-tuple-element.83), channel_id=1, source_target_pairs={{0,8},{1,9},{8,0},{9,1},{16,24},{17,25},{24,16},{25,17},{2,10},{3,... | collective-permute-start | bytes 442376 | tf_op jit(solution)/shard_map/ppermute | solution.py:403
  139.1 3.9 %collective-permute-done.35.rest_5_ = bf16[72,1024]{1,0:T(8,128)(2,1)S(1)} collective-permute-done((bf16[72,1024]{1,0:T(8,128)(2,1)}, bf16[72,1024]{1,0:T(8,128)(2,1)S(1)}, u32[]{:S(2)}, u32[]{:S(2)}) %collective-permute-start.35) | collective-permute-done | bytes 147488 | tf_op jit(solution)/shard_map/ppermute | solution.py:403
  143.0 2.1 %collective-permute-done.30.rest_0_ = bf16[72,1024]{1,0:T(8,128)(2,1)S(1)} collective-permute-done((bf16[72,1024]{1,0:T(8,128)(2,1)}, bf16[72,1024]{1,0:T(8,128)(2,1)S(1)}, u32[]{:S(2)}, u32[]{:S(2)}) %collective-permute-start.30) | collective-permute-done | bytes 147488 | tf_op jit(solution)/shard_map/ppermute | solution.py:403
  146.0 1.8 %combine.1 = bf16[192,1024]{1,0:T(8,128)(2,1)} custom-call(s32[192,2]{1,0:T(8,128)S(1)} %get-tuple-element.73.target_ref, f32[192,2]{1,0:T(8,128)S(1)} %bitcast.28, bf16[192,1024]{1,0:T(8,128)(2,1)S(1)} %copy-done, bf16[72,1024]{1,0:T(8,128)(2,1)S(1)} %copy-done.1, bf16[72,1024]{1,0:T(8,128)(2,1)S(1)} %collective-permute-done.30.rest_0_, ...), custom_call_target="tpu_custom_call" | custom-call | tf_op jit(solution)/shard_map/combine/pallas_call | solution.py:288
  (149 shorter events, 17.2 us)
Async XLA Ops:
  1.6 15.1 %collective-permute-start = (bf16[192,512]{1,0:T(8,128)(2,1)S(1)}, bf16[192,512]{1,0:T(8,128)(2,1)S(1)}, u32[]{:S(2)}, u32[]{:S(2)}) collective-permute-start(bf16[192,512]{1,0:T(8,128)(2,1)S(1)} %pad_maximum_fusion.rest_0_), channel_id=1, source_target_pairs={{0,16},{2,18},{4,20},{6,22},{8,24},{10,26},{12,28},{14,30},{16,0},... | collective-permute-start | bytes 589832 | tf_op jit(solution)/shard_map/ppermute | solution.py:334
  5.7 12.2 %collective-permute-start.7 = (bf16[192,512]{1,0:T(8,128)(2,1)S(1)}, bf16[192,512]{1,0:T(8,128)(2,1)S(1)}, u32[]{:S(2)}, u32[]{:S(2)}) collective-permute-start(bf16[192,512]{1,0:T(8,128)(2,1)S(1)} %pad_maximum_fusion.rest_0_), channel_id=1, source_target_pairs={{0,8},{2,10},{4,12},{6,14},{8,0},{10,2},{12,4},{14,6},{16,24},{18,... | collective-permute-start | bytes 589832 | tf_op jit(solution)/shard_map/ppermute | solution.py:334
  7.3 10.7 %collective-permute-start.5 = (bf16[192,512]{1,0:T(8,128)(2,1)S(1)}, bf16[192,512]{1,0:T(8,128)(2,1)S(1)}, u32[]{:S(2)}, u32[]{:S(2)}) collective-permute-start(bf16[192,512]{1,0:T(8,128)(2,1)S(1)} %pad_maximum_fusion.rest_0_), channel_id=1, source_target_pairs={{0,4},{2,6},{4,0},{6,2},{8,12},{10,14},{12,8},{14,10},{16,20},{18,... | collective-permute-start | bytes 589832 | tf_op jit(solution)/shard_map/ppermute | solution.py:334
  13.8 27.2 %collective-permute-start.3 = (bf16[3,64,1792]{2,1,0:T(8,128)(2,1)}, bf16[3,64,1792]{2,1,0:T(8,128)(2,1)S(1)}, u32[]{:S(2)}, u32[]{:S(2)}) collective-permute-start(bf16[3,64,1792]{2,1,0:T(8,128)(2,1)} %get-tuple-element.46.rest_0_), channel_id=1, source_target_pairs={{0,4},{2,6},{4,0},{6,2},{8,12},{10,14},{12,8},{14,10},{16,20},{18,... | collective-permute-start | bytes 2064392 | tf_op jit(solution)/shard_map/ppermute | solution.py:334
  14.3 31.8 %collective-permute-start.16 = (bf16[3,64,1792]{2,1,0:T(8,128)(2,1)}, bf16[3,64,1792]{2,1,0:T(8,128)(2,1)S(1)}, u32[]{:S(2)}, u32[]{:S(2)}) collective-permute-start(bf16[3,64,1792]{2,1,0:T(8,128)(2,1)} %get-tuple-element.55), channel_id=1, source_target_pairs={{0,16},{2,18},{4,20},{6,22},{8,24},{10,26},{12,28},{14,30},{16,0},... | collective-permute-start | bytes 2064392 | tf_op jit(solution)/shard_map/ppermute | solution.py:334
  16.7 16.4 %collective-permute-start.1 = (bf16[192,512]{1,0:T(8,128)(2,1)S(1)}, bf16[192,512]{1,0:T(8,128)(2,1)S(1)}, u32[]{:S(2)}, u32[]{:S(2)}) collective-permute-start(bf16[192,512]{1,0:T(8,128)(2,1)S(1)} %collective-permute-done.rest_8_), channel_id=1, source_target_pairs={{0,8},{2,10},{4,12},{6,14},{8,0},{10,2},{12,4},{14,6},{16,24},{18,... | collective-permute-start | bytes 589832 | tf_op jit(solution)/shard_map/ppermute | solution.py:334
  17.9 17.6 %collective-permute-start.4 = (bf16[192,512]{1,0:T(8,128)(2,1)S(1)}, bf16[192,512]{1,0:T(8,128)(2,1)S(1)}, u32[]{:S(2)}, u32[]{:S(2)}) collective-permute-start(bf16[192,512]{1,0:T(8,128)(2,1)S(1)} %pad_maximum_fusion.rest_0_), channel_id=1, source_target_pairs={{0,2},{2,0},{4,6},{6,4},{8,10},{10,8},{12,14},{14,12},{16,18},{18,... | collective-permute-start | bytes 589832 | tf_op jit(solution)/shard_map/ppermute | solution.py:334
  18.0 18.1 %collective-permute-start.9 = (bf16[192,512]{1,0:T(8,128)(2,1)S(1)}, bf16[192,512]{1,0:T(8,128)(2,1)S(1)}, u32[]{:S(2)}, u32[]{:S(2)}) collective-permute-start(bf16[192,512]{1,0:T(8,128)(2,1)S(1)} %collective-permute-done.7.rest_4_), channel_id=1, source_target_pairs={{0,4},{2,6},{4,0},{6,2},{8,12},{10,14},{12,8},{14,10},{16,20},{18,... | collective-permute-start | bytes 589832 | tf_op jit(solution)/shard_map/ppermute | solution.py:334
  33.1 7.8 %collective-permute-start.2 = (bf16[192,512]{1,0:T(8,128)(2,1)S(1)}, bf16[192,512]{1,0:T(8,128)(2,1)S(1)}, u32[]{:S(2)}, u32[]{:S(2)}) collective-permute-start(bf16[192,512]{1,0:T(8,128)(2,1)S(1)} %collective-permute-done.1.rest_12_), channel_id=1, source_target_pairs={{0,4},{2,6},{4,0},{6,2},{8,12},{10,14},{12,8},{14,10},{16,20},{18,... | collective-permute-start | bytes 589832 | tf_op jit(solution)/shard_map/ppermute | solution.py:334
  35.5 7.5 %collective-permute-start.12 = (bf16[192,512]{1,0:T(8,128)(2,1)S(1)}, bf16[192,512]{1,0:T(8,128)(2,1)S(1)}, u32[]{:S(2)}, u32[]{:S(2)}) collective-permute-start(bf16[192,512]{1,0:T(8,128)(2,1)S(1)} %collective-permute-done.rest_8_), channel_id=1, source_target_pairs={{0,4},{2,6},{4,0},{6,2},{8,12},{10,14},{12,8},{14,10},{16,20},{18,... | collective-permute-start | bytes 589832 | tf_op jit(solution)/shard_map/ppermute | solution.py:334
  36.1 7.0 %collective-permute-start.11 = (bf16[192,512]{1,0:T(8,128)(2,1)S(1)}, bf16[192,512]{1,0:T(8,128)(2,1)S(1)}, u32[]{:S(2)}, u32[]{:S(2)}) collective-permute-start(bf16[192,512]{1,0:T(8,128)(2,1)S(1)} %collective-permute-done.rest_8_), channel_id=1, source_target_pairs={{0,2},{2,0},{4,6},{6,4},{8,10},{10,8},{12,14},{14,12},{16,18},{18,... | collective-permute-start | bytes 589832 | tf_op jit(solution)/shard_map/ppermute | solution.py:334
  40.9 2.7 %collective-permute-start.6 = (bf16[192,512]{1,0:T(8,128)(2,1)S(1)}, bf16[192,512]{1,0:T(8,128)(2,1)S(1)}, u32[]{:S(2)}, u32[]{:S(2)}) collective-permute-start(bf16[192,512]{1,0:T(8,128)(2,1)S(1)} %collective-permute-done.5.rest_2_), channel_id=1, source_target_pairs={{0,2},{2,0},{4,6},{6,4},{8,10},{10,8},{12,14},{14,12},{16,18},{18,... | collective-permute-start | bytes 589832 | tf_op jit(solution)/shard_map/ppermute | solution.py:334
  46.2 17.4 %collective-permute-start.17 = (bf16[3,64,1792]{2,1,0:T(8,128)(2,1)S(1)}, bf16[3,64,1792]{2,1,0:T(8,128)(2,1)S(1)}, u32[]{:S(2)}, u32[]{:S(2)}) collective-permute-start(bf16[3,64,1792]{2,1,0:T(8,128)(2,1)S(1)} %collective-permute-done.16.rest_2_), channel_id=1, source_target_pairs={{0,4},{2,6},{4,0},{6,2},{8,12},{10,14},{12,8},{14,10},{16,20},{18,... | collective-permute-start | bytes 2064392 | tf_op jit(solution)/shard_map/ppermute | solution.py:334
  47.8 21.1 %collective-permute-start.18 = (bf16[3,64,1792]{2,1,0:T(8,128)(2,1)}, bf16[3,64,1792]{2,1,0:T(8,128)(2,1)}, u32[]{:S(2)}, u32[]{:S(2)}) collective-permute-start(bf16[3,64,1792]{2,1,0:T(8,128)(2,1)} %get-tuple-element.78), channel_id=1, source_target_pairs={{0,8},{2,10},{4,12},{6,14},{8,0},{10,2},{12,4},{14,6},{16,24},{18,... | collective-permute-start | bytes 2064392 | tf_op jit(solution)/shard_map/ppermute | solution.py:334
  48.7 33.1 %collective-permute-start.19 = (bf16[3,64,1792]{2,1,0:T(8,128)(2,1)}, bf16[3,64,1792]{2,1,0:T(8,128)(2,1)}, u32[]{:S(2)}, u32[]{:S(2)}) collective-permute-start(bf16[3,64,1792]{2,1,0:T(8,128)(2,1)} %get-tuple-element.79), channel_id=1, source_target_pairs={{0,24},{2,26},{4,28},{6,30},{8,16},{10,18},{12,20},{14,22},{16,8},... | collective-permute-start | bytes 2064392 | tf_op jit(solution)/shard_map/ppermute | solution.py:334
  64.5 42.8 %all-to-all-start = ((bf16[8,72,1024]{2,1,0:T(8,128)(2,1)}), bf16[8,72,1024]{2,1,0:T(8,128)(2,1)S(1)}, u32[]{:S(2)}, u32[]{:S(2)}) async-start(bf16[8,72,1024]{2,1,0:T(8,128)(2,1)} %bitcast.29), calls=%async_computation | async-start | bytes 2359296 | tf_op jit(solution)/shard_map/all_to_all | solution.py:391
  68.3 14.1 %collective-permute-start.20 = (bf16[3,64,1792]{2,1,0:T(8,128)(2,1)S(1)}, bf16[3,64,1792]{2,1,0:T(8,128)(2,1)S(1)}, u32[]{:S(2)}, u32[]{:S(2)}) collective-permute-start(bf16[3,64,1792]{2,1,0:T(8,128)(2,1)S(1)} %copy-done.4), channel_id=1, source_target_pairs={{0,2},{2,0},{4,6},{6,4},{8,10},{10,8},{12,14},{14,12},{16,18},{18,... | collective-permute-start | bytes 2064392 | tf_op jit(solution)/shard_map/ppermute | solution.py:334
  68.3 14.1 %collective-permute-start.26 = (bf16[3,64,1792]{2,1,0:T(8,128)(2,1)S(1)}, bf16[3,64,1792]{2,1,0:T(8,128)(2,1)S(1)}, u32[]{:S(2)}, u32[]{:S(2)}) collective-permute-start(bf16[3,64,1792]{2,1,0:T(8,128)(2,1)S(1)} %collective-permute-done.3.rest_8_), channel_id=1, source_target_pairs={{0,2},{2,0},{4,6},{6,4},{8,10},{10,8},{12,14},{14,12},{16,18},{18,... | collective-permute-start | bytes 2064392 | tf_op jit(solution)/shard_map/ppermute | solution.py:334
  68.8 18.5 %collective-permute-start.24 = (bf16[3,64,1792]{2,1,0:T(8,128)(2,1)}, bf16[3,64,1792]{2,1,0:T(8,128)(2,1)S(1)}, u32[]{:S(2)}, u32[]{:S(2)}) collective-permute-start(bf16[3,64,1792]{2,1,0:T(8,128)(2,1)} %collective-permute-done.18.rest_1_), channel_id=1, source_target_pairs={{0,4},{2,6},{4,0},{6,2},{8,12},{10,14},{12,8},{14,10},{16,20},{18,... | collective-permute-start | bytes 2064392 | tf_op jit(solution)/shard_map/ppermute | solution.py:334
  70.4 17.0 %collective-permute-start.21 = (bf16[3,64,1792]{2,1,0:T(8,128)(2,1)}, bf16[3,64,1792]{2,1,0:T(8,128)(2,1)S(1)}, u32[]{:S(2)}, u32[]{:S(2)}) collective-permute-start(bf16[3,64,1792]{2,1,0:T(8,128)(2,1)} %collective-permute-done.18.rest_1_), channel_id=1, source_target_pairs={{0,2},{2,0},{4,6},{6,4},{8,10},{10,8},{12,14},{14,12},{16,18},{18,... | collective-permute-start | bytes 2064392 | tf_op jit(solution)/shard_map/ppermute | solution.py:334
  81.8 19.4 %collective-permute-start.25 = (bf16[3,64,1792]{2,1,0:T(8,128)(2,1)}, bf16[3,64,1792]{2,1,0:T(8,128)(2,1)S(1)}, u32[]{:S(2)}, u32[]{:S(2)}) collective-permute-start(bf16[3,64,1792]{2,1,0:T(8,128)(2,1)} %collective-permute-done.19.rest_3_), channel_id=1, source_target_pairs={{0,4},{2,6},{4,0},{6,2},{8,12},{10,14},{12,8},{14,10},{16,20},{18,... | collective-permute-start | bytes 2064392 | tf_op jit(solution)/shard_map/ppermute | solution.py:334
  82.3 18.9 %collective-permute-start.22 = (bf16[3,64,1792]{2,1,0:T(8,128)(2,1)S(1)}, bf16[3,64,1792]{2,1,0:T(8,128)(2,1)S(1)}, u32[]{:S(2)}, u32[]{:S(2)}) collective-permute-start(bf16[3,64,1792]{2,1,0:T(8,128)(2,1)S(1)} %collective-permute-done.16.rest_2_), channel_id=1, source_target_pairs={{0,2},{2,0},{4,6},{6,4},{8,10},{10,8},{12,14},{14,12},{16,18},{18,... | collective-permute-start | bytes 2064392 | tf_op jit(solution)/shard_map/ppermute | solution.py:334
  82.4 18.8 %collective-permute-start.23 = (bf16[3,64,1792]{2,1,0:T(8,128)(2,1)}, bf16[3,64,1792]{2,1,0:T(8,128)(2,1)S(1)}, u32[]{:S(2)}, u32[]{:S(2)}) collective-permute-start(bf16[3,64,1792]{2,1,0:T(8,128)(2,1)} %collective-permute-done.19.rest_3_), channel_id=1, source_target_pairs={{0,2},{2,0},{4,6},{6,4},{8,10},{10,8},{12,14},{14,12},{16,18},{18,... | collective-permute-start | bytes 2064392 | tf_op jit(solution)/shard_map/ppermute | solution.py:334
  87.3 13.9 %collective-permute-start.27 = (bf16[3,64,1792]{2,1,0:T(8,128)(2,1)S(1)}, bf16[3,64,1792]{2,1,0:T(8,128)(2,1)S(1)}, u32[]{:S(2)}, u32[]{:S(2)}) collective-permute-start(bf16[3,64,1792]{2,1,0:T(8,128)(2,1)S(1)} %collective-permute-done.24.rest_9_), channel_id=1, source_target_pairs={{0,2},{2,0},{4,6},{6,4},{8,10},{10,8},{12,14},{14,12},{16,18},{18,... | collective-permute-start | bytes 2064392 | tf_op jit(solution)/shard_map/ppermute | solution.py:334
  87.4 13.9 %collective-permute-start.28 = (bf16[3,64,1792]{2,1,0:T(8,128)(2,1)}, bf16[3,64,1792]{2,1,0:T(8,128)(2,1)S(1)}, u32[]{:S(2)}, u32[]{:S(2)}) collective-permute-start(bf16[3,64,1792]{2,1,0:T(8,128)(2,1)} %copy-done.7), channel_id=1, source_target_pairs={{0,2},{2,0},{4,6},{6,4},{8,10},{10,8},{12,14},{14,12},{16,18},{18,... | collective-permute-start | bytes 2064392 | tf_op jit(solution)/shard_map/ppermute | solution.py:334
  118.2 14.2 %collective-permute-start.31 = (bf16[72,1024]{1,0:T(8,128)(2,1)}, bf16[72,1024]{1,0:T(8,128)(2,1)S(1)}, u32[]{:S(2)}, u32[]{:S(2)}) collective-permute-start(bf16[72,1024]{1,0:T(8,128)(2,1)} %get-tuple-element.84), channel_id=1, source_target_pairs={{0,16},{1,17},{8,24},{9,25},{16,0},{17,1},{24,8},{25,9},{2,18},{3,... | collective-permute-start | bytes 442376 | tf_op jit(solution)/shard_map/ppermute | solution.py:403
  118.3 16.0 %collective-permute-start.32 = (bf16[72,1024]{1,0:T(8,128)(2,1)}, bf16[72,1024]{1,0:T(8,128)(2,1)S(1)}, u32[]{:S(2)}, u32[]{:S(2)}) collective-permute-start(bf16[72,1024]{1,0:T(8,128)(2,1)} %get-tuple-element.85), channel_id=1, source_target_pairs={{0,24},{1,25},{8,16},{9,17},{16,8},{17,9},{24,0},{25,1},{2,26},{3,... | collective-permute-start | bytes 442376 | tf_op jit(solution)/shard_map/ppermute | solution.py:403
  118.9 20.2 %collective-permute-start.33 = (bf16[72,1024]{1,0:T(8,128)(2,1)}, bf16[72,1024]{1,0:T(8,128)(2,1)S(1)}, u32[]{:S(2)}, u32[]{:S(2)}) collective-permute-start(bf16[72,1024]{1,0:T(8,128)(2,1)} %get-tuple-element.86), channel_id=1, source_target_pairs={{0,1},{1,0},{8,9},{9,8},{16,17},{17,16},{24,25},{25,24},{2,3},{3,2... | collective-permute-start | bytes 442376 | tf_op jit(solution)/shard_map/ppermute | solution.py:403
  120.3 18.7 %collective-permute-start.34 = (bf16[72,1024]{1,0:T(8,128)(2,1)}, bf16[72,1024]{1,0:T(8,128)(2,1)S(1)}, u32[]{:S(2)}, u32[]{:S(2)}) collective-permute-start(bf16[72,1024]{1,0:T(8,128)(2,1)} %get-tuple-element.87), channel_id=1, source_target_pairs={{0,9},{1,8},{8,1},{9,0},{16,25},{17,24},{24,17},{25,16},{2,11},{3,... | collective-permute-start | bytes 442376 | tf_op jit(solution)/shard_map/ppermute | solution.py:403
  123.2 19.8 %collective-permute-start.35 = (bf16[72,1024]{1,0:T(8,128)(2,1)}, bf16[72,1024]{1,0:T(8,128)(2,1)S(1)}, u32[]{:S(2)}, u32[]{:S(2)}) collective-permute-start(bf16[72,1024]{1,0:T(8,128)(2,1)} %get-tuple-element.88), channel_id=1, source_target_pairs={{0,17},{1,16},{8,25},{9,24},{16,1},{17,0},{24,9},{25,8},{2,19},{3,... | collective-permute-start | bytes 442376 | tf_op jit(solution)/shard_map/ppermute | solution.py:403
  132.4 10.6 %collective-permute-start.36 = (bf16[72,1024]{1,0:T(8,128)(2,1)S(1)}, bf16[72,1024]{1,0:T(8,128)(2,1)S(1)}, u32[]{:S(2)}, u32[]{:S(2)}) collective-permute-start(bf16[72,1024]{1,0:T(8,128)(2,1)S(1)} %copy-done.35), channel_id=1, source_target_pairs={{0,25},{1,24},{8,17},{9,16},{16,9},{17,8},{24,1},{25,0},{2,27},{3,... | collective-permute-start | bytes 442376 | tf_op jit(solution)/shard_map/ppermute | solution.py:403
  134.3 10.8 %collective-permute-start.30 = (bf16[72,1024]{1,0:T(8,128)(2,1)}, bf16[72,1024]{1,0:T(8,128)(2,1)S(1)}, u32[]{:S(2)}, u32[]{:S(2)}) collective-permute-start(bf16[72,1024]{1,0:T(8,128)(2,1)} %get-tuple-element.83), channel_id=1, source_target_pairs={{0,8},{1,9},{8,0},{9,1},{16,24},{17,25},{24,16},{25,17},{2,10},{3,... | collective-permute-start | bytes 442376 | tf_op jit(solution)/shard_map/ppermute | solution.py:403
  (42 other events, 422.1 us)

commit v8 on v7

--- a/solution.py
+++ b/solution.py
@@ -200,13 +200,9 @@
 def expert_kernel(planes, shared, cuts, step, group, place_ref, rows_in, *rest):
     count, groups = planes * shared, len(group)
     pieces, out_refs = rest[:count], rest[count : count + groups]
-    loaded, rows_ref, full, total, sems = rest[count + groups :]
+    rows_ref, full, total, sems = rest[count + groups :]
     depth = pieces[0].shape[1]
     plane, seat = place_ref[0], place_ref[1]
-    loads = [
-        pltpu.make_async_copy(rows_in.at[place_ref[2] ^ j], loaded.at[g], sems.at[count * len(cuts) + g])
-        for g, j in enumerate(group)
-    ]
     copies = []
     for c, (low, high) in enumerate(cuts):
         for n in range(count):
@@ -215,12 +211,8 @@
             target = full.at[:, pl.ds(pl.multiple_of(at, depth), depth), pl.ds(low, high - low)]
             copies.append(pltpu.make_async_copy(pieces[n].at[:, :, pl.ds(low, high - low)], target, sems.at[c * count + n]))
             copies[-1].start()
-        if c == 0:
-            for load in loads:
-                load.start()
-    for load in loads:
-        load.wait()
-    rows_ref[...] = loaded[...].astype(jnp.float32).reshape(rows_ref.shape).astype(jnp.bfloat16)
+    loaded = [rows_in[place_ref[2] ^ j].astype(jnp.float32) for j in group]
+    rows_ref[...] = jnp.concatenate(loaded, axis=0).astype(jnp.bfloat16)
     for c, (low, high) in enumerate(cuts):
         for copy in copies[c * count : (c + 1) * count]:
             copy.wait()
@@ -249,16 +241,15 @@
     return pl.pallas_call(
         functools.partial(expert_kernel, planes, shared, cuts, step, group),
         out_shape=[jax.ShapeDtypeStruct((CAP, D), jnp.bfloat16)] * groups,
-        in_specs=[SMEM, ANY] + [ANY] * count,
+        in_specs=[SMEM, VMEM] + [ANY] * count,
         out_specs=[VMEM] * groups,
         scratch_shapes=[
-            pltpu.VMEM((groups, CAP, D), jnp.bfloat16),
             pltpu.VMEM((groups * CAP, D), jnp.bfloat16),
             pltpu.VMEM((3, D, ff), jnp.bfloat16),
             pltpu.VMEM((groups * CAP, D), jnp.float32),
-            pltpu.SemaphoreType.DMA((count * len(cuts) + groups,)),
+            pltpu.SemaphoreType.DMA((count * len(cuts),)),
         ],
-        compiler_params=pltpu.CompilerParams(vmem_limit_bytes=60 * MB),
+        compiler_params=pltpu.CompilerParams(vmem_limit_bytes=56 * MB),
         cost_estimate=pl.CostEstimate(
             flops=6 * groups * CAP * D * ff, bytes_accessed=3 * D * ff * 2, transcendentals=groups * CAP * ff
         ),
@@ -266,14 +257,11 @@
     )(place, rows, *pieces)
 
 
-def combine_kernel(target_ref, probs_ref, residual_ref, own_in, *rest):
-    returned_refs, out_ref, own_ref, sem = rest[:-3], rest[-3], rest[-2], rest[-1]
-    load = pltpu.make_async_copy(own_in, own_ref, sem.at[0])
-    load.start()
+def combine_kernel(target_ref, probs_ref, residual_ref, *rest):
+    returned_refs, out_ref = rest[:-1], rest[-1]
     rows = residual_ref.shape[0]
-    load.wait()
     slot = lax.broadcasted_iota(jnp.int32, (rows, EXPERTS * CAP), 1)
-    parts = [own_ref[...], *[ref[...] for ref in returned_refs]]
+    parts = [ref[...] for ref in returned_refs]
     parts = jnp.concatenate([part.astype(jnp.float32) for part in parts], axis=0).astype(jnp.bfloat16)
     selector = [(slot == target_ref[:, k : k + 1]).astype(jnp.float32) for k in range(TOP)]
     selector = jnp.concatenate(selector, axis=0).astype(jnp.bfloat16)
@@ -288,9 +276,8 @@
     return pl.pallas_call(
         combine_kernel,
         out_shape=jax.ShapeDtypeStruct(residual.shape, jnp.bfloat16),
-        in_specs=[VMEM] * 3 + [ANY] + [VMEM] * (len(returned) - 1),
+        in_specs=[VMEM] * (3 + len(returned)),
         out_specs=VMEM,
-        scratch_shapes=[pltpu.VMEM((CAP, D), jnp.bfloat16), pltpu.SemaphoreType.DMA((1,))],
         compiler_params=pltpu.CompilerParams(vmem_limit_bytes=24 * MB),
         name="combine",
     )(target, probs, residual, *returned)
@@ -343,6 +330,7 @@
     spot = places_of(ids)
     target = ids * CAP + spot
     back = (ids ^ mine) * CAP + spot
+    target = target.T
     order = key_order(tile_mask[0], me, world)
     own = jnp.concatenate([key_proj[0], value_proj[0]], axis=1)
     bit = world // 2
@@ -381,7 +369,7 @@
         where,
         allowed,
         queries[0],
-        target.T,
+        target,
         out_weight,
         hidden_in[0],
         moe_gain[None],

time: 148 us -> 148 us (level)
  transfers between devices with their start and end apart: 38 -> 38, of which waited for: 15 -> 15; matrix products, arithmetic and copies ran while one was open for 3% -> 3% of each run, Pallas kernels for 14% -> 15%
where the time goes in v8:
time: 148 us
  waiting for transfers between devices  64.3 us (43%)
  starting transfers between devices  38.3 us (26%)
  Pallas kernels  33.3 us (22%)
  local copies, waits for them, and re-layouts  7.45 us (5%)
  other arithmetic  2.35 us (2%)
    ppermute x30, waiting for transfers between devices, swap(): return lax.ppermute(x, ctx, [(i, i ^ bit) for i in range(world)])  54.6 us
    ppermute x30, starting transfers between devices, swap(): return lax.ppermute(x, ctx, [(i, i ^ bit) for i in range(world)])  21.7 us
    pallas_call x2, Pallas kernels, run_expert(): pl.pallas_call(functools.partial(expert_kernel, planes, shared, cuts, ste...  18.1 us
    ppermute x7, starting transfers between devices, shards(): returned[j] = lax.ppermute(x, ('plane', 'exp'), pairs) if j else x  12.8 us
    pallas_call x1, Pallas kernels, attend(): pl.pallas_call(functools.partial(attend_kernel, n), out_shape=[jax.ShapeD...  9.31 us
    ppermute x7, waiting for transfers between devices, shards(): returned[j] = lax.ppermute(x, ('plane', 'exp'), pairs) if j else x  6 us
    unnamed x74, local copies, waits for them, and re-layouts  4.96 us
    pallas_call x1, Pallas kernels, pack(): pl.pallas_call(functools.partial(pack_kernel, planes), out_shape=[jax.Sha...  4.31 us
  transfers between devices with their start and end apart: 38, of which 15 were waited for; matrix products, arithmetic and copies ran while one was open for 3% of the time, Pallas kernels for 15%

profile of v8, /device:TPU:0, one launch (start us, length us, event | category | flops | bytes accessed | tf_op | source)
XLA Modules:
  0.0 147.9 jit_solution(8326029115768757743)
XLA Ops:
  0.6 1.0 pad_maximum_fusion.rest_0_
  1.6 4.1 %collective-permute-start = (bf16[192,512]{1,0:T(8,128)(2,1)S(1)}, bf16[192,512]{1,0:T(8,128)(2,1)S(1)}, u32[]{:S(2)}, u32[]{:S(2)}) collective-permute-start(bf16[192,512]{1,0:T(8,128)(2,1)S(1)} %pad_maximum_fusion.rest_0_), channel_id=1, source_target_pairs={{0,16},{2,18},{4,20},{6,22},{8,24},{10,26},{12,28},{14,30},{16,0},... | collective-permute-start | bytes 589832 | tf_op jit(solution)/shard_map/ppermute | solution.py:321
  5.7 1.6 %collective-permute-start.7 = (bf16[192,512]{1,0:T(8,128)(2,1)S(1)}, bf16[192,512]{1,0:T(8,128)(2,1)S(1)}, u32[]{:S(2)}, u32[]{:S(2)}) collective-permute-start(bf16[192,512]{1,0:T(8,128)(2,1)S(1)} %pad_maximum_fusion.rest_0_), channel_id=1, source_target_pairs={{0,8},{2,10},{4,12},{6,14},{8,0},{10,2},{12,4},{14,6},{16,24},{18,... | collective-permute-start | bytes 589832 | tf_op jit(solution)/shard_map/ppermute | solution.py:321
  7.3 1.5 %collective-permute-start.5 = (bf16[192,512]{1,0:T(8,128)(2,1)S(1)}, bf16[192,512]{1,0:T(8,128)(2,1)S(1)}, u32[]{:S(2)}, u32[]{:S(2)}) collective-permute-start(bf16[192,512]{1,0:T(8,128)(2,1)S(1)} %pad_maximum_fusion.rest_0_), channel_id=1, source_target_pairs={{0,4},{2,6},{4,0},{6,2},{8,12},{10,14},{12,8},{14,10},{16,20},{18,... | collective-permute-start | bytes 589832 | tf_op jit(solution)/shard_map/ppermute | solution.py:321
  9.5 4.3 %pack_weights.1 = (bf16[3,64,1792]{2,1,0:T(8,128)(2,1)}, bf16[3,64,1792]{2,1,0:T(8,128)(2,1)}, bf16[3,64,1792]{2,1,0:T(8,128)(2,1)}, bf16[3,64,1792]{2,1,0:T(8,128)(2,1)}) custom-call(s32[3]{0:T(128)} %pad_add_fusion.place_ref, bf16[4,64,1792]{2,1,0:T(8,128)(2,1)} %gate_ref.1, bf16[4,64,1792]{2,1,0:T(8,128)(2,1)} %up_ref.1, bf16[4,64,1792]{2,1,0:T(8,128)(2,1)} %down_ref.1), custom_call_target="tpu_custom_call" | custom-call | tf_op jit(solution)/shard_map/pack_weights/pallas_call | solution.py:44
  18.0 1.8 %collective-permute-start.9 = (bf16[192,512]{1,0:T(8,128)(2,1)S(1)}, bf16[192,512]{1,0:T(8,128)(2,1)S(1)}, u32[]{:S(2)}, u32[]{:S(2)}) collective-permute-start(bf16[192,512]{1,0:T(8,128)(2,1)S(1)} %collective-permute-done.7.rest_4_), channel_id=1, source_target_pairs={{0,4},{2,6},{4,0},{6,2},{8,12},{10,14},{12,8},{14,10},{16,20},{18,... | collective-permute-start | bytes 589832 | tf_op jit(solution)/shard_map/ppermute | solution.py:321
  19.8 13.3 %collective-permute-done.1.rest_12_ = bf16[192,512]{1,0:T(8,128)(2,1)S(1)} collective-permute-done((bf16[192,512]{1,0:T(8,128)(2,1)S(1)}, bf16[192,512]{1,0:T(8,128)(2,1)S(1)}, u32[]{:S(2)}, u32[]{:S(2)}) %collective-permute-start.1) | collective-permute-done | bytes 196640 | tf_op jit(solution)/shard_map/ppermute | solution.py:321
  33.1 1.5 %collective-permute-start.2 = (bf16[192,512]{1,0:T(8,128)(2,1)S(1)}, bf16[192,512]{1,0:T(8,128)(2,1)S(1)}, u32[]{:S(2)}, u32[]{:S(2)}) collective-permute-start(bf16[192,512]{1,0:T(8,128)(2,1)S(1)} %collective-permute-done.1.rest_12_), channel_id=1, source_target_pairs={{0,4},{2,6},{4,0},{6,2},{8,12},{10,14},{12,8},{14,10},{16,20},{18,... | collective-permute-start | bytes 589832 | tf_op jit(solution)/shard_map/ppermute | solution.py:321
  36.1 4.8 %collective-permute-done.2.rest_14_ = bf16[192,512]{1,0:T(8,128)(2,1)S(1)} collective-permute-done((bf16[192,512]{1,0:T(8,128)(2,1)S(1)}, bf16[192,512]{1,0:T(8,128)(2,1)S(1)}, u32[]{:S(2)}, u32[]{:S(2)}) %collective-permute-start.2) | collective-permute-done | bytes 196640 | tf_op jit(solution)/shard_map/ppermute | solution.py:321
  41.5 1.6 %collective-permute-done.12.rest_10_ = bf16[192,512]{1,0:T(8,128)(2,1)S(1)} collective-permute-done((bf16[192,512]{1,0:T(8,128)(2,1)S(1)}, bf16[192,512]{1,0:T(8,128)(2,1)S(1)}, u32[]{:S(2)}, u32[]{:S(2)}) %collective-permute-start.12) | collective-permute-done | bytes 196640 | tf_op jit(solution)/shard_map/ppermute | solution.py:321
  45.0 1.1 collective-permute-done.16.rest_2_
  46.2 1.6 %collective-permute-start.17 = (bf16[3,64,1792]{2,1,0:T(8,128)(2,1)S(1)}, bf16[3,64,1792]{2,1,0:T(8,128)(2,1)S(1)}, u32[]{:S(2)}, u32[]{:S(2)}) collective-permute-start(bf16[3,64,1792]{2,1,0:T(8,128)(2,1)S(1)} %collective-permute-done.16.rest_2_), channel_id=1, source_target_pairs={{0,4},{2,6},{4,0},{6,2},{8,12},{10,14},{12,8},{14,10},{16,20},{18,... | collective-permute-start | bytes 2064392 | tf_op jit(solution)/shard_map/ppermute | solution.py:321
  48.7 1.7 %collective-permute-start.19 = (bf16[3,64,1792]{2,1,0:T(8,128)(2,1)}, bf16[3,64,1792]{2,1,0:T(8,128)(2,1)}, u32[]{:S(2)}, u32[]{:S(2)}) collective-permute-start(bf16[3,64,1792]{2,1,0:T(8,128)(2,1)} %get-tuple-element.79), channel_id=1, source_target_pairs={{0,24},{2,26},{4,28},{6,30},{8,16},{10,18},{12,20},{14,22},{16,8},... | collective-permute-start | bytes 2064392 | tf_op jit(solution)/shard_map/ppermute | solution.py:321
  51.1 9.3 %attend.1 = (bf16[192,1024]{1,0:T(8,128)(2,1)}, bf16[192,1024]{1,0:T(8,128)(2,1)}, bf16[576,1024]{1,0:T(8,128)(2,1)}) custom-call(s32[96]{0:T(128)} %convert_element_type.35.live_ref, s32[96]{0:T(128)} %get-tuple-element.49.spot_ref, bf16[8,16,128]{2,1,0:T(8,128)(2,1)} %pad.5.allowed_ref, bf16[192,1024]{1,0:T(8,128)(2,1)} %bitcast.33, ...), custom_call_target="tpu_custom_call" | custom-call | tf_op jit(solution)/shard_map/attend/pallas_call | solution.py:157
  60.4 3.2 %collective-permute-done.17.rest_10_ = bf16[3,64,1792]{2,1,0:T(8,128)(2,1)S(1)} collective-permute-done((bf16[3,64,1792]{2,1,0:T(8,128)(2,1)S(1)}, bf16[3,64,1792]{2,1,0:T(8,128)(2,1)S(1)}, u32[]{:S(2)}, u32[]{:S(2)}) %collective-permute-start.17) | collective-permute-done | bytes 688160 | tf_op jit(solution)/shard_map/ppermute | solution.py:321
  64.5 3.8 %all-to-all-start = ((bf16[8,72,1024]{2,1,0:T(8,128)(2,1)}), bf16[8,72,1024]{2,1,0:T(8,128)(2,1)S(1)}, u32[]{:S(2)}, u32[]{:S(2)}) async-start(bf16[8,72,1024]{2,1,0:T(8,128)(2,1)} %bitcast.30), calls=%async_computation | async-start | bytes 2359296 | tf_op jit(solution)/shard_map/all_to_all | solution.py:379
  68.8 1.5 %collective-permute-start.24 = (bf16[3,64,1792]{2,1,0:T(8,128)(2,1)}, bf16[3,64,1792]{2,1,0:T(8,128)(2,1)S(1)}, u32[]{:S(2)}, u32[]{:S(2)}) collective-permute-start(bf16[3,64,1792]{2,1,0:T(8,128)(2,1)} %collective-permute-done.18.rest_1_), channel_id=1, source_target_pairs={{0,4},{2,6},{4,0},{6,2},{8,12},{10,14},{12,8},{14,10},{16,20},{18,... | collective-permute-start | bytes 2064392 | tf_op jit(solution)/shard_map/ppermute | solution.py:321
  70.4 11.4 %collective-permute-done.19.rest_3_ = bf16[3,64,1792]{2,1,0:T(8,128)(2,1)} collective-permute-done((bf16[3,64,1792]{2,1,0:T(8,128)(2,1)}, bf16[3,64,1792]{2,1,0:T(8,128)(2,1)}, u32[]{:S(2)}, u32[]{:S(2)}) %collective-permute-start.19) | collective-permute-done | bytes 688160 | tf_op jit(solution)/shard_map/ppermute | solution.py:321
  82.9 4.4 %collective-permute-done.24.rest_9_ = bf16[3,64,1792]{2,1,0:T(8,128)(2,1)S(1)} collective-permute-done((bf16[3,64,1792]{2,1,0:T(8,128)(2,1)}, bf16[3,64,1792]{2,1,0:T(8,128)(2,1)S(1)}, u32[]{:S(2)}, u32[]{:S(2)}) %collective-permute-start.24) | collective-permute-done | bytes 688160 | tf_op jit(solution)/shard_map/ppermute | solution.py:321
  87.9 13.4 %collective-permute-done.25.rest_11_ = bf16[3,64,1792]{2,1,0:T(8,128)(2,1)S(1)} collective-permute-done((bf16[3,64,1792]{2,1,0:T(8,128)(2,1)}, bf16[3,64,1792]{2,1,0:T(8,128)(2,1)S(1)}, u32[]{:S(2)}, u32[]{:S(2)}) %collective-permute-start.25) | collective-permute-done | bytes 688160 | tf_op jit(solution)/shard_map/ppermute | solution.py:321
  103.5 3.8 %all-to-all-done.rows_in = bf16[8,72,1024]{2,1,0:T(8,128)(2,1)S(1)} async-done(((bf16[8,72,1024]{2,1,0:T(8,128)(2,1)}), bf16[8,72,1024]{2,1,0:T(8,128)(2,1)S(1)}, u32[]{:S(2)}, u32[]{:S(2)}) %all-to-all-start) | async-done | bytes 1179680 | tf_op jit(solution)/shard_map/all_to_all | solution.py:379
  107.3 1.1 copy-done.2
  108.3 10.2 %expert.3 = (bf16[72,1024]{1,0:T(8,128)(2,1)}, bf16[72,1024]{1,0:T(8,128)(2,1)}, bf16[72,1024]{1,0:T(8,128)(2,1)}, bf16[72,1024]{1,0:T(8,128)(2,1)}, bf16[72,1024]{1,0:T(8,128)(2,1)}, /*index=5*/bf16[72,1024]{1,0:T(8,128)(2,1)}) custom-call(s32[3]{0:T(128)} %pad_add_fusion.place_ref, bf16[8,72,1024]{2,1,0:T(8,128)(2,1)} %copy-done.2, ...), custom_call_target="tpu_custom_call" | custom-call | flops 4756340736 | bytes 11010048 | tf_op jit(solution)/shard_map/expert/pallas_call | solution.py:241
  119.1 1.5 %collective-permute-start.33 = (bf16[72,1024]{1,0:T(8,128)(2,1)}, bf16[72,1024]{1,0:T(8,128)(2,1)S(1)}, u32[]{:S(2)}, u32[]{:S(2)}) collective-permute-start(bf16[72,1024]{1,0:T(8,128)(2,1)} %get-tuple-element.86), channel_id=1, source_target_pairs={{0,1},{1,0},{8,9},{9,8},{16,17},{17,16},{24,25},{25,24},{2,3},{3,2... | collective-permute-start | bytes 442376 | tf_op jit(solution)/shard_map/ppermute | solution.py:391
  120.6 2.9 %collective-permute-start.34 = (bf16[72,1024]{1,0:T(8,128)(2,1)}, bf16[72,1024]{1,0:T(8,128)(2,1)S(1)}, u32[]{:S(2)}, u32[]{:S(2)}) collective-permute-start(bf16[72,1024]{1,0:T(8,128)(2,1)} %get-tuple-element.87), channel_id=1, source_target_pairs={{0,9},{1,8},{8,1},{9,0},{16,25},{17,24},{24,17},{25,16},{2,11},{3,... | collective-permute-start | bytes 442376 | tf_op jit(solution)/shard_map/ppermute | solution.py:391
  123.5 1.7 %collective-permute-start.35 = (bf16[72,1024]{1,0:T(8,128)(2,1)}, bf16[72,1024]{1,0:T(8,128)(2,1)S(1)}, u32[]{:S(2)}, u32[]{:S(2)}) collective-permute-start(bf16[72,1024]{1,0:T(8,128)(2,1)} %get-tuple-element.88), channel_id=1, source_target_pairs={{0,17},{1,16},{8,25},{9,24},{16,1},{17,0},{24,9},{25,8},{2,19},{3,... | collective-permute-start | bytes 442376 | tf_op jit(solution)/shard_map/ppermute | solution.py:391
  125.2 7.9 %expert.2 = (bf16[72,1024]{1,0:T(8,128)(2,1)}, bf16[72,1024]{1,0:T(8,128)(2,1)}) custom-call(s32[3]{0:T(128)} %pad_add_fusion.place_ref, bf16[8,72,1024]{2,1,0:T(8,128)(2,1)} %copy-done.2, bf16[3,64,1792]{2,1,0:T(8,128)(2,1)} %get-tuple-element.46.rest_0_, bf16[3,64,1792]{2,1,0:T(8,128)(2,1)} %collective-permute-done.18.rest_1_, ...), custom_call_target="tpu_custom_call" | custom-call | flops 1585446912 | bytes 11010048 | tf_op jit(solution)/shard_map/expert/pallas_call | solution.py:241
  133.2 1.4 collective-permute-start.36
  134.5 4.7 %collective-permute-start.30 = (bf16[72,1024]{1,0:T(8,128)(2,1)}, bf16[72,1024]{1,0:T(8,128)(2,1)S(1)}, u32[]{:S(2)}, u32[]{:S(2)}) collective-permute-start(bf16[72,1024]{1,0:T(8,128)(2,1)} %get-tuple-element.83), channel_id=1, source_target_pairs={{0,8},{1,9},{8,0},{9,1},{16,24},{17,25},{24,16},{25,17},{2,10},{3,... | collective-permute-start | bytes 442376 | tf_op jit(solution)/shard_map/ppermute | solution.py:391
  139.4 3.9 %collective-permute-done.35.rest_6_ = bf16[72,1024]{1,0:T(8,128)(2,1)S(1)} collective-permute-done((bf16[72,1024]{1,0:T(8,128)(2,1)}, bf16[72,1024]{1,0:T(8,128)(2,1)S(1)}, u32[]{:S(2)}, u32[]{:S(2)}) %collective-permute-start.35) | collective-permute-done | bytes 147488 | tf_op jit(solution)/shard_map/ppermute | solution.py:391
  143.3 2.1 %collective-permute-done.30.rest_1_ = bf16[72,1024]{1,0:T(8,128)(2,1)S(1)} collective-permute-done((bf16[72,1024]{1,0:T(8,128)(2,1)}, bf16[72,1024]{1,0:T(8,128)(2,1)S(1)}, u32[]{:S(2)}, u32[]{:S(2)}) %collective-permute-start.30) | collective-permute-done | bytes 147488 | tf_op jit(solution)/shard_map/ppermute | solution.py:391
  146.3 1.6 %combine.1 = bf16[192,1024]{1,0:T(8,128)(2,1)} custom-call(s32[192,2]{1,0:T(8,128)S(1)} %get-tuple-element.73.target_ref, f32[192,2]{1,0:T(8,128)S(1)} %bitcast.29, bf16[192,1024]{1,0:T(8,128)(2,1)S(1)} %copy-done, bf16[72,1024]{1,0:T(8,128)(2,1)S(1)} %copy-done.1, bf16[72,1024]{1,0:T(8,128)(2,1)S(1)} %collective-permute-done.30.rest_1_, ...), custom_call_target="tpu_custom_call" | custom-call | tf_op jit(solution)/shard_map/combine/pallas_call | solution.py:276
  (150 shorter events, 17.1 us)
Async XLA Ops:
  1.6 15.1 %collective-permute-start = (bf16[192,512]{1,0:T(8,128)(2,1)S(1)}, bf16[192,512]{1,0:T(8,128)(2,1)S(1)}, u32[]{:S(2)}, u32[]{:S(2)}) collective-permute-start(bf16[192,512]{1,0:T(8,128)(2,1)S(1)} %pad_maximum_fusion.rest_0_), channel_id=1, source_target_pairs={{0,16},{2,18},{4,20},{6,22},{8,24},{10,26},{12,28},{14,30},{16,0},... | collective-permute-start | bytes 589832 | tf_op jit(solution)/shard_map/ppermute | solution.py:321
  5.7 12.2 %collective-permute-start.7 = (bf16[192,512]{1,0:T(8,128)(2,1)S(1)}, bf16[192,512]{1,0:T(8,128)(2,1)S(1)}, u32[]{:S(2)}, u32[]{:S(2)}) collective-permute-start(bf16[192,512]{1,0:T(8,128)(2,1)S(1)} %pad_maximum_fusion.rest_0_), channel_id=1, source_target_pairs={{0,8},{2,10},{4,12},{6,14},{8,0},{10,2},{12,4},{14,6},{16,24},{18,... | collective-permute-start | bytes 589832 | tf_op jit(solution)/shard_map/ppermute | solution.py:321
  7.3 10.7 %collective-permute-start.5 = (bf16[192,512]{1,0:T(8,128)(2,1)S(1)}, bf16[192,512]{1,0:T(8,128)(2,1)S(1)}, u32[]{:S(2)}, u32[]{:S(2)}) collective-permute-start(bf16[192,512]{1,0:T(8,128)(2,1)S(1)} %pad_maximum_fusion.rest_0_), channel_id=1, source_target_pairs={{0,4},{2,6},{4,0},{6,2},{8,12},{10,14},{12,8},{14,10},{16,20},{18,... | collective-permute-start | bytes 589832 | tf_op jit(solution)/shard_map/ppermute | solution.py:321
  13.8 27.2 %collective-permute-start.3 = (bf16[3,64,1792]{2,1,0:T(8,128)(2,1)}, bf16[3,64,1792]{2,1,0:T(8,128)(2,1)S(1)}, u32[]{:S(2)}, u32[]{:S(2)}) collective-permute-start(bf16[3,64,1792]{2,1,0:T(8,128)(2,1)} %get-tuple-element.46.rest_0_), channel_id=1, source_target_pairs={{0,4},{2,6},{4,0},{6,2},{8,12},{10,14},{12,8},{14,10},{16,20},{18,... | collective-permute-start | bytes 2064392 | tf_op jit(solution)/shard_map/ppermute | solution.py:321
  14.3 31.8 %collective-permute-start.16 = (bf16[3,64,1792]{2,1,0:T(8,128)(2,1)}, bf16[3,64,1792]{2,1,0:T(8,128)(2,1)S(1)}, u32[]{:S(2)}, u32[]{:S(2)}) collective-permute-start(bf16[3,64,1792]{2,1,0:T(8,128)(2,1)} %get-tuple-element.55), channel_id=1, source_target_pairs={{0,16},{2,18},{4,20},{6,22},{8,24},{10,26},{12,28},{14,30},{16,0},... | collective-permute-start | bytes 2064392 | tf_op jit(solution)/shard_map/ppermute | solution.py:321
  16.7 16.4 %collective-permute-start.1 = (bf16[192,512]{1,0:T(8,128)(2,1)S(1)}, bf16[192,512]{1,0:T(8,128)(2,1)S(1)}, u32[]{:S(2)}, u32[]{:S(2)}) collective-permute-start(bf16[192,512]{1,0:T(8,128)(2,1)S(1)} %collective-permute-done.rest_8_), channel_id=1, source_target_pairs={{0,8},{2,10},{4,12},{6,14},{8,0},{10,2},{12,4},{14,6},{16,24},{18,... | collective-permute-start | bytes 589832 | tf_op jit(solution)/shard_map/ppermute | solution.py:321
  17.9 17.6 %collective-permute-start.4 = (bf16[192,512]{1,0:T(8,128)(2,1)S(1)}, bf16[192,512]{1,0:T(8,128)(2,1)S(1)}, u32[]{:S(2)}, u32[]{:S(2)}) collective-permute-start(bf16[192,512]{1,0:T(8,128)(2,1)S(1)} %pad_maximum_fusion.rest_0_), channel_id=1, source_target_pairs={{0,2},{2,0},{4,6},{6,4},{8,10},{10,8},{12,14},{14,12},{16,18},{18,... | collective-permute-start | bytes 589832 | tf_op jit(solution)/shard_map/ppermute | solution.py:321
  18.0 18.1 %collective-permute-start.9 = (bf16[192,512]{1,0:T(8,128)(2,1)S(1)}, bf16[192,512]{1,0:T(8,128)(2,1)S(1)}, u32[]{:S(2)}, u32[]{:S(2)}) collective-permute-start(bf16[192,512]{1,0:T(8,128)(2,1)S(1)} %collective-permute-done.7.rest_4_), channel_id=1, source_target_pairs={{0,4},{2,6},{4,0},{6,2},{8,12},{10,14},{12,8},{14,10},{16,20},{18,... | collective-permute-start | bytes 589832 | tf_op jit(solution)/shard_map/ppermute | solution.py:321
  33.1 7.8 %collective-permute-start.2 = (bf16[192,512]{1,0:T(8,128)(2,1)S(1)}, bf16[192,512]{1,0:T(8,128)(2,1)S(1)}, u32[]{:S(2)}, u32[]{:S(2)}) collective-permute-start(bf16[192,512]{1,0:T(8,128)(2,1)S(1)} %collective-permute-done.1.rest_12_), channel_id=1, source_target_pairs={{0,4},{2,6},{4,0},{6,2},{8,12},{10,14},{12,8},{14,10},{16,20},{18,... | collective-permute-start | bytes 589832 | tf_op jit(solution)/shard_map/ppermute | solution.py:321
  35.5 7.5 %collective-permute-start.12 = (bf16[192,512]{1,0:T(8,128)(2,1)S(1)}, bf16[192,512]{1,0:T(8,128)(2,1)S(1)}, u32[]{:S(2)}, u32[]{:S(2)}) collective-permute-start(bf16[192,512]{1,0:T(8,128)(2,1)S(1)} %collective-permute-done.rest_8_), channel_id=1, source_target_pairs={{0,4},{2,6},{4,0},{6,2},{8,12},{10,14},{12,8},{14,10},{16,20},{18,... | collective-permute-start | bytes 589832 | tf_op jit(solution)/shard_map/ppermute | solution.py:321
  36.1 7.0 %collective-permute-start.11 = (bf16[192,512]{1,0:T(8,128)(2,1)S(1)}, bf16[192,512]{1,0:T(8,128)(2,1)S(1)}, u32[]{:S(2)}, u32[]{:S(2)}) collective-permute-start(bf16[192,512]{1,0:T(8,128)(2,1)S(1)} %collective-permute-done.rest_8_), channel_id=1, source_target_pairs={{0,2},{2,0},{4,6},{6,4},{8,10},{10,8},{12,14},{14,12},{16,18},{18,... | collective-permute-start | bytes 589832 | tf_op jit(solution)/shard_map/ppermute | solution.py:321
  40.9 2.7 %collective-permute-start.6 = (bf16[192,512]{1,0:T(8,128)(2,1)S(1)}, bf16[192,512]{1,0:T(8,128)(2,1)S(1)}, u32[]{:S(2)}, u32[]{:S(2)}) collective-permute-start(bf16[192,512]{1,0:T(8,128)(2,1)S(1)} %collective-permute-done.5.rest_2_), channel_id=1, source_target_pairs={{0,2},{2,0},{4,6},{6,4},{8,10},{10,8},{12,14},{14,12},{16,18},{18,... | collective-permute-start | bytes 589832 | tf_op jit(solution)/shard_map/ppermute | solution.py:321
  46.2 17.4 %collective-permute-start.17 = (bf16[3,64,1792]{2,1,0:T(8,128)(2,1)S(1)}, bf16[3,64,1792]{2,1,0:T(8,128)(2,1)S(1)}, u32[]{:S(2)}, u32[]{:S(2)}) collective-permute-start(bf16[3,64,1792]{2,1,0:T(8,128)(2,1)S(1)} %collective-permute-done.16.rest_2_), channel_id=1, source_target_pairs={{0,4},{2,6},{4,0},{6,2},{8,12},{10,14},{12,8},{14,10},{16,20},{18,... | collective-permute-start | bytes 2064392 | tf_op jit(solution)/shard_map/ppermute | solution.py:321
  47.8 21.1 %collective-permute-start.18 = (bf16[3,64,1792]{2,1,0:T(8,128)(2,1)}, bf16[3,64,1792]{2,1,0:T(8,128)(2,1)}, u32[]{:S(2)}, u32[]{:S(2)}) collective-permute-start(bf16[3,64,1792]{2,1,0:T(8,128)(2,1)} %get-tuple-element.78), channel_id=1, source_target_pairs={{0,8},{2,10},{4,12},{6,14},{8,0},{10,2},{12,4},{14,6},{16,24},{18,... | collective-permute-start | bytes 2064392 | tf_op jit(solution)/shard_map/ppermute | solution.py:321
  48.7 33.1 %collective-permute-start.19 = (bf16[3,64,1792]{2,1,0:T(8,128)(2,1)}, bf16[3,64,1792]{2,1,0:T(8,128)(2,1)}, u32[]{:S(2)}, u32[]{:S(2)}) collective-permute-start(bf16[3,64,1792]{2,1,0:T(8,128)(2,1)} %get-tuple-element.79), channel_id=1, source_target_pairs={{0,24},{2,26},{4,28},{6,30},{8,16},{10,18},{12,20},{14,22},{16,8},... | collective-permute-start | bytes 2064392 | tf_op jit(solution)/shard_map/ppermute | solution.py:321
  64.5 42.8 %all-to-all-start = ((bf16[8,72,1024]{2,1,0:T(8,128)(2,1)}), bf16[8,72,1024]{2,1,0:T(8,128)(2,1)S(1)}, u32[]{:S(2)}, u32[]{:S(2)}) async-start(bf16[8,72,1024]{2,1,0:T(8,128)(2,1)} %bitcast.30), calls=%async_computation | async-start | bytes 2359296 | tf_op jit(solution)/shard_map/all_to_all | solution.py:379
  68.3 14.1 %collective-permute-start.20 = (bf16[3,64,1792]{2,1,0:T(8,128)(2,1)S(1)}, bf16[3,64,1792]{2,1,0:T(8,128)(2,1)S(1)}, u32[]{:S(2)}, u32[]{:S(2)}) collective-permute-start(bf16[3,64,1792]{2,1,0:T(8,128)(2,1)S(1)} %copy-done.4), channel_id=1, source_target_pairs={{0,2},{2,0},{4,6},{6,4},{8,10},{10,8},{12,14},{14,12},{16,18},{18,... | collective-permute-start | bytes 2064392 | tf_op jit(solution)/shard_map/ppermute | solution.py:321
  68.3 14.1 %collective-permute-start.26 = (bf16[3,64,1792]{2,1,0:T(8,128)(2,1)S(1)}, bf16[3,64,1792]{2,1,0:T(8,128)(2,1)S(1)}, u32[]{:S(2)}, u32[]{:S(2)}) collective-permute-start(bf16[3,64,1792]{2,1,0:T(8,128)(2,1)S(1)} %collective-permute-done.3.rest_8_), channel_id=1, source_target_pairs={{0,2},{2,0},{4,6},{6,4},{8,10},{10,8},{12,14},{14,12},{16,18},{18,... | collective-permute-start | bytes 2064392 | tf_op jit(solution)/shard_map/ppermute | solution.py:321
  68.8 18.5 %collective-permute-start.24 = (bf16[3,64,1792]{2,1,0:T(8,128)(2,1)}, bf16[3,64,1792]{2,1,0:T(8,128)(2,1)S(1)}, u32[]{:S(2)}, u32[]{:S(2)}) collective-permute-start(bf16[3,64,1792]{2,1,0:T(8,128)(2,1)} %collective-permute-done.18.rest_1_), channel_id=1, source_target_pairs={{0,4},{2,6},{4,0},{6,2},{8,12},{10,14},{12,8},{14,10},{16,20},{18,... | collective-permute-start | bytes 2064392 | tf_op jit(solution)/shard_map/ppermute | solution.py:321
  70.4 17.0 %collective-permute-start.21 = (bf16[3,64,1792]{2,1,0:T(8,128)(2,1)}, bf16[3,64,1792]{2,1,0:T(8,128)(2,1)S(1)}, u32[]{:S(2)}, u32[]{:S(2)}) collective-permute-start(bf16[3,64,1792]{2,1,0:T(8,128)(2,1)} %collective-permute-done.18.rest_1_), channel_id=1, source_target_pairs={{0,2},{2,0},{4,6},{6,4},{8,10},{10,8},{12,14},{14,12},{16,18},{18,... | collective-permute-start | bytes 2064392 | tf_op jit(solution)/shard_map/ppermute | solution.py:321
  81.8 19.4 %collective-permute-start.25 = (bf16[3,64,1792]{2,1,0:T(8,128)(2,1)}, bf16[3,64,1792]{2,1,0:T(8,128)(2,1)S(1)}, u32[]{:S(2)}, u32[]{:S(2)}) collective-permute-start(bf16[3,64,1792]{2,1,0:T(8,128)(2,1)} %collective-permute-done.19.rest_3_), channel_id=1, source_target_pairs={{0,4},{2,6},{4,0},{6,2},{8,12},{10,14},{12,8},{14,10},{16,20},{18,... | collective-permute-start | bytes 2064392 | tf_op jit(solution)/shard_map/ppermute | solution.py:321
  82.3 18.9 %collective-permute-start.22 = (bf16[3,64,1792]{2,1,0:T(8,128)(2,1)S(1)}, bf16[3,64,1792]{2,1,0:T(8,128)(2,1)S(1)}, u32[]{:S(2)}, u32[]{:S(2)}) collective-permute-start(bf16[3,64,1792]{2,1,0:T(8,128)(2,1)S(1)} %collective-permute-done.16.rest_2_), channel_id=1, source_target_pairs={{0,2},{2,0},{4,6},{6,4},{8,10},{10,8},{12,14},{14,12},{16,18},{18,... | collective-permute-start | bytes 2064392 | tf_op jit(solution)/shard_map/ppermute | solution.py:321
  82.4 18.8 %collective-permute-start.23 = (bf16[3,64,1792]{2,1,0:T(8,128)(2,1)}, bf16[3,64,1792]{2,1,0:T(8,128)(2,1)S(1)}, u32[]{:S(2)}, u32[]{:S(2)}) collective-permute-start(bf16[3,64,1792]{2,1,0:T(8,128)(2,1)} %collective-permute-done.19.rest_3_), channel_id=1, source_target_pairs={{0,2},{2,0},{4,6},{6,4},{8,10},{10,8},{12,14},{14,12},{16,18},{18,... | collective-permute-start | bytes 2064392 | tf_op jit(solution)/shard_map/ppermute | solution.py:321
  87.3 13.9 %collective-permute-start.27 = (bf16[3,64,1792]{2,1,0:T(8,128)(2,1)S(1)}, bf16[3,64,1792]{2,1,0:T(8,128)(2,1)S(1)}, u32[]{:S(2)}, u32[]{:S(2)}) collective-permute-start(bf16[3,64,1792]{2,1,0:T(8,128)(2,1)S(1)} %collective-permute-done.24.rest_9_), channel_id=1, source_target_pairs={{0,2},{2,0},{4,6},{6,4},{8,10},{10,8},{12,14},{14,12},{16,18},{18,... | collective-permute-start | bytes 2064392 | tf_op jit(solution)/shard_map/ppermute | solution.py:321
  87.4 13.9 %collective-permute-start.28 = (bf16[3,64,1792]{2,1,0:T(8,128)(2,1)}, bf16[3,64,1792]{2,1,0:T(8,128)(2,1)S(1)}, u32[]{:S(2)}, u32[]{:S(2)}) collective-permute-start(bf16[3,64,1792]{2,1,0:T(8,128)(2,1)} %copy-done.7), channel_id=1, source_target_pairs={{0,2},{2,0},{4,6},{6,4},{8,10},{10,8},{12,14},{14,12},{16,18},{18,... | collective-permute-start | bytes 2064392 | tf_op jit(solution)/shard_map/ppermute | solution.py:321
  118.5 14.6 %collective-permute-start.31 = (bf16[72,1024]{1,0:T(8,128)(2,1)}, bf16[72,1024]{1,0:T(8,128)(2,1)S(1)}, u32[]{:S(2)}, u32[]{:S(2)}) collective-permute-start(bf16[72,1024]{1,0:T(8,128)(2,1)} %get-tuple-element.84), channel_id=1, source_target_pairs={{0,16},{1,17},{8,24},{9,25},{16,0},{17,1},{24,8},{25,9},{2,18},{3,... | collective-permute-start | bytes 442376 | tf_op jit(solution)/shard_map/ppermute | solution.py:391
  118.6 16.0 %collective-permute-start.32 = (bf16[72,1024]{1,0:T(8,128)(2,1)}, bf16[72,1024]{1,0:T(8,128)(2,1)S(1)}, u32[]{:S(2)}, u32[]{:S(2)}) collective-permute-start(bf16[72,1024]{1,0:T(8,128)(2,1)} %get-tuple-element.85), channel_id=1, source_target_pairs={{0,24},{1,25},{8,16},{9,17},{16,8},{17,9},{24,0},{25,1},{2,26},{3,... | collective-permute-start | bytes 442376 | tf_op jit(solution)/shard_map/ppermute | solution.py:391
  119.1 20.2 %collective-permute-start.33 = (bf16[72,1024]{1,0:T(8,128)(2,1)}, bf16[72,1024]{1,0:T(8,128)(2,1)S(1)}, u32[]{:S(2)}, u32[]{:S(2)}) collective-permute-start(bf16[72,1024]{1,0:T(8,128)(2,1)} %get-tuple-element.86), channel_id=1, source_target_pairs={{0,1},{1,0},{8,9},{9,8},{16,17},{17,16},{24,25},{25,24},{2,3},{3,2... | collective-permute-start | bytes 442376 | tf_op jit(solution)/shard_map/ppermute | solution.py:391
  120.6 18.8 %collective-permute-start.34 = (bf16[72,1024]{1,0:T(8,128)(2,1)}, bf16[72,1024]{1,0:T(8,128)(2,1)S(1)}, u32[]{:S(2)}, u32[]{:S(2)}) collective-permute-start(bf16[72,1024]{1,0:T(8,128)(2,1)} %get-tuple-element.87), channel_id=1, source_target_pairs={{0,9},{1,8},{8,1},{9,0},{16,25},{17,24},{24,17},{25,16},{2,11},{3,... | collective-permute-start | bytes 442376 | tf_op jit(solution)/shard_map/ppermute | solution.py:391
  123.5 19.7 %collective-permute-start.35 = (bf16[72,1024]{1,0:T(8,128)(2,1)}, bf16[72,1024]{1,0:T(8,128)(2,1)S(1)}, u32[]{:S(2)}, u32[]{:S(2)}) collective-permute-start(bf16[72,1024]{1,0:T(8,128)(2,1)} %get-tuple-element.88), channel_id=1, source_target_pairs={{0,17},{1,16},{8,25},{9,24},{16,1},{17,0},{24,9},{25,8},{2,19},{3,... | collective-permute-start | bytes 442376 | tf_op jit(solution)/shard_map/ppermute | solution.py:391
  133.2 10.1 %collective-permute-start.36 = (bf16[72,1024]{1,0:T(8,128)(2,1)S(1)}, bf16[72,1024]{1,0:T(8,128)(2,1)S(1)}, u32[]{:S(2)}, u32[]{:S(2)}) collective-permute-start(bf16[72,1024]{1,0:T(8,128)(2,1)S(1)} %copy-done.35), channel_id=1, source_target_pairs={{0,25},{1,24},{8,17},{9,16},{16,9},{17,8},{24,1},{25,0},{2,27},{3,... | collective-permute-start | bytes 442376 | tf_op jit(solution)/shard_map/ppermute | solution.py:391
  134.5 10.8 %collective-permute-start.30 = (bf16[72,1024]{1,0:T(8,128)(2,1)}, bf16[72,1024]{1,0:T(8,128)(2,1)S(1)}, u32[]{:S(2)}, u32[]{:S(2)}) collective-permute-start(bf16[72,1024]{1,0:T(8,128)(2,1)} %get-tuple-element.83), channel_id=1, source_target_pairs={{0,8},{1,9},{8,0},{9,1},{16,24},{17,25},{24,16},{25,17},{2,10},{3,... | collective-permute-start | bytes 442376 | tf_op jit(solution)/shard_map/ppermute | solution.py:391
  (42 other events, 419.7 us)

commit v9 on v8

--- a/solution.py
+++ b/solution.py
@@ -236,7 +236,7 @@
     depth, ff = pieces[0].shape[1:]
     count, groups = planes * shared, len(group)
     step = 256
-    edges = [0, step, 3 * step, 5 * step, ff]
+    edges = [0, step, 3 * step, ff]
     cuts = list(zip(edges[:-1], edges[1:]))
     return pl.pallas_call(
         functools.partial(expert_kernel, planes, shared, cuts, step, group),

time: 148 us -> 148 us (level)
  no operation moved by 1% of the time
where the time goes in v9:
time: 148 us
  waiting for transfers between devices  64.4 us (44%)
  starting transfers between devices  37.6 us (25%)
  Pallas kernels  33.8 us (23%)
  local copies, waits for them, and re-layouts  7.45 us (5%)
  other arithmetic  2.35 us (2%)
    ppermute x30, waiting for transfers between devices, swap(): return lax.ppermute(x, ctx, [(i, i ^ bit) for i in range(world)])  54.6 us
    ppermute x30, starting transfers between devices, swap(): return lax.ppermute(x, ctx, [(i, i ^ bit) for i in range(world)])  21.7 us
    pallas_call x2, Pallas kernels, run_expert(): pl.pallas_call(functools.partial(expert_kernel, planes, shared, cuts, ste...  18.6 us
    ppermute x7, starting transfers between devices, shards(): returned[j] = lax.ppermute(x, ('plane', 'exp'), pairs) if j else x  12.1 us
    pallas_call x1, Pallas kernels, attend(): pl.pallas_call(functools.partial(attend_kernel, n), out_shape=[jax.ShapeD...  9.3 us
    ppermute x7, waiting for transfers between devices, shards(): returned[j] = lax.ppermute(x, ('plane', 'exp'), pairs) if j else x  6.03 us
    unnamed x74, local copies, waits for them, and re-layouts  4.96 us
    pallas_call x1, Pallas kernels, pack(): pl.pallas_call(functools.partial(pack_kernel, planes), out_shape=[jax.Sha...  4.31 us
  transfers between devices with their start and end apart: 38, of which 15 were waited for; matrix products, arithmetic and copies ran while one was open for 3% of the time, Pallas kernels for 15%

profile of v9, /device:TPU:0, one launch (start us, length us, event | category | flops | bytes accessed | tf_op | source)
XLA Modules:
  0.0 147.8 jit_solution(3978393573116103575)
XLA Ops:
  0.6 1.0 pad_maximum_fusion.rest_0_
  1.6 4.1 %collective-permute-start = (bf16[192,512]{1,0:T(8,128)(2,1)S(1)}, bf16[192,512]{1,0:T(8,128)(2,1)S(1)}, u32[]{:S(2)}, u32[]{:S(2)}) collective-permute-start(bf16[192,512]{1,0:T(8,128)(2,1)S(1)} %pad_maximum_fusion.rest_0_), channel_id=1, source_target_pairs={{0,16},{2,18},{4,20},{6,22},{8,24},{10,26},{12,28},{14,30},{16,0},... | collective-permute-start | bytes 589832 | tf_op jit(solution)/shard_map/ppermute | solution.py:321
  5.7 1.6 %collective-permute-start.7 = (bf16[192,512]{1,0:T(8,128)(2,1)S(1)}, bf16[192,512]{1,0:T(8,128)(2,1)S(1)}, u32[]{:S(2)}, u32[]{:S(2)}) collective-permute-start(bf16[192,512]{1,0:T(8,128)(2,1)S(1)} %pad_maximum_fusion.rest_0_), channel_id=1, source_target_pairs={{0,8},{2,10},{4,12},{6,14},{8,0},{10,2},{12,4},{14,6},{16,24},{18,... | collective-permute-start | bytes 589832 | tf_op jit(solution)/shard_map/ppermute | solution.py:321
  7.3 1.5 %collective-permute-start.5 = (bf16[192,512]{1,0:T(8,128)(2,1)S(1)}, bf16[192,512]{1,0:T(8,128)(2,1)S(1)}, u32[]{:S(2)}, u32[]{:S(2)}) collective-permute-start(bf16[192,512]{1,0:T(8,128)(2,1)S(1)} %pad_maximum_fusion.rest_0_), channel_id=1, source_target_pairs={{0,4},{2,6},{4,0},{6,2},{8,12},{10,14},{12,8},{14,10},{16,20},{18,... | collective-permute-start | bytes 589832 | tf_op jit(solution)/shard_map/ppermute | solution.py:321
  9.5 4.3 %pack_weights.1 = (bf16[3,64,1792]{2,1,0:T(8,128)(2,1)}, bf16[3,64,1792]{2,1,0:T(8,128)(2,1)}, bf16[3,64,1792]{2,1,0:T(8,128)(2,1)}, bf16[3,64,1792]{2,1,0:T(8,128)(2,1)}) custom-call(s32[3]{0:T(128)} %pad_add_fusion.place_ref, bf16[4,64,1792]{2,1,0:T(8,128)(2,1)} %gate_ref.1, bf16[4,64,1792]{2,1,0:T(8,128)(2,1)} %up_ref.1, bf16[4,64,1792]{2,1,0:T(8,128)(2,1)} %down_ref.1), custom_call_target="tpu_custom_call" | custom-call | tf_op jit(solution)/shard_map/pack_weights/pallas_call | solution.py:44
  18.0 1.8 %collective-permute-start.9 = (bf16[192,512]{1,0:T(8,128)(2,1)S(1)}, bf16[192,512]{1,0:T(8,128)(2,1)S(1)}, u32[]{:S(2)}, u32[]{:S(2)}) collective-permute-start(bf16[192,512]{1,0:T(8,128)(2,1)S(1)} %collective-permute-done.7.rest_4_), channel_id=1, source_target_pairs={{0,4},{2,6},{4,0},{6,2},{8,12},{10,14},{12,8},{14,10},{16,20},{18,... | collective-permute-start | bytes 589832 | tf_op jit(solution)/shard_map/ppermute | solution.py:321
  19.8 13.3 %collective-permute-done.1.rest_12_ = bf16[192,512]{1,0:T(8,128)(2,1)S(1)} collective-permute-done((bf16[192,512]{1,0:T(8,128)(2,1)S(1)}, bf16[192,512]{1,0:T(8,128)(2,1)S(1)}, u32[]{:S(2)}, u32[]{:S(2)}) %collective-permute-start.1) | collective-permute-done | bytes 196640 | tf_op jit(solution)/shard_map/ppermute | solution.py:321
  33.1 1.5 %collective-permute-start.2 = (bf16[192,512]{1,0:T(8,128)(2,1)S(1)}, bf16[192,512]{1,0:T(8,128)(2,1)S(1)}, u32[]{:S(2)}, u32[]{:S(2)}) collective-permute-start(bf16[192,512]{1,0:T(8,128)(2,1)S(1)} %collective-permute-done.1.rest_12_), channel_id=1, source_target_pairs={{0,4},{2,6},{4,0},{6,2},{8,12},{10,14},{12,8},{14,10},{16,20},{18,... | collective-permute-start | bytes 589832 | tf_op jit(solution)/shard_map/ppermute | solution.py:321
  36.1 4.8 %collective-permute-done.2.rest_14_ = bf16[192,512]{1,0:T(8,128)(2,1)S(1)} collective-permute-done((bf16[192,512]{1,0:T(8,128)(2,1)S(1)}, bf16[192,512]{1,0:T(8,128)(2,1)S(1)}, u32[]{:S(2)}, u32[]{:S(2)}) %collective-permute-start.2) | collective-permute-done | bytes 196640 | tf_op jit(solution)/shard_map/ppermute | solution.py:321
  41.5 1.6 %collective-permute-done.12.rest_10_ = bf16[192,512]{1,0:T(8,128)(2,1)S(1)} collective-permute-done((bf16[192,512]{1,0:T(8,128)(2,1)S(1)}, bf16[192,512]{1,0:T(8,128)(2,1)S(1)}, u32[]{:S(2)}, u32[]{:S(2)}) %collective-permute-start.12) | collective-permute-done | bytes 196640 | tf_op jit(solution)/shard_map/ppermute | solution.py:321
  45.0 1.1 collective-permute-done.16.rest_2_
  46.2 1.6 %collective-permute-start.17 = (bf16[3,64,1792]{2,1,0:T(8,128)(2,1)S(1)}, bf16[3,64,1792]{2,1,0:T(8,128)(2,1)S(1)}, u32[]{:S(2)}, u32[]{:S(2)}) collective-permute-start(bf16[3,64,1792]{2,1,0:T(8,128)(2,1)S(1)} %collective-permute-done.16.rest_2_), channel_id=1, source_target_pairs={{0,4},{2,6},{4,0},{6,2},{8,12},{10,14},{12,8},{14,10},{16,20},{18,... | collective-permute-start | bytes 2064392 | tf_op jit(solution)/shard_map/ppermute | solution.py:321
  48.7 1.7 %collective-permute-start.19 = (bf16[3,64,1792]{2,1,0:T(8,128)(2,1)}, bf16[3,64,1792]{2,1,0:T(8,128)(2,1)}, u32[]{:S(2)}, u32[]{:S(2)}) collective-permute-start(bf16[3,64,1792]{2,1,0:T(8,128)(2,1)} %get-tuple-element.79), channel_id=1, source_target_pairs={{0,24},{2,26},{4,28},{6,30},{8,16},{10,18},{12,20},{14,22},{16,8},... | collective-permute-start | bytes 2064392 | tf_op jit(solution)/shard_map/ppermute | solution.py:321
  51.1 9.3 %attend.1 = (bf16[192,1024]{1,0:T(8,128)(2,1)}, bf16[192,1024]{1,0:T(8,128)(2,1)}, bf16[576,1024]{1,0:T(8,128)(2,1)}) custom-call(s32[96]{0:T(128)} %convert_element_type.35.live_ref, s32[96]{0:T(128)} %get-tuple-element.49.spot_ref, bf16[8,16,128]{2,1,0:T(8,128)(2,1)} %pad.5.allowed_ref, bf16[192,1024]{1,0:T(8,128)(2,1)} %bitcast.33, ...), custom_call_target="tpu_custom_call" | custom-call | tf_op jit(solution)/shard_map/attend/pallas_call | solution.py:157
  60.4 3.2 %collective-permute-done.17.rest_10_ = bf16[3,64,1792]{2,1,0:T(8,128)(2,1)S(1)} collective-permute-done((bf16[3,64,1792]{2,1,0:T(8,128)(2,1)S(1)}, bf16[3,64,1792]{2,1,0:T(8,128)(2,1)S(1)}, u32[]{:S(2)}, u32[]{:S(2)}) %collective-permute-start.17) | collective-permute-done | bytes 688160 | tf_op jit(solution)/shard_map/ppermute | solution.py:321
  64.5 3.8 %all-to-all-start = ((bf16[8,72,1024]{2,1,0:T(8,128)(2,1)}), bf16[8,72,1024]{2,1,0:T(8,128)(2,1)S(1)}, u32[]{:S(2)}, u32[]{:S(2)}) async-start(bf16[8,72,1024]{2,1,0:T(8,128)(2,1)} %bitcast.30), calls=%async_computation | async-start | bytes 2359296 | tf_op jit(solution)/shard_map/all_to_all | solution.py:379
  68.8 1.5 %collective-permute-start.24 = (bf16[3,64,1792]{2,1,0:T(8,128)(2,1)}, bf16[3,64,1792]{2,1,0:T(8,128)(2,1)S(1)}, u32[]{:S(2)}, u32[]{:S(2)}) collective-permute-start(bf16[3,64,1792]{2,1,0:T(8,128)(2,1)} %collective-permute-done.18.rest_1_), channel_id=1, source_target_pairs={{0,4},{2,6},{4,0},{6,2},{8,12},{10,14},{12,8},{14,10},{16,20},{18,... | collective-permute-start | bytes 2064392 | tf_op jit(solution)/shard_map/ppermute | solution.py:321
  70.4 11.4 %collective-permute-done.19.rest_3_ = bf16[3,64,1792]{2,1,0:T(8,128)(2,1)} collective-permute-done((bf16[3,64,1792]{2,1,0:T(8,128)(2,1)}, bf16[3,64,1792]{2,1,0:T(8,128)(2,1)}, u32[]{:S(2)}, u32[]{:S(2)}) %collective-permute-start.19) | collective-permute-done | bytes 688160 | tf_op jit(solution)/shard_map/ppermute | solution.py:321
  82.9 4.4 %collective-permute-done.24.rest_9_ = bf16[3,64,1792]{2,1,0:T(8,128)(2,1)S(1)} collective-permute-done((bf16[3,64,1792]{2,1,0:T(8,128)(2,1)}, bf16[3,64,1792]{2,1,0:T(8,128)(2,1)S(1)}, u32[]{:S(2)}, u32[]{:S(2)}) %collective-permute-start.24) | collective-permute-done | bytes 688160 | tf_op jit(solution)/shard_map/ppermute | solution.py:321
  87.9 13.4 %collective-permute-done.25.rest_11_ = bf16[3,64,1792]{2,1,0:T(8,128)(2,1)S(1)} collective-permute-done((bf16[3,64,1792]{2,1,0:T(8,128)(2,1)}, bf16[3,64,1792]{2,1,0:T(8,128)(2,1)S(1)}, u32[]{:S(2)}, u32[]{:S(2)}) %collective-permute-start.25) | collective-permute-done | bytes 688160 | tf_op jit(solution)/shard_map/ppermute | solution.py:321
  101.3 1.0 copy-done.12
  103.5 3.8 %all-to-all-done.rows_in = bf16[8,72,1024]{2,1,0:T(8,128)(2,1)S(1)} async-done(((bf16[8,72,1024]{2,1,0:T(8,128)(2,1)}), bf16[8,72,1024]{2,1,0:T(8,128)(2,1)S(1)}, u32[]{:S(2)}, u32[]{:S(2)}) %all-to-all-start) | async-done | bytes 1179680 | tf_op jit(solution)/shard_map/all_to_all | solution.py:379
  107.3 1.1 copy-done.2
  108.3 10.0 %expert.3 = (bf16[72,1024]{1,0:T(8,128)(2,1)}, bf16[72,1024]{1,0:T(8,128)(2,1)}, bf16[72,1024]{1,0:T(8,128)(2,1)}, bf16[72,1024]{1,0:T(8,128)(2,1)}, bf16[72,1024]{1,0:T(8,128)(2,1)}, /*index=5*/bf16[72,1024]{1,0:T(8,128)(2,1)}) custom-call(s32[3]{0:T(128)} %pad_add_fusion.place_ref, bf16[8,72,1024]{2,1,0:T(8,128)(2,1)} %copy-done.2, ...), custom_call_target="tpu_custom_call" | custom-call | flops 4756340736 | bytes 11010048 | tf_op jit(solution)/shard_map/expert/pallas_call | solution.py:241
  119.0 1.5 collective-permute-start.33
  120.4 3.0 %collective-permute-start.34 = (bf16[72,1024]{1,0:T(8,128)(2,1)}, bf16[72,1024]{1,0:T(8,128)(2,1)S(1)}, u32[]{:S(2)}, u32[]{:S(2)}) collective-permute-start(bf16[72,1024]{1,0:T(8,128)(2,1)} %get-tuple-element.87), channel_id=1, source_target_pairs={{0,9},{1,8},{8,1},{9,0},{16,25},{17,24},{24,17},{25,16},{2,11},{3,... | collective-permute-start | bytes 442376 | tf_op jit(solution)/shard_map/ppermute | solution.py:391
  123.4 1.7 %collective-permute-start.35 = (bf16[72,1024]{1,0:T(8,128)(2,1)}, bf16[72,1024]{1,0:T(8,128)(2,1)S(1)}, u32[]{:S(2)}, u32[]{:S(2)}) collective-permute-start(bf16[72,1024]{1,0:T(8,128)(2,1)} %get-tuple-element.88), channel_id=1, source_target_pairs={{0,17},{1,16},{8,25},{9,24},{16,1},{17,0},{24,9},{25,8},{2,19},{3,... | collective-permute-start | bytes 442376 | tf_op jit(solution)/shard_map/ppermute | solution.py:391
  125.1 8.5 %expert.2 = (bf16[72,1024]{1,0:T(8,128)(2,1)}, bf16[72,1024]{1,0:T(8,128)(2,1)}) custom-call(s32[3]{0:T(128)} %pad_add_fusion.place_ref, bf16[8,72,1024]{2,1,0:T(8,128)(2,1)} %copy-done.2, bf16[3,64,1792]{2,1,0:T(8,128)(2,1)} %get-tuple-element.46.rest_0_, bf16[3,64,1792]{2,1,0:T(8,128)(2,1)} %collective-permute-done.18.rest_1_, ...), custom_call_target="tpu_custom_call" | custom-call | flops 1585446912 | bytes 11010048 | tf_op jit(solution)/shard_map/expert/pallas_call | solution.py:241
  134.4 4.6 %collective-permute-start.30 = (bf16[72,1024]{1,0:T(8,128)(2,1)}, bf16[72,1024]{1,0:T(8,128)(2,1)S(1)}, u32[]{:S(2)}, u32[]{:S(2)}) collective-permute-start(bf16[72,1024]{1,0:T(8,128)(2,1)} %get-tuple-element.83), channel_id=1, source_target_pairs={{0,8},{1,9},{8,0},{9,1},{16,24},{17,25},{24,16},{25,17},{2,10},{3,... | collective-permute-start | bytes 442376 | tf_op jit(solution)/shard_map/ppermute | solution.py:391
  139.2 3.9 %collective-permute-done.35.rest_6_ = bf16[72,1024]{1,0:T(8,128)(2,1)S(1)} collective-permute-done((bf16[72,1024]{1,0:T(8,128)(2,1)}, bf16[72,1024]{1,0:T(8,128)(2,1)S(1)}, u32[]{:S(2)}, u32[]{:S(2)}) %collective-permute-start.35) | collective-permute-done | bytes 147488 | tf_op jit(solution)/shard_map/ppermute | solution.py:391
  143.1 2.1 %collective-permute-done.30.rest_1_ = bf16[72,1024]{1,0:T(8,128)(2,1)S(1)} collective-permute-done((bf16[72,1024]{1,0:T(8,128)(2,1)}, bf16[72,1024]{1,0:T(8,128)(2,1)S(1)}, u32[]{:S(2)}, u32[]{:S(2)}) %collective-permute-start.30) | collective-permute-done | bytes 147488 | tf_op jit(solution)/shard_map/ppermute | solution.py:391
  146.1 1.6 %combine.1 = bf16[192,1024]{1,0:T(8,128)(2,1)} custom-call(s32[192,2]{1,0:T(8,128)S(1)} %get-tuple-element.73.target_ref, f32[192,2]{1,0:T(8,128)S(1)} %bitcast.29, bf16[192,1024]{1,0:T(8,128)(2,1)S(1)} %copy-done, bf16[72,1024]{1,0:T(8,128)(2,1)S(1)} %copy-done.1, bf16[72,1024]{1,0:T(8,128)(2,1)S(1)} %collective-permute-done.30.rest_1_, ...), custom_call_target="tpu_custom_call" | custom-call | tf_op jit(solution)/shard_map/combine/pallas_call | solution.py:276
  (150 shorter events, 17.0 us)
Async XLA Ops:
  1.6 15.1 %collective-permute-start = (bf16[192,512]{1,0:T(8,128)(2,1)S(1)}, bf16[192,512]{1,0:T(8,128)(2,1)S(1)}, u32[]{:S(2)}, u32[]{:S(2)}) collective-permute-start(bf16[192,512]{1,0:T(8,128)(2,1)S(1)} %pad_maximum_fusion.rest_0_), channel_id=1, source_target_pairs={{0,16},{2,18},{4,20},{6,22},{8,24},{10,26},{12,28},{14,30},{16,0},... | collective-permute-start | bytes 589832 | tf_op jit(solution)/shard_map/ppermute | solution.py:321
  5.7 12.2 %collective-permute-start.7 = (bf16[192,512]{1,0:T(8,128)(2,1)S(1)}, bf16[192,512]{1,0:T(8,128)(2,1)S(1)}, u32[]{:S(2)}, u32[]{:S(2)}) collective-permute-start(bf16[192,512]{1,0:T(8,128)(2,1)S(1)} %pad_maximum_fusion.rest_0_), channel_id=1, source_target_pairs={{0,8},{2,10},{4,12},{6,14},{8,0},{10,2},{12,4},{14,6},{16,24},{18,... | collective-permute-start | bytes 589832 | tf_op jit(solution)/shard_map/ppermute | solution.py:321
  7.3 10.7 %collective-permute-start.5 = (bf16[192,512]{1,0:T(8,128)(2,1)S(1)}, bf16[192,512]{1,0:T(8,128)(2,1)S(1)}, u32[]{:S(2)}, u32[]{:S(2)}) collective-permute-start(bf16[192,512]{1,0:T(8,128)(2,1)S(1)} %pad_maximum_fusion.rest_0_), channel_id=1, source_target_pairs={{0,4},{2,6},{4,0},{6,2},{8,12},{10,14},{12,8},{14,10},{16,20},{18,... | collective-permute-start | bytes 589832 | tf_op jit(solution)/shard_map/ppermute | solution.py:321
  13.8 27.2 %collective-permute-start.3 = (bf16[3,64,1792]{2,1,0:T(8,128)(2,1)}, bf16[3,64,1792]{2,1,0:T(8,128)(2,1)S(1)}, u32[]{:S(2)}, u32[]{:S(2)}) collective-permute-start(bf16[3,64,1792]{2,1,0:T(8,128)(2,1)} %get-tuple-element.46.rest_0_), channel_id=1, source_target_pairs={{0,4},{2,6},{4,0},{6,2},{8,12},{10,14},{12,8},{14,10},{16,20},{18,... | collective-permute-start | bytes 2064392 | tf_op jit(solution)/shard_map/ppermute | solution.py:321
  14.3 31.8 %collective-permute-start.16 = (bf16[3,64,1792]{2,1,0:T(8,128)(2,1)}, bf16[3,64,1792]{2,1,0:T(8,128)(2,1)S(1)}, u32[]{:S(2)}, u32[]{:S(2)}) collective-permute-start(bf16[3,64,1792]{2,1,0:T(8,128)(2,1)} %get-tuple-element.55), channel_id=1, source_target_pairs={{0,16},{2,18},{4,20},{6,22},{8,24},{10,26},{12,28},{14,30},{16,0},... | collective-permute-start | bytes 2064392 | tf_op jit(solution)/shard_map/ppermute | solution.py:321
  16.7 16.4 %collective-permute-start.1 = (bf16[192,512]{1,0:T(8,128)(2,1)S(1)}, bf16[192,512]{1,0:T(8,128)(2,1)S(1)}, u32[]{:S(2)}, u32[]{:S(2)}) collective-permute-start(bf16[192,512]{1,0:T(8,128)(2,1)S(1)} %collective-permute-done.rest_8_), channel_id=1, source_target_pairs={{0,8},{2,10},{4,12},{6,14},{8,0},{10,2},{12,4},{14,6},{16,24},{18,... | collective-permute-start | bytes 589832 | tf_op jit(solution)/shard_map/ppermute | solution.py:321
  17.9 17.6 %collective-permute-start.4 = (bf16[192,512]{1,0:T(8,128)(2,1)S(1)}, bf16[192,512]{1,0:T(8,128)(2,1)S(1)}, u32[]{:S(2)}, u32[]{:S(2)}) collective-permute-start(bf16[192,512]{1,0:T(8,128)(2,1)S(1)} %pad_maximum_fusion.rest_0_), channel_id=1, source_target_pairs={{0,2},{2,0},{4,6},{6,4},{8,10},{10,8},{12,14},{14,12},{16,18},{18,... | collective-permute-start | bytes 589832 | tf_op jit(solution)/shard_map/ppermute | solution.py:321
  18.0 18.1 %collective-permute-start.9 = (bf16[192,512]{1,0:T(8,128)(2,1)S(1)}, bf16[192,512]{1,0:T(8,128)(2,1)S(1)}, u32[]{:S(2)}, u32[]{:S(2)}) collective-permute-start(bf16[192,512]{1,0:T(8,128)(2,1)S(1)} %collective-permute-done.7.rest_4_), channel_id=1, source_target_pairs={{0,4},{2,6},{4,0},{6,2},{8,12},{10,14},{12,8},{14,10},{16,20},{18,... | collective-permute-start | bytes 589832 | tf_op jit(solution)/shard_map/ppermute | solution.py:321
  33.1 7.8 %collective-permute-start.2 = (bf16[192,512]{1,0:T(8,128)(2,1)S(1)}, bf16[192,512]{1,0:T(8,128)(2,1)S(1)}, u32[]{:S(2)}, u32[]{:S(2)}) collective-permute-start(bf16[192,512]{1,0:T(8,128)(2,1)S(1)} %collective-permute-done.1.rest_12_), channel_id=1, source_target_pairs={{0,4},{2,6},{4,0},{6,2},{8,12},{10,14},{12,8},{14,10},{16,20},{18,... | collective-permute-start | bytes 589832 | tf_op jit(solution)/shard_map/ppermute | solution.py:321
  35.5 7.5 %collective-permute-start.12 = (bf16[192,512]{1,0:T(8,128)(2,1)S(1)}, bf16[192,512]{1,0:T(8,128)(2,1)S(1)}, u32[]{:S(2)}, u32[]{:S(2)}) collective-permute-start(bf16[192,512]{1,0:T(8,128)(2,1)S(1)} %collective-permute-done.rest_8_), channel_id=1, source_target_pairs={{0,4},{2,6},{4,0},{6,2},{8,12},{10,14},{12,8},{14,10},{16,20},{18,... | collective-permute-start | bytes 589832 | tf_op jit(solution)/shard_map/ppermute | solution.py:321
  36.1 7.0 %collective-permute-start.11 = (bf16[192,512]{1,0:T(8,128)(2,1)S(1)}, bf16[192,512]{1,0:T(8,128)(2,1)S(1)}, u32[]{:S(2)}, u32[]{:S(2)}) collective-permute-start(bf16[192,512]{1,0:T(8,128)(2,1)S(1)} %collective-permute-done.rest_8_), channel_id=1, source_target_pairs={{0,2},{2,0},{4,6},{6,4},{8,10},{10,8},{12,14},{14,12},{16,18},{18,... | collective-permute-start | bytes 589832 | tf_op jit(solution)/shard_map/ppermute | solution.py:321
  40.9 2.7 %collective-permute-start.6 = (bf16[192,512]{1,0:T(8,128)(2,1)S(1)}, bf16[192,512]{1,0:T(8,128)(2,1)S(1)}, u32[]{:S(2)}, u32[]{:S(2)}) collective-permute-start(bf16[192,512]{1,0:T(8,128)(2,1)S(1)} %collective-permute-done.5.rest_2_), channel_id=1, source_target_pairs={{0,2},{2,0},{4,6},{6,4},{8,10},{10,8},{12,14},{14,12},{16,18},{18,... | collective-permute-start | bytes 589832 | tf_op jit(solution)/shard_map/ppermute | solution.py:321
  46.2 17.4 %collective-permute-start.17 = (bf16[3,64,1792]{2,1,0:T(8,128)(2,1)S(1)}, bf16[3,64,1792]{2,1,0:T(8,128)(2,1)S(1)}, u32[]{:S(2)}, u32[]{:S(2)}) collective-permute-start(bf16[3,64,1792]{2,1,0:T(8,128)(2,1)S(1)} %collective-permute-done.16.rest_2_), channel_id=1, source_target_pairs={{0,4},{2,6},{4,0},{6,2},{8,12},{10,14},{12,8},{14,10},{16,20},{18,... | collective-permute-start | bytes 2064392 | tf_op jit(solution)/shard_map/ppermute | solution.py:321
  47.8 21.1 %collective-permute-start.18 = (bf16[3,64,1792]{2,1,0:T(8,128)(2,1)}, bf16[3,64,1792]{2,1,0:T(8,128)(2,1)}, u32[]{:S(2)}, u32[]{:S(2)}) collective-permute-start(bf16[3,64,1792]{2,1,0:T(8,128)(2,1)} %get-tuple-element.78), channel_id=1, source_target_pairs={{0,8},{2,10},{4,12},{6,14},{8,0},{10,2},{12,4},{14,6},{16,24},{18,... | collective-permute-start | bytes 2064392 | tf_op jit(solution)/shard_map/ppermute | solution.py:321
  48.7 33.1 %collective-permute-start.19 = (bf16[3,64,1792]{2,1,0:T(8,128)(2,1)}, bf16[3,64,1792]{2,1,0:T(8,128)(2,1)}, u32[]{:S(2)}, u32[]{:S(2)}) collective-permute-start(bf16[3,64,1792]{2,1,0:T(8,128)(2,1)} %get-tuple-element.79), channel_id=1, source_target_pairs={{0,24},{2,26},{4,28},{6,30},{8,16},{10,18},{12,20},{14,22},{16,8},... | collective-permute-start | bytes 2064392 | tf_op jit(solution)/shard_map/ppermute | solution.py:321
  64.5 42.8 %all-to-all-start = ((bf16[8,72,1024]{2,1,0:T(8,128)(2,1)}), bf16[8,72,1024]{2,1,0:T(8,128)(2,1)S(1)}, u32[]{:S(2)}, u32[]{:S(2)}) async-start(bf16[8,72,1024]{2,1,0:T(8,128)(2,1)} %bitcast.30), calls=%async_computation | async-start | bytes 2359296 | tf_op jit(solution)/shard_map/all_to_all | solution.py:379
  68.3 14.1 %collective-permute-start.20 = (bf16[3,64,1792]{2,1,0:T(8,128)(2,1)S(1)}, bf16[3,64,1792]{2,1,0:T(8,128)(2,1)S(1)}, u32[]{:S(2)}, u32[]{:S(2)}) collective-permute-start(bf16[3,64,1792]{2,1,0:T(8,128)(2,1)S(1)} %copy-done.4), channel_id=1, source_target_pairs={{0,2},{2,0},{4,6},{6,4},{8,10},{10,8},{12,14},{14,12},{16,18},{18,... | collective-permute-start | bytes 2064392 | tf_op jit(solution)/shard_map/ppermute | solution.py:321
  68.3 14.1 %collective-permute-start.26 = (bf16[3,64,1792]{2,1,0:T(8,128)(2,1)S(1)}, bf16[3,64,1792]{2,1,0:T(8,128)(2,1)S(1)}, u32[]{:S(2)}, u32[]{:S(2)}) collective-permute-start(bf16[3,64,1792]{2,1,0:T(8,128)(2,1)S(1)} %collective-permute-done.3.rest_8_), channel_id=1, source_target_pairs={{0,2},{2,0},{4,6},{6,4},{8,10},{10,8},{12,14},{14,12},{16,18},{18,... | collective-permute-start | bytes 2064392 | tf_op jit(solution)/shard_map/ppermute | solution.py:321
  68.8 18.5 %collective-permute-start.24 = (bf16[3,64,1792]{2,1,0:T(8,128)(2,1)}, bf16[3,64,1792]{2,1,0:T(8,128)(2,1)S(1)}, u32[]{:S(2)}, u32[]{:S(2)}) collective-permute-start(bf16[3,64,1792]{2,1,0:T(8,128)(2,1)} %collective-permute-done.18.rest_1_), channel_id=1, source_target_pairs={{0,4},{2,6},{4,0},{6,2},{8,12},{10,14},{12,8},{14,10},{16,20},{18,... | collective-permute-start | bytes 2064392 | tf_op jit(solution)/shard_map/ppermute | solution.py:321
  70.4 17.0 %collective-permute-start.21 = (bf16[3,64,1792]{2,1,0:T(8,128)(2,1)}, bf16[3,64,1792]{2,1,0:T(8,128)(2,1)S(1)}, u32[]{:S(2)}, u32[]{:S(2)}) collective-permute-start(bf16[3,64,1792]{2,1,0:T(8,128)(2,1)} %collective-permute-done.18.rest_1_), channel_id=1, source_target_pairs={{0,2},{2,0},{4,6},{6,4},{8,10},{10,8},{12,14},{14,12},{16,18},{18,... | collective-permute-start | bytes 2064392 | tf_op jit(solution)/shard_map/ppermute | solution.py:321
  81.8 19.4 %collective-permute-start.25 = (bf16[3,64,1792]{2,1,0:T(8,128)(2,1)}, bf16[3,64,1792]{2,1,0:T(8,128)(2,1)S(1)}, u32[]{:S(2)}, u32[]{:S(2)}) collective-permute-start(bf16[3,64,1792]{2,1,0:T(8,128)(2,1)} %collective-permute-done.19.rest_3_), channel_id=1, source_target_pairs={{0,4},{2,6},{4,0},{6,2},{8,12},{10,14},{12,8},{14,10},{16,20},{18,... | collective-permute-start | bytes 2064392 | tf_op jit(solution)/shard_map/ppermute | solution.py:321
  82.3 18.9 %collective-permute-start.22 = (bf16[3,64,1792]{2,1,0:T(8,128)(2,1)S(1)}, bf16[3,64,1792]{2,1,0:T(8,128)(2,1)S(1)}, u32[]{:S(2)}, u32[]{:S(2)}) collective-permute-start(bf16[3,64,1792]{2,1,0:T(8,128)(2,1)S(1)} %collective-permute-done.16.rest_2_), channel_id=1, source_target_pairs={{0,2},{2,0},{4,6},{6,4},{8,10},{10,8},{12,14},{14,12},{16,18},{18,... | collective-permute-start | bytes 2064392 | tf_op jit(solution)/shard_map/ppermute | solution.py:321
  82.4 18.8 %collective-permute-start.23 = (bf16[3,64,1792]{2,1,0:T(8,128)(2,1)}, bf16[3,64,1792]{2,1,0:T(8,128)(2,1)S(1)}, u32[]{:S(2)}, u32[]{:S(2)}) collective-permute-start(bf16[3,64,1792]{2,1,0:T(8,128)(2,1)} %collective-permute-done.19.rest_3_), channel_id=1, source_target_pairs={{0,2},{2,0},{4,6},{6,4},{8,10},{10,8},{12,14},{14,12},{16,18},{18,... | collective-permute-start | bytes 2064392 | tf_op jit(solution)/shard_map/ppermute | solution.py:321
  87.3 13.9 %collective-permute-start.27 = (bf16[3,64,1792]{2,1,0:T(8,128)(2,1)S(1)}, bf16[3,64,1792]{2,1,0:T(8,128)(2,1)S(1)}, u32[]{:S(2)}, u32[]{:S(2)}) collective-permute-start(bf16[3,64,1792]{2,1,0:T(8,128)(2,1)S(1)} %collective-permute-done.24.rest_9_), channel_id=1, source_target_pairs={{0,2},{2,0},{4,6},{6,4},{8,10},{10,8},{12,14},{14,12},{16,18},{18,... | collective-permute-start | bytes 2064392 | tf_op jit(solution)/shard_map/ppermute | solution.py:321
  87.4 13.9 %collective-permute-start.28 = (bf16[3,64,1792]{2,1,0:T(8,128)(2,1)}, bf16[3,64,1792]{2,1,0:T(8,128)(2,1)S(1)}, u32[]{:S(2)}, u32[]{:S(2)}) collective-permute-start(bf16[3,64,1792]{2,1,0:T(8,128)(2,1)} %copy-done.7), channel_id=1, source_target_pairs={{0,2},{2,0},{4,6},{6,4},{8,10},{10,8},{12,14},{14,12},{16,18},{18,... | collective-permute-start | bytes 2064392 | tf_op jit(solution)/shard_map/ppermute | solution.py:321
  118.4 15.3 %collective-permute-start.31 = (bf16[72,1024]{1,0:T(8,128)(2,1)}, bf16[72,1024]{1,0:T(8,128)(2,1)S(1)}, u32[]{:S(2)}, u32[]{:S(2)}) collective-permute-start(bf16[72,1024]{1,0:T(8,128)(2,1)} %get-tuple-element.84), channel_id=1, source_target_pairs={{0,16},{1,17},{8,24},{9,25},{16,0},{17,1},{24,8},{25,9},{2,18},{3,... | collective-permute-start | bytes 442376 | tf_op jit(solution)/shard_map/ppermute | solution.py:391
  118.5 16.0 %collective-permute-start.32 = (bf16[72,1024]{1,0:T(8,128)(2,1)}, bf16[72,1024]{1,0:T(8,128)(2,1)S(1)}, u32[]{:S(2)}, u32[]{:S(2)}) collective-permute-start(bf16[72,1024]{1,0:T(8,128)(2,1)} %get-tuple-element.85), channel_id=1, source_target_pairs={{0,24},{1,25},{8,16},{9,17},{16,8},{17,9},{24,0},{25,1},{2,26},{3,... | collective-permute-start | bytes 442376 | tf_op jit(solution)/shard_map/ppermute | solution.py:391
  119.0 20.2 %collective-permute-start.33 = (bf16[72,1024]{1,0:T(8,128)(2,1)}, bf16[72,1024]{1,0:T(8,128)(2,1)S(1)}, u32[]{:S(2)}, u32[]{:S(2)}) collective-permute-start(bf16[72,1024]{1,0:T(8,128)(2,1)} %get-tuple-element.86), channel_id=1, source_target_pairs={{0,1},{1,0},{8,9},{9,8},{16,17},{17,16},{24,25},{25,24},{2,3},{3,2... | collective-permute-start | bytes 442376 | tf_op jit(solution)/shard_map/ppermute | solution.py:391
  120.4 18.8 %collective-permute-start.34 = (bf16[72,1024]{1,0:T(8,128)(2,1)}, bf16[72,1024]{1,0:T(8,128)(2,1)S(1)}, u32[]{:S(2)}, u32[]{:S(2)}) collective-permute-start(bf16[72,1024]{1,0:T(8,128)(2,1)} %get-tuple-element.87), channel_id=1, source_target_pairs={{0,9},{1,8},{8,1},{9,0},{16,25},{17,24},{24,17},{25,16},{2,11},{3,... | collective-permute-start | bytes 442376 | tf_op jit(solution)/shard_map/ppermute | solution.py:391
  123.4 19.7 %collective-permute-start.35 = (bf16[72,1024]{1,0:T(8,128)(2,1)}, bf16[72,1024]{1,0:T(8,128)(2,1)S(1)}, u32[]{:S(2)}, u32[]{:S(2)}) collective-permute-start(bf16[72,1024]{1,0:T(8,128)(2,1)} %get-tuple-element.88), channel_id=1, source_target_pairs={{0,17},{1,16},{8,25},{9,24},{16,1},{17,0},{24,9},{25,8},{2,19},{3,... | collective-permute-start | bytes 442376 | tf_op jit(solution)/shard_map/ppermute | solution.py:391
  133.7 9.4 %collective-permute-start.36 = (bf16[72,1024]{1,0:T(8,128)(2,1)S(1)}, bf16[72,1024]{1,0:T(8,128)(2,1)S(1)}, u32[]{:S(2)}, u32[]{:S(2)}) collective-permute-start(bf16[72,1024]{1,0:T(8,128)(2,1)S(1)} %copy-done.35), channel_id=1, source_target_pairs={{0,25},{1,24},{8,17},{9,16},{16,9},{17,8},{24,1},{25,0},{2,27},{3,... | collective-permute-start | bytes 442376 | tf_op jit(solution)/shard_map/ppermute | solution.py:391
  134.4 10.8 %collective-permute-start.30 = (bf16[72,1024]{1,0:T(8,128)(2,1)}, bf16[72,1024]{1,0:T(8,128)(2,1)S(1)}, u32[]{:S(2)}, u32[]{:S(2)}) collective-permute-start(bf16[72,1024]{1,0:T(8,128)(2,1)} %get-tuple-element.83), channel_id=1, source_target_pairs={{0,8},{1,9},{8,0},{9,1},{16,24},{17,25},{24,16},{25,17},{2,10},{3,... | collective-permute-start | bytes 442376 | tf_op jit(solution)/shard_map/ppermute | solution.py:391
  (42 other events, 420.2 us)
